TPU v7x, 32 devices: a whole 2x2x4 slice. The times are simulated.
32 devices in a mesh: blade: 8 (over z, y), span: 4 (over x, core).
Axes of the slice: x: 2, y: 2, z: 4, core: 2. Of those that a mesh axis runs over, the one named last changes fastest.
Arguments:
- conductance: float32 [8, 32, 32, 512], P('blade', None, 'span'), may hold values from 0.02 to 0.2
- depth_inverse: float32 [8, 32, 32], P('blade')
- surface_residual: float32 [8, 4, 32, 512], P('blade', None, 'span'), may hold values from -6 to 6
- surface_excess: float32 [8, 3, 32, 512], P('blade', None, 'span'), may hold values from 0.3 to 3
- segment_map: int32 [32, 4], P('span'), may hold values from 0 to 2047, as said below
- frame_index: int32 [3], replicated, may hold values from 0 to 3
Outputs:
- adjoint: float32 [8, 32, 32, 512], P('blade', None, 'span')
- gradient: float32 [2048], P(('blade', 'span'))
Inputs may be any that keep to these rules, and one draw needn't show every extreme that they name: `segment_map`: every entry is a passage segment number.
All inputs are finite; a program needn't handle non-finite values.
Results may differ from a plain program's by a relative error of at most 0.0003.
Values sent between devices are 32-bit elements; how exact they have to be, the bound alone decides.
No kernel may reach another device: no remote copies, remote signals or barrier semaphores. Data moves between devices by JAX's collectives and lax.ppermute only.
A program may use at most 64 MiB of HBM per device.

v0:
```python
import math

import jax
import jax.numpy as jnp
from jax import lax
from jax.sharding import PartitionSpec as P

STEPS = 3
SEGS = 2048


def with_halo(cells, sides, width):
    for axis, dim in sides:
        count = lax.axis_size(axis)
        ends = count - 1
        head = lax.slice_in_dim(cells, 0, width, axis=dim)
        tail = lax.slice_in_dim(cells, cells.shape[dim] - width, cells.shape[dim], axis=dim)
        cells = jnp.concatenate(
            [
                lax.ppermute(tail, axis, [(i, (i + 1) % count) for i in range(ends)]),
                cells,
                lax.ppermute(head, axis, [((i + 1) % count, i) for i in range(ends)]),
            ],
            axis=dim,
        )
    return cells


def lateral(lam_pad, kap_pad):
    lp = jnp.pad(lam_pad, ((0, 0), (0, 0), (0, 0), (1, 1)))
    kp = jnp.pad(kap_pad, ((0, 0), (0, 0), (0, 0), (1, 1)))
    rows = lp.shape[2] - 2
    cols = lp.shape[3] - 2
    center = lp[:, :, 1 : 1 + rows, 1 : 1 + cols]
    kcen = kp[:, :, 1 : 1 + rows, 1 : 1 + cols]
    total = jnp.zeros_like(center)
    for first, second in ((2, 1), (0, 1), (1, 2), (1, 0)):
        near = lp[:, :, first : first + rows, second : second + cols]
        knear = kp[:, :, first : first + rows, second : second + cols]
        total = total + 0.5 * (kcen + knear) * (near - center)
    return total


def per_device(
    conductance, depth_inverse, surface_residual, surface_excess, segment_map, frame_index
):
    frames = surface_residual.shape[1]
    rows = conductance.shape[2]
    cols = conductance.shape[3]
    blocks = cols // 128
    segments = SEGS
    frame_ids = jnp.arange(frames, dtype=jnp.int32)
    contribution = jnp.zeros((rows, cols), jnp.float32)
    kap_pad = with_halo(conductance, (("span", 2),), 1)
    adjoint = jnp.zeros_like(conductance)
    for step in range(STEPS - 1, -1, -1):
        if step == STEPS - 1:
            source = adjoint
        else:
            lam_pad = with_halo(adjoint, (("span", 2),), 1)
            source = adjoint + lateral(lam_pad, kap_pad)
        pick = (frame_ids == frame_index[step]).astype(jnp.float32)
        frame = jnp.sum(surface_residual[0] * pick[:, None, None], axis=0)
        source = source.at[0, 0].add(frame)
        adjoint = jnp.einsum(
            "ij,bjsc->bisc", depth_inverse[0], source, precision=lax.Precision.HIGHEST
        )
        contribution = contribution + adjoint[0, 0] * surface_excess[0, step]
    block_sums = contribution.reshape(rows, blocks, 128).sum(axis=2)
    seg_ids = jnp.arange(segments, dtype=jnp.int32)
    scale = 1.0 / math.sqrt(128.0 * STEPS)
    onehot = (segment_map.reshape(-1, 1) == seg_ids[None, :]).astype(jnp.float32)
    partial_sums = jnp.dot(
        block_sums.reshape(1, -1),
        onehot,
        precision=lax.Precision.HIGHEST,
        preferred_element_type=jnp.float32,
    )[0]
    owned = lax.psum_scatter(partial_sums, ("blade", "span"), scatter_dimension=0, tiled=True)
    return (adjoint, owned * scale)


def solution(mesh):
    placed = (
        P("blade", None, "span", None),
        P("blade", None, None),
        P("blade", None, "span", None),
        P("blade", None, "span", None),
        P("span", None),
        P(),
    )
    return jax.shard_map(
        per_device,
        mesh=mesh,
        in_specs=placed,
        out_specs=(P("blade", None, "span", None), P(("blade", "span"))),
        check_vma=False,
    )
```

profile of v0, /device:TPU:0, one launch (start us, length us, event | category | flops | bytes accessed | tf_op | source)
XLA Modules:
  0.0 76.1 jit_solution(16872286984991394931)
XLA Ops:
  0.7 1.4 %fusion.54 = (s32[1]{0:T(128)}, s32[1]{0:T(128)}, s32[1]{0:T(128)}) fusion(s32[3]{0:T(128)} %param.17), kind=kLoop, calls=%fused_computation.90 | loop fusion | bytes 24 | tf_op jit(solution)/shard_map/slice | solution.py:62
  2.1 0.6 compare_convert_fusion.2
  2.7 1.3 %compare_convert_fusion = (f32[4]{0:T(128)S(1)}, f32[4]{0:T(128)S(1)}) fusion(s32[]{:T(128)} %bitcast.16, s32[]{:T(128)} %bitcast.9), kind=kLoop, calls=%fused_computation.82 | loop fusion | flops 16 | bytes 40 | tf_op jit(solution)/shard_map/convert_element_type | solution.py:62
  4.0 0.9 %fusion.38 = (f32[8,512]{1,0:T(8,128)S(1)}, f32[8,512]{1,0:T(8,128)S(1)}, f32[8,512]{1,0:T(8,128)S(1)}) fusion(f32[1,4,8,512]{3,2,1,0:T(8,128)} %param.14, f32[4]{0:T(128)S(1)} %get-tuple-element.56, f32[4]{0:T(128)S(1)} %get-tuple-element.57, f32[4]{0:T(128)S(1)} %compare_convert_fusion.2), kind=kLoop, calls=%fused_computation.65 | loop fusion | flops 86016 | bytes 114736 | tf_op jit(solution)/shard_map/reduce_sum | solution.py:63
  5.0 0.6 fusion.27
  5.6 0.3 copy.72
  6.0 1.3 %collective-permute-start.1 = (f32[1,32,1,512]{3,2,1,0:T(1,128)S(1)}, f32[1,32,1,512]{3,2,1,0:T(1,128)S(1)}, u32[]{:S(2)}, u32[]{:S(2)}) collective-permute-start(f32[1,32,1,512]{3,2,1,0:T(1,128)S(1)} %get-tuple-element.52), channel_id=1, source_target_pairs={{1,0},{2,1},{3,2},{5,4},{6,5},{7,6},{9,8},{10,9},{11,10},{13,12},{... | collective-permute-start | bytes 196616 | tf_op jit(solution)/shard_map/ppermute | solution.py:22
  7.3 3.0 %collective-permute-start.3 = (f32[1,32,1,512]{3,2,1,0:T(1,128)S(1)}, f32[1,32,1,512]{3,2,1,0:T(1,128)S(1)}, u32[]{:S(2)}, u32[]{:S(2)}) collective-permute-start(f32[1,32,1,512]{3,2,1,0:T(1,128)S(1)} %get-tuple-element.51), channel_id=1, source_target_pairs={{0,1},{1,2},{2,3},{4,5},{5,6},{6,7},{8,9},{9,10},{10,11},{12,13},{... | collective-permute-start | bytes 196616 | tf_op jit(solution)/shard_map/ppermute | solution.py:20
  10.4 1.3 %collective-permute-start = (f32[1,32,1,512]{3,2,1,0:T(1,128)S(1)}, f32[1,32,1,512]{3,2,1,0:T(1,128)S(1)}, u32[]{:S(2)}, u32[]{:S(2)}) collective-permute-start(f32[1,32,1,512]{3,2,1,0:T(1,128)S(1)} %get-tuple-element.50), channel_id=1, source_target_pairs={{1,0},{2,1},{3,2},{5,4},{6,5},{7,6},{9,8},{10,9},{11,10},{13,12},{... | collective-permute-start | bytes 196616 | tf_op jit(solution)/shard_map/ppermute | solution.py:22
  11.7 5.1 %collective-permute-start.2 = (f32[1,32,1,512]{3,2,1,0:T(1,128)S(1)}, f32[1,32,1,512]{3,2,1,0:T(1,128)S(1)}, u32[]{:S(2)}, u32[]{:S(2)}) collective-permute-start(f32[1,32,1,512]{3,2,1,0:T(1,128)S(1)} %get-tuple-element.49), channel_id=1, source_target_pairs={{0,1},{1,2},{2,3},{4,5},{5,6},{6,7},{8,9},{9,10},{10,11},{12,13},{... | collective-permute-start | bytes 196616 | tf_op jit(solution)/shard_map/ppermute | solution.py:20
  16.8 0.8 %select_maximum_fusion.2 = f32[1,32,10,514]{3,2,1,0:T(8,128)S(1)} fusion(f32[1,32,1,512]{3,2,1,0:T(1,128)S(1)} %collective-permute-done.1, f32[1,32,8,512]{3,2,1,0:T(8,128)S(1)} %bitcast.60, f32[1,32,1,512]{3,2,1,0:T(1,128)S(1)} %collective-permute-done.3), kind=kLoop, calls=%fused_computation.4 | loop fusion | flops 1315840 | bytes 1313280 | tf_op jit(solution)/shard_map/concatenate | solution.py:18
  17.7 0.8 %select_maximum_fusion.4 = f32[1,32,10,514]{3,2,1,0:T(8,128)S(1)} fusion(f32[1,32,1,512]{3,2,1,0:T(1,128)S(1)} %collective-permute-done, f32[1,32,8,512]{3,2,1,0:T(8,128)S(1)} %copy-done.1, f32[1,32,1,512]{3,2,1,0:T(1,128)S(1)} %collective-permute-done.2), kind=kLoop, calls=%fused_computation.6 | loop fusion | flops 1315840 | bytes 1313280 | tf_op jit(solution)/shard_map/concatenate | solution.py:18
  18.5 0.9 %fusion.13 = f32[1,32,8,512]{3,2,1,0:T(8,128)S(1)} fusion(f32[1,32,8,512]{3,2,1,0:T(8,128)S(1)} %bitcast.61, f32[1,32,10,514]{3,2,1,0:T(8,128)S(1)} %select_maximum_fusion.2, f32[1,32,1,512]{3,2,1,0:T(1,128)S(1)} %collective-permute-done.3, f32[1,32,1,512]{3,2,1,0:T(1,128)S(1)} %collective-permute-done.1, f32[1,32,8,512]{3,2,1,0:T(8,128)S(1)} %copy-done.1, ...), kind=kLoop, calls=%fused_computation.26 | loop fusion | flops 3145728 | bytes 3932160 | tf_op jit(solution)/shard_map/add | solution.py:61
  19.5 0.9 %fusion.31 = f32[8,512,32]{1,2,0:T(8,128)S(1)} fusion(f32[32,8,512]{2,1,0:T(8,128)S(1)} %fusion.46, f32[1,32,32]{2,1,0:T(8,128)S(1)} %copy-done), kind=kOutput, calls=%fused_computation.53 | convolution fusion | flops 50331648 | bytes 1052672 | tf_op jit(solution)/shard_map/ij,bjsc->bisc/dot_general | solution.py:65
  20.4 0.3 copy.71
  20.8 1.3 %collective-permute-start.4 = (f32[1,32,1,512]{3,2,1,0:T(1,128)S(1)}, f32[1,32,1,512]{3,2,1,0:T(1,128)S(1)}, u32[]{:S(2)}, u32[]{:S(2)}) collective-permute-start(f32[1,32,1,512]{3,2,1,0:T(1,128)S(1)} %get-tuple-element.48), channel_id=1, source_target_pairs={{1,0},{2,1},{3,2},{5,4},{6,5},{7,6},{9,8},{10,9},{11,10},{13,12},{... | collective-permute-start | bytes 196616 | tf_op jit(solution)/shard_map/ppermute | solution.py:22
  22.1 4.7 %collective-permute-start.5 = (f32[1,32,1,512]{3,2,1,0:T(1,128)S(1)}, f32[1,32,1,512]{3,2,1,0:T(1,128)S(1)}, u32[]{:S(2)}, u32[]{:S(2)}) collective-permute-start(f32[1,32,1,512]{3,2,1,0:T(1,128)S(1)} %get-tuple-element.47), channel_id=1, source_target_pairs={{0,1},{1,2},{2,3},{4,5},{5,6},{6,7},{8,9},{9,10},{10,11},{12,13},{... | collective-permute-start | bytes 196616 | tf_op jit(solution)/shard_map/ppermute | solution.py:20
  27.0 0.7 collective-permute-done.5
  27.7 0.8 %select_maximum_fusion = f32[1,32,10,514]{3,2,1,0:T(8,128)S(1)} fusion(f32[1,32,1,512]{3,2,1,0:T(1,128)S(1)} %collective-permute-done.4, f32[1,32,8,512]{3,2,1,0:T(8,128)S(1)} %bitcast.64, f32[1,32,1,512]{3,2,1,0:T(1,128)S(1)} %collective-permute-done.5), kind=kLoop, calls=%fused_computation.2 | loop fusion | flops 1315840 | bytes 1313280 | tf_op jit(solution)/shard_map/concatenate | solution.py:18
  28.5 0.9 %fusion.3 = f32[1,32,8,512]{3,2,1,0:T(8,128)S(1)} fusion(f32[1,32,8,512]{3,2,1,0:T(8,128)S(1)} %bitcast.65, f32[1,32,10,514]{3,2,1,0:T(8,128)S(1)} %select_maximum_fusion, f32[1,32,1,512]{3,2,1,0:T(1,128)S(1)} %collective-permute-done.5, f32[1,32,1,512]{3,2,1,0:T(1,128)S(1)} %collective-permute-done.4, f32[1,32,8,512]{3,2,1,0:T(8,128)S(1)} %copy-done.1, ...), kind=kLoop, calls=%fused_computation.12 | loop fusion | flops 3145728 | bytes 3932160 | tf_op jit(solution)/shard_map/add | solution.py:61
  29.6 0.9 %fusion.29 = f32[8,512,32]{1,2,0:T(8,128)S(1)} fusion(f32[32,8,512]{2,1,0:T(8,128)S(1)} %fusion.44, f32[1,32,32]{2,1,0:T(8,128)S(1)} %copy-done), kind=kOutput, calls=%fused_computation.50 | convolution fusion | flops 50331648 | bytes 1052672 | tf_op jit(solution)/shard_map/ij,bjsc->bisc/dot_general | solution.py:65
  30.5 0.3 copy.70
  31.3 44.2 %all-reduce.4 = f32[2048]{0:T(1024)S(1)} all-reduce(f32[2048]{0:T(1024)S(1)} %bitcast.71), channel_id=2, replica_groups=mesh['blade'=8,'span'=4] {'blade','span'}, use_global_device_ids=true, to_apply=%region_4.5.clone | all-reduce | flops 2048 | bytes 16384
  75.5 0.6 dynamic-slice_multiply_fusion
  (29 shorter events, 1.1 us)
Async XLA Ops:
  0.6 4.3 %copy-start = (f32[1,32,32]{2,1,0:T(8,128)S(1)}, f32[1,32,32]{2,1,0:T(8,128)}, u32[]{:S(2)}) copy-start(f32[1,32,32]{2,1,0:T(8,128)} %param.13) | copy-start | bytes 12292
  0.6 9.7 %copy-start.1 = (f32[1,32,8,512]{3,2,1,0:T(8,128)S(1)}, f32[1,32,8,512]{3,2,1,0:T(8,128)}, u32[]{:S(2)}) copy-start(f32[1,32,8,512]{3,2,1,0:T(8,128)} %param.12) | copy-start | bytes 1572868
  6.0 10.8 %collective-permute-start.1 = (f32[1,32,1,512]{3,2,1,0:T(1,128)S(1)}, f32[1,32,1,512]{3,2,1,0:T(1,128)S(1)}, u32[]{:S(2)}, u32[]{:S(2)}) collective-permute-start(f32[1,32,1,512]{3,2,1,0:T(1,128)S(1)} %get-tuple-element.52), channel_id=1, source_target_pairs={{1,0},{2,1},{3,2},{5,4},{6,5},{7,6},{9,8},{10,9},{11,10},{13,12},{... | collective-permute-start | bytes 196616 | tf_op jit(solution)/shard_map/ppermute | solution.py:22
  7.3 9.6 %collective-permute-start.3 = (f32[1,32,1,512]{3,2,1,0:T(1,128)S(1)}, f32[1,32,1,512]{3,2,1,0:T(1,128)S(1)}, u32[]{:S(2)}, u32[]{:S(2)}) collective-permute-start(f32[1,32,1,512]{3,2,1,0:T(1,128)S(1)} %get-tuple-element.51), channel_id=1, source_target_pairs={{0,1},{1,2},{2,3},{4,5},{5,6},{6,7},{8,9},{9,10},{10,11},{12,13},{... | collective-permute-start | bytes 196616 | tf_op jit(solution)/shard_map/ppermute | solution.py:20
  10.4 7.2 %collective-permute-start = (f32[1,32,1,512]{3,2,1,0:T(1,128)S(1)}, f32[1,32,1,512]{3,2,1,0:T(1,128)S(1)}, u32[]{:S(2)}, u32[]{:S(2)}) collective-permute-start(f32[1,32,1,512]{3,2,1,0:T(1,128)S(1)} %get-tuple-element.50), channel_id=1, source_target_pairs={{1,0},{2,1},{3,2},{5,4},{6,5},{7,6},{9,8},{10,9},{11,10},{13,12},{... | collective-permute-start | bytes 196616 | tf_op jit(solution)/shard_map/ppermute | solution.py:22
  11.7 6.0 %collective-permute-start.2 = (f32[1,32,1,512]{3,2,1,0:T(1,128)S(1)}, f32[1,32,1,512]{3,2,1,0:T(1,128)S(1)}, u32[]{:S(2)}, u32[]{:S(2)}) collective-permute-start(f32[1,32,1,512]{3,2,1,0:T(1,128)S(1)} %get-tuple-element.49), channel_id=1, source_target_pairs={{0,1},{1,2},{2,3},{4,5},{5,6},{6,7},{8,9},{9,10},{10,11},{12,13},{... | collective-permute-start | bytes 196616 | tf_op jit(solution)/shard_map/ppermute | solution.py:20
  19.5 7.4 %copy-start.4 = (s32[8,4]{0,1:T(4,128)S(1)}, s32[8,4]{0,1:T(4,128)}, u32[]{:S(2)}) copy-start(s32[8,4]{0,1:T(4,128)} %param.16) | copy-start | bytes 388
  20.8 6.2 %collective-permute-start.4 = (f32[1,32,1,512]{3,2,1,0:T(1,128)S(1)}, f32[1,32,1,512]{3,2,1,0:T(1,128)S(1)}, u32[]{:S(2)}, u32[]{:S(2)}) collective-permute-start(f32[1,32,1,512]{3,2,1,0:T(1,128)S(1)} %get-tuple-element.48), channel_id=1, source_target_pairs={{1,0},{2,1},{3,2},{5,4},{6,5},{7,6},{9,8},{10,9},{11,10},{13,12},{... | collective-permute-start | bytes 196616 | tf_op jit(solution)/shard_map/ppermute | solution.py:22
  22.1 5.6 %collective-permute-start.5 = (f32[1,32,1,512]{3,2,1,0:T(1,128)S(1)}, f32[1,32,1,512]{3,2,1,0:T(1,128)S(1)}, u32[]{:S(2)}, u32[]{:S(2)}) collective-permute-start(f32[1,32,1,512]{3,2,1,0:T(1,128)S(1)} %get-tuple-element.47), channel_id=1, source_target_pairs={{0,1},{1,2},{2,3},{4,5},{5,6},{6,7},{8,9},{9,10},{10,11},{12,13},{... | collective-permute-start | bytes 196616 | tf_op jit(solution)/shard_map/ppermute | solution.py:20
  29.5 1.3 %copy-start.3 = (f32[1,3,8,512]{3,2,1,0:T(8,128)S(1)}, f32[1,3,8,512]{3,2,1,0:T(8,128)}, u32[]{:S(2)}) copy-start(f32[1,3,8,512]{3,2,1,0:T(8,128)} %param.15) | copy-start | bytes 147460
  30.8 45.3 %copy-start.2 = (f32[8,512,32]{1,0,2:T(8,128)}, f32[8,512,32]{1,0,2:T(8,128)S(1)}, u32[]{:S(2)}) copy-start(f32[8,512,32]{1,0,2:T(8,128)S(1)} %copy.70) | copy-start | bytes 1572868
where the time goes:
time: 76.5 us; the launch traced here: 76.1 us
  blocking collectives  44.2 us (58%)
  starting transfers between devices  16.7 us (22%)
  other arithmetic  7.85 us (10%)
  local copies, waits for them, and re-layouts  3.04 us (4%)
  matrix products  2.65 us (3%)
  between operations  0.96 us (1%)
    unnamed x1, blocking collectives  44.2 us
    ppermute x3, starting transfers between devices, with_halo(): lax.ppermute(tail, axis, [(i, (i + 1) % count) for i in range(ends)])  12.8 us
    ppermute x3, starting transfers between devices, with_halo(): lax.ppermute(head, axis, [((i + 1) % count, i) for i in range(ends)])  3.88 us
    concatenate x3, other arithmetic, with_halo(): jnp.concatenate([lax.ppermute(tail, axis, [(i, (i + 1) % count) for i in...  2.44 us
    dot_general x3, matrix products, per_device(): jnp.einsum('ij,bjsc->bisc', depth_inverse[0], source, precision=lax.Preci...  2.39 us
    convert_element_type x2, other arithmetic, per_device(): pick = (frame_ids == frame_index[step]).astype(jnp.float32)  1.93 us
    add x2, other arithmetic, per_device(): source = adjoint + lateral(lam_pad, kap_pad)  1.87 us
  transfers between devices with their start and end apart: 6, of which 1 were waited for; matrix products, arithmetic and copies ran while one was open for 1% of the time, Pallas kernels for 0%

commit v1 on v0

--- a/solution.py
+++ b/solution.py
@@ -76,8 +76,11 @@
         precision=lax.Precision.HIGHEST,
         preferred_element_type=jnp.float32,
     )[0]
-    owned = lax.psum_scatter(partial_sums, ("blade", "span"), scatter_dimension=0, tiled=True)
-    return (adjoint, owned * scale)
+    devices = lax.axis_size("blade") * lax.axis_size("span")
+    pieces = lax.all_to_all(
+        partial_sums.reshape(devices, -1), ("blade", "span"), 0, 0, tiled=True
+    )
+    return (adjoint, jnp.sum(pieces, axis=0) * scale)
 
 
 def solution(mesh):

time: 76.5 us -> 49.7 us (0.65)
  blocking collectives: 44.2 us -> 16.4 us
  matrix products: 2.65 us -> 3.77 us
    unnamed x1 -> x0, blocking collectives: 44.2 us -> none
    all_to_all x0 -> x1, blocking collectives: none -> 16.4 us  [per_device(): lax.all_to_all(partial_sums.reshape(devices, -1), ('blade', 'span'), 0, 0...]
    dot_general x1, matrix products: 0.26 us -> 1.37 us  [per_device(): jnp.dot(block_sums.reshape(1, -1), onehot, precision=lax.Precision.HIGHES...]
  transfers between devices with their start and end apart: 6 -> 6, of which waited for: 1 -> 1; matrix products, arithmetic and copies ran while one was open for 1% -> 2% of each run, Pallas kernels for 0% -> 0%
where the time goes in v1:
time: 49.7 us; the launch traced here: 49.4 us
  starting transfers between devices  16.6 us (33%)
  blocking collectives  16.4 us (33%)
  other arithmetic  7.85 us (16%)
  matrix products  3.77 us (8%)
  local copies, waits for them, and re-layouts  3.03 us (6%)
  between operations  0.96 us (2%)
  waiting for transfers between devices  0.87 us (2%)
    all_to_all x1, blocking collectives, per_device(): lax.all_to_all(partial_sums.reshape(devices, -1), ('blade', 'span'), 0, 0...  16.4 us
    ppermute x3, starting transfers between devices, with_halo(): lax.ppermute(tail, axis, [(i, (i + 1) % count) for i in range(ends)])  12.7 us
    ppermute x3, starting transfers between devices, with_halo(): lax.ppermute(head, axis, [((i + 1) % count, i) for i in range(ends)])  3.88 us
    concatenate x3, other arithmetic, with_halo(): jnp.concatenate([lax.ppermute(tail, axis, [(i, (i + 1) % count) for i in...  2.44 us
    dot_general x3, matrix products, per_device(): jnp.einsum('ij,bjsc->bisc', depth_inverse[0], source, precision=lax.Preci...  2.39 us
    convert_element_type x2, other arithmetic, per_device(): pick = (frame_ids == frame_index[step]).astype(jnp.float32)  1.93 us
    add x2, other arithmetic, per_device(): source = adjoint + lateral(lam_pad, kap_pad)  1.87 us
    slice x1, local copies, waits for them, and re-layouts, per_device(): pick = (frame_ids == frame_index[step]).astype(jnp.float32)  1.42 us
  transfers between devices with their start and end apart: 6, of which 1 were waited for; matrix products, arithmetic and copies ran while one was open for 2% of the time, Pallas kernels for 0%

profile of v1, /device:TPU:0, one launch (start us, length us, event | category | flops | bytes accessed | tf_op | source)
XLA Modules:
  0.0 49.4 jit_solution(7110144205263609634)
XLA Ops:
  0.7 1.4 %fusion.55 = (s32[1]{0:T(128)}, s32[1]{0:T(128)}, s32[1]{0:T(128)}) fusion(s32[3]{0:T(128)} %param.17), kind=kLoop, calls=%fused_computation.92 | loop fusion | bytes 24 | tf_op jit(solution)/shard_map/slice | solution.py:62
  2.1 0.6 %compare_convert_fusion.2 = f32[4]{0:T(128)S(1)} fusion(s32[]{:T(128)} %bitcast.1), kind=kLoop, calls=%fused_computation.86 | loop fusion | flops 8 | bytes 20 | tf_op jit(solution)/shard_map/convert_element_type | solution.py:62
  2.7 1.3 %compare_convert_fusion = (f32[4]{0:T(128)S(1)}, f32[4]{0:T(128)S(1)}) fusion(s32[]{:T(128)} %bitcast.16, s32[]{:T(128)} %bitcast.9), kind=kLoop, calls=%fused_computation.84 | loop fusion | flops 16 | bytes 40 | tf_op jit(solution)/shard_map/convert_element_type | solution.py:62
  4.0 0.9 %fusion.39 = (f32[8,512]{1,0:T(8,128)S(1)}, f32[8,512]{1,0:T(8,128)S(1)}, f32[8,512]{1,0:T(8,128)S(1)}) fusion(f32[1,4,8,512]{3,2,1,0:T(8,128)} %param.14, f32[4]{0:T(128)S(1)} %get-tuple-element.56, f32[4]{0:T(128)S(1)} %get-tuple-element.57, f32[4]{0:T(128)S(1)} %compare_convert_fusion.2), kind=kLoop, calls=%fused_computation.66 | loop fusion | flops 86016 | bytes 114736 | tf_op jit(solution)/shard_map/reduce_sum | solution.py:63
  5.0 0.6 %fusion.28 = f32[8,512,32]{1,2,0:T(8,128)S(1)} fusion(f32[1,1,8,512]{3,1,2,0:T(1,128)S(1)} %reshape.191, f32[1,32,32]{2,1,0:T(8,128)S(1)} %copy-done), kind=kOutput, calls=%fused_computation.49 | convolution fusion | flops 50331648 | bytes 544768 | tf_op jit(solution)/shard_map/ij,bjsc->bisc/dot_general | solution.py:65
  5.6 0.3 copy.73
  6.0 1.3 %collective-permute-start.1 = (f32[1,32,1,512]{3,2,1,0:T(1,128)S(1)}, f32[1,32,1,512]{3,2,1,0:T(1,128)S(1)}, u32[]{:S(2)}, u32[]{:S(2)}) collective-permute-start(f32[1,32,1,512]{3,2,1,0:T(1,128)S(1)} %get-tuple-element.52), channel_id=1, source_target_pairs={{1,0},{2,1},{3,2},{5,4},{6,5},{7,6},{9,8},{10,9},{11,10},{13,12},{... | collective-permute-start | bytes 196616 | tf_op jit(solution)/shard_map/ppermute | solution.py:22
  7.3 3.0 %collective-permute-start.3 = (f32[1,32,1,512]{3,2,1,0:T(1,128)S(1)}, f32[1,32,1,512]{3,2,1,0:T(1,128)S(1)}, u32[]{:S(2)}, u32[]{:S(2)}) collective-permute-start(f32[1,32,1,512]{3,2,1,0:T(1,128)S(1)} %get-tuple-element.51), channel_id=1, source_target_pairs={{0,1},{1,2},{2,3},{4,5},{5,6},{6,7},{8,9},{9,10},{10,11},{12,13},{... | collective-permute-start | bytes 196616 | tf_op jit(solution)/shard_map/ppermute | solution.py:20
  10.4 1.3 %collective-permute-start = (f32[1,32,1,512]{3,2,1,0:T(1,128)S(1)}, f32[1,32,1,512]{3,2,1,0:T(1,128)S(1)}, u32[]{:S(2)}, u32[]{:S(2)}) collective-permute-start(f32[1,32,1,512]{3,2,1,0:T(1,128)S(1)} %get-tuple-element.50), channel_id=1, source_target_pairs={{1,0},{2,1},{3,2},{5,4},{6,5},{7,6},{9,8},{10,9},{11,10},{13,12},{... | collective-permute-start | bytes 196616 | tf_op jit(solution)/shard_map/ppermute | solution.py:22
  11.7 5.1 %collective-permute-start.2 = (f32[1,32,1,512]{3,2,1,0:T(1,128)S(1)}, f32[1,32,1,512]{3,2,1,0:T(1,128)S(1)}, u32[]{:S(2)}, u32[]{:S(2)}) collective-permute-start(f32[1,32,1,512]{3,2,1,0:T(1,128)S(1)} %get-tuple-element.49), channel_id=1, source_target_pairs={{0,1},{1,2},{2,3},{4,5},{5,6},{6,7},{8,9},{9,10},{10,11},{12,13},{... | collective-permute-start | bytes 196616 | tf_op jit(solution)/shard_map/ppermute | solution.py:20
  17.0 0.8 %select_maximum_fusion.2 = f32[1,32,10,514]{3,2,1,0:T(8,128)S(1)} fusion(f32[1,32,1,512]{3,2,1,0:T(1,128)S(1)} %collective-permute-done.1, f32[1,32,8,512]{3,2,1,0:T(8,128)S(1)} %bitcast.63, f32[1,32,1,512]{3,2,1,0:T(1,128)S(1)} %collective-permute-done.3), kind=kLoop, calls=%fused_computation.4 | loop fusion | flops 1315840 | bytes 1313280 | tf_op jit(solution)/shard_map/concatenate | solution.py:18
  17.9 0.8 %select_maximum_fusion.4 = f32[1,32,10,514]{3,2,1,0:T(8,128)S(1)} fusion(f32[1,32,1,512]{3,2,1,0:T(1,128)S(1)} %collective-permute-done, f32[1,32,8,512]{3,2,1,0:T(8,128)S(1)} %copy-done.1, f32[1,32,1,512]{3,2,1,0:T(1,128)S(1)} %collective-permute-done.2), kind=kLoop, calls=%fused_computation.6 | loop fusion | flops 1315840 | bytes 1313280 | tf_op jit(solution)/shard_map/concatenate | solution.py:18
  18.7 0.9 %fusion.14 = f32[1,32,8,512]{3,2,1,0:T(8,128)S(1)} fusion(f32[1,32,8,512]{3,2,1,0:T(8,128)S(1)} %bitcast.64, f32[1,32,10,514]{3,2,1,0:T(8,128)S(1)} %select_maximum_fusion.2, f32[1,32,1,512]{3,2,1,0:T(1,128)S(1)} %collective-permute-done.3, f32[1,32,1,512]{3,2,1,0:T(1,128)S(1)} %collective-permute-done.1, f32[1,32,8,512]{3,2,1,0:T(8,128)S(1)} %copy-done.1, ...), kind=kLoop, calls=%fused_computation.28 | loop fusion | flops 3145728 | bytes 3932160 | tf_op jit(solution)/shard_map/add | solution.py:61
  19.7 0.9 %fusion.32 = f32[8,512,32]{1,2,0:T(8,128)S(1)} fusion(f32[32,8,512]{2,1,0:T(8,128)S(1)} %fusion.47, f32[1,32,32]{2,1,0:T(8,128)S(1)} %copy-done), kind=kOutput, calls=%fused_computation.55 | convolution fusion | flops 50331648 | bytes 1052672 | tf_op jit(solution)/shard_map/ij,bjsc->bisc/dot_general | solution.py:65
  20.6 0.3 copy.72
  21.0 1.3 %collective-permute-start.4 = (f32[1,32,1,512]{3,2,1,0:T(1,128)S(1)}, f32[1,32,1,512]{3,2,1,0:T(1,128)S(1)}, u32[]{:S(2)}, u32[]{:S(2)}) collective-permute-start(f32[1,32,1,512]{3,2,1,0:T(1,128)S(1)} %get-tuple-element.48), channel_id=1, source_target_pairs={{1,0},{2,1},{3,2},{5,4},{6,5},{7,6},{9,8},{10,9},{11,10},{13,12},{... | collective-permute-start | bytes 196616 | tf_op jit(solution)/shard_map/ppermute | solution.py:22
  22.3 4.5 %collective-permute-start.5 = (f32[1,32,1,512]{3,2,1,0:T(1,128)S(1)}, f32[1,32,1,512]{3,2,1,0:T(1,128)S(1)}, u32[]{:S(2)}, u32[]{:S(2)}) collective-permute-start(f32[1,32,1,512]{3,2,1,0:T(1,128)S(1)} %get-tuple-element.47), channel_id=1, source_target_pairs={{0,1},{1,2},{2,3},{4,5},{5,6},{6,7},{8,9},{9,10},{10,11},{12,13},{... | collective-permute-start | bytes 196616 | tf_op jit(solution)/shard_map/ppermute | solution.py:20
  26.9 0.9 %collective-permute-done.5 = f32[1,32,1,512]{3,2,1,0:T(1,128)S(1)} collective-permute-done((f32[1,32,1,512]{3,2,1,0:T(1,128)S(1)}, f32[1,32,1,512]{3,2,1,0:T(1,128)S(1)}, u32[]{:S(2)}, u32[]{:S(2)}) %collective-permute-start.5) | collective-permute-done | bytes 65568 | tf_op jit(solution)/shard_map/ppermute | solution.py:20
  27.7 0.8 %select_maximum_fusion = f32[1,32,10,514]{3,2,1,0:T(8,128)S(1)} fusion(f32[1,32,1,512]{3,2,1,0:T(1,128)S(1)} %collective-permute-done.4, f32[1,32,8,512]{3,2,1,0:T(8,128)S(1)} %bitcast.67, f32[1,32,1,512]{3,2,1,0:T(1,128)S(1)} %collective-permute-done.5), kind=kLoop, calls=%fused_computation.2 | loop fusion | flops 1315840 | bytes 1313280 | tf_op jit(solution)/shard_map/concatenate | solution.py:18
  28.6 0.9 %fusion.4 = f32[1,32,8,512]{3,2,1,0:T(8,128)S(1)} fusion(f32[1,32,8,512]{3,2,1,0:T(8,128)S(1)} %bitcast.68, f32[1,32,10,514]{3,2,1,0:T(8,128)S(1)} %select_maximum_fusion, f32[1,32,1,512]{3,2,1,0:T(1,128)S(1)} %collective-permute-done.5, f32[1,32,1,512]{3,2,1,0:T(1,128)S(1)} %collective-permute-done.4, f32[1,32,8,512]{3,2,1,0:T(8,128)S(1)} %copy-done.1, ...), kind=kLoop, calls=%fused_computation.14 | loop fusion | flops 3145728 | bytes 3932160 | tf_op jit(solution)/shard_map/add | solution.py:61
  29.6 0.9 %fusion.30 = f32[8,512,32]{1,2,0:T(8,128)S(1)} fusion(f32[32,8,512]{2,1,0:T(8,128)S(1)} %fusion.45, f32[1,32,32]{2,1,0:T(8,128)S(1)} %copy-done), kind=kOutput, calls=%fused_computation.52 | convolution fusion | flops 50331648 | bytes 1052672 | tf_op jit(solution)/shard_map/ij,bjsc->bisc/dot_general | solution.py:65
  31.1 1.4 %convolution_bitcast_fusion = f32[32,1,64]{2,1,0:T(1,128)S(1)} fusion(f32[32,1,1]{0,1,2:T(1,128)S(1)} %reshape.201, s32[32,64]{1,0:T(8,128)S(1)} %multiply_add_fusion, s32[32]{0:T(128)S(1)} %eq.67), kind=kOutput, calls=%fused_computation.9 | convolution fusion | flops 851968 | bytes 16640 | tf_op jit(solution)/shard_map/dot_general | solution.py:73
  32.5 16.4 %all_to_all.9 = f32[32,1,64]{2,1,0:T(1,128)S(1)} all-to-all(f32[32,1,64]{2,1,0:T(1,128)S(1)} %convolution_bitcast_fusion), channel_id=1, replica_groups=mesh['blade'=8,'span'=4] {'blade','span'}, dimensions={0} | all-to-all | bytes 16384 | tf_op jit(solution)/shard_map/all_to_all | solution.py:80
  48.9 0.5 %broadcast_multiply_fusion = f32[64]{0:T(128)} fusion(f32[64]{0:T(128)S(1)} %reduce_sum.49), kind=kLoop, calls=%fused_computation.87 | loop fusion | flops 64 | bytes 512 | tf_op jit(solution)/shard_map/mul | solution.py:83
  (31 shorter events, 1.2 us)
Async XLA Ops:
  0.6 4.4 %copy-start = (f32[1,32,32]{2,1,0:T(8,128)S(1)}, f32[1,32,32]{2,1,0:T(8,128)}, u32[]{:S(2)}) copy-start(f32[1,32,32]{2,1,0:T(8,128)} %param.13) | copy-start | bytes 12292
  0.6 9.7 %copy-start.1 = (f32[1,32,8,512]{3,2,1,0:T(8,128)S(1)}, f32[1,32,8,512]{3,2,1,0:T(8,128)}, u32[]{:S(2)}) copy-start(f32[1,32,8,512]{3,2,1,0:T(8,128)} %param.12) | copy-start | bytes 1572868
  0.7 16.2 %copy-start.4 = (s32[8,4]{0,1:T(4,128)S(1)}, s32[8,4]{0,1:T(4,128)}, u32[]{:S(2)}) copy-start(s32[8,4]{0,1:T(4,128)} %param.16) | copy-start | bytes 388
  6.0 11.0 %collective-permute-start.1 = (f32[1,32,1,512]{3,2,1,0:T(1,128)S(1)}, f32[1,32,1,512]{3,2,1,0:T(1,128)S(1)}, u32[]{:S(2)}, u32[]{:S(2)}) collective-permute-start(f32[1,32,1,512]{3,2,1,0:T(1,128)S(1)} %get-tuple-element.52), channel_id=1, source_target_pairs={{1,0},{2,1},{3,2},{5,4},{6,5},{7,6},{9,8},{10,9},{11,10},{13,12},{... | collective-permute-start | bytes 196616 | tf_op jit(solution)/shard_map/ppermute | solution.py:22
  7.3 9.7 %collective-permute-start.3 = (f32[1,32,1,512]{3,2,1,0:T(1,128)S(1)}, f32[1,32,1,512]{3,2,1,0:T(1,128)S(1)}, u32[]{:S(2)}, u32[]{:S(2)}) collective-permute-start(f32[1,32,1,512]{3,2,1,0:T(1,128)S(1)} %get-tuple-element.51), channel_id=1, source_target_pairs={{0,1},{1,2},{2,3},{4,5},{5,6},{6,7},{8,9},{9,10},{10,11},{12,13},{... | collective-permute-start | bytes 196616 | tf_op jit(solution)/shard_map/ppermute | solution.py:20
  10.4 7.4 %collective-permute-start = (f32[1,32,1,512]{3,2,1,0:T(1,128)S(1)}, f32[1,32,1,512]{3,2,1,0:T(1,128)S(1)}, u32[]{:S(2)}, u32[]{:S(2)}) collective-permute-start(f32[1,32,1,512]{3,2,1,0:T(1,128)S(1)} %get-tuple-element.50), channel_id=1, source_target_pairs={{1,0},{2,1},{3,2},{5,4},{6,5},{7,6},{9,8},{10,9},{11,10},{13,12},{... | collective-permute-start | bytes 196616 | tf_op jit(solution)/shard_map/ppermute | solution.py:22
  11.7 6.1 %collective-permute-start.2 = (f32[1,32,1,512]{3,2,1,0:T(1,128)S(1)}, f32[1,32,1,512]{3,2,1,0:T(1,128)S(1)}, u32[]{:S(2)}, u32[]{:S(2)}) collective-permute-start(f32[1,32,1,512]{3,2,1,0:T(1,128)S(1)} %get-tuple-element.49), channel_id=1, source_target_pairs={{0,1},{1,2},{2,3},{4,5},{5,6},{6,7},{8,9},{9,10},{10,11},{12,13},{... | collective-permute-start | bytes 196616 | tf_op jit(solution)/shard_map/ppermute | solution.py:20
  21.0 5.9 %collective-permute-start.4 = (f32[1,32,1,512]{3,2,1,0:T(1,128)S(1)}, f32[1,32,1,512]{3,2,1,0:T(1,128)S(1)}, u32[]{:S(2)}, u32[]{:S(2)}) collective-permute-start(f32[1,32,1,512]{3,2,1,0:T(1,128)S(1)} %get-tuple-element.48), channel_id=1, source_target_pairs={{1,0},{2,1},{3,2},{5,4},{6,5},{7,6},{9,8},{10,9},{11,10},{13,12},{... | collective-permute-start | bytes 196616 | tf_op jit(solution)/shard_map/ppermute | solution.py:22
  22.3 5.4 %collective-permute-start.5 = (f32[1,32,1,512]{3,2,1,0:T(1,128)S(1)}, f32[1,32,1,512]{3,2,1,0:T(1,128)S(1)}, u32[]{:S(2)}, u32[]{:S(2)}) collective-permute-start(f32[1,32,1,512]{3,2,1,0:T(1,128)S(1)} %get-tuple-element.47), channel_id=1, source_target_pairs={{0,1},{1,2},{2,3},{4,5},{5,6},{6,7},{8,9},{9,10},{10,11},{12,13},{... | collective-permute-start | bytes 196616 | tf_op jit(solution)/shard_map/ppermute | solution.py:20
  29.5 1.3 %copy-start.3 = (f32[1,3,8,512]{3,2,1,0:T(8,128)S(1)}, f32[1,3,8,512]{3,2,1,0:T(8,128)}, u32[]{:S(2)}) copy-start(f32[1,3,8,512]{3,2,1,0:T(8,128)} %param.15) | copy-start | bytes 147460
  30.8 18.6 %copy-start.2 = (f32[8,512,32]{1,0,2:T(8,128)}, f32[8,512,32]{1,0,2:T(8,128)S(1)}, u32[]{:S(2)}) copy-start(f32[8,512,32]{1,0,2:T(8,128)S(1)} %copy.71) | copy-start | bytes 1572868

commit v2 on v0

v2 whole, which is shorter than its diff:
```python
import functools
import math

import jax
import jax.numpy as jnp
from jax import lax
from jax.experimental import pallas as pl
from jax.experimental.pallas import tpu as pltpu
from jax.sharding import PartitionSpec as P

STEPS = 3
SEGS = 2048
F32 = jnp.float32
BF16 = jnp.bfloat16
VMEM = pl.BlockSpec(memory_space=pltpu.VMEM)
SMEM = pl.BlockSpec(memory_space=pltpu.SMEM)


def split(x):
    high = x.astype(BF16)
    return high, (x - high.astype(F32)).astype(BF16)


def dot(a, b):
    return jnp.dot(a, b, preferred_element_type=F32)


def dot3(a_high, a_low, b):
    b_high, b_low = split(b)
    return dot(a_high, b_high) + dot(a_high, b_low) + dot(a_low, b_high)


def iota(shape, dim):
    return lax.broadcasted_iota(jnp.int32, shape, dim)


def chord_next(x):
    last = x.ndim - 1
    size = x.shape[last]
    moved = pltpu.roll(x, size - 1, last)
    return jnp.where(iota(x.shape, last) == size - 1, 0.0, moved)


def chord_prev(x):
    last = x.ndim - 1
    moved = pltpu.roll(x, 1, last)
    return jnp.where(iota(x.shape, last) == 0, 0.0, moved)


def row_prev(x, edge):
    axis = x.ndim - 2
    return jnp.where(iota(x.shape, axis) == 0, edge, pltpu.roll(x, 1, axis))


def row_next(x, edge):
    axis = x.ndim - 2
    rows = x.shape[axis]
    return jnp.where(iota(x.shape, axis) == rows - 1, edge, pltpu.roll(x, rows - 1, axis))


def pack_kernel(k_ref, res_ref, up_ref, down_ref):
    depth, rows, _ = k_ref.shape
    frames = res_ref.shape[0]
    for out, near, far in ((up_ref, 0, 1), (down_ref, rows - 1, rows - 2)):
        out[0:depth, :] = k_ref[:, near, :]
        out[depth : 2 * depth, :] = k_ref[:, far, :]
        base = 2 * depth
        out[base : base + frames, :] = res_ref[:, near, :]
        out[base + frames : base + 2 * frames, :] = res_ref[:, far, :]


def weights_kernel(k_ref, d_ref, w_ref, mat_ref, edge_ref):
    depth, rows, cols = k_ref.shape
    size = depth * rows

    def body(i, _):
        half = 0.5 * k_ref[i]
        w_next = half + chord_next(half)
        w_prev = half + chord_prev(half)
        w_up = half + row_prev(half, 0.0)
        w_down = half + row_next(half, 0.0)
        w_ref[0, i] = 1.0 - (w_next + w_prev + w_up + w_down)
        w_ref[1, i] = w_next
        w_ref[2, i] = w_prev
        w_ref[3, i] = w_up
        w_ref[4, i] = w_down
        return 0

    lax.fori_loop(0, depth, body, 0, unroll=4)

    d_high, d_low = split(d_ref[...])
    tall = (iota((size, depth), 0) // rows == iota((size, depth), 1)).astype(BF16)
    wide = (iota((depth, size), 0) == iota((depth, size), 1) // rows).astype(BF16)
    same = iota((size, size), 0) % rows == iota((size, size), 1) % rows
    both = (iota((depth, 2 * depth), 0) == iota((depth, 2 * depth), 1) % depth).astype(BF16)
    row = iota((size, 2 * depth), 0) % rows
    left = iota((size, 2 * depth), 1) < depth
    at_edge = jnp.logical_or(
        jnp.logical_and(left, row == 0),
        jnp.logical_and(jnp.logical_not(left), row == rows - 1),
    )
    for n, part in enumerate((d_high, d_low)):
        column = dot(tall, part).astype(BF16)
        mat_ref[n] = jnp.where(same, dot(column, wide), 0.0).astype(BF16)
        edge_ref[n] = jnp.where(at_edge, dot(column, both), 0.0).astype(BF16)


def main_kernel(
    per_device_segments,
    scale,
    frame_ref,
    map_ref,
    d_ref,
    res_ref,
    excess_ref,
    w_ref,
    mat_ref,
    edge_ref,
    own_top_ref,
    own_bottom_ref,
    top_ref,
    bottom_ref,
    adj_ref,
    part_ref,
    halo_ref,
    source_ref,
    first_ref,
):
    depth, rows, cols = adj_ref.shape
    frames = res_ref.shape[0]
    size = depth * rows
    blocks = cols // 128
    span = lax.axis_index("span")
    last = lax.axis_size("span") - 1
    frame2 = frame_ref[2]
    frame1 = frame_ref[1]
    frame0 = frame_ref[0]
    base = 2 * depth
    first = d_ref[:, 0:1]
    is_surface = iota((depth, 1), 0) == 0

    halo_ref[...] = jnp.zeros_like(halo_ref)
    sources = []
    edges = ((top_ref, own_top_ref, 0, span > 0), (bottom_ref, own_bottom_ref, rows - 1, span < last))
    field_edges = []
    for got, own, row, inside in edges:
        half = 0.5 * got[0:depth, :]
        half_far = 0.5 * got[depth : 2 * depth, :]
        half_own = 0.5 * own[0:depth, :]
        f = got[pl.ds(base + frame2, 1), :]
        f_far = got[pl.ds(base + frames + frame2, 1), :]
        f_own = own[pl.ds(base + frame2, 1), :]
        g = got[pl.ds(base + frame1, 1), :]
        halo_ref[:, row, :] = half
        w_next = half + chord_next(half)
        w_prev = half + chord_prev(half)
        w_far = half + half_far
        w_own = half + half_own
        moved = (
            f
            + w_next * (chord_next(f) - f)
            + w_prev * (chord_prev(f) - f)
            + w_far * (f_far - f)
            + w_own * (f_own - f)
        )
        source = first * moved + jnp.where(is_surface, g, 0.0)
        sources.append(jnp.where(inside, source, 0.0))
        field_edges.append(f)
    halo_first = dot3(edge_ref[0], edge_ref[1], jnp.concatenate(sources, axis=0))

    f = res_ref[frame2]
    f_top, f_bottom = field_edges
    f_next = chord_next(f)
    f_prev = chord_prev(f)
    f_up = row_prev(f, f_top)
    f_down = row_next(f, f_bottom)
    row_id = iota((rows, cols), 0)
    f_edge = jnp.where(row_id == 0, f_top, f_bottom) - f

    def first_source(i, _):
        moved = (
            w_ref[0, i] * f
            + w_ref[1, i] * f_next
            + w_ref[2, i] * f_prev
            + w_ref[3, i] * f_up
            + w_ref[4, i] * f_down
            + halo_ref[i] * f_edge
        )
        source_ref[pl.ds(i * rows, rows), :] = d_ref[pl.ds(i, 1), 0:1] * moved
        return 0

    lax.fori_loop(0, depth, first_source, 0, unroll=4)
    source_ref[0:rows, :] += res_ref[frame1]
    first_ref[...] = dot3(mat_ref[0], mat_ref[1], source_ref[...])
    source_ref[...] = halo_first

    def second_source(i, _):
        v = first_ref[pl.ds(i * rows, rows), :]
        edge = source_ref[pl.ds(i * rows, rows), :]
        source_ref[pl.ds(i * rows, rows), :] = (
            w_ref[0, i] * v
            + w_ref[1, i] * chord_next(v)
            + w_ref[2, i] * chord_prev(v)
            + w_ref[3, i] * row_prev(v, edge)
            + w_ref[4, i] * row_next(v, edge)
            + halo_ref[i] * (edge - v)
        )
        return 0

    lax.fori_loop(0, depth, second_source, 0, unroll=4)
    source_ref[0:rows, :] += res_ref[frame0]
    result = dot3(mat_ref[0], mat_ref[1], source_ref[...])
    adj_ref[...] = result.reshape(depth, rows, cols)

    contribution = (
        d_ref[0:1, 0:1] * f * excess_ref[2]
        + first_ref[0:rows, :] * excess_ref[1]
        + result[0:rows, :] * excess_ref[0]
    ) * scale
    owners = part_ref.shape[0]
    lanes = part_ref.shape[-1]
    shape = (owners, 128)
    lane = iota(shape, 1)
    segment = jnp.where(lane < lanes, iota(shape, 0) * lanes + lane, -1)
    total = jnp.zeros(shape, F32)
    for block in range(blocks):
        sums = jnp.sum(contribution[:, block * 128 : (block + 1) * 128], axis=1, keepdims=True)
        for row in range(rows):
            total += jnp.where(segment == map_ref[row, block], sums[row : row + 1, :], 0.0)
    part_ref[...] = total[:, :lanes].reshape(part_ref.shape)


def per_device(
    conductance, depth_inverse, surface_residual, surface_excess, segment_map, frame_index
):
    _, depth, rows, cols = conductance.shape
    frames = surface_residual.shape[1]
    k = conductance[0]
    inverse = depth_inverse[0]
    residual = surface_residual[0]
    excess = surface_excess[0]
    size = depth * rows
    count = lax.axis_size("span")
    devices = count * lax.axis_size("blade")
    lanes = SEGS // devices
    packed = jax.ShapeDtypeStruct((2 * (depth + frames), cols), F32)
    up, down = pl.pallas_call(
        pack_kernel,
        out_shape=(packed, packed),
        in_specs=[VMEM] * 2,
        out_specs=(VMEM,) * 2,
        name="pack_edges",
    )(k, residual)
    top = lax.ppermute(down, "span", [(i, i + 1) for i in range(count - 1)])
    bottom = lax.ppermute(up, "span", [(i + 1, i) for i in range(count - 1)])
    weights, mat, edge = pl.pallas_call(
        weights_kernel,
        out_shape=(
            jax.ShapeDtypeStruct((5, depth, rows, cols), F32),
            jax.ShapeDtypeStruct((2, size, size), BF16),
            jax.ShapeDtypeStruct((2, size, 2 * depth), BF16),
        ),
        in_specs=[VMEM] * 2,
        out_specs=(VMEM,) * 3,
        compiler_params=pltpu.CompilerParams(vmem_limit_bytes=24 * 2**20),
        name="weights",
    )(k, inverse)
    scale = 1.0 / math.sqrt(128.0 * STEPS)
    adjoint, partial = pl.pallas_call(
        functools.partial(main_kernel, lanes, scale),
        out_shape=(
            jax.ShapeDtypeStruct((depth, rows, cols), F32),
            jax.ShapeDtypeStruct((devices, lanes), F32),
        ),
        in_specs=[SMEM, SMEM] + [VMEM] * 10,
        out_specs=(VMEM,) * 2,
        scratch_shapes=[pltpu.VMEM((depth, rows, cols), F32)] + [pltpu.VMEM((size, cols), F32)] * 2,
        compiler_params=pltpu.CompilerParams(vmem_limit_bytes=24 * 2**20),
        name="steps",
    )(
        frame_index,
        segment_map,
        inverse,
        residual,
        excess,
        weights,
        mat,
        edge,
        up,
        down,
        top,
        bottom,
    )
    pieces = lax.all_to_all(partial, ("blade", "span"), 0, 0, tiled=True)
    return (adjoint[None], jnp.sum(pieces, axis=0))


def solution(mesh):
    placed = (
        P("blade", None, "span", None),
        P("blade", None, None),
        P("blade", None, "span", None),
        P("blade", None, "span", None),
        P("span", None),
        P(),
    )
    return jax.shard_map(
        per_device,
        mesh=mesh,
        in_specs=placed,
        out_specs=(P("blade", None, "span", None), P(("blade", "span"))),
        check_vma=False,
    )
```

time: 76.5 us -> 34.4 us (0.45)
  blocking collectives: 44.2 us -> 14.6 us
  starting transfers between devices: 16.7 us -> 4.32 us
  other arithmetic: 7.85 us -> 0.56 us
  Pallas kernels: 0 us -> 7.19 us
  local copies, waits for them, and re-layouts: 3.04 us -> 6.62 us
  matrix products: 2.65 us -> 0 us
    unnamed x1 -> x0, blocking collectives: 44.2 us -> none
    all_to_all x0 -> x1, blocking collectives: none -> 14.6 us  [per_device(): pieces = lax.all_to_all(partial, ('blade', 'span'), 0, 0, tiled=True)]
    ppermute x6 -> x2, starting transfers between devices: 16.7 us -> 4.32 us  [the longest x1 3.04 us: per_device(): top = lax.ppermute(down, 'span', [(i, i + 1) for i in range(count - 1)])]
    pallas_call x0 -> x3, Pallas kernels: none -> 7.19 us  [the longest x1 4.05 us: per_device(): pl.pallas_call(functools.partial(main_kernel, lanes, scale), out_shape=(j...]
    unnamed x13 -> x15, local copies, waits for them, and re-layouts: 0.19 us -> 6.62 us
    dot_general x4 -> x0, matrix products: 2.65 us -> none  [the longest x3 2.39 us: per_device(): jnp.einsum('ij,bjsc->bisc', depth_inverse[0], source, precision=lax.Preci...]
    concatenate x3 -> x0, other arithmetic: 2.44 us -> none  [with_halo(): jnp.concatenate([lax.ppermute(tail, axis, [(i, (i + 1) % count) for i in...]
    convert_element_type x2 -> x0, other arithmetic: 1.93 us -> none  [per_device(): pick = (frame_ids == frame_index[step]).astype(jnp.float32)]
  transfers between devices with their start and end apart: 6 -> 2, of which waited for: 1 -> 0; matrix products, arithmetic and copies ran while one was open for 1% -> 2% of each run, Pallas kernels for 0% -> 4%
where the time goes in v2:
time: 34.4 us; the launch traced here: 34 us
  blocking collectives  14.6 us (42%)
  Pallas kernels  7.19 us (21%)
  local copies, waits for them, and re-layouts  6.62 us (19%)
  starting transfers between devices  4.32 us (13%)
  between operations  0.68 us (2%)
  other arithmetic  0.56 us (2%)
    all_to_all x1, blocking collectives, per_device(): pieces = lax.all_to_all(partial, ('blade', 'span'), 0, 0, tiled=True)  14.6 us
    unnamed x15, local copies, waits for them, and re-layouts  6.62 us
    pallas_call x1, Pallas kernels, per_device(): pl.pallas_call(functools.partial(main_kernel, lanes, scale), out_shape=(j...  4.05 us
    ppermute x1, starting transfers between devices, per_device(): top = lax.ppermute(down, 'span', [(i, i + 1) for i in range(count - 1)])  3.04 us
    pallas_call x1, Pallas kernels, per_device(): pl.pallas_call(pack_kernel, out_shape=(packed, packed), in_specs=[VMEM] *...  1.78 us
    pallas_call x1, Pallas kernels, per_device(): pl.pallas_call(weights_kernel, out_shape=(jax.ShapeDtypeStruct((5, depth,...  1.35 us
    ppermute x1, starting transfers between devices, per_device(): bottom = lax.ppermute(up, 'span', [(i + 1, i) for i in range(count - 1)])  1.28 us
  transfers between devices with their start and end apart: 2, of which 0 were waited for; matrix products, arithmetic and copies ran while one was open for 2% of the time, Pallas kernels for 4%

profile of v2, /device:TPU:0, one launch (start us, length us, event | category | flops | bytes accessed | tf_op | source)
XLA Modules:
  0.0 34.0 jit_solution(15799961617543292556)
XLA Ops:
  0.6 1.8 %pack_edges.1 = (f32[72,512]{1,0:T(8,128)}, f32[72,512]{1,0:T(8,128)}) custom-call(f32[32,8,512]{2,1,0:T(8,128)} %bitcast.8, f32[4,8,512]{2,1,0:T(8,128)} %bitcast.10), custom_call_target="tpu_custom_call" | custom-call | tf_op jit(solution)/shard_map/pack_edges/pallas_call | solution.py:247
  2.4 1.3 %collective-permute-start.1 = (f32[72,512]{1,0:T(8,128)}, f32[72,512]{1,0:T(8,128)S(1)}, u32[]{:S(2)}, u32[]{:S(2)}) collective-permute-start(f32[72,512]{1,0:T(8,128)} %get-tuple-element.12.own_top_ref), channel_id=1, source_target_pairs={{1,0},{2,1},{3,2},{5,4},{6,5},{7,6},{9,8},{10,9},{11,10},{13,12},{... | collective-permute-start | bytes 442376 | tf_op jit(solution)/shard_map/ppermute | solution.py:255
  3.7 3.0 %collective-permute-start = (f32[72,512]{1,0:T(8,128)}, f32[72,512]{1,0:T(8,128)S(1)}, u32[]{:S(2)}, u32[]{:S(2)}) collective-permute-start(f32[72,512]{1,0:T(8,128)} %get-tuple-element.13.own_bottom_ref), channel_id=1, source_target_pairs={{0,1},{1,2},{2,3},{4,5},{5,6},{6,7},{8,9},{9,10},{10,11},{12,13},{... | collective-permute-start | bytes 442376 | tf_op jit(solution)/shard_map/ppermute | solution.py:254
  6.7 0.8 %copy.9.map_ref = s32[8,4]{1,0:T(8,128)S(1)} copy(s32[8,4]{0,1:T(4,128)} %param.10) | data formatting | bytes 256 | tf_op args[4]
  7.5 0.0 copy-start
  7.5 1.0 %copy-done = f32[1,32,8,512]{3,2,1,0:T(8,128)S(1)} copy-done((f32[1,32,8,512]{3,2,1,0:T(8,128)S(1)}, f32[1,32,8,512]{3,2,1,0:T(8,128)}, u32[]{:S(2)}) %copy-start) | copy-done | bytes 524312
  8.5 0.0 copy-start.4
  8.6 0.7 %copy-done.4 = f32[1,32,32]{2,1,0:T(8,128)S(1)} copy-done((f32[1,32,32]{2,1,0:T(8,128)S(1)}, f32[1,32,32]{2,1,0:T(8,128)}, u32[]{:S(2)}) %copy-start.4) | copy-done | bytes 4120
  9.3 1.4 %weights.1 = (f32[5,32,8,512]{3,2,1,0:T(8,128)S(1)}, bf16[2,256,256]{2,1,0:T(8,128)(2,1)S(1)}, bf16[2,256,64]{2,1,0:T(8,128)(2,1)S(1)}) custom-call(f32[32,8,512]{2,1,0:T(8,128)S(1)} %bitcast.9, f32[32,32]{1,0:T(8,128)S(1)} %bitcast.12), custom_call_target="tpu_custom_call" | custom-call | tf_op jit(solution)/shard_map/weights/pallas_call | solution.py:256
  10.6 0.0 collective-permute-done.1.bottom_ref
  10.6 0.0 collective-permute-done.top_ref
  10.6 0.0 copy-start.1
  10.7 0.8 %copy-done.1 = f32[1,4,8,512]{3,2,1,0:T(8,128)S(1)} copy-done((f32[1,4,8,512]{3,2,1,0:T(8,128)S(1)}, f32[1,4,8,512]{3,2,1,0:T(8,128)}, u32[]{:S(2)}) %copy-start.1) | copy-done | bytes 65560
  11.5 0.0 copy-start.2
  11.5 0.9 %copy-done.2 = f32[72,512]{1,0:T(8,128)S(1)} copy-done((f32[72,512]{1,0:T(8,128)S(1)}, f32[72,512]{1,0:T(8,128)}, u32[]{:S(2)}) %copy-start.2) | copy-done | bytes 147480
  12.4 0.0 copy-start.3
  12.4 0.9 %copy-done.3 = f32[72,512]{1,0:T(8,128)S(1)} copy-done((f32[72,512]{1,0:T(8,128)S(1)}, f32[72,512]{1,0:T(8,128)}, u32[]{:S(2)}) %copy-start.3) | copy-done | bytes 147480
  13.3 0.0 copy-start.5
  13.3 0.8 %copy-done.5 = f32[1,3,8,512]{3,2,1,0:T(8,128)S(1)} copy-done((f32[1,3,8,512]{3,2,1,0:T(8,128)S(1)}, f32[1,3,8,512]{3,2,1,0:T(8,128)}, u32[]{:S(2)}) %copy-start.5) | copy-done | bytes 49176
  14.1 0.0 copy-start.6
  14.1 0.7 %copy-done.6 = s32[3]{0:T(128)S(1)} copy-done((s32[3]{0:T(128)S(1)}, s32[3]{0:T(128)}, u32[]{:S(2)}) %copy-start.6) | copy-done | bytes 36
  14.8 4.0 %steps.1 = (f32[32,8,512]{2,1,0:T(8,128)}, f32[32,64]{1,0:T(8,128)S(1)}) custom-call(s32[3]{0:T(128)S(1)} %copy-done.6, s32[8,4]{1,0:T(8,128)S(1)} %copy.9.map_ref, f32[32,32]{1,0:T(8,128)S(1)} %bitcast.13, f32[4,8,512]{2,1,0:T(8,128)S(1)} %bitcast.11, f32[3,8,512]{2,1,0:T(8,128)S(1)} %bitcast.14, f32[5,32,8,512]{3,2,1,0:T(8,128)S(1)} %get-tuple-element.9.w_ref, ...), custom_call_target="tpu_custom_call" | custom-call | tf_op jit(solution)/shard_map/steps/pallas_call | solution.py:269
  18.8 14.6 %all_to_all.9 = f32[32,1,64]{2,1,0:T(1,128)S(1)} all-to-all(f32[32,1,64]{2,1,0:T(1,128)S(1)} %bitcast.15), channel_id=1, replica_groups=mesh['blade'=8,'span'=4] {'blade','span'}, dimensions={0} | all-to-all | bytes 16384 | tf_op jit(solution)/shard_map/all_to_all | solution.py:294
  33.4 0.6 %reduce_sum.9 = f32[64]{0:T(128)} reduce(f32[32,1,64]{2,1,0:T(1,128)S(1)} %all_to_all.9, f32[]{:T(128)} %constant.0.clone.1), dimensions={0,1}, to_apply=%region_0.0 | reduce | flops 1984 | bytes 8452 | tf_op jit(solution)/shard_map/reduce_sum | solution.py:295
Async XLA Ops:
  2.4 8.2 %collective-permute-start.1 = (f32[72,512]{1,0:T(8,128)}, f32[72,512]{1,0:T(8,128)S(1)}, u32[]{:S(2)}, u32[]{:S(2)}) collective-permute-start(f32[72,512]{1,0:T(8,128)} %get-tuple-element.12.own_top_ref), channel_id=1, source_target_pairs={{1,0},{2,1},{3,2},{5,4},{6,5},{7,6},{9,8},{10,9},{11,10},{13,12},{... | collective-permute-start | bytes 442376 | tf_op jit(solution)/shard_map/ppermute | solution.py:255
  3.7 6.9 %collective-permute-start = (f32[72,512]{1,0:T(8,128)}, f32[72,512]{1,0:T(8,128)S(1)}, u32[]{:S(2)}, u32[]{:S(2)}) collective-permute-start(f32[72,512]{1,0:T(8,128)} %get-tuple-element.13.own_bottom_ref), channel_id=1, source_target_pairs={{0,1},{1,2},{2,3},{4,5},{5,6},{6,7},{8,9},{9,10},{10,11},{12,13},{... | collective-permute-start | bytes 442376 | tf_op jit(solution)/shard_map/ppermute | solution.py:254
  7.5 1.0 %copy-start = (f32[1,32,8,512]{3,2,1,0:T(8,128)S(1)}, f32[1,32,8,512]{3,2,1,0:T(8,128)}, u32[]{:S(2)}) copy-start(f32[1,32,8,512]{3,2,1,0:T(8,128)} %param.6) | copy-start | bytes 1572868
  8.5 0.7 %copy-start.4 = (f32[1,32,32]{2,1,0:T(8,128)S(1)}, f32[1,32,32]{2,1,0:T(8,128)}, u32[]{:S(2)}) copy-start(f32[1,32,32]{2,1,0:T(8,128)} %param.7) | copy-start | bytes 12292
  10.6 0.8 %copy-start.1 = (f32[1,4,8,512]{3,2,1,0:T(8,128)S(1)}, f32[1,4,8,512]{3,2,1,0:T(8,128)}, u32[]{:S(2)}) copy-start(f32[1,4,8,512]{3,2,1,0:T(8,128)} %param.8) | copy-start | bytes 196612
  11.5 0.9 %copy-start.2 = (f32[72,512]{1,0:T(8,128)S(1)}, f32[72,512]{1,0:T(8,128)}, u32[]{:S(2)}) copy-start(f32[72,512]{1,0:T(8,128)} %get-tuple-element.12.own_top_ref) | copy-start | bytes 442372
  12.4 0.9 %copy-start.3 = (f32[72,512]{1,0:T(8,128)S(1)}, f32[72,512]{1,0:T(8,128)}, u32[]{:S(2)}) copy-start(f32[72,512]{1,0:T(8,128)} %get-tuple-element.13.own_bottom_ref) | copy-start | bytes 442372
  13.3 0.8 %copy-start.5 = (f32[1,3,8,512]{3,2,1,0:T(8,128)S(1)}, f32[1,3,8,512]{3,2,1,0:T(8,128)}, u32[]{:S(2)}) copy-start(f32[1,3,8,512]{3,2,1,0:T(8,128)} %param.9) | copy-start | bytes 147460
  14.1 0.7 %copy-start.6 = (s32[3]{0:T(128)S(1)}, s32[3]{0:T(128)}, u32[]{:S(2)}) copy-start(s32[3]{0:T(128)} %frame_ref.1) | copy-start | bytes 40

commit v3 on v2

--- a/solution.py
+++ b/solution.py
@@ -13,7 +13,7 @@
 F32 = jnp.float32
 BF16 = jnp.bfloat16
 VMEM = pl.BlockSpec(memory_space=pltpu.VMEM)
-SMEM = pl.BlockSpec(memory_space=pltpu.SMEM)
+HBM = pl.BlockSpec(memory_space=pltpu.HBM)
 
 
 def split(x):
@@ -58,15 +58,56 @@
     return jnp.where(iota(x.shape, axis) == rows - 1, edge, pltpu.roll(x, rows - 1, axis))
 
 
-def pack_kernel(k_ref, res_ref, up_ref, down_ref):
-    depth, rows, _ = k_ref.shape
-    frames = res_ref.shape[0]
+def load_kernel(
+    frame_hbm,
+    k_hbm,
+    res_hbm,
+    excess_hbm,
+    d_hbm,
+    map_hbm,
+    up_ref,
+    down_ref,
+    k_ref,
+    frames_ref,
+    excess_ref,
+    d_ref,
+    map_ref,
+    frame_ref,
+    res_ref,
+    sems,
+):
+    pairs = (
+        (frame_hbm, frame_ref),
+        (res_hbm, res_ref),
+        (k_hbm, k_ref),
+        (excess_hbm, excess_ref),
+        (d_hbm, d_ref),
+        (map_hbm, map_ref),
+    )
+    copies = [pltpu.make_async_copy(a, b, sems.at[n]) for n, (a, b) in enumerate(pairs)]
+    for copy in copies:
+        copy.start()
+    depth, rows, cols = k_ref.shape
+    base = 2 * depth
+    copies[0].wait()
+    copies[1].wait()
+    for step in range(STEPS):
+        frames_ref[step] = res_ref[frame_ref[step]]
+    copies[2].wait()
     for out, near, far in ((up_ref, 0, 1), (down_ref, rows - 1, rows - 2)):
         out[0:depth, :] = k_ref[:, near, :]
-        out[depth : 2 * depth, :] = k_ref[:, far, :]
-        base = 2 * depth
-        out[base : base + frames, :] = res_ref[:, near, :]
-        out[base + frames : base + 2 * frames, :] = res_ref[:, far, :]
+        out[depth:base, :] = k_ref[:, far, :]
+        out[base : base + 8, :] = jnp.concatenate(
+            [
+                frames_ref[2, near : near + 1, :],
+                frames_ref[1, near : near + 1, :],
+                frames_ref[2, far : far + 1, :],
+                jnp.zeros((5, cols), F32),
+            ],
+            axis=0,
+        )
+    for copy in copies[3:]:
+        copy.wait()
 
 
 def weights_kernel(k_ref, d_ref, w_ref, mat_ref, edge_ref):
@@ -106,12 +147,11 @@
 
 
 def main_kernel(
-    per_device_segments,
+    lanes,
     scale,
-    frame_ref,
-    map_ref,
+    map_vmem,
     d_ref,
-    res_ref,
+    frames_ref,
     excess_ref,
     w_ref,
     mat_ref,
@@ -125,16 +165,15 @@
     halo_ref,
     source_ref,
     first_ref,
+    map_ref,
+    map_sem,
 ):
+    map_copy = pltpu.make_async_copy(map_vmem, map_ref, map_sem)
+    map_copy.start()
     depth, rows, cols = adj_ref.shape
-    frames = res_ref.shape[0]
-    size = depth * rows
     blocks = cols // 128
     span = lax.axis_index("span")
     last = lax.axis_size("span") - 1
-    frame2 = frame_ref[2]
-    frame1 = frame_ref[1]
-    frame0 = frame_ref[0]
     base = 2 * depth
     first = d_ref[:, 0:1]
     is_surface = iota((depth, 1), 0) == 0
@@ -147,10 +186,10 @@
         half = 0.5 * got[0:depth, :]
         half_far = 0.5 * got[depth : 2 * depth, :]
         half_own = 0.5 * own[0:depth, :]
-        f = got[pl.ds(base + frame2, 1), :]
-        f_far = got[pl.ds(base + frames + frame2, 1), :]
-        f_own = own[pl.ds(base + frame2, 1), :]
-        g = got[pl.ds(base + frame1, 1), :]
+        f = got[base : base + 1, :]
+        g = got[base + 1 : base + 2, :]
+        f_far = got[base + 2 : base + 3, :]
+        f_own = own[base : base + 1, :]
         halo_ref[:, row, :] = half
         w_next = half + chord_next(half)
         w_prev = half + chord_prev(half)
@@ -168,7 +207,7 @@
         field_edges.append(f)
     halo_first = dot3(edge_ref[0], edge_ref[1], jnp.concatenate(sources, axis=0))
 
-    f = res_ref[frame2]
+    f = frames_ref[2]
     f_top, f_bottom = field_edges
     f_next = chord_next(f)
     f_prev = chord_prev(f)
@@ -190,7 +229,7 @@
         return 0
 
     lax.fori_loop(0, depth, first_source, 0, unroll=4)
-    source_ref[0:rows, :] += res_ref[frame1]
+    source_ref[0:rows, :] += frames_ref[1]
     first_ref[...] = dot3(mat_ref[0], mat_ref[1], source_ref[...])
     source_ref[...] = halo_first
 
@@ -208,7 +247,7 @@
         return 0
 
     lax.fori_loop(0, depth, second_source, 0, unroll=4)
-    source_ref[0:rows, :] += res_ref[frame0]
+    source_ref[0:rows, :] += frames_ref[0]
     result = dot3(mat_ref[0], mat_ref[1], source_ref[...])
     adj_ref[...] = result.reshape(depth, rows, cols)
 
@@ -217,17 +256,23 @@
         + first_ref[0:rows, :] * excess_ref[1]
         + result[0:rows, :] * excess_ref[0]
     ) * scale
-    owners = part_ref.shape[0]
-    lanes = part_ref.shape[-1]
-    shape = (owners, 128)
-    lane = iota(shape, 1)
-    segment = jnp.where(lane < lanes, iota(shape, 0) * lanes + lane, -1)
+    shape = part_ref.shape[0], part_ref.shape[2]
+    place = iota(shape, 1)
+    segment = (place // lanes * shape[0] + iota(shape, 0)) * lanes + place % lanes
     total = jnp.zeros(shape, F32)
+    map_copy.wait()
     for block in range(blocks):
         sums = jnp.sum(contribution[:, block * 128 : (block + 1) * 128], axis=1, keepdims=True)
         for row in range(rows):
-            total += jnp.where(segment == map_ref[row, block], sums[row : row + 1, :], 0.0)
-    part_ref[...] = total[:, :lanes].reshape(part_ref.shape)
+            total += jnp.where(segment == map_ref[block, row], sums[row : row + 1, :], 0.0)
+    part_ref[...] = total[:, None, :]
+
+
+def regroup_kernel(got_ref, out_ref):
+    total = jnp.sum(got_ref[:, 0, :], axis=0, keepdims=True)
+    lanes = out_ref.shape[2]
+    for n in range(out_ref.shape[0]):
+        out_ref[n] = total[:, n * lanes : (n + 1) * lanes]
 
 
 def per_device(
@@ -235,24 +280,42 @@
 ):
     _, depth, rows, cols = conductance.shape
     frames = surface_residual.shape[1]
-    k = conductance[0]
-    inverse = depth_inverse[0]
-    residual = surface_residual[0]
-    excess = surface_excess[0]
+    blocks = segment_map.shape[1]
     size = depth * rows
-    count = lax.axis_size("span")
-    devices = count * lax.axis_size("blade")
-    lanes = SEGS // devices
-    packed = jax.ShapeDtypeStruct((2 * (depth + frames), cols), F32)
-    up, down = pl.pallas_call(
-        pack_kernel,
-        out_shape=(packed, packed),
-        in_specs=[VMEM] * 2,
-        out_specs=(VMEM,) * 2,
-        name="pack_edges",
-    )(k, residual)
-    top = lax.ppermute(down, "span", [(i, i + 1) for i in range(count - 1)])
-    bottom = lax.ppermute(up, "span", [(i + 1, i) for i in range(count - 1)])
+    spans = lax.axis_size("span")
+    blades = lax.axis_size("blade")
+    lanes = SEGS // (spans * blades)
+    packed = jax.ShapeDtypeStruct((2 * depth + 8, cols), F32)
+    up, down, k, picked, excess, inverse, ids = pl.pallas_call(
+        load_kernel,
+        out_shape=(
+            packed,
+            packed,
+            jax.ShapeDtypeStruct((depth, rows, cols), F32),
+            jax.ShapeDtypeStruct((STEPS, rows, cols), F32),
+            jax.ShapeDtypeStruct((STEPS, rows, cols), F32),
+            jax.ShapeDtypeStruct((depth, depth), F32),
+            jax.ShapeDtypeStruct((blocks, rows), jnp.int32),
+        ),
+        in_specs=[HBM] * 6,
+        out_specs=(VMEM,) * 7,
+        scratch_shapes=[
+            pltpu.SMEM((STEPS,), jnp.int32),
+            pltpu.VMEM((frames, rows, cols), F32),
+            pltpu.SemaphoreType.DMA((6,)),
+        ],
+        compiler_params=pltpu.CompilerParams(vmem_limit_bytes=60 * 2**20),
+        name="load",
+    )(
+        frame_index,
+        conductance[0],
+        surface_residual[0],
+        surface_excess[0],
+        depth_inverse[0],
+        segment_map.T,
+    )
+    top = lax.ppermute(down, "span", [(i, i + 1) for i in range(spans - 1)])
+    bottom = lax.ppermute(up, "span", [(i + 1, i) for i in range(spans - 1)])
     weights, mat, edge = pl.pallas_call(
         weights_kernel,
         out_shape=(
@@ -270,29 +333,29 @@
         functools.partial(main_kernel, lanes, scale),
         out_shape=(
             jax.ShapeDtypeStruct((depth, rows, cols), F32),
-            jax.ShapeDtypeStruct((devices, lanes), F32),
+            jax.ShapeDtypeStruct((spans, 1, blades * lanes), F32),
         ),
-        in_specs=[SMEM, SMEM] + [VMEM] * 10,
+        in_specs=[VMEM] * 11,
         out_specs=(VMEM,) * 2,
-        scratch_shapes=[pltpu.VMEM((depth, rows, cols), F32)] + [pltpu.VMEM((size, cols), F32)] * 2,
+        scratch_shapes=[
+            pltpu.VMEM((depth, rows, cols), F32),
+            pltpu.VMEM((size, cols), F32),
+            pltpu.VMEM((size, cols), F32),
+            pltpu.SMEM((blocks, rows), jnp.int32),
+            pltpu.SemaphoreType.DMA,
+        ],
         compiler_params=pltpu.CompilerParams(vmem_limit_bytes=24 * 2**20),
         name="steps",
-    )(
-        frame_index,
-        segment_map,
-        inverse,
-        residual,
-        excess,
-        weights,
-        mat,
-        edge,
-        up,
-        down,
-        top,
-        bottom,
-    )
-    pieces = lax.all_to_all(partial, ("blade", "span"), 0, 0, tiled=True)
-    return (adjoint[None], jnp.sum(pieces, axis=0))
+    )(ids, inverse, picked, excess, weights, mat, edge, up, down, top, bottom)
+    pieces = pl.pallas_call(
+        regroup_kernel,
+        out_shape=jax.ShapeDtypeStruct((blades, 1, lanes), F32),
+        in_specs=[VMEM],
+        out_specs=VMEM,
+        name="regroup",
+    )(lax.all_to_all(partial, "span", 0, 0, tiled=True))
+    owned = jnp.sum(lax.all_to_all(pieces, "blade", 0, 0, tiled=True), axis=(0, 1))
+    return (adjoint[None], owned)
 
 
 def solution(mesh):

time: 34.4 us -> 41.6 us (1.21)
  blocking collectives: 14.6 us -> 21.3 us
  Pallas kernels: 7.19 us -> 8.28 us
  local copies, waits for them, and re-layouts: 6.62 us -> 5.82 us
    all_to_all x1 -> x2, blocking collectives: 14.6 us -> 21.3 us  [the longest x1 12.3 us: per_device(): lax.all_to_all(pieces, 'blade', 0, 0, tiled=True)]
    pallas_call x1 -> x2, Pallas kernels: 1.78 us -> 3.49 us  [the longest x1 2.12 us: per_device(): pl.pallas_call(load_kernel, out_shape=(packed, packed, jax.ShapeDtypeStru...]
    unnamed x15 -> x14, local copies, waits for them, and re-layouts: 6.62 us -> 5.82 us
    pallas_call x1, Pallas kernels: 4.05 us -> 3.44 us  [per_device(): pl.pallas_call(functools.partial(main_kernel, lanes, scale), out_shape=(j...]
  transfers between devices with their start and end apart: 2 -> 2, of which waited for: 0 -> 0; matrix products, arithmetic and copies ran while one was open for 2% -> 0% of each run, Pallas kernels for 4% -> 3%
where the time goes in v3:
time: 41.6 us; the launch traced here: 41 us
  blocking collectives  21.3 us (51%)
  Pallas kernels  8.28 us (20%)
  local copies, waits for them, and re-layouts  5.82 us (14%)
  starting transfers between devices  4.33 us (10%)
  between operations  0.71 us (2%)
  other arithmetic  0.54 us (1%)
    all_to_all x1, blocking collectives, per_device(): lax.all_to_all(pieces, 'blade', 0, 0, tiled=True)  12.3 us
    all_to_all x1, blocking collectives, per_device(): lax.all_to_all(partial, 'span', 0, 0, tiled=True)  9.04 us
    unnamed x14, local copies, waits for them, and re-layouts  5.82 us
    pallas_call x1, Pallas kernels, per_device(): pl.pallas_call(functools.partial(main_kernel, lanes, scale), out_shape=(j...  3.44 us
    ppermute x1, starting transfers between devices, per_device(): top = lax.ppermute(down, 'span', [(i, i + 1) for i in range(spans - 1)])  3.04 us
    pallas_call x1, Pallas kernels, per_device(): pl.pallas_call(load_kernel, out_shape=(packed, packed, jax.ShapeDtypeStru...  2.12 us
    pallas_call x1, Pallas kernels, per_device(): pl.pallas_call(regroup_kernel, out_shape=jax.ShapeDtypeStruct((blades, 1,...  1.37 us
    pallas_call x1, Pallas kernels, per_device(): pl.pallas_call(weights_kernel, out_shape=(jax.ShapeDtypeStruct((5, depth,...  1.35 us
  transfers between devices with their start and end apart: 2, of which 0 were waited for; matrix products, arithmetic and copies ran while one was open for 0% of the time, Pallas kernels for 3%

profile of v3, /device:TPU:0, one launch (start us, length us, event | category | flops | bytes accessed | tf_op | source)
XLA Modules:
  0.0 41.0 jit_solution(8190289581317466455)
XLA Ops:
  0.6 2.1 %load.1 = (f32[72,512]{1,0:T(8,128)}, f32[72,512]{1,0:T(8,128)}, f32[32,8,512]{2,1,0:T(8,128)}, f32[3,8,512]{2,1,0:T(8,128)}, f32[3,8,512]{2,1,0:T(8,128)}, /*index=5*/f32[32,32]{1,0:T(8,128)}, s32[4,8]{1,0:T(4,128)}) custom-call(s32[3]{0:T(128)} %frame_hbm.1, f32[32,8,512]{2,1,0:T(8,128)} %bitcast.6, f32[4,8,512]{2,1,0:T(8,128)} %bitcast.7, ...), custom_call_target="tpu_custom_call" | custom-call | tf_op jit(solution)/shard_map/load/pallas_call | solution.py:289
  2.8 1.3 %collective-permute-start.1 = (f32[72,512]{1,0:T(8,128)}, f32[72,512]{1,0:T(8,128)S(1)}, u32[]{:S(2)}, u32[]{:S(2)}) collective-permute-start(f32[72,512]{1,0:T(8,128)} %get-tuple-element.22.own_top_ref), channel_id=1, source_target_pairs={{1,0},{2,1},{3,2},{5,4},{6,5},{7,6},{9,8},{10,9},{11,10},{13,12},{... | collective-permute-start | bytes 442376 | tf_op jit(solution)/shard_map/ppermute | solution.py:318
  4.1 3.0 %collective-permute-start = (f32[72,512]{1,0:T(8,128)}, f32[72,512]{1,0:T(8,128)S(1)}, u32[]{:S(2)}, u32[]{:S(2)}) collective-permute-start(f32[72,512]{1,0:T(8,128)} %get-tuple-element.23.own_bottom_ref), channel_id=1, source_target_pairs={{0,1},{1,2},{2,3},{4,5},{5,6},{6,7},{8,9},{9,10},{10,11},{12,13},{... | collective-permute-start | bytes 442376 | tf_op jit(solution)/shard_map/ppermute | solution.py:317
  7.1 0.0 copy-start
  7.1 1.0 %copy-done = f32[32,8,512]{2,1,0:T(8,128)S(1)} copy-done((f32[32,8,512]{2,1,0:T(8,128)S(1)}, f32[32,8,512]{2,1,0:T(8,128)}, u32[]{:S(2)}) %copy-start) | copy-done | bytes 524312
  8.1 0.0 copy-start.3
  8.1 0.7 %copy-done.3 = f32[32,32]{1,0:T(8,128)S(1)} copy-done((f32[32,32]{1,0:T(8,128)S(1)}, f32[32,32]{1,0:T(8,128)}, u32[]{:S(2)}) %copy-start.3) | copy-done | bytes 4120
  8.9 1.4 %weights.1 = (f32[5,32,8,512]{3,2,1,0:T(8,128)S(1)}, bf16[2,256,256]{2,1,0:T(8,128)(2,1)S(1)}, bf16[2,256,64]{2,1,0:T(8,128)(2,1)S(1)}) custom-call(f32[32,8,512]{2,1,0:T(8,128)S(1)} %copy-done, f32[32,32]{1,0:T(8,128)S(1)} %copy-done.3), custom_call_target="tpu_custom_call" | custom-call | tf_op jit(solution)/shard_map/weights/pallas_call | solution.py:319
  10.2 0.0 collective-permute-done.1.bottom_ref
  10.2 0.0 collective-permute-done.top_ref
  10.2 0.0 copy-start.1
  10.3 0.9 %copy-done.1 = f32[72,512]{1,0:T(8,128)S(1)} copy-done((f32[72,512]{1,0:T(8,128)S(1)}, f32[72,512]{1,0:T(8,128)}, u32[]{:S(2)}) %copy-start.1) | copy-done | bytes 147480
  11.2 0.0 copy-start.2
  11.2 0.9 %copy-done.2 = f32[72,512]{1,0:T(8,128)S(1)} copy-done((f32[72,512]{1,0:T(8,128)S(1)}, f32[72,512]{1,0:T(8,128)}, u32[]{:S(2)}) %copy-start.2) | copy-done | bytes 147480
  12.1 0.0 copy-start.4
  12.1 0.8 %copy-done.4 = f32[3,8,512]{2,1,0:T(8,128)S(1)} copy-done((f32[3,8,512]{2,1,0:T(8,128)S(1)}, f32[3,8,512]{2,1,0:T(8,128)}, u32[]{:S(2)}) %copy-start.4) | copy-done | bytes 49176
  12.9 0.0 copy-start.5
  12.9 0.8 %copy-done.5 = f32[3,8,512]{2,1,0:T(8,128)S(1)} copy-done((f32[3,8,512]{2,1,0:T(8,128)S(1)}, f32[3,8,512]{2,1,0:T(8,128)}, u32[]{:S(2)}) %copy-start.5) | copy-done | bytes 49176
  13.7 0.7 %copy-done.6 = s32[4,8]{1,0:T(4,128)S(1)} copy-done((s32[4,8]{1,0:T(4,128)S(1)}, s32[4,8]{1,0:T(4,128)}, u32[]{:S(2)}) %copy-start.6) | copy-done | bytes 152
  14.3 3.4 %steps.1 = (f32[32,8,512]{2,1,0:T(8,128)}, f32[4,1,512]{2,1,0:T(1,128)S(1)}) custom-call(s32[4,8]{1,0:T(4,128)S(1)} %copy-done.6, f32[32,32]{1,0:T(8,128)S(1)} %copy-done.3, f32[3,8,512]{2,1,0:T(8,128)S(1)} %copy-done.4, f32[3,8,512]{2,1,0:T(8,128)S(1)} %copy-done.5, f32[5,32,8,512]{3,2,1,0:T(8,128)S(1)} %get-tuple-element.19.w_ref, ...), custom_call_target="tpu_custom_call" | custom-call | tf_op jit(solution)/shard_map/steps/pallas_call | solution.py:332
  17.8 9.0 %all_to_all.10.got_ref = f32[4,1,512]{2,1,0:T(1,128)} all-to-all(f32[4,1,512]{2,1,0:T(1,128)S(1)} %get-tuple-element.25), channel_id=1, replica_groups=mesh['blade'=8,'span'=4] {'span'}, dimensions={0} | all-to-all | bytes 16384 | tf_op jit(solution)/shard_map/all_to_all | solution.py:356
  26.8 1.4 %regroup.1 = f32[8,1,64]{2,1,0:T(1,128)} custom-call(f32[4,1,512]{2,1,0:T(1,128)} %all_to_all.10.got_ref), custom_call_target="tpu_custom_call" | custom-call | tf_op jit(solution)/shard_map/regroup/pallas_call | solution.py:350
  28.2 12.3 %all_to_all.11 = f32[8,1,64]{2,1,0:T(1,128)S(1)} all-to-all(f32[8,1,64]{2,1,0:T(1,128)} %regroup.1), channel_id=1, replica_groups=mesh['blade'=8,'span'=4] {'blade'}, dimensions={0} | all-to-all | bytes 4096 | tf_op jit(solution)/shard_map/all_to_all | solution.py:357
  40.5 0.5 %reduce_sum.9 = f32[64]{0:T(128)} reduce(f32[8,1,64]{2,1,0:T(1,128)S(1)} %all_to_all.11, f32[]{:T(128)} %constant.0.clone.1), dimensions={0,1}, to_apply=%region_0.0 | reduce | flops 448 | bytes 2308 | tf_op jit(solution)/shard_map/reduce_sum | solution.py:357
  (1 shorter events, 0.0 us)
Async XLA Ops:
  2.8 7.5 %collective-permute-start.1 = (f32[72,512]{1,0:T(8,128)}, f32[72,512]{1,0:T(8,128)S(1)}, u32[]{:S(2)}, u32[]{:S(2)}) collective-permute-start(f32[72,512]{1,0:T(8,128)} %get-tuple-element.22.own_top_ref), channel_id=1, source_target_pairs={{1,0},{2,1},{3,2},{5,4},{6,5},{7,6},{9,8},{10,9},{11,10},{13,12},{... | collective-permute-start | bytes 442376 | tf_op jit(solution)/shard_map/ppermute | solution.py:318
  4.1 6.2 %collective-permute-start = (f32[72,512]{1,0:T(8,128)}, f32[72,512]{1,0:T(8,128)S(1)}, u32[]{:S(2)}, u32[]{:S(2)}) collective-permute-start(f32[72,512]{1,0:T(8,128)} %get-tuple-element.23.own_bottom_ref), channel_id=1, source_target_pairs={{0,1},{1,2},{2,3},{4,5},{5,6},{6,7},{8,9},{9,10},{10,11},{12,13},{... | collective-permute-start | bytes 442376 | tf_op jit(solution)/shard_map/ppermute | solution.py:317
  7.1 1.0 %copy-start = (f32[32,8,512]{2,1,0:T(8,128)S(1)}, f32[32,8,512]{2,1,0:T(8,128)}, u32[]{:S(2)}) copy-start(f32[32,8,512]{2,1,0:T(8,128)} %get-tuple-element.18.k_ref) | copy-start | bytes 1572868
  8.1 0.7 %copy-start.3 = (f32[32,32]{1,0:T(8,128)S(1)}, f32[32,32]{1,0:T(8,128)}, u32[]{:S(2)}) copy-start(f32[32,32]{1,0:T(8,128)} %get-tuple-element.15.d_ref) | copy-start | bytes 12292
  10.2 0.9 %copy-start.1 = (f32[72,512]{1,0:T(8,128)S(1)}, f32[72,512]{1,0:T(8,128)}, u32[]{:S(2)}) copy-start(f32[72,512]{1,0:T(8,128)} %get-tuple-element.22.own_top_ref) | copy-start | bytes 442372
  11.2 0.9 %copy-start.2 = (f32[72,512]{1,0:T(8,128)S(1)}, f32[72,512]{1,0:T(8,128)}, u32[]{:S(2)}) copy-start(f32[72,512]{1,0:T(8,128)} %get-tuple-element.23.own_bottom_ref) | copy-start | bytes 442372
  12.1 0.8 %copy-start.4 = (f32[3,8,512]{2,1,0:T(8,128)S(1)}, f32[3,8,512]{2,1,0:T(8,128)}, u32[]{:S(2)}) copy-start(f32[3,8,512]{2,1,0:T(8,128)} %get-tuple-element.16.frames_ref) | copy-start | bytes 147460
  12.9 0.8 %copy-start.5 = (f32[3,8,512]{2,1,0:T(8,128)S(1)}, f32[3,8,512]{2,1,0:T(8,128)}, u32[]{:S(2)}) copy-start(f32[3,8,512]{2,1,0:T(8,128)} %get-tuple-element.17.excess_ref) | copy-start | bytes 147460
  13.7 0.7 %copy-start.6 = (s32[4,8]{1,0:T(4,128)S(1)}, s32[4,8]{1,0:T(4,128)}, u32[]{:S(2)}) copy-start(s32[4,8]{1,0:T(4,128)} %get-tuple-element.14.map_vmem) | copy-start | bytes 388

commit v4 on v3

--- a/solution.py
+++ b/solution.py
@@ -14,6 +14,7 @@
 BF16 = jnp.bfloat16
 VMEM = pl.BlockSpec(memory_space=pltpu.VMEM)
 HBM = pl.BlockSpec(memory_space=pltpu.HBM)
+GRANT = 16 * 2**20
 
 
 def split(x):
@@ -147,7 +148,6 @@
 
 
 def main_kernel(
-    lanes,
     scale,
     map_vmem,
     d_ref,
@@ -160,15 +160,16 @@
     own_bottom_ref,
     top_ref,
     bottom_ref,
+    adj_hbm,
+    part_ref,
     adj_ref,
-    part_ref,
     halo_ref,
     source_ref,
     first_ref,
     map_ref,
-    map_sem,
+    sems,
 ):
-    map_copy = pltpu.make_async_copy(map_vmem, map_ref, map_sem)
+    map_copy = pltpu.make_async_copy(map_vmem, map_ref, sems.at[0])
     map_copy.start()
     depth, rows, cols = adj_ref.shape
     blocks = cols // 128
@@ -250,29 +251,26 @@
     source_ref[0:rows, :] += frames_ref[0]
     result = dot3(mat_ref[0], mat_ref[1], source_ref[...])
     adj_ref[...] = result.reshape(depth, rows, cols)
+    adj_copy = pltpu.make_async_copy(adj_ref, adj_hbm, sems.at[1])
+    adj_copy.start()
 
     contribution = (
         d_ref[0:1, 0:1] * f * excess_ref[2]
         + first_ref[0:rows, :] * excess_ref[1]
         + result[0:rows, :] * excess_ref[0]
     ) * scale
-    shape = part_ref.shape[0], part_ref.shape[2]
-    place = iota(shape, 1)
-    segment = (place // lanes * shape[0] + iota(shape, 0)) * lanes + place % lanes
+    owners, _, lanes = part_ref.shape
+    shape = (owners, 128)
+    lane = iota(shape, 1)
+    segment = jnp.where(lane < lanes, iota(shape, 0) * lanes + lane, -1)
     total = jnp.zeros(shape, F32)
     map_copy.wait()
     for block in range(blocks):
         sums = jnp.sum(contribution[:, block * 128 : (block + 1) * 128], axis=1, keepdims=True)
         for row in range(rows):
             total += jnp.where(segment == map_ref[block, row], sums[row : row + 1, :], 0.0)
-    part_ref[...] = total[:, None, :]
-
-
-def regroup_kernel(got_ref, out_ref):
-    total = jnp.sum(got_ref[:, 0, :], axis=0, keepdims=True)
-    lanes = out_ref.shape[2]
-    for n in range(out_ref.shape[0]):
-        out_ref[n] = total[:, n * lanes : (n + 1) * lanes]
+    part_ref[...] = total[:, None, :lanes]
+    adj_copy.wait()
 
 
 def per_device(
@@ -285,17 +283,17 @@
     spans = lax.axis_size("span")
     blades = lax.axis_size("blade")
     lanes = SEGS // (spans * blades)
-    packed = jax.ShapeDtypeStruct((2 * depth + 8, cols), F32)
+    packed = pltpu.VMEM((2 * depth + 8, cols), F32)
     up, down, k, picked, excess, inverse, ids = pl.pallas_call(
         load_kernel,
         out_shape=(
             packed,
             packed,
-            jax.ShapeDtypeStruct((depth, rows, cols), F32),
-            jax.ShapeDtypeStruct((STEPS, rows, cols), F32),
-            jax.ShapeDtypeStruct((STEPS, rows, cols), F32),
-            jax.ShapeDtypeStruct((depth, depth), F32),
-            jax.ShapeDtypeStruct((blocks, rows), jnp.int32),
+            pltpu.VMEM((depth, rows, cols), F32),
+            pltpu.VMEM((STEPS, rows, cols), F32),
+            pltpu.VMEM((STEPS, rows, cols), F32),
+            pltpu.VMEM((depth, depth), F32),
+            pltpu.VMEM((blocks, rows), jnp.int32),
         ),
         in_specs=[HBM] * 6,
         out_specs=(VMEM,) * 7,
@@ -304,57 +302,57 @@
             pltpu.VMEM((frames, rows, cols), F32),
             pltpu.SemaphoreType.DMA((6,)),
         ],
-        compiler_params=pltpu.CompilerParams(vmem_limit_bytes=60 * 2**20),
+        compiler_params=pltpu.CompilerParams(vmem_limit_bytes=GRANT),
         name="load",
     )(
-        frame_index,
-        conductance[0],
-        surface_residual[0],
-        surface_excess[0],
-        depth_inverse[0],
-        segment_map.T,
+        *(
+            pltpu.with_memory_space_constraint(x, pltpu.HBM)
+            for x in (
+                frame_index,
+                conductance[0],
+                surface_residual[0],
+                surface_excess[0],
+                depth_inverse[0],
+                segment_map.T,
+            )
+        )
     )
     top = lax.ppermute(down, "span", [(i, i + 1) for i in range(spans - 1)])
     bottom = lax.ppermute(up, "span", [(i + 1, i) for i in range(spans - 1)])
     weights, mat, edge = pl.pallas_call(
         weights_kernel,
         out_shape=(
-            jax.ShapeDtypeStruct((5, depth, rows, cols), F32),
-            jax.ShapeDtypeStruct((2, size, size), BF16),
-            jax.ShapeDtypeStruct((2, size, 2 * depth), BF16),
+            pltpu.VMEM((5, depth, rows, cols), F32),
+            pltpu.VMEM((2, size, size), BF16),
+            pltpu.VMEM((2, size, 2 * depth), BF16),
         ),
         in_specs=[VMEM] * 2,
         out_specs=(VMEM,) * 3,
-        compiler_params=pltpu.CompilerParams(vmem_limit_bytes=24 * 2**20),
+        compiler_params=pltpu.CompilerParams(vmem_limit_bytes=GRANT),
         name="weights",
     )(k, inverse)
     scale = 1.0 / math.sqrt(128.0 * STEPS)
     adjoint, partial = pl.pallas_call(
-        functools.partial(main_kernel, lanes, scale),
+        functools.partial(main_kernel, scale),
         out_shape=(
-            jax.ShapeDtypeStruct((depth, rows, cols), F32),
-            jax.ShapeDtypeStruct((spans, 1, blades * lanes), F32),
+            pltpu.HBM((depth, rows, cols), F32),
+            pltpu.VMEM((spans * blades, 1, lanes), F32),
         ),
         in_specs=[VMEM] * 11,
-        out_specs=(VMEM,) * 2,
+        out_specs=(HBM, VMEM),
         scratch_shapes=[
+            pltpu.VMEM((depth, rows, cols), F32),
             pltpu.VMEM((depth, rows, cols), F32),
             pltpu.VMEM((size, cols), F32),
             pltpu.VMEM((size, cols), F32),
             pltpu.SMEM((blocks, rows), jnp.int32),
-            pltpu.SemaphoreType.DMA,
+            pltpu.SemaphoreType.DMA((2,)),
         ],
-        compiler_params=pltpu.CompilerParams(vmem_limit_bytes=24 * 2**20),
+        compiler_params=pltpu.CompilerParams(vmem_limit_bytes=GRANT),
         name="steps",
     )(ids, inverse, picked, excess, weights, mat, edge, up, down, top, bottom)
-    pieces = pl.pallas_call(
-        regroup_kernel,
-        out_shape=jax.ShapeDtypeStruct((blades, 1, lanes), F32),
-        in_specs=[VMEM],
-        out_specs=VMEM,
-        name="regroup",
-    )(lax.all_to_all(partial, "span", 0, 0, tiled=True))
-    owned = jnp.sum(lax.all_to_all(pieces, "blade", 0, 0, tiled=True), axis=(0, 1))
+    pieces = lax.all_to_all(partial, ("blade", "span"), 0, 0, tiled=True)
+    owned = jnp.sum(pieces, axis=(0, 1))
     return (adjoint[None], owned)
 
 

time: 41.6 us -> 28.7 us (0.69)
  local copies, waits for them, and re-layouts: 5.82 us -> 0 us
  blocking collectives: 21.3 us -> 16.9 us
  Pallas kernels: 8.28 us -> 6.03 us
    unnamed x14 -> x0, local copies, waits for them, and re-layouts: 5.82 us -> none
    all_to_all x2 -> x1, blocking collectives: 21.3 us -> 16.9 us  [per_device(): pieces = lax.all_to_all(partial, ('blade', 'span'), 0, 0, tiled=True)]
    pallas_call x4 -> x3, Pallas kernels: 8.28 us -> 6.03 us  [the longest x1 3.47 us: per_device(): pl.pallas_call(functools.partial(main_kernel, scale), out_shape=(pltpu.HB...]
  transfers between devices with their start and end apart: 2 -> 2, of which waited for: 0 -> 0; matrix products, arithmetic and copies ran while one was open for 0% -> 0% of each run, Pallas kernels for 3% -> 5%
where the time goes in v4:
time: 28.7 us; the launch traced here: 28.5 us
  blocking collectives  16.9 us (59%)
  Pallas kernels  6.03 us (21%)
  starting transfers between devices  4.33 us (15%)
  between operations  0.69 us (2%)
  other arithmetic  0.56 us (2%)
    all_to_all x1, blocking collectives, per_device(): pieces = lax.all_to_all(partial, ('blade', 'span'), 0, 0, tiled=True)  16.9 us
    pallas_call x1, Pallas kernels, per_device(): pl.pallas_call(functools.partial(main_kernel, scale), out_shape=(pltpu.HB...  3.47 us
    ppermute x1, starting transfers between devices, per_device(): top = lax.ppermute(down, 'span', [(i, i + 1) for i in range(spans - 1)])  3.04 us
    pallas_call x1, Pallas kernels, per_device(): pl.pallas_call(weights_kernel, out_shape=(pltpu.VMEM((5, depth, rows, col...  1.36 us
    ppermute x1, starting transfers between devices, per_device(): bottom = lax.ppermute(up, 'span', [(i + 1, i) for i in range(spans - 1)])  1.29 us
    pallas_call x1, Pallas kernels, per_device(): pl.pallas_call(load_kernel, out_shape=(packed, packed, pltpu.VMEM((depth,...  1.2 us
  transfers between devices with their start and end apart: 2, of which 0 were waited for; matrix products, arithmetic and copies ran while one was open for 0% of the time, Pallas kernels for 5%

profile of v4, /device:TPU:0, one launch (start us, length us, event | category | flops | bytes accessed | tf_op | source)
XLA Modules:
  0.0 28.5 jit_solution(7880570233985244687)
XLA Ops:
  0.6 1.2 %load.1 = (f32[72,512]{1,0:T(8,128)S(1)}, f32[72,512]{1,0:T(8,128)S(1)}, f32[32,8,512]{2,1,0:T(8,128)S(1)}, f32[3,8,512]{2,1,0:T(8,128)S(1)}, f32[3,8,512]{2,1,0...) custom-call(s32[3]{0:T(128)} %frame_hbm.1, f32[32,8,512]{2,1,0:T(8,128)} %bitcast.6, f32[4,8,512]{2,1,0:T(8,128)} %bitcast.7, ...), custom_call_target="tpu_custom_call" | custom-call | tf_op jit(solution)/shard_map/load/pallas_call | solution.py:287
  1.8 1.3 %collective-permute-start.1 = (f32[72,512]{1,0:T(8,128)S(1)}, f32[72,512]{1,0:T(8,128)S(1)}, u32[]{:S(2)}, u32[]{:S(2)}) collective-permute-start(f32[72,512]{1,0:T(8,128)S(1)} %get-tuple-element.22.own_top_ref), channel_id=1, source_target_pairs={{1,0},{2,1},{3,2},{5,4},{6,5},{7,6},{9,8},{10,9},{11,10},{13,12},{... | collective-permute-start | bytes 442376 | tf_op jit(solution)/shard_map/ppermute | solution.py:321
  3.1 3.0 %collective-permute-start = (f32[72,512]{1,0:T(8,128)S(1)}, f32[72,512]{1,0:T(8,128)S(1)}, u32[]{:S(2)}, u32[]{:S(2)}) collective-permute-start(f32[72,512]{1,0:T(8,128)S(1)} %get-tuple-element.23.own_bottom_ref), channel_id=1, source_target_pairs={{0,1},{1,2},{2,3},{4,5},{5,6},{6,7},{8,9},{9,10},{10,11},{12,13},{... | collective-permute-start | bytes 442376 | tf_op jit(solution)/shard_map/ppermute | solution.py:320
  6.2 1.4 %weights.1 = (f32[5,32,8,512]{3,2,1,0:T(8,128)S(1)}, bf16[2,256,256]{2,1,0:T(8,128)(2,1)S(1)}, bf16[2,256,64]{2,1,0:T(8,128)(2,1)S(1)}) custom-call(f32[32,8,512]{2,1,0:T(8,128)S(1)} %get-tuple-element.18.k_ref, f32[32,32]{1,0:T(8,128)S(1)} %get-tuple-element.15.d_ref), custom_call_target="tpu_custom_call" | custom-call | tf_op jit(solution)/shard_map/weights/pallas_call | solution.py:322
  7.6 0.0 collective-permute-done.1.bottom_ref
  7.6 0.0 collective-permute-done.top_ref
  7.6 3.5 %steps.1 = (f32[32,8,512]{2,1,0:T(8,128)}, f32[32,1,64]{2,1,0:T(1,128)S(1)}) custom-call(s32[4,8]{1,0:T(4,128)S(1)} %get-tuple-element.14.map_vmem, f32[32,32]{1,0:T(8,128)S(1)} %get-tuple-element.15.d_ref, f32[3,8,512]{2,1,0:T(8,128)S(1)} %get-tuple-element.16.frames_ref, f32[3,8,512]{2,1,0:T(8,128)S(1)} %get-tuple-element.17.excess_ref, ...), custom_call_target="tpu_custom_call" | custom-call | tf_op jit(solution)/shard_map/steps/pallas_call | solution.py:335
  11.1 16.9 %all_to_all.5 = f32[32,1,64]{2,1,0:T(1,128)S(1)} all-to-all(f32[32,1,64]{2,1,0:T(1,128)S(1)} %get-tuple-element.25), channel_id=1, replica_groups=mesh['blade'=8,'span'=4] {'blade','span'}, dimensions={0} | all-to-all | bytes 16384 | tf_op jit(solution)/shard_map/all_to_all | solution.py:354
  28.0 0.6 %reduce_sum.9 = f32[64]{0:T(128)} reduce(f32[32,1,64]{2,1,0:T(1,128)S(1)} %all_to_all.5, f32[]{:T(128)} %constant.0.clone.1), dimensions={0,1}, to_apply=%region_0.0 | reduce | flops 1984 | bytes 8452 | tf_op jit(solution)/shard_map/reduce_sum | solution.py:355
Async XLA Ops:
  1.8 5.7 %collective-permute-start.1 = (f32[72,512]{1,0:T(8,128)S(1)}, f32[72,512]{1,0:T(8,128)S(1)}, u32[]{:S(2)}, u32[]{:S(2)}) collective-permute-start(f32[72,512]{1,0:T(8,128)S(1)} %get-tuple-element.22.own_top_ref), channel_id=1, source_target_pairs={{1,0},{2,1},{3,2},{5,4},{6,5},{7,6},{9,8},{10,9},{11,10},{13,12},{... | collective-permute-start | bytes 442376 | tf_op jit(solution)/shard_map/ppermute | solution.py:321
  3.1 4.4 %collective-permute-start = (f32[72,512]{1,0:T(8,128)S(1)}, f32[72,512]{1,0:T(8,128)S(1)}, u32[]{:S(2)}, u32[]{:S(2)}) collective-permute-start(f32[72,512]{1,0:T(8,128)S(1)} %get-tuple-element.23.own_bottom_ref), channel_id=1, source_target_pairs={{0,1},{1,2},{2,3},{4,5},{5,6},{6,7},{8,9},{9,10},{10,11},{12,13},{... | collective-permute-start | bytes 442376 | tf_op jit(solution)/shard_map/ppermute | solution.py:320

commit v5 on v4

v5 whole, which is shorter than its diff:
```python
import functools
import math

import jax
import jax.numpy as jnp
from jax import lax
from jax.experimental import pallas as pl
from jax.experimental.pallas import tpu as pltpu
from jax.sharding import PartitionSpec as P

STEPS = 3
SEGS = 2048
F32 = jnp.float32
BF16 = jnp.bfloat16
VMEM = pl.BlockSpec(memory_space=pltpu.VMEM)
HBM = pl.BlockSpec(memory_space=pltpu.HBM)
GRANT = pltpu.CompilerParams(vmem_limit_bytes=16 * 2**20)


def split(x):
    high = x.astype(BF16)
    return high, (x - high.astype(F32)).astype(BF16)


def dot(a, b):
    return jnp.dot(a, b, preferred_element_type=F32)


def left_three(matrix):
    high, low = matrix
    return jnp.concatenate([high, low, high], axis=1)


def right_three(x):
    high, low = split(x)
    return jnp.concatenate([high, high, low], axis=0)


def iota(shape, dim):
    return lax.broadcasted_iota(jnp.int32, shape, dim)


def shift_next(x, axis):
    size = x.shape[axis]
    return jnp.where(iota(x.shape, axis) == size - 1, 0.0, pltpu.roll(x, size - 1, axis))


def shift_prev(x, axis, first):
    return jnp.where(iota(x.shape, axis) == 0, first, pltpu.roll(x, 1, axis))


def divergence(v, weight, half, axis):
    flux = weight * (shift_next(v, axis) - v)
    return flux - shift_prev(flux, axis, half * v)


def sides(rows):
    span = lax.axis_index("span")
    count = lax.axis_size("span")
    even = lax.rem(span, 2) == 0
    has_next = span + 1 < count
    has_prev = span > 0
    return (
        (even, jnp.where(even, has_next, has_prev)),
        (jnp.logical_not(even), jnp.where(even, has_prev, has_next)),
    )


def load_kernel(
    frame_hbm,
    k_hbm,
    res_hbm,
    excess_hbm,
    d_hbm,
    map_hbm,
    far_ref,
    near_ref,
    k_ref,
    frames_ref,
    excess_ref,
    d_ref,
    map_ref,
    frame_ref,
    res_ref,
    sems,
):
    pairs = (
        (frame_hbm, frame_ref),
        (res_hbm, res_ref),
        (k_hbm, k_ref),
        (excess_hbm, excess_ref),
        (d_hbm, d_ref),
        (map_hbm, map_ref),
    )
    copies = [pltpu.make_async_copy(a, b, sems.at[n]) for n, (a, b) in enumerate(pairs)]
    for copy in copies:
        copy.start()
    depth, rows, cols = k_ref.shape
    base = 2 * depth
    even = lax.rem(lax.axis_index("span"), 2) == 0
    copies[0].wait()
    copies[1].wait()
    for step in range(STEPS):
        frames_ref[step] = res_ref[frame_ref[step]]
    copies[2].wait()
    edges = []
    for edge, second in ((0, 1), (rows - 1, rows - 2)):
        fields = [
            frames_ref[2, edge : edge + 1, :],
            frames_ref[1, edge : edge + 1, :],
            frames_ref[2, second : second + 1, :],
            jnp.zeros((5, cols), F32),
        ]
        edges.append((k_ref[:, edge, :], k_ref[:, second, :], jnp.concatenate(fields, axis=0)))
    starts = (0, depth, base, base + 8)
    for n in range(3):
        first, last = edges[0][n], edges[1][n]
        near_ref[starts[n] : starts[n + 1], :] = jnp.where(even, last, first)
        far_ref[starts[n] : starts[n + 1], :] = jnp.where(even, first, last)
    for copy in copies[3:]:
        copy.wait()


def base_kernel(
    scale,
    k_ref,
    frames_ref,
    excess_ref,
    d_ref,
    adj_ref,
    edge_ref,
    contribution_ref,
    quad_ref,
    place_ref,
    mat_ref,
    right_ref,
    first_ref,
    chord_ref,
    span_ref,
    factor_ref,
):
    depth, rows, cols = k_ref.shape
    size = depth * rows
    factor_ref[...] = jnp.broadcast_to(d_ref[:, 0:1], factor_ref.shape)

    parts = split(d_ref[...])
    tall = (iota((size, depth), 0) // rows == iota((size, depth), 1)).astype(BF16)
    wide = (iota((depth, size), 0) == iota((depth, size), 1) // rows).astype(BF16)
    four = 4 * depth
    tile = (iota((depth, four), 0) == iota((depth, four), 1) % depth).astype(BF16)
    same = iota((size, size), 0) % rows == iota((size, size), 1) % rows
    quad_same = iota((four, four), 0) // depth == iota((four, four), 1) // depth
    targets = []
    for after, _ in sides(rows):
        targets.append(jnp.where(after, rows - 1, 0))
        targets.append(jnp.where(after, rows - 2, 1))
    which = iota((size, four), 1) // depth
    target = jnp.where(
        which == 0,
        targets[0],
        jnp.where(which == 1, targets[1], jnp.where(which == 2, targets[2], targets[3])),
    )
    placed = iota((size, four), 0) % rows == target
    mats, quads, places = [], [], []
    for part in parts:
        column = dot(tall, part).astype(BF16)
        row = dot(part, tile)
        mats.append(jnp.where(same, dot(column, wide), 0.0).astype(BF16))
        places.append(jnp.where(placed, dot(column, tile), 0.0).astype(BF16))
        stacked = jnp.concatenate([row] * 4, axis=0)
        quads.append(jnp.where(quad_same, stacked, 0.0).astype(BF16))
    mat_ref[...] = left_three(mats)
    quad_ref[...] = left_three(quads)
    place_ref[...] = left_three(places)

    f = frames_ref[2]
    f_chord = shift_next(f, 1) - f
    f_span = shift_next(f, 0) - f

    def put(i, both):
        high, low = split(both)
        span = pl.ds(i * rows, 2 * rows)
        right_ref[0, span, :] = high
        right_ref[1, span, :] = high
        right_ref[2, span, :] = low

    for i in range(0, depth, 2):
        found = []
        for j in (i, i + 1):
            half = 0.5 * k_ref[j]
            w_chord = half + shift_next(half, 1)
            w_span = half + shift_next(half, 0)
            chord_ref[j] = w_chord
            span_ref[j] = w_span
            edge = half * f
            flux_chord = w_chord * f_chord
            flux_span = w_span * f_span
            moved = f + flux_chord - shift_prev(flux_chord, 1, edge)
            moved = moved + flux_span - shift_prev(flux_span, 0, edge)
            factor = jnp.concatenate(
                [jnp.broadcast_to(factor_ref[j : j + 1, :], (rows, 128))] * (cols // 128), axis=1
            )
            source = factor * moved
            found.append(source + frames_ref[1] if j == 0 else source)
        put(i, jnp.concatenate(found, axis=0))
    right = right_ref[...].reshape(3 * size, cols)
    first_ref[...] = dot(mat_ref[...], right).reshape(depth, rows, cols)

    for i in range(0, depth, 2):
        found = []
        for j in (i, i + 1):
            v = first_ref[j]
            half = 0.5 * k_ref[j]
            source = (
                v + divergence(v, chord_ref[j], half, 1) + divergence(v, span_ref[j], half, 0)
            )
            found.append(source + frames_ref[0] if j == 0 else source)
        put(i, jnp.concatenate(found, axis=0))
    right = right_ref[...].reshape(3 * size, cols)
    adj_ref[...] = dot(mat_ref[...], right).reshape(depth, rows, cols)

    top = first_ref[:, 0, :]
    bottom = first_ref[:, rows - 1, :]
    for n, (after, _) in enumerate(sides(rows)):
        edge_ref[n] = jnp.where(after, bottom, top)
    contribution_ref[...] = scale * (
        d_ref[0:1, 0:1] * f * excess_ref[2]
        + first_ref[0] * excess_ref[1]
        + adj_ref[0] * excess_ref[0]
    )


def correct_kernel(
    scale,
    map_vmem,
    d_ref,
    excess_ref,
    base_ref,
    edge_ref,
    contribution_ref,
    quad_ref,
    place_ref,
    own_far_ref,
    own_near_ref,
    far_ref,
    near_ref,
    adj_hbm,
    part_ref,
    adj_ref,
    map_ref,
    sems,
):
    map_copy = pltpu.make_async_copy(map_vmem, map_ref, sems.at[0])
    map_copy.start()
    depth, rows, cols = base_ref.shape
    blocks = cols // 128
    base = 2 * depth
    factor = d_ref[:, 0:1]
    surface = iota((depth, 1), 0) == 0

    kept = []
    sources = []
    pairs = ((near_ref, own_near_ref), (far_ref, own_far_ref))
    for (got, own), (after, inside) in zip(pairs, sides(rows)):
        half = 0.5 * got[0:depth, :]
        half_next = 0.5 * got[depth:base, :]
        half_own = 0.5 * own[0:depth, :]
        half_second = 0.5 * own[depth:base, :]
        f = got[base : base + 1, :]
        frame = got[base + 1 : base + 2, :]
        f_next = got[base + 2 : base + 3, :]
        f_own = own[base : base + 1, :]
        face = half + half_own
        w_chord = half + shift_next(half, 1)
        flux = w_chord * (shift_next(f, 1) - f)
        moved = (
            f
            + flux
            - shift_prev(flux, 1, half * f)
            + (half + half_next) * (f_next - f)
            + face * (f_own - f)
        )
        outer = factor * moved + jnp.where(surface, frame, 0.0)
        sources.append(factor * (face * f - half * f_own))
        sources.append(jnp.where(inside, outer, 0.0))
        kept.append((half, half_own, half_own + half_second, face, after))
    found = dot(quad_ref[...], right_three(jnp.concatenate(sources, axis=0)))

    sources = []
    surfaces = []
    for n, (half, half_own, inner, face, after) in enumerate(kept):
        e = found[2 * n * depth : (2 * n + 1) * depth]
        outer = found[(2 * n + 1) * depth : (2 * n + 2) * depth]
        w_chord = half_own + shift_next(half_own, 1)
        change = (
            e
            + divergence(e, w_chord, half_own, 1)
            - (half + half_own + inner) * e
            + face * outer
            - half * edge_ref[n]
        )
        sources.append(change)
        sources.append(inner * e)
        row = jnp.where(after, rows - 1, 0)
        surfaces.append(jnp.where(iota((rows, cols), 0) == row, e[0:1, :], 0.0))
    found = dot(place_ref[...], right_three(jnp.concatenate(sources, axis=0)))
    adj_ref[...] = base_ref[...] + found.reshape(depth, rows, cols)
    adj_copy = pltpu.make_async_copy(adj_ref, adj_hbm, sems.at[1])
    adj_copy.start()

    contribution = contribution_ref[...] + scale * (
        (surfaces[0] + surfaces[1]) * excess_ref[1] + found[0:rows, :] * excess_ref[0]
    )
    owners, _, lanes = part_ref.shape
    shape = (owners, 128)
    lane = iota(shape, 1)
    segment = jnp.where(lane < lanes, iota(shape, 0) * lanes + lane, -1)
    total = jnp.zeros(shape, F32)
    map_copy.wait()
    for block in range(blocks):
        sums = jnp.sum(contribution[:, block * 128 : (block + 1) * 128], axis=1, keepdims=True)
        for row in range(rows):
            total += jnp.where(segment == map_ref[block, row], sums[row : row + 1, :], 0.0)
    part_ref[...] = total[:, None, :lanes]
    adj_copy.wait()


def per_device(
    conductance, depth_inverse, surface_residual, surface_excess, segment_map, frame_index
):
    _, depth, rows, cols = conductance.shape
    frames = surface_residual.shape[1]
    blocks = segment_map.shape[1]
    size = depth * rows
    four = 4 * depth
    spans = lax.axis_size("span")
    devices = spans * lax.axis_size("blade")
    lanes = SEGS // devices
    field = pltpu.VMEM((depth, rows, cols), F32)
    packed = pltpu.VMEM((2 * depth + 8, cols), F32)
    own_far, own_near, k, picked, excess, inverse, ids = pl.pallas_call(
        load_kernel,
        out_shape=(
            packed,
            packed,
            field,
            pltpu.VMEM((STEPS, rows, cols), F32),
            pltpu.VMEM((STEPS, rows, cols), F32),
            pltpu.VMEM((depth, depth), F32),
            pltpu.VMEM((blocks, rows), jnp.int32),
        ),
        in_specs=[HBM] * 6,
        out_specs=(VMEM,) * 7,
        scratch_shapes=[
            pltpu.SMEM((STEPS,), jnp.int32),
            pltpu.VMEM((frames, rows, cols), F32),
            pltpu.SemaphoreType.DMA((6,)),
        ],
        compiler_params=GRANT,
        name="load",
    )(
        *(
            pltpu.with_memory_space_constraint(x, pltpu.HBM)
            for x in (
                frame_index,
                conductance[0],
                surface_residual[0],
                surface_excess[0],
                depth_inverse[0],
                segment_map.T,
            )
        )
    )
    across = [(i, i + 1) for i in range(1, spans - 1, 2)]
    within = [(i, i + 1) for i in range(0, spans - 1, 2)]
    near = lax.ppermute(own_near, "span", within + [(b, a) for a, b in within])
    far = lax.ppermute(own_far, "span", across + [(b, a) for a, b in across])
    scale = 1.0 / math.sqrt(128.0 * STEPS)
    base, edge, contribution, quad, place = pl.pallas_call(
        functools.partial(base_kernel, scale),
        out_shape=(
            field,
            pltpu.VMEM((2, depth, cols), F32),
            pltpu.VMEM((rows, cols), F32),
            pltpu.VMEM((four, 3 * four), BF16),
            pltpu.VMEM((size, 3 * four), BF16),
        ),
        in_specs=[VMEM] * 4,
        out_specs=(VMEM,) * 5,
        scratch_shapes=[
            pltpu.VMEM((size, 3 * size), BF16),
            pltpu.VMEM((3, size, cols), BF16),
            field,
            field,
            field,
            pltpu.VMEM((depth, 128), F32),
        ],
        compiler_params=GRANT,
        name="base",
    )(k, picked, excess, inverse)
    adjoint, partial = pl.pallas_call(
        functools.partial(correct_kernel, scale),
        out_shape=(
            pltpu.HBM((depth, rows, cols), F32),
            pltpu.VMEM((devices, 1, lanes), F32),
        ),
        in_specs=[VMEM] * 12,
        out_specs=(HBM, VMEM),
        scratch_shapes=[
            field,
            pltpu.SMEM((blocks, rows), jnp.int32),
            pltpu.SemaphoreType.DMA((2,)),
        ],
        compiler_params=GRANT,
        name="correct",
    )(
        ids,
        inverse,
        excess,
        base,
        edge,
        contribution,
        quad,
        place,
        own_far,
        own_near,
        far,
        near,
    )
    pieces = lax.all_to_all(partial, ("blade", "span"), 0, 0, tiled=True)
    return (adjoint[None], jnp.sum(pieces, axis=(0, 1)))


def solution(mesh):
    placed = (
        P("blade", None, "span", None),
        P("blade", None, None),
        P("blade", None, "span", None),
        P("blade", None, "span", None),
        P("span", None),
        P(),
    )
    return jax.shard_map(
        per_device,
        mesh=mesh,
        in_specs=placed,
        out_specs=(P("blade", None, "span", None), P(("blade", "span"))),
        check_vma=False,
    )
```

time: 28.7 us -> 25 us (0.87)
  blocking collectives: 16.9 us -> 14 us
  Pallas kernels: 6.03 us -> 4.6 us
  starting transfers between devices: 4.33 us -> 5.03 us
    all_to_all x1, blocking collectives: 16.9 us -> 14 us  [per_device(): pieces = lax.all_to_all(partial, ('blade', 'span'), 0, 0, tiled=True)]
    pallas_call x3, Pallas kernels: 6.03 us -> 4.6 us  [the longest x1 1.71 us: per_device(): pl.pallas_call(functools.partial(correct_kernel, scale), out_shape=(pltpu...]
    ppermute x2, starting transfers between devices: 4.33 us -> 5.03 us  [the longest x1 4.36 us: per_device(): near = lax.ppermute(own_near, 'span', within + [(b, a) for a, b in within])]
  transfers between devices with their start and end apart: 2 -> 2, of which waited for: 0 -> 0; matrix products, arithmetic and copies ran while one was open for 0% -> 0% of each run, Pallas kernels for 5% -> 7%
where the time goes in v5:
time: 25 us; the launch traced here: 24.9 us
  blocking collectives  14 us (56%)
  starting transfers between devices  5.03 us (20%)
  Pallas kernels  4.6 us (18%)
  between operations  0.68 us (3%)
  other arithmetic  0.56 us (2%)
    all_to_all x1, blocking collectives, per_device(): pieces = lax.all_to_all(partial, ('blade', 'span'), 0, 0, tiled=True)  14 us
    ppermute x1, starting transfers between devices, per_device(): near = lax.ppermute(own_near, 'span', within + [(b, a) for a, b in within])  4.36 us
    pallas_call x1, Pallas kernels, per_device(): pl.pallas_call(functools.partial(correct_kernel, scale), out_shape=(pltpu...  1.71 us
    pallas_call x1, Pallas kernels, per_device(): pl.pallas_call(functools.partial(base_kernel, scale), out_shape=(field, p...  1.67 us
    pallas_call x1, Pallas kernels, per_device(): pl.pallas_call(load_kernel, out_shape=(packed, packed, field, pltpu.VMEM(...  1.22 us
    ppermute x1, starting transfers between devices, per_device(): far = lax.ppermute(own_far, 'span', across + [(b, a) for a, b in across])  0.67 us
    reduce_sum x1, other arithmetic, per_device(): return (adjoint[None], jnp.sum(pieces, axis=(0, 1)))  0.56 us
  transfers between devices with their start and end apart: 2, of which 0 were waited for; matrix products, arithmetic and copies ran while one was open for 0% of the time, Pallas kernels for 7%

profile of v5, /device:TPU:0, one launch (start us, length us, event | category | flops | bytes accessed | tf_op | source)
XLA Modules:
  0.0 24.9 jit_solution(11679737639486178584)
XLA Ops:
  0.6 1.2 %load.1 = (f32[72,512]{1,0:T(8,128)S(1)}, f32[72,512]{1,0:T(8,128)S(1)}, f32[32,8,512]{2,1,0:T(8,128)S(1)}, f32[3,8,512]{2,1,0:T(8,128)S(1)}, f32[3,8,512]{2,1,0...) custom-call(s32[3]{0:T(128)} %frame_hbm.1, f32[32,8,512]{2,1,0:T(8,128)} %bitcast.6, f32[4,8,512]{2,1,0:T(8,128)} %bitcast.7, ...), custom_call_target="tpu_custom_call" | custom-call | tf_op jit(solution)/shard_map/load/pallas_call | solution.py:341
  1.9 0.7 %collective-permute-start = (f32[72,512]{1,0:T(8,128)S(1)}, f32[72,512]{1,0:T(8,128)S(1)}, u32[]{:S(2)}, u32[]{:S(2)}) collective-permute-start(f32[72,512]{1,0:T(8,128)S(1)} %get-tuple-element.26.own_far_ref), channel_id=1, source_target_pairs={{1,2},{2,1},{5,6},{6,5},{9,10},{10,9},{13,14},{14,13},{17,18},{18,... | collective-permute-start | bytes 442376 | tf_op jit(solution)/shard_map/ppermute | solution.py:377
  2.5 4.4 %collective-permute-start.1 = (f32[72,512]{1,0:T(8,128)S(1)}, f32[72,512]{1,0:T(8,128)S(1)}, u32[]{:S(2)}, u32[]{:S(2)}) collective-permute-start(f32[72,512]{1,0:T(8,128)S(1)} %get-tuple-element.27.own_near_ref), channel_id=1, source_target_pairs={{0,1},{2,3},{1,0},{3,2},{4,5},{6,7},{5,4},{7,6},{8,9},{10,11},{9,8... | collective-permute-start | bytes 442376 | tf_op jit(solution)/shard_map/ppermute | solution.py:376
  6.9 1.7 %base.1 = (f32[32,8,512]{2,1,0:T(8,128)S(1)}, f32[2,32,512]{2,1,0:T(8,128)S(1)}, f32[8,512]{1,0:T(8,128)S(1)}, bf16[128,384]{1,0:T(8,128)(2,1)S(1)}, bf16[256,384]{1,0:T(8,128)(2,1)S(1)}) custom-call(f32[32,8,512]{2,1,0:T(8,128)S(1)} %get-tuple-element.19.k_ref, f32[3,8,512]{2,1,0:T(8,128)S(1)} %get-tuple-element.20.frames_ref, ...), custom_call_target="tpu_custom_call" | custom-call | tf_op jit(solution)/shard_map/base/pallas_call | solution.py:379
  8.6 0.0 collective-permute-done.far_ref
  8.6 0.0 collective-permute-done.1.near_ref
  8.6 1.7 %correct.1 = (f32[32,8,512]{2,1,0:T(8,128)}, f32[32,1,64]{2,1,0:T(1,128)S(1)}) custom-call(s32[4,8]{1,0:T(4,128)S(1)} %get-tuple-element.16.map_vmem, f32[32,32]{1,0:T(8,128)S(1)} %get-tuple-element.17.d_ref, f32[3,8,512]{2,1,0:T(8,128)S(1)} %get-tuple-element.18.excess_ref, f32[32,8,512]{2,1,0:T(8,128)S(1)} %get-tuple-element.21.base_ref, ...), custom_call_target="tpu_custom_call" | custom-call | tf_op jit(solution)/shard_map/correct/pallas_call | solution.py:401
  10.3 14.0 %all_to_all.5 = f32[32,1,64]{2,1,0:T(1,128)S(1)} all-to-all(f32[32,1,64]{2,1,0:T(1,128)S(1)} %get-tuple-element.29), channel_id=1, replica_groups=mesh['blade'=8,'span'=4] {'blade','span'}, dimensions={0} | all-to-all | bytes 16384 | tf_op jit(solution)/shard_map/all_to_all | solution.py:430
  24.3 0.6 %reduce_sum.9 = f32[64]{0:T(128)} reduce(f32[32,1,64]{2,1,0:T(1,128)S(1)} %all_to_all.5, f32[]{:T(128)} %constant.0.clone.1), dimensions={0,1}, to_apply=%region_0.0 | reduce | flops 1984 | bytes 8452 | tf_op jit(solution)/shard_map/reduce_sum | solution.py:431
Async XLA Ops:
  1.9 6.7 %collective-permute-start = (f32[72,512]{1,0:T(8,128)S(1)}, f32[72,512]{1,0:T(8,128)S(1)}, u32[]{:S(2)}, u32[]{:S(2)}) collective-permute-start(f32[72,512]{1,0:T(8,128)S(1)} %get-tuple-element.26.own_far_ref), channel_id=1, source_target_pairs={{1,2},{2,1},{5,6},{6,5},{9,10},{10,9},{13,14},{14,13},{17,18},{18,... | collective-permute-start | bytes 442376 | tf_op jit(solution)/shard_map/ppermute | solution.py:377
  2.5 6.0 %collective-permute-start.1 = (f32[72,512]{1,0:T(8,128)S(1)}, f32[72,512]{1,0:T(8,128)S(1)}, u32[]{:S(2)}, u32[]{:S(2)}) collective-permute-start(f32[72,512]{1,0:T(8,128)S(1)} %get-tuple-element.27.own_near_ref), channel_id=1, source_target_pairs={{0,1},{2,3},{1,0},{3,2},{4,5},{6,7},{5,4},{7,6},{8,9},{10,11},{9,8... | collective-permute-start | bytes 442376 | tf_op jit(solution)/shard_map/ppermute | solution.py:376

commit v6 on v5

--- a/solution.py
+++ b/solution.py
@@ -311,18 +311,39 @@
     contribution = contribution_ref[...] + scale * (
         (surfaces[0] + surfaces[1]) * excess_ref[1] + found[0:rows, :] * excess_ref[0]
     )
-    owners, _, lanes = part_ref.shape
-    shape = (owners, 128)
+    shape = (rows, 128)
     lane = iota(shape, 1)
-    segment = jnp.where(lane < lanes, iota(shape, 0) * lanes + lane, -1)
-    total = jnp.zeros(shape, F32)
+    held = jnp.zeros(shape, F32)
+    for block in range(blocks):
+        sums = jnp.sum(contribution[:, block * 128 : (block + 1) * 128], axis=1, keepdims=True)
+        held += jnp.where(lane == block * rows + iota(shape, 0), sums, 0.0)
+    line = jnp.sum(held, axis=0, keepdims=True)
+    place = iota((1, 128), 1)
     map_copy.wait()
     for block in range(blocks):
-        sums = jnp.sum(contribution[:, block * 128 : (block + 1) * 128], axis=1, keepdims=True)
         for row in range(rows):
-            total += jnp.where(segment == map_ref[block, row], sums[row : row + 1, :], 0.0)
-    part_ref[...] = total[:, None, :lanes]
+            spot = (blocks + block) * rows + row
+            line = jnp.where(place == spot, map_ref[block, row].astype(F32), line)
+    part_ref[...] = line
     adj_copy.wait()
+
+
+def pick_kernel(spans, lanes, entries, got_ref, out_ref):
+    devices = got_ref.shape[0]
+    mine = lax.axis_index("blade") * spans + lax.axis_index("span")
+    segment = (iota((lanes, entries), 0) + mine * lanes).astype(F32)
+    sums = jnp.sum(got_ref[...].reshape(devices // spans, spans, 128), axis=0)
+    total = jnp.zeros((8, lanes), F32)
+    for n in range(spans):
+        hit = (got_ref[n : n + 1, entries : 2 * entries] == segment).astype(BF16)
+        value = sums[n : n + 1, 0:entries]
+        high, rest = split(value)
+        low = (value - high.astype(F32) - rest.astype(F32)).astype(BF16)
+        rows = jnp.concatenate([high, rest, low, jnp.zeros((5, entries), BF16)], axis=0)
+        total += lax.dot_general(
+            rows, hit, (((1,), (1,)), ((), ())), preferred_element_type=F32
+        )
+    out_ref[...] = jnp.sum(total, axis=0)
 
 
 def per_device(
@@ -402,7 +423,7 @@
         functools.partial(correct_kernel, scale),
         out_shape=(
             pltpu.HBM((depth, rows, cols), F32),
-            pltpu.VMEM((devices, 1, lanes), F32),
+            pltpu.VMEM((1, 128), F32),
         ),
         in_specs=[VMEM] * 12,
         out_specs=(HBM, VMEM),
@@ -427,8 +448,16 @@
         far,
         near,
     )
-    pieces = lax.all_to_all(partial, ("blade", "span"), 0, 0, tiled=True)
-    return (adjoint[None], jnp.sum(pieces, axis=(0, 1)))
+    pieces = lax.all_gather(partial, ("blade", "span"), axis=0, tiled=True)
+    owned = pl.pallas_call(
+        functools.partial(pick_kernel, spans, lanes, blocks * rows),
+        out_shape=pltpu.HBM((lanes,), F32),
+        in_specs=[VMEM],
+        out_specs=VMEM,
+        compiler_params=GRANT,
+        name="pick",
+    )(pieces)
+    return (adjoint[None], owned)
 
 
 def solution(mesh):

time: 25 us -> 54 us (2.16)
  blocking collectives: 14 us -> 42.8 us
  Pallas kernels: 4.6 us -> 5.34 us
  other arithmetic: 0.56 us -> 0 us
    all_gather x0 -> x1, blocking collectives: none -> 42.8 us  [per_device(): pieces = lax.all_gather(partial, ('blade', 'span'), axis=0, tiled=True)]
    all_to_all x1 -> x0, blocking collectives: 14 us -> none  [per_device(): pieces = lax.all_to_all(partial, ('blade', 'span'), 0, 0, tiled=True)]
    pallas_call x0 -> x1, Pallas kernels: none -> 0.74 us  [per_device(): pl.pallas_call(functools.partial(pick_kernel, spans, lanes, blocks * rows...]
    reduce_sum x1 -> x0, other arithmetic: 0.56 us -> none  [per_device(): return (adjoint[None], jnp.sum(pieces, axis=(0, 1)))]
  transfers between devices with their start and end apart: 2 -> 2, of which waited for: 0 -> 0; matrix products, arithmetic and copies ran while one was open for 0% -> 0% of each run, Pallas kernels for 7% -> 3%
where the time goes in v6:
time: 54 us; the launch traced here: 53.8 us
  blocking collectives  42.8 us (79%)
  Pallas kernels  5.34 us (10%)
  starting transfers between devices  5.03 us (9%)
  between operations  0.68 us (1%)
    all_gather x1, blocking collectives, per_device(): pieces = lax.all_gather(partial, ('blade', 'span'), axis=0, tiled=True)  42.8 us
    ppermute x1, starting transfers between devices, per_device(): near = lax.ppermute(own_near, 'span', within + [(b, a) for a, b in within])  4.36 us
    pallas_call x1, Pallas kernels, per_device(): pl.pallas_call(functools.partial(correct_kernel, scale), out_shape=(pltpu...  1.71 us
    pallas_call x1, Pallas kernels, per_device(): pl.pallas_call(functools.partial(base_kernel, scale), out_shape=(field, p...  1.67 us
    pallas_call x1, Pallas kernels, per_device(): pl.pallas_call(load_kernel, out_shape=(packed, packed, field, pltpu.VMEM(...  1.22 us
  transfers between devices with their start and end apart: 2, of which 0 were waited for; matrix products, arithmetic and copies ran while one was open for 0% of the time, Pallas kernels for 3%

profile of v6, /device:TPU:0, one launch (start us, length us, event | category | flops | bytes accessed | tf_op | source)
XLA Modules:
  0.0 53.8 jit_solution(9703948637444029107)
XLA Ops:
  0.6 1.2 %load.1 = (f32[72,512]{1,0:T(8,128)S(1)}, f32[72,512]{1,0:T(8,128)S(1)}, f32[32,8,512]{2,1,0:T(8,128)S(1)}, f32[3,8,512]{2,1,0:T(8,128)S(1)}, f32[3,8,512]{2,1,0...) custom-call(s32[3]{0:T(128)} %frame_hbm.1, f32[32,8,512]{2,1,0:T(8,128)} %bitcast.10, f32[4,8,512]{2,1,0:T(8,128)} %bitcast.11, ...), custom_call_target="tpu_custom_call" | custom-call | tf_op jit(solution)/shard_map/load/pallas_call | solution.py:362
  1.9 0.7 %collective-permute-start = (f32[72,512]{1,0:T(8,128)S(1)}, f32[72,512]{1,0:T(8,128)S(1)}, u32[]{:S(2)}, u32[]{:S(2)}) collective-permute-start(f32[72,512]{1,0:T(8,128)S(1)} %get-tuple-element.26.own_far_ref), channel_id=1, source_target_pairs={{1,2},{2,1},{5,6},{6,5},{9,10},{10,9},{13,14},{14,13},{17,18},{18,... | collective-permute-start | bytes 442376 | tf_op jit(solution)/shard_map/ppermute | solution.py:398
  2.5 4.4 %collective-permute-start.1 = (f32[72,512]{1,0:T(8,128)S(1)}, f32[72,512]{1,0:T(8,128)S(1)}, u32[]{:S(2)}, u32[]{:S(2)}) collective-permute-start(f32[72,512]{1,0:T(8,128)S(1)} %get-tuple-element.27.own_near_ref), channel_id=1, source_target_pairs={{0,1},{2,3},{1,0},{3,2},{4,5},{6,7},{5,4},{7,6},{8,9},{10,11},{9,8... | collective-permute-start | bytes 442376 | tf_op jit(solution)/shard_map/ppermute | solution.py:397
  6.9 1.7 %base.1 = (f32[32,8,512]{2,1,0:T(8,128)S(1)}, f32[2,32,512]{2,1,0:T(8,128)S(1)}, f32[8,512]{1,0:T(8,128)S(1)}, bf16[128,384]{1,0:T(8,128)(2,1)S(1)}, bf16[256,384]{1,0:T(8,128)(2,1)S(1)}) custom-call(f32[32,8,512]{2,1,0:T(8,128)S(1)} %get-tuple-element.19.k_ref, f32[3,8,512]{2,1,0:T(8,128)S(1)} %get-tuple-element.20.frames_ref, ...), custom_call_target="tpu_custom_call" | custom-call | tf_op jit(solution)/shard_map/base/pallas_call | solution.py:400
  8.6 0.0 collective-permute-done.far_ref
  8.6 0.0 collective-permute-done.1.near_ref
  8.6 1.7 %correct.1 = (f32[32,8,512]{2,1,0:T(8,128)}, f32[1,128]{1,0:T(1,128)S(1)}) custom-call(s32[4,8]{1,0:T(4,128)S(1)} %get-tuple-element.16.map_vmem, f32[32,32]{1,0:T(8,128)S(1)} %get-tuple-element.17.d_ref, f32[3,8,512]{2,1,0:T(8,128)S(1)} %get-tuple-element.18.excess_ref, f32[32,8,512]{2,1,0:T(8,128)S(1)} %get-tuple-element.21.base_ref, ...), custom_call_target="tpu_custom_call" | custom-call | tf_op jit(solution)/shard_map/correct/pallas_call | solution.py:422
  10.3 42.8 %all-gather = f32[32,1,128]{2,1,0:T(1,128)S(1)} all-gather(f32[1,1,128]{2,1,0:T(1,128)S(1)} %bitcast.9), channel_id=1, replica_groups=mesh['blade'=8,'span'=4] {'blade','span'}, dimensions={0}, use_global_device_ids=true | all-gather | bytes 16896 | tf_op jit(solution)/shard_map/all_gather | solution.py:451
  53.1 0.7 %pick.1 = f32[64]{0:T(128)} custom-call(f32[32,128]{1,0:T(8,128)S(1)} %bitcast.8), custom_call_target="tpu_custom_call" | custom-call | tf_op jit(solution)/shard_map/pick/pallas_call | solution.py:452
Async XLA Ops:
  1.9 6.7 %collective-permute-start = (f32[72,512]{1,0:T(8,128)S(1)}, f32[72,512]{1,0:T(8,128)S(1)}, u32[]{:S(2)}, u32[]{:S(2)}) collective-permute-start(f32[72,512]{1,0:T(8,128)S(1)} %get-tuple-element.26.own_far_ref), channel_id=1, source_target_pairs={{1,2},{2,1},{5,6},{6,5},{9,10},{10,9},{13,14},{14,13},{17,18},{18,... | collective-permute-start | bytes 442376 | tf_op jit(solution)/shard_map/ppermute | solution.py:398
  2.5 6.0 %collective-permute-start.1 = (f32[72,512]{1,0:T(8,128)S(1)}, f32[72,512]{1,0:T(8,128)S(1)}, u32[]{:S(2)}, u32[]{:S(2)}) collective-permute-start(f32[72,512]{1,0:T(8,128)S(1)} %get-tuple-element.27.own_near_ref), channel_id=1, source_target_pairs={{0,1},{2,3},{1,0},{3,2},{4,5},{6,7},{5,4},{7,6},{8,9},{10,11},{9,8... | collective-permute-start | bytes 442376 | tf_op jit(solution)/shard_map/ppermute | solution.py:397

commit v7 on v5

v7 whole, which is shorter than its diff:
```python
import functools
import math

import jax
import jax.numpy as jnp
from jax import lax
from jax.experimental import pallas as pl
from jax.experimental.pallas import tpu as pltpu
from jax.sharding import PartitionSpec as P

STEPS = 3
SEGS = 2048
CHUNKS = 4
F32 = jnp.float32
BF16 = jnp.bfloat16
VMEM = pl.BlockSpec(memory_space=pltpu.VMEM)
HBM = pl.BlockSpec(memory_space=pltpu.HBM)
GRANT = pltpu.CompilerParams(vmem_limit_bytes=16 * 2**20)


def split(x):
    high = x.astype(BF16)
    return high, (x - high.astype(F32)).astype(BF16)


def dot(a, b):
    return jnp.dot(a, b, preferred_element_type=F32)


def left_three(matrix):
    high, low = matrix
    return jnp.concatenate([high, low, high], axis=1)


def right_three(x):
    high, low = split(x)
    return jnp.concatenate([high, high, low], axis=0)


def iota(shape, dim):
    return lax.broadcasted_iota(jnp.int32, shape, dim)


def shift_next(x, axis):
    size = x.shape[axis]
    return jnp.where(iota(x.shape, axis) == size - 1, 0.0, pltpu.roll(x, size - 1, axis))


def shift_prev(x, axis, first):
    return jnp.where(iota(x.shape, axis) == 0, first, pltpu.roll(x, 1, axis))


def divergence(v, weight, half, axis):
    flux = weight * (shift_next(v, axis) - v)
    return flux - shift_prev(flux, axis, half * v)


def sides():
    span = lax.axis_index("span")
    count = lax.axis_size("span")
    even = lax.rem(span, 2) == 0
    has_next = span + 1 < count
    has_prev = span > 0
    return (
        (even, jnp.where(even, has_next, has_prev)),
        (jnp.logical_not(even), jnp.where(even, has_prev, has_next)),
    )


def load_kernel(
    frame_hbm,
    k_hbm,
    res_hbm,
    excess_hbm,
    d_hbm,
    map_hbm,
    far_ref,
    near_ref,
    k_ref,
    frames_ref,
    excess_ref,
    d_ref,
    map_ref,
    frame_ref,
    res_ref,
    line_ref,
    sems,
):
    depth, rows, cols = k_ref.shape
    base = 2 * depth
    pairs = []
    sent = (near_ref, far_ref)
    for n, (after, _) in enumerate(sides()):
        edge = jnp.where(after, rows - 1, 0)
        second = jnp.where(after, rows - 2, 1)
        pairs += [
            (k_hbm.at[:, edge, :], sent[n].at[0:depth, :]),
            (k_hbm.at[:, second, :], sent[n].at[depth:base, :]),
            (res_hbm.at[:, edge, :], line_ref.at[2 * n]),
            (res_hbm.at[:, second, :], line_ref.at[2 * n + 1]),
        ]
    pairs += [
        (frame_hbm, frame_ref),
        (res_hbm, res_ref),
        (k_hbm, k_ref),
        (excess_hbm, excess_ref),
        (d_hbm, d_ref),
        (map_hbm, map_ref),
    ]
    copies = [pltpu.make_async_copy(a, b, sems.at[n]) for n, (a, b) in enumerate(pairs)]
    for copy in copies:
        copy.start()
    for copy in copies:
        copy.wait()
    for step in range(STEPS):
        frames_ref[step] = res_ref[frame_ref[step]]
    for n, ref in enumerate(sent):
        lines = [
            line_ref[2 * n, pl.ds(frame_ref[2], 1), :],
            line_ref[2 * n, pl.ds(frame_ref[1], 1), :],
            line_ref[2 * n + 1, pl.ds(frame_ref[2], 1), :],
        ]
        rest = ref.shape[0] - base - len(lines)
        if rest:
            lines.append(jnp.zeros((rest, cols), F32))
        ref[base:, :] = jnp.concatenate(lines, axis=0)


def base_kernel(
    scale,
    k_ref,
    frames_ref,
    excess_ref,
    d_ref,
    adj_ref,
    edge_ref,
    contribution_ref,
    pair_ref,
    place_ref,
    mat_ref,
    right_ref,
    first_ref,
    chord_ref,
    span_ref,
    factor_ref,
):
    depth, rows, cols = k_ref.shape
    size = depth * rows
    factor_ref[...] = jnp.broadcast_to(d_ref[:, 0:1], factor_ref.shape)

    parts = split(d_ref[...])
    tall = (iota((size, depth), 0) // rows == iota((size, depth), 1)).astype(BF16)
    wide = (iota((depth, size), 0) == iota((depth, size), 1) // rows).astype(BF16)
    two = 2 * depth
    tile = (iota((depth, two), 0) == iota((depth, two), 1) % depth).astype(BF16)
    same = iota((size, size), 0) % rows == iota((size, size), 1) % rows
    pair_same = iota((two, two), 0) // depth == iota((two, two), 1) // depth
    row_of = iota((size, two), 0) % rows
    first_half = iota((size, two), 1) < depth
    placed = []
    for after, _ in sides():
        edge = jnp.where(after, rows - 1, 0)
        second = jnp.where(after, rows - 2, 1)
        placed.append(row_of == jnp.where(first_half, edge, second))
    mats, pairs, places = [], [], ([], [])
    for part in parts:
        column = dot(tall, part).astype(BF16)
        row = dot(part, tile)
        mats.append(jnp.where(same, dot(column, wide), 0.0).astype(BF16))
        columns = dot(column, tile)
        for found, target in zip(places, placed):
            found.append(jnp.where(target, columns, 0.0).astype(BF16))
        pairs.append(
            jnp.where(pair_same, jnp.concatenate([row] * 2, axis=0), 0.0).astype(BF16)
        )
    mat_ref[...] = left_three(mats)
    pair_ref[...] = left_three(pairs)
    for n in range(2):
        place_ref[n] = left_three(places[n])

    f = frames_ref[2]
    f_chord = shift_next(f, 1) - f
    f_span = shift_next(f, 0) - f

    def put(i, both):
        high, low = split(both)
        span = pl.ds(i * rows, 2 * rows)
        right_ref[0, span, :] = high
        right_ref[1, span, :] = high
        right_ref[2, span, :] = low

    for i in range(0, depth, 2):
        found = []
        for j in (i, i + 1):
            half = 0.5 * k_ref[j]
            w_chord = half + shift_next(half, 1)
            w_span = half + shift_next(half, 0)
            chord_ref[j] = w_chord
            span_ref[j] = w_span
            edge = half * f
            flux_chord = w_chord * f_chord
            flux_span = w_span * f_span
            moved = f + flux_chord - shift_prev(flux_chord, 1, edge)
            moved = moved + flux_span - shift_prev(flux_span, 0, edge)
            factor = jnp.concatenate(
                [jnp.broadcast_to(factor_ref[j : j + 1, :], (rows, 128))] * (cols // 128), axis=1
            )
            source = factor * moved
            found.append(source + frames_ref[1] if j == 0 else source)
        put(i, jnp.concatenate(found, axis=0))
    right = right_ref[...].reshape(3 * size, cols)
    first_ref[...] = dot(mat_ref[...], right).reshape(depth, rows, cols)

    for i in range(0, depth, 2):
        found = []
        for j in (i, i + 1):
            v = first_ref[j]
            half = 0.5 * k_ref[j]
            source = (
                v + divergence(v, chord_ref[j], half, 1) + divergence(v, span_ref[j], half, 0)
            )
            found.append(source + frames_ref[0] if j == 0 else source)
        put(i, jnp.concatenate(found, axis=0))
    right = right_ref[...].reshape(3 * size, cols)
    adj_ref[...] = dot(mat_ref[...], right).reshape(depth, rows, cols)

    top = first_ref[:, 0, :]
    bottom = first_ref[:, rows - 1, :]
    for n, (after, _) in enumerate(sides()):
        edge_ref[n] = jnp.where(after, bottom, top)
    contribution_ref[...] = scale * (
        d_ref[0:1, 0:1] * f * excess_ref[2]
        + first_ref[0] * excess_ref[1]
        + adj_ref[0] * excess_ref[0]
    )


def correction(n, got, own, d_ref, edge_ref, pair_ref, place_ref):
    _, depth, cols = edge_ref.shape
    rows = place_ref.shape[1] // depth
    base = 2 * depth
    after, inside = sides()[n]
    factor = d_ref[:, 0:1]
    half = 0.5 * got[0:depth, :]
    half_next = 0.5 * got[depth:base, :]
    half_own = 0.5 * own[0:depth, :]
    inner = half_own + 0.5 * own[depth:base, :]
    f = got[base : base + 1, :]
    frame = got[base + 1 : base + 2, :]
    f_next = got[base + 2 : base + 3, :]
    f_own = own[base : base + 1, :]
    face = half + half_own
    flux = (half + shift_next(half, 1)) * (shift_next(f, 1) - f)
    moved = (
        f
        + flux
        - shift_prev(flux, 1, half * f)
        + (half + half_next) * (f_next - f)
        + face * (f_own - f)
    )
    outer = factor * moved + jnp.where(iota((depth, 1), 0) == 0, frame, 0.0)
    sources = [factor * (face * f - half * f_own), jnp.where(inside, outer, 0.0)]
    found = dot(pair_ref[...], right_three(jnp.concatenate(sources, axis=0)))
    e = found[0:depth]
    outer = found[depth:base]
    w_chord = half_own + shift_next(half_own, 1)
    change = (
        e
        + divergence(e, w_chord, half_own, 1)
        - (half + half_own + inner) * e
        + face * outer
        - half * edge_ref[n]
    )
    found = dot(place_ref[n], right_three(jnp.concatenate([change, inner * e], axis=0)))
    row = jnp.where(after, rows - 1, 0)
    return found, jnp.where(iota((rows, cols), 0) == row, e[0:1, :], 0.0)


def near_kernel(
    scale,
    d_ref,
    excess_ref,
    edge_ref,
    pair_ref,
    place_ref,
    base_ref,
    contribution_ref,
    own_ref,
    got_ref,
    adj_ref,
    out_ref,
):
    rows = base_ref.shape[1]
    found, surface = correction(0, got_ref, own_ref, d_ref, edge_ref, pair_ref, place_ref)
    adj_ref[...] = base_ref[...] + found.reshape(base_ref.shape)
    out_ref[...] = contribution_ref[...] + scale * (
        surface * excess_ref[1] + found[0:rows, :] * excess_ref[0]
    )


def far_kernel(
    scale,
    own_ref,
    got_ref,
    d_ref,
    excess_ref,
    edge_ref,
    pair_ref,
    place_ref,
    base_ref,
    contribution_ref,
    map_vmem,
    adj_hbm,
    part_ref,
    adj_ref,
    map_ref,
    map_sem,
    sems,
):
    map_copy = pltpu.make_async_copy(map_vmem, map_ref, map_sem)
    map_copy.start()
    depth, rows, cols = base_ref.shape
    blocks = cols // 128
    found, surface = correction(1, got_ref, own_ref, d_ref, edge_ref, pair_ref, place_ref)
    step = depth // CHUNKS
    copies = []
    for n in range(CHUNKS):
        part = pl.ds(n * step, step)
        new = found[n * step * rows : (n + 1) * step * rows].reshape(step, rows, cols)
        adj_ref[part] = base_ref[part] + new
        copies.append(pltpu.make_async_copy(adj_ref.at[part], adj_hbm.at[part], sems.at[n]))
        copies[-1].start()

    contribution = contribution_ref[...] + scale * (
        surface * excess_ref[1] + found[0:rows, :] * excess_ref[0]
    )
    owners, _, lanes = part_ref.shape
    shape = (owners, 128)
    lane = iota(shape, 1)
    segment = jnp.where(lane < lanes, iota(shape, 0) * lanes + lane, -1)
    total = jnp.zeros(shape, F32)
    map_copy.wait()
    for block in range(blocks):
        sums = jnp.sum(contribution[:, block * 128 : (block + 1) * 128], axis=1, keepdims=True)
        for row in range(rows):
            total += jnp.where(segment == map_ref[block, row], sums[row : row + 1, :], 0.0)
    part_ref[...] = total[:, None, :lanes]
    for copy in copies:
        copy.wait()


def per_device(
    conductance, depth_inverse, surface_residual, surface_excess, segment_map, frame_index
):
    _, depth, rows, cols = conductance.shape
    frames = surface_residual.shape[1]
    blocks = segment_map.shape[1]
    size = depth * rows
    spans = lax.axis_size("span")
    devices = spans * lax.axis_size("blade")
    lanes = SEGS // devices
    field = pltpu.VMEM((depth, rows, cols), F32)
    packed_far = pltpu.VMEM((2 * depth + 8, cols), F32)
    packed_near = pltpu.VMEM((2 * depth + 3, cols), F32)
    own_far, own_near, k, picked, excess, inverse, ids = pl.pallas_call(
        load_kernel,
        out_shape=(
            packed_far,
            packed_near,
            field,
            pltpu.VMEM((STEPS, rows, cols), F32),
            pltpu.VMEM((STEPS, rows, cols), F32),
            pltpu.VMEM((depth, depth), F32),
            pltpu.VMEM((blocks, rows), jnp.int32),
        ),
        in_specs=[HBM] * 6,
        out_specs=(VMEM,) * 7,
        scratch_shapes=[
            pltpu.SMEM((STEPS,), jnp.int32),
            pltpu.VMEM((frames, rows, cols), F32),
            pltpu.VMEM((4, frames, cols), F32),
            pltpu.SemaphoreType.DMA((14,)),
        ],
        compiler_params=GRANT,
        name="load",
    )(
        *(
            pltpu.with_memory_space_constraint(x, pltpu.HBM)
            for x in (
                frame_index,
                conductance[0],
                surface_residual[0],
                surface_excess[0],
                depth_inverse[0],
                segment_map.T,
            )
        )
    )
    across = [(i, i + 1) for i in range(1, spans - 1, 2)]
    within = [(i, i + 1) for i in range(0, spans - 1, 2)]
    near = lax.ppermute(own_near, "span", within + [(b, a) for a, b in within])
    far = lax.ppermute(own_far, "span", across + [(b, a) for a, b in across])
    scale = 1.0 / math.sqrt(128.0 * STEPS)
    line = pltpu.VMEM((rows, cols), F32)
    base, edge, contribution, pair, place = pl.pallas_call(
        functools.partial(base_kernel, scale),
        out_shape=(
            field,
            pltpu.VMEM((2, depth, cols), F32),
            line,
            pltpu.VMEM((2 * depth, 6 * depth), BF16),
            pltpu.VMEM((2, size, 6 * depth), BF16),
        ),
        in_specs=[VMEM] * 4,
        out_specs=(VMEM,) * 5,
        scratch_shapes=[
            pltpu.VMEM((size, 3 * size), BF16),
            pltpu.VMEM((3, size, cols), BF16),
            field,
            field,
            field,
            pltpu.VMEM((depth, 128), F32),
        ],
        compiler_params=GRANT,
        name="base",
    )(k, picked, excess, inverse)
    fixed = (inverse, excess, edge, pair, place)
    base, contribution = pl.pallas_call(
        functools.partial(near_kernel, scale),
        out_shape=(field, line),
        in_specs=[VMEM] * 9,
        out_specs=(VMEM,) * 2,
        compiler_params=GRANT,
        name="near",
    )(*fixed, base, contribution, own_near, near)
    adjoint, partial = pl.pallas_call(
        functools.partial(far_kernel, scale),
        out_shape=(
            pltpu.HBM((depth, rows, cols), F32),
            pltpu.VMEM((devices, 1, lanes), F32),
        ),
        in_specs=[VMEM] * 10,
        out_specs=(HBM, VMEM),
        scratch_shapes=[
            field,
            pltpu.SMEM((blocks, rows), jnp.int32),
            pltpu.SemaphoreType.DMA,
            pltpu.SemaphoreType.DMA((CHUNKS,)),
        ],
        compiler_params=GRANT,
        name="far",
    )(own_far, far, *fixed, base, contribution, ids)
    pieces = lax.all_to_all(partial, ("blade", "span"), 0, 0, tiled=True)
    return (adjoint[None], jnp.sum(pieces, axis=(0, 1)))


def solution(mesh):
    placed = (
        P("blade", None, "span", None),
        P("blade", None, None),
        P("blade", None, "span", None),
        P("blade", None, "span", None),
        P("span", None),
        P(),
    )
    return jax.shard_map(
        per_device,
        mesh=mesh,
        in_specs=placed,
        out_specs=(P("blade", None, "span", None), P(("blade", "span"))),
        check_vma=False,
    )
```

time: 25 us -> 25 us (level)
  Pallas kernels: 4.6 us -> 5.3 us
  blocking collectives: 14 us -> 13.3 us
    pallas_call x2 -> x3, Pallas kernels: 2.93 us -> 3.64 us  [the longest x1 1.47 us: per_device(): pl.pallas_call(load_kernel, out_shape=(packed_far, packed_near, field, pl...]
    all_to_all x1, blocking collectives: 14 us -> 13.3 us  [per_device(): pieces = lax.all_to_all(partial, ('blade', 'span'), 0, 0, tiled=True)]
  transfers between devices with their start and end apart: 2 -> 2, of which waited for: 0 -> 0; matrix products, arithmetic and copies ran while one was open for 0% -> 0% of each run, Pallas kernels for 7% -> 9%
where the time goes in v7:
time: 25 us; the launch traced here: 24.9 us
  blocking collectives  13.3 us (53%)
  Pallas kernels  5.3 us (21%)
  starting transfers between devices  5.03 us (20%)
  between operations  0.69 us (3%)
  other arithmetic  0.56 us (2%)
    all_to_all x1, blocking collectives, per_device(): pieces = lax.all_to_all(partial, ('blade', 'span'), 0, 0, tiled=True)  13.3 us
    ppermute x1, starting transfers between devices, per_device(): near = lax.ppermute(own_near, 'span', within + [(b, a) for a, b in within])  4.36 us
    pallas_call x1, Pallas kernels, per_device(): pl.pallas_call(functools.partial(base_kernel, scale), out_shape=(field, p...  1.66 us
    pallas_call x1, Pallas kernels, per_device(): pl.pallas_call(load_kernel, out_shape=(packed_far, packed_near, field, pl...  1.47 us
    pallas_call x1, Pallas kernels, per_device(): pl.pallas_call(functools.partial(far_kernel, scale), out_shape=(pltpu.HBM...  1.47 us
    pallas_call x1, Pallas kernels, per_device(): pl.pallas_call(functools.partial(near_kernel, scale), out_shape=(field, l...  0.7 us
    ppermute x1, starting transfers between devices, per_device(): far = lax.ppermute(own_far, 'span', across + [(b, a) for a, b in across])  0.67 us
    reduce_sum x1, other arithmetic, per_device(): return (adjoint[None], jnp.sum(pieces, axis=(0, 1)))  0.56 us
  transfers between devices with their start and end apart: 2, of which 0 were waited for; matrix products, arithmetic and copies ran while one was open for 0% of the time, Pallas kernels for 9%

profile of v7, /device:TPU:0, one launch (start us, length us, event | category | flops | bytes accessed | tf_op | source)
XLA Modules:
  0.0 24.9 jit_solution(13075862522989137675)
XLA Ops:
  0.6 1.5 %load.1 = (f32[72,512]{1,0:T(8,128)S(1)}, f32[67,512]{1,0:T(8,128)S(1)}, f32[32,8,512]{2,1,0:T(8,128)S(1)}, f32[3,8,512]{2,1,0:T(8,128)S(1)}, f32[3,8,512]{2,1,0...) custom-call(s32[3]{0:T(128)} %frame_hbm.1, f32[32,8,512]{2,1,0:T(8,128)} %bitcast.6, f32[4,8,512]{2,1,0:T(8,128)} %bitcast.7, ...), custom_call_target="tpu_custom_call" | custom-call | tf_op jit(solution)/shard_map/load/pallas_call | solution.py:365
  2.1 0.7 %collective-permute-start = (f32[72,512]{1,0:T(8,128)S(1)}, f32[72,512]{1,0:T(8,128)S(1)}, u32[]{:S(2)}, u32[]{:S(2)}) collective-permute-start(f32[72,512]{1,0:T(8,128)S(1)} %get-tuple-element.18.own_ref), channel_id=1, source_target_pairs={{1,2},{2,1},{5,6},{6,5},{9,10},{10,9},{13,14},{14,13},{17,18},{18,... | collective-permute-start | bytes 442376 | tf_op jit(solution)/shard_map/ppermute | solution.py:402
  2.8 4.4 %collective-permute-start.1 = (f32[67,512]{1,0:T(8,128)S(1)}, f32[67,512]{1,0:T(8,128)S(1)}, u32[]{:S(2)}, u32[]{:S(2)}) collective-permute-start(f32[67,512]{1,0:T(8,128)S(1)} %get-tuple-element.28.own_ref), channel_id=1, source_target_pairs={{0,1},{2,3},{1,0},{3,2},{4,5},{6,7},{5,4},{7,6},{8,9},{10,11},{9,8... | collective-permute-start | bytes 411656 | tf_op jit(solution)/shard_map/ppermute | solution.py:401
  7.1 1.7 %base.1 = (f32[32,8,512]{2,1,0:T(8,128)S(1)}, f32[2,32,512]{2,1,0:T(8,128)S(1)}, f32[8,512]{1,0:T(8,128)S(1)}, bf16[64,192]{1,0:T(8,128)(2,1)S(1)}, bf16[2,256,192]{2,1,0:T(8,128)(2,1)S(1)}) custom-call(f32[32,8,512]{2,1,0:T(8,128)S(1)} %get-tuple-element.21.k_ref, f32[3,8,512]{2,1,0:T(8,128)S(1)} %get-tuple-element.22.frames_ref, ...), custom_call_target="tpu_custom_call" | custom-call | tf_op jit(solution)/shard_map/base/pallas_call | solution.py:405
  8.8 0.0 collective-permute-done.1.got_ref
  8.8 0.7 %near.1 = (f32[32,8,512]{2,1,0:T(8,128)S(1)}, f32[8,512]{1,0:T(8,128)S(1)}) custom-call(f32[32,32]{1,0:T(8,128)S(1)} %get-tuple-element.19.d_ref, f32[3,8,512]{2,1,0:T(8,128)S(1)} %get-tuple-element.20.excess_ref, f32[2,32,512]{2,1,0:T(8,128)S(1)} %get-tuple-element.23.edge_ref, bf16[64,192]{1,0:T(8,128)(2,1)S(1)} %get-tuple-element.24.pair_ref, ...), custom_call_target="tpu_custom_call" | custom-call | tf_op jit(solution)/shard_map/near/pallas_call | solution.py:428
  9.5 0.0 collective-permute-done.got_ref
  9.5 1.5 %far.1 = (f32[32,8,512]{2,1,0:T(8,128)}, f32[32,1,64]{2,1,0:T(1,128)S(1)}) custom-call(f32[72,512]{1,0:T(8,128)S(1)} %get-tuple-element.18.own_ref, f32[72,512]{1,0:T(8,128)S(1)} %collective-permute-done.got_ref, f32[32,32]{1,0:T(8,128)S(1)} %get-tuple-element.19.d_ref, f32[3,8,512]{2,1,0:T(8,128)S(1)} %get-tuple-element.20.excess_ref, ...), custom_call_target="tpu_custom_call" | custom-call | tf_op jit(solution)/shard_map/far/pallas_call | solution.py:436
  11.0 13.3 %all_to_all.5 = f32[32,1,64]{2,1,0:T(1,128)S(1)} all-to-all(f32[32,1,64]{2,1,0:T(1,128)S(1)} %get-tuple-element.33), channel_id=1, replica_groups=mesh['blade'=8,'span'=4] {'blade','span'}, dimensions={0} | all-to-all | bytes 16384 | tf_op jit(solution)/shard_map/all_to_all | solution.py:453
  24.3 0.6 %reduce_sum.9 = f32[64]{0:T(128)} reduce(f32[32,1,64]{2,1,0:T(1,128)S(1)} %all_to_all.5, f32[]{:T(128)} %constant.0.clone.1), dimensions={0,1}, to_apply=%region_0.0 | reduce | flops 1984 | bytes 8452 | tf_op jit(solution)/shard_map/reduce_sum | solution.py:454
Async XLA Ops:
  2.1 7.4 %collective-permute-start = (f32[72,512]{1,0:T(8,128)S(1)}, f32[72,512]{1,0:T(8,128)S(1)}, u32[]{:S(2)}, u32[]{:S(2)}) collective-permute-start(f32[72,512]{1,0:T(8,128)S(1)} %get-tuple-element.18.own_ref), channel_id=1, source_target_pairs={{1,2},{2,1},{5,6},{6,5},{9,10},{10,9},{13,14},{14,13},{17,18},{18,... | collective-permute-start | bytes 442376 | tf_op jit(solution)/shard_map/ppermute | solution.py:402
  2.8 6.0 %collective-permute-start.1 = (f32[67,512]{1,0:T(8,128)S(1)}, f32[67,512]{1,0:T(8,128)S(1)}, u32[]{:S(2)}, u32[]{:S(2)}) collective-permute-start(f32[67,512]{1,0:T(8,128)S(1)} %get-tuple-element.28.own_ref), channel_id=1, source_target_pairs={{0,1},{2,3},{1,0},{3,2},{4,5},{6,7},{5,4},{7,6},{8,9},{10,11},{9,8... | collective-permute-start | bytes 411656 | tf_op jit(solution)/shard_map/ppermute | solution.py:401

commit v8 on v7

--- a/solution.py
+++ b/solution.py
@@ -10,7 +10,6 @@
 
 STEPS = 3
 SEGS = 2048
-CHUNKS = 4
 F32 = jnp.float32
 BF16 = jnp.bfloat16
 VMEM = pl.BlockSpec(memory_space=pltpu.VMEM)
@@ -67,7 +66,30 @@
     )
 
 
+def chunked(ref, start, count, step):
+    chunks = ref.shape[0] // step
+    return jnp.concatenate(
+        [ref[c * step + start : c * step + start + count, :] for c in range(chunks)], axis=1
+    )
+
+
+def packed_field(ref, depth, cols, n):
+    chunks = cols // 128
+    return chunked(ref.at[n * chunks * depth : (n + 1) * chunks * depth], 0, depth, depth)
+
+
+def packed_line(ref, depth, cols, n):
+    chunks = cols // 128
+    base = (2 * depth + n) * chunks
+    return chunked(ref.at[base : base + chunks], 0, 1, 1)
+
+
+def row_of_each(ref, chunk, depth, rows, row):
+    return ref[pl.ds(chunk * depth * rows + row, depth, stride=rows), :]
+
+
 def load_kernel(
+    rows,
     frame_hbm,
     k_hbm,
     res_hbm,
@@ -83,47 +105,43 @@
     map_ref,
     frame_ref,
     res_ref,
-    line_ref,
     sems,
 ):
-    depth, rows, cols = k_ref.shape
-    base = 2 * depth
-    pairs = []
-    sent = (near_ref, far_ref)
-    for n, (after, _) in enumerate(sides()):
-        edge = jnp.where(after, rows - 1, 0)
-        second = jnp.where(after, rows - 2, 1)
-        pairs += [
-            (k_hbm.at[:, edge, :], sent[n].at[0:depth, :]),
-            (k_hbm.at[:, second, :], sent[n].at[depth:base, :]),
-            (res_hbm.at[:, edge, :], line_ref.at[2 * n]),
-            (res_hbm.at[:, second, :], line_ref.at[2 * n + 1]),
-        ]
-    pairs += [
-        (frame_hbm, frame_ref),
-        (res_hbm, res_ref),
-        (k_hbm, k_ref),
-        (excess_hbm, excess_ref),
-        (d_hbm, d_ref),
-        (map_hbm, map_ref),
-    ]
+    size, cols = k_hbm.shape
+    depth = size // rows
+    chunks = cols // 128
+    pairs = [(frame_hbm, frame_ref), (res_hbm, res_ref)]
+    for c in range(chunks):
+        pairs.append((k_hbm.at[:, pl.ds(c * 128, 128)], k_ref.at[pl.ds(c * size, size)]))
+    pairs += [(excess_hbm, excess_ref), (d_hbm, d_ref), (map_hbm, map_ref)]
     copies = [pltpu.make_async_copy(a, b, sems.at[n]) for n, (a, b) in enumerate(pairs)]
     for copy in copies:
         copy.start()
-    for copy in copies:
-        copy.wait()
+    sent = (near_ref, far_ref)
+    picks = []
+    for after, _ in sides():
+        picks.append((jnp.where(after, rows - 1, 0), jnp.where(after, rows - 2, 1)))
+    copies[0].wait()
+    copies[1].wait()
     for step in range(STEPS):
         frames_ref[step] = res_ref[frame_ref[step]]
-    for n, ref in enumerate(sent):
-        lines = [
-            line_ref[2 * n, pl.ds(frame_ref[2], 1), :],
-            line_ref[2 * n, pl.ds(frame_ref[1], 1), :],
-            line_ref[2 * n + 1, pl.ds(frame_ref[2], 1), :],
-        ]
-        rest = ref.shape[0] - base - len(lines)
-        if rest:
-            lines.append(jnp.zeros((rest, cols), F32))
-        ref[base:, :] = jnp.concatenate(lines, axis=0)
+    base = 2 * chunks * depth
+    for ref, (edge, second) in zip(sent, picks):
+        for n, (step, row) in enumerate(((2, edge), (1, edge), (2, second))):
+            line = frames_ref[step, pl.ds(row, 1), :]
+            for c in range(chunks):
+                spot = base + n * chunks + c
+                ref[spot : spot + 1, :] = line[:, c * 128 : (c + 1) * 128]
+        if ref.shape[0] > base + 3 * chunks:
+            ref[base + 3 * chunks :, :] = jnp.zeros((ref.shape[0] - base - 3 * chunks, 128), F32)
+    for c in range(chunks):
+        copies[2 + c].wait()
+        for ref, row_pair in zip(sent, picks):
+            for n, row in enumerate(row_pair):
+                spot = (n * chunks + c) * depth
+                ref[spot : spot + depth, :] = row_of_each(k_ref, c, depth, rows, row)
+    for copy in copies[2 + chunks :]:
+        copy.wait()
 
 
 def base_kernel(
@@ -144,7 +162,7 @@
     span_ref,
     factor_ref,
 ):
-    depth, rows, cols = k_ref.shape
+    depth, rows, cols = adj_ref.shape
     size = depth * rows
     factor_ref[...] = jnp.broadcast_to(d_ref[:, 0:1], factor_ref.shape)
 
@@ -192,7 +210,7 @@
     for i in range(0, depth, 2):
         found = []
         for j in (i, i + 1):
-            half = 0.5 * k_ref[j]
+            half = 0.5 * chunked(k_ref, j * rows, rows, size)
             w_chord = half + shift_next(half, 1)
             w_span = half + shift_next(half, 0)
             chord_ref[j] = w_chord
@@ -209,13 +227,15 @@
             found.append(source + frames_ref[1] if j == 0 else source)
         put(i, jnp.concatenate(found, axis=0))
     right = right_ref[...].reshape(3 * size, cols)
-    first_ref[...] = dot(mat_ref[...], right).reshape(depth, rows, cols)
+    first = dot(mat_ref[...], right)
+    for c in range(cols // 128):
+        first_ref[c * size : (c + 1) * size, :] = first[:, c * 128 : (c + 1) * 128]
 
     for i in range(0, depth, 2):
         found = []
         for j in (i, i + 1):
-            v = first_ref[j]
-            half = 0.5 * k_ref[j]
+            v = chunked(first_ref, j * rows, rows, size)
+            half = 0.5 * chunked(k_ref, j * rows, rows, size)
             source = (
                 v + divergence(v, chord_ref[j], half, 1) + divergence(v, span_ref[j], half, 0)
             )
@@ -224,13 +244,13 @@
     right = right_ref[...].reshape(3 * size, cols)
     adj_ref[...] = dot(mat_ref[...], right).reshape(depth, rows, cols)
 
-    top = first_ref[:, 0, :]
-    bottom = first_ref[:, rows - 1, :]
     for n, (after, _) in enumerate(sides()):
-        edge_ref[n] = jnp.where(after, bottom, top)
+        row = jnp.where(after, rows - 1, 0)
+        for c in range(cols // 128):
+            edge_ref[n, :, c * 128 : (c + 1) * 128] = row_of_each(first_ref, c, depth, rows, row)
     contribution_ref[...] = scale * (
         d_ref[0:1, 0:1] * f * excess_ref[2]
-        + first_ref[0] * excess_ref[1]
+        + chunked(first_ref, 0, rows, size) * excess_ref[1]
         + adj_ref[0] * excess_ref[0]
     )
 
@@ -238,17 +258,16 @@
 def correction(n, got, own, d_ref, edge_ref, pair_ref, place_ref):
     _, depth, cols = edge_ref.shape
     rows = place_ref.shape[1] // depth
-    base = 2 * depth
     after, inside = sides()[n]
     factor = d_ref[:, 0:1]
-    half = 0.5 * got[0:depth, :]
-    half_next = 0.5 * got[depth:base, :]
-    half_own = 0.5 * own[0:depth, :]
-    inner = half_own + 0.5 * own[depth:base, :]
-    f = got[base : base + 1, :]
-    frame = got[base + 1 : base + 2, :]
-    f_next = got[base + 2 : base + 3, :]
-    f_own = own[base : base + 1, :]
+    half = 0.5 * packed_field(got, depth, cols, 0)
+    half_next = 0.5 * packed_field(got, depth, cols, 1)
+    half_own = 0.5 * packed_field(own, depth, cols, 0)
+    inner = half_own + 0.5 * packed_field(own, depth, cols, 1)
+    f = packed_line(got, depth, cols, 0)
+    frame = packed_line(got, depth, cols, 1)
+    f_next = packed_line(got, depth, cols, 2)
+    f_own = packed_line(own, depth, cols, 0)
     face = half + half_own
     flux = (half + shift_next(half, 1)) * (shift_next(f, 1) - f)
     moved = (
@@ -262,7 +281,7 @@
     sources = [factor * (face * f - half * f_own), jnp.where(inside, outer, 0.0)]
     found = dot(pair_ref[...], right_three(jnp.concatenate(sources, axis=0)))
     e = found[0:depth]
-    outer = found[depth:base]
+    outer = found[depth:]
     w_chord = half_own + shift_next(half_own, 1)
     change = (
         e
@@ -310,27 +329,17 @@
     base_ref,
     contribution_ref,
     map_vmem,
-    adj_hbm,
+    adj_ref,
     part_ref,
-    adj_ref,
     map_ref,
     map_sem,
-    sems,
 ):
     map_copy = pltpu.make_async_copy(map_vmem, map_ref, map_sem)
     map_copy.start()
     depth, rows, cols = base_ref.shape
     blocks = cols // 128
     found, surface = correction(1, got_ref, own_ref, d_ref, edge_ref, pair_ref, place_ref)
-    step = depth // CHUNKS
-    copies = []
-    for n in range(CHUNKS):
-        part = pl.ds(n * step, step)
-        new = found[n * step * rows : (n + 1) * step * rows].reshape(step, rows, cols)
-        adj_ref[part] = base_ref[part] + new
-        copies.append(pltpu.make_async_copy(adj_ref.at[part], adj_hbm.at[part], sems.at[n]))
-        copies[-1].start()
-
+    adj_ref[...] = base_ref[...] + found.reshape(depth, rows, cols)
     contribution = contribution_ref[...] + scale * (
         surface * excess_ref[1] + found[0:rows, :] * excess_ref[0]
     )
@@ -345,8 +354,16 @@
         for row in range(rows):
             total += jnp.where(segment == map_ref[block, row], sums[row : row + 1, :], 0.0)
     part_ref[...] = total[:, None, :lanes]
-    for copy in copies:
-        copy.wait()
+
+
+def finish_kernel(adj_vmem, got_ref, adj_hbm, out_hbm, out_ref, sems):
+    adj_copy = pltpu.make_async_copy(adj_vmem, adj_hbm, sems.at[0])
+    adj_copy.start()
+    out_ref[...] = jnp.sum(got_ref[:, 0, :], axis=0)
+    out_copy = pltpu.make_async_copy(out_ref, out_hbm, sems.at[1])
+    out_copy.start()
+    adj_copy.wait()
+    out_copy.wait()
 
 
 def per_device(
@@ -360,14 +377,15 @@
     devices = spans * lax.axis_size("blade")
     lanes = SEGS // devices
     field = pltpu.VMEM((depth, rows, cols), F32)
-    packed_far = pltpu.VMEM((2 * depth + 8, cols), F32)
-    packed_near = pltpu.VMEM((2 * depth + 3, cols), F32)
+    chunks = cols // 128
+    packed_far = pltpu.VMEM(((2 * depth + 4) * chunks, 128), F32)
+    packed_near = pltpu.VMEM(((2 * depth + 3) * chunks, 128), F32)
     own_far, own_near, k, picked, excess, inverse, ids = pl.pallas_call(
-        load_kernel,
+        functools.partial(load_kernel, rows),
         out_shape=(
             packed_far,
             packed_near,
-            field,
+            pltpu.VMEM((chunks * size, 128), F32),
             pltpu.VMEM((STEPS, rows, cols), F32),
             pltpu.VMEM((STEPS, rows, cols), F32),
             pltpu.VMEM((depth, depth), F32),
@@ -378,8 +396,7 @@
         scratch_shapes=[
             pltpu.SMEM((STEPS,), jnp.int32),
             pltpu.VMEM((frames, rows, cols), F32),
-            pltpu.VMEM((4, frames, cols), F32),
-            pltpu.SemaphoreType.DMA((14,)),
+            pltpu.SemaphoreType.DMA((5 + chunks,)),
         ],
         compiler_params=GRANT,
         name="load",
@@ -388,7 +405,7 @@
             pltpu.with_memory_space_constraint(x, pltpu.HBM)
             for x in (
                 frame_index,
-                conductance[0],
+                conductance.reshape(size, cols),
                 surface_residual[0],
                 surface_excess[0],
                 depth_inverse[0],
@@ -416,7 +433,7 @@
         scratch_shapes=[
             pltpu.VMEM((size, 3 * size), BF16),
             pltpu.VMEM((3, size, cols), BF16),
-            field,
+            pltpu.VMEM((chunks * size, 128), F32),
             field,
             field,
             pltpu.VMEM((depth, 128), F32),
@@ -436,22 +453,29 @@
     adjoint, partial = pl.pallas_call(
         functools.partial(far_kernel, scale),
         out_shape=(
-            pltpu.HBM((depth, rows, cols), F32),
+            field,
             pltpu.VMEM((devices, 1, lanes), F32),
         ),
         in_specs=[VMEM] * 10,
-        out_specs=(HBM, VMEM),
+        out_specs=(VMEM,) * 2,
         scratch_shapes=[
-            field,
             pltpu.SMEM((blocks, rows), jnp.int32),
             pltpu.SemaphoreType.DMA,
-            pltpu.SemaphoreType.DMA((CHUNKS,)),
         ],
         compiler_params=GRANT,
         name="far",
     )(own_far, far, *fixed, base, contribution, ids)
     pieces = lax.all_to_all(partial, ("blade", "span"), 0, 0, tiled=True)
-    return (adjoint[None], jnp.sum(pieces, axis=(0, 1)))
+    adjoint, owned = pl.pallas_call(
+        finish_kernel,
+        out_shape=(pltpu.HBM((depth, rows, cols), F32), pltpu.HBM((lanes,), F32)),
+        in_specs=[VMEM] * 2,
+        out_specs=(HBM,) * 2,
+        scratch_shapes=[pltpu.VMEM((lanes,), F32), pltpu.SemaphoreType.DMA((2,))],
+        compiler_params=GRANT,
+        name="finish",
+    )(adjoint, pltpu.with_memory_space_constraint(pieces, pltpu.VMEM))
+    return (adjoint[None], owned)
 
 
 def solution(mesh):

time: 25 us -> 24.7 us (0.988)
  other arithmetic: 0.56 us -> 0 us
  Pallas kernels: 5.3 us -> 5.66 us
    reduce_sum x1 -> x0, other arithmetic: 0.56 us -> none  [per_device(): return (adjoint[None], jnp.sum(pieces, axis=(0, 1)))]
    pallas_call x2 -> x3, Pallas kernels: 2.94 us -> 3.23 us  [the longest x1 1.24 us: per_device(): pl.pallas_call(functools.partial(load_kernel, rows), out_shape=(packed_fa...]
  transfers between devices with their start and end apart: 2 -> 2, of which waited for: 0 -> 0; matrix products, arithmetic and copies ran while one was open for 0% -> 0% of each run, Pallas kernels for 9% -> 10%
where the time goes in v8:
time: 24.7 us; the launch traced here: 24.5 us
  blocking collectives  13.1 us (53%)
  Pallas kernels  5.66 us (23%)
  starting transfers between devices  5.03 us (20%)
  between operations  0.69 us (3%)
    all_to_all x1, blocking collectives, per_device(): pieces = lax.all_to_all(partial, ('blade', 'span'), 0, 0, tiled=True)  13.1 us
    ppermute x1, starting transfers between devices, per_device(): near = lax.ppermute(own_near, 'span', within + [(b, a) for a, b in within])  4.36 us
    pallas_call x1, Pallas kernels, per_device(): pl.pallas_call(functools.partial(base_kernel, scale), out_shape=(field, p...  1.73 us
    pallas_call x1, Pallas kernels, per_device(): pl.pallas_call(functools.partial(load_kernel, rows), out_shape=(packed_fa...  1.24 us
    pallas_call x1, Pallas kernels, per_device(): pl.pallas_call(functools.partial(far_kernel, scale), out_shape=(field, pl...  1.18 us
    pallas_call x1, Pallas kernels, per_device(): pl.pallas_call(finish_kernel, out_shape=(pltpu.HBM((depth, rows, cols), F...  0.81 us
    pallas_call x1, Pallas kernels, per_device(): pl.pallas_call(functools.partial(near_kernel, scale), out_shape=(field, l...  0.7 us
    ppermute x1, starting transfers between devices, per_device(): far = lax.ppermute(own_far, 'span', across + [(b, a) for a, b in across])  0.67 us
  transfers between devices with their start and end apart: 2, of which 0 were waited for; matrix products, arithmetic and copies ran while one was open for 0% of the time, Pallas kernels for 10%

profile of v8, /device:TPU:0, one launch (start us, length us, event | category | flops | bytes accessed | tf_op | source)
XLA Modules:
  0.0 24.5 jit_solution(2770989072703979884)
XLA Ops:
  0.6 1.2 %load.1 = (f32[272,128]{1,0:T(8,128)S(1)}, f32[268,128]{1,0:T(8,128)S(1)}, f32[1024,128]{1,0:T(8,128)S(1)}, f32[3,8,512]{2,1,0:T(8,128)S(1)}, f32[3,8,512]{2,1,0...) custom-call(s32[3]{0:T(128)} %frame_hbm.1, f32[256,512]{1,0:T(8,128)} %bitcast.6, f32[4,8,512]{2,1,0:T(8,128)} %bitcast.7, ...), custom_call_target="tpu_custom_call" | custom-call | tf_op jit(solution)/shard_map/load/pallas_call | solution.py:383
  1.9 0.7 %collective-permute-start = (f32[272,128]{1,0:T(8,128)S(1)}, f32[272,128]{1,0:T(8,128)S(1)}, u32[]{:S(2)}, u32[]{:S(2)}) collective-permute-start(f32[272,128]{1,0:T(8,128)S(1)} %get-tuple-element.20.own_ref), channel_id=1, source_target_pairs={{1,2},{2,1},{5,6},{6,5},{9,10},{10,9},{13,14},{14,13},{17,18},{18,... | collective-permute-start | bytes 417800 | tf_op jit(solution)/shard_map/ppermute | solution.py:419
  2.6 4.4 %collective-permute-start.1 = (f32[268,128]{1,0:T(8,128)S(1)}, f32[268,128]{1,0:T(8,128)S(1)}, u32[]{:S(2)}, u32[]{:S(2)}) collective-permute-start(f32[268,128]{1,0:T(8,128)S(1)} %get-tuple-element.30.own_ref), channel_id=1, source_target_pairs={{0,1},{2,3},{1,0},{3,2},{4,5},{6,7},{5,4},{7,6},{8,9},{10,11},{9,8... | collective-permute-start | bytes 411656 | tf_op jit(solution)/shard_map/ppermute | solution.py:418
  6.9 1.7 %base.1 = (f32[32,8,512]{2,1,0:T(8,128)S(1)}, f32[2,32,512]{2,1,0:T(8,128)S(1)}, f32[8,512]{1,0:T(8,128)S(1)}, bf16[64,192]{1,0:T(8,128)(2,1)S(1)}, bf16[2,256,192]{2,1,0:T(8,128)(2,1)S(1)}) custom-call(f32[1024,128]{1,0:T(8,128)S(1)} %get-tuple-element.23.k_ref, f32[3,8,512]{2,1,0:T(8,128)S(1)} %get-tuple-element.24.frames_ref, ...), custom_call_target="tpu_custom_call" | custom-call | tf_op jit(solution)/shard_map/base/pallas_call | solution.py:422
  8.7 0.0 collective-permute-done.1.got_ref
  8.7 0.7 %near.1 = (f32[32,8,512]{2,1,0:T(8,128)S(1)}, f32[8,512]{1,0:T(8,128)S(1)}) custom-call(f32[32,32]{1,0:T(8,128)S(1)} %get-tuple-element.21.d_ref, f32[3,8,512]{2,1,0:T(8,128)S(1)} %get-tuple-element.22.excess_ref, f32[2,32,512]{2,1,0:T(8,128)S(1)} %get-tuple-element.25.edge_ref, bf16[64,192]{1,0:T(8,128)(2,1)S(1)} %get-tuple-element.26.pair_ref, ...), custom_call_target="tpu_custom_call" | custom-call | tf_op jit(solution)/shard_map/near/pallas_call | solution.py:445
  9.4 0.0 collective-permute-done.got_ref
  9.4 1.2 %far.1 = (f32[32,8,512]{2,1,0:T(8,128)S(1)}, f32[32,1,64]{2,1,0:T(1,128)S(1)}) custom-call(f32[272,128]{1,0:T(8,128)S(1)} %get-tuple-element.20.own_ref, f32[272,128]{1,0:T(8,128)S(1)} %collective-permute-done.got_ref, f32[32,32]{1,0:T(8,128)S(1)} %get-tuple-element.21.d_ref, f32[3,8,512]{2,1,0:T(8,128)S(1)} %get-tuple-element.22.excess_ref, ...), custom_call_target="tpu_custom_call" | custom-call | tf_op jit(solution)/shard_map/far/pallas_call | solution.py:453
  10.6 13.1 %all_to_all.5.got_ref = f32[32,1,64]{2,1,0:T(1,128)S(1)} all-to-all(f32[32,1,64]{2,1,0:T(1,128)S(1)} %get-tuple-element.35), channel_id=1, replica_groups=mesh['blade'=8,'span'=4] {'blade','span'}, dimensions={0} | all-to-all | bytes 16384 | tf_op jit(solution)/shard_map/all_to_all | solution.py:468
  23.7 0.8 %finish.1 = (f32[32,8,512]{2,1,0:T(8,128)}, f32[64]{0:T(128)}) custom-call(f32[32,8,512]{2,1,0:T(8,128)S(1)} %get-tuple-element.34.adj_vmem, f32[32,1,64]{2,1,0:T(1,128)S(1)} %all_to_all.5.got_ref), custom_call_target="tpu_custom_call" | custom-call | tf_op jit(solution)/shard_map/finish/pallas_call | solution.py:469
Async XLA Ops:
  1.9 7.5 %collective-permute-start = (f32[272,128]{1,0:T(8,128)S(1)}, f32[272,128]{1,0:T(8,128)S(1)}, u32[]{:S(2)}, u32[]{:S(2)}) collective-permute-start(f32[272,128]{1,0:T(8,128)S(1)} %get-tuple-element.20.own_ref), channel_id=1, source_target_pairs={{1,2},{2,1},{5,6},{6,5},{9,10},{10,9},{13,14},{14,13},{17,18},{18,... | collective-permute-start | bytes 417800 | tf_op jit(solution)/shard_map/ppermute | solution.py:419
  2.6 6.1 %collective-permute-start.1 = (f32[268,128]{1,0:T(8,128)S(1)}, f32[268,128]{1,0:T(8,128)S(1)}, u32[]{:S(2)}, u32[]{:S(2)}) collective-permute-start(f32[268,128]{1,0:T(8,128)S(1)} %get-tuple-element.30.own_ref), channel_id=1, source_target_pairs={{0,1},{2,3},{1,0},{3,2},{4,5},{6,7},{5,4},{7,6},{8,9},{10,11},{9,8... | collective-permute-start | bytes 411656 | tf_op jit(solution)/shard_map/ppermute | solution.py:418

commit v9 on v8

--- a/solution.py
+++ b/solution.py
@@ -10,6 +10,7 @@
 
 STEPS = 3
 SEGS = 2048
+PIECES = 4
 F32 = jnp.float32
 BF16 = jnp.bfloat16
 VMEM = pl.BlockSpec(memory_space=pltpu.VMEM)
@@ -295,6 +296,20 @@
     return found, jnp.where(iota((rows, cols), 0) == row, e[0:1, :], 0.0)
 
 
+def add_segments(total, contribution, picked_rows, map_ref):
+    owners, _, lanes = total.shape
+    shape = (owners, 128)
+    lane = iota(shape, 1)
+    segment = jnp.where(lane < lanes, iota(shape, 0) * lanes + lane, -1)
+    found = jnp.zeros(shape, F32)
+    for block in range(contribution.shape[1] // 128):
+        part = contribution[:, block * 128 : (block + 1) * 128]
+        sums = jnp.sum(part, axis=1, keepdims=True)
+        for n, row in enumerate(picked_rows):
+            found += jnp.where(segment == map_ref[block, row], sums[n : n + 1, :], 0.0)
+    return total + found[:, None, :lanes]
+
+
 def near_kernel(
     scale,
     d_ref,
@@ -302,18 +317,27 @@
     edge_ref,
     pair_ref,
     place_ref,
+    map_vmem,
     base_ref,
     contribution_ref,
     own_ref,
     got_ref,
     adj_ref,
-    out_ref,
+    part_ref,
+    map_ref,
+    map_sem,
 ):
+    map_copy = pltpu.make_async_copy(map_vmem, map_ref, map_sem)
+    map_copy.start()
     rows = base_ref.shape[1]
     found, surface = correction(0, got_ref, own_ref, d_ref, edge_ref, pair_ref, place_ref)
     adj_ref[...] = base_ref[...] + found.reshape(base_ref.shape)
-    out_ref[...] = contribution_ref[...] + scale * (
+    contribution = contribution_ref[...] + scale * (
         surface * excess_ref[1] + found[0:rows, :] * excess_ref[0]
+    )
+    map_copy.wait()
+    part_ref[...] = add_segments(
+        jnp.zeros(part_ref.shape, F32), contribution, range(rows), map_ref
     )
 
 
@@ -326,9 +350,9 @@
     edge_ref,
     pair_ref,
     place_ref,
+    map_vmem,
     base_ref,
-    contribution_ref,
-    map_vmem,
+    part_in_ref,
     adj_ref,
     part_ref,
     map_ref,
@@ -336,34 +360,35 @@
 ):
     map_copy = pltpu.make_async_copy(map_vmem, map_ref, map_sem)
     map_copy.start()
-    depth, rows, cols = base_ref.shape
-    blocks = cols // 128
+    rows = base_ref.shape[1]
     found, surface = correction(1, got_ref, own_ref, d_ref, edge_ref, pair_ref, place_ref)
-    adj_ref[...] = base_ref[...] + found.reshape(depth, rows, cols)
-    contribution = contribution_ref[...] + scale * (
-        surface * excess_ref[1] + found[0:rows, :] * excess_ref[0]
-    )
-    owners, _, lanes = part_ref.shape
-    shape = (owners, 128)
-    lane = iota(shape, 1)
-    segment = jnp.where(lane < lanes, iota(shape, 0) * lanes + lane, -1)
-    total = jnp.zeros(shape, F32)
+    contribution = scale * (surface * excess_ref[1] + found[0:rows, :] * excess_ref[0])
+    after = sides()[1][0]
+    two = jnp.where(
+        after,
+        jnp.concatenate([contribution[rows - 1 :], contribution[rows - 2 : rows - 1]], axis=0),
+        contribution[0:2],
+    )
+    picked_rows = (jnp.where(after, rows - 1, 0), jnp.where(after, rows - 2, 1))
     map_copy.wait()
-    for block in range(blocks):
-        sums = jnp.sum(contribution[:, block * 128 : (block + 1) * 128], axis=1, keepdims=True)
-        for row in range(rows):
-            total += jnp.where(segment == map_ref[block, row], sums[row : row + 1, :], 0.0)
-    part_ref[...] = total[:, None, :lanes]
+    part_ref[...] = add_segments(part_in_ref[...], two, picked_rows, map_ref)
+    adj_ref[...] = base_ref[...] + found.reshape(base_ref.shape)
 
 
 def finish_kernel(adj_vmem, got_ref, adj_hbm, out_hbm, out_ref, sems):
-    adj_copy = pltpu.make_async_copy(adj_vmem, adj_hbm, sems.at[0])
-    adj_copy.start()
+    step = adj_vmem.shape[0] // PIECES
+    copies = []
+    for n in range(PIECES):
+        piece = pl.ds(n * step, step)
+        copies.append(
+            pltpu.make_async_copy(adj_vmem.at[piece], adj_hbm.at[piece], sems.at[n])
+        )
+        copies[-1].start()
     out_ref[...] = jnp.sum(got_ref[:, 0, :], axis=0)
-    out_copy = pltpu.make_async_copy(out_ref, out_hbm, sems.at[1])
-    out_copy.start()
-    adj_copy.wait()
-    out_copy.wait()
+    copies.append(pltpu.make_async_copy(out_ref, out_hbm, sems.at[PIECES]))
+    copies[-1].start()
+    for copy in copies:
+        copy.wait()
 
 
 def per_device(
@@ -441,37 +466,34 @@
         compiler_params=GRANT,
         name="base",
     )(k, picked, excess, inverse)
-    fixed = (inverse, excess, edge, pair, place)
-    base, contribution = pl.pallas_call(
+    fixed = (inverse, excess, edge, pair, place, ids)
+    sums = pltpu.VMEM((devices, 1, lanes), F32)
+    map_scratch = [pltpu.SMEM((blocks, rows), jnp.int32), pltpu.SemaphoreType.DMA]
+    base, partial = pl.pallas_call(
         functools.partial(near_kernel, scale),
-        out_shape=(field, line),
-        in_specs=[VMEM] * 9,
+        out_shape=(field, sums),
+        in_specs=[VMEM] * 10,
         out_specs=(VMEM,) * 2,
+        scratch_shapes=map_scratch,
         compiler_params=GRANT,
         name="near",
     )(*fixed, base, contribution, own_near, near)
     adjoint, partial = pl.pallas_call(
         functools.partial(far_kernel, scale),
-        out_shape=(
-            field,
-            pltpu.VMEM((devices, 1, lanes), F32),
-        ),
+        out_shape=(field, sums),
         in_specs=[VMEM] * 10,
         out_specs=(VMEM,) * 2,
-        scratch_shapes=[
-            pltpu.SMEM((blocks, rows), jnp.int32),
-            pltpu.SemaphoreType.DMA,
-        ],
+        scratch_shapes=map_scratch,
         compiler_params=GRANT,
         name="far",
-    )(own_far, far, *fixed, base, contribution, ids)
+    )(own_far, far, *fixed, base, partial)
     pieces = lax.all_to_all(partial, ("blade", "span"), 0, 0, tiled=True)
     adjoint, owned = pl.pallas_call(
         finish_kernel,
         out_shape=(pltpu.HBM((depth, rows, cols), F32), pltpu.HBM((lanes,), F32)),
         in_specs=[VMEM] * 2,
         out_specs=(HBM,) * 2,
-        scratch_shapes=[pltpu.VMEM((lanes,), F32), pltpu.SemaphoreType.DMA((2,))],
+        scratch_shapes=[pltpu.VMEM((lanes,), F32), pltpu.SemaphoreType.DMA((PIECES + 1,))],
         compiler_params=GRANT,
         name="finish",
     )(adjoint, pltpu.with_memory_space_constraint(pieces, pltpu.VMEM))

time: 24.7 us -> 24.3 us (0.984)
  blocking collectives: 13.1 us -> 12.6 us
    all_to_all x1, blocking collectives: 13.1 us -> 12.6 us  [per_device(): pieces = lax.all_to_all(partial, ('blade', 'span'), 0, 0, tiled=True)]
  transfers between devices with their start and end apart: 2 -> 2, of which waited for: 0 -> 0; matrix products, arithmetic and copies ran while one was open for 0% -> 0% of each run, Pallas kernels for 10% -> 12%
where the time goes in v9:
time: 24.3 us; the launch traced here: 24.2 us
  blocking collectives  12.6 us (52%)
  Pallas kernels  5.8 us (24%)
  starting transfers between devices  5.03 us (21%)
  between operations  0.69 us (3%)
    all_to_all x1, blocking collectives, per_device(): pieces = lax.all_to_all(partial, ('blade', 'span'), 0, 0, tiled=True)  12.6 us
    ppermute x1, starting transfers between devices, per_device(): near = lax.ppermute(own_near, 'span', within + [(b, a) for a, b in within])  4.36 us
    pallas_call x1, Pallas kernels, per_device(): pl.pallas_call(functools.partial(base_kernel, scale), out_shape=(field, p...  1.73 us
    pallas_call x1, Pallas kernels, per_device(): pl.pallas_call(functools.partial(load_kernel, rows), out_shape=(packed_fa...  1.24 us
    pallas_call x1, Pallas kernels, per_device(): pl.pallas_call(functools.partial(near_kernel, scale), out_shape=(field, s...  1.18 us
    pallas_call x1, Pallas kernels, per_device(): pl.pallas_call(finish_kernel, out_shape=(pltpu.HBM((depth, rows, cols), F...  0.83 us
    pallas_call x1, Pallas kernels, per_device(): pl.pallas_call(functools.partial(far_kernel, scale), out_shape=(field, su...  0.82 us
    ppermute x1, starting transfers between devices, per_device(): far = lax.ppermute(own_far, 'span', across + [(b, a) for a, b in across])  0.67 us
  transfers between devices with their start and end apart: 2, of which 0 were waited for; matrix products, arithmetic and copies ran while one was open for 0% of the time, Pallas kernels for 12%

profile of v9, /device:TPU:0, one launch (start us, length us, event | category | flops | bytes accessed | tf_op | source)
XLA Modules:
  0.0 24.2 jit_solution(16693229170191610035)
XLA Ops:
  0.6 1.2 %load.1 = (f32[272,128]{1,0:T(8,128)S(1)}, f32[268,128]{1,0:T(8,128)S(1)}, f32[1024,128]{1,0:T(8,128)S(1)}, f32[3,8,512]{2,1,0:T(8,128)S(1)}, f32[3,8,512]{2,1,0...) custom-call(s32[3]{0:T(128)} %frame_hbm.1, f32[256,512]{1,0:T(8,128)} %bitcast.6, f32[4,8,512]{2,1,0:T(8,128)} %bitcast.7, ...), custom_call_target="tpu_custom_call" | custom-call | tf_op jit(solution)/shard_map/load/pallas_call | solution.py:408
  1.9 0.7 %collective-permute-start = (f32[272,128]{1,0:T(8,128)S(1)}, f32[272,128]{1,0:T(8,128)S(1)}, u32[]{:S(2)}, u32[]{:S(2)}) collective-permute-start(f32[272,128]{1,0:T(8,128)S(1)} %get-tuple-element.20.own_ref), channel_id=1, source_target_pairs={{1,2},{2,1},{5,6},{6,5},{9,10},{10,9},{13,14},{14,13},{17,18},{18,... | collective-permute-start | bytes 417800 | tf_op jit(solution)/shard_map/ppermute | solution.py:444
  2.6 4.4 %collective-permute-start.1 = (f32[268,128]{1,0:T(8,128)S(1)}, f32[268,128]{1,0:T(8,128)S(1)}, u32[]{:S(2)}, u32[]{:S(2)}) collective-permute-start(f32[268,128]{1,0:T(8,128)S(1)} %get-tuple-element.31.own_ref), channel_id=1, source_target_pairs={{0,1},{2,3},{1,0},{3,2},{4,5},{6,7},{5,4},{7,6},{8,9},{10,11},{9,8... | collective-permute-start | bytes 411656 | tf_op jit(solution)/shard_map/ppermute | solution.py:443
  6.9 1.7 %base.1 = (f32[32,8,512]{2,1,0:T(8,128)S(1)}, f32[2,32,512]{2,1,0:T(8,128)S(1)}, f32[8,512]{1,0:T(8,128)S(1)}, bf16[64,192]{1,0:T(8,128)(2,1)S(1)}, bf16[2,256,192]{2,1,0:T(8,128)(2,1)S(1)}) custom-call(f32[1024,128]{1,0:T(8,128)S(1)} %get-tuple-element.23.k_ref, f32[3,8,512]{2,1,0:T(8,128)S(1)} %get-tuple-element.24.frames_ref, ...), custom_call_target="tpu_custom_call" | custom-call | tf_op jit(solution)/shard_map/base/pallas_call | solution.py:447
  8.7 0.0 collective-permute-done.1.got_ref
  8.7 1.2 %near.1 = (f32[32,8,512]{2,1,0:T(8,128)S(1)}, f32[32,1,64]{2,1,0:T(1,128)S(1)}) custom-call(f32[32,32]{1,0:T(8,128)S(1)} %get-tuple-element.21.d_ref, f32[3,8,512]{2,1,0:T(8,128)S(1)} %get-tuple-element.22.excess_ref, f32[2,32,512]{2,1,0:T(8,128)S(1)} %get-tuple-element.25.edge_ref, bf16[64,192]{1,0:T(8,128)(2,1)S(1)} %get-tuple-element.26.pair_ref, ...), custom_call_target="tpu_custom_call" | custom-call | tf_op jit(solution)/shard_map/near/pallas_call | solution.py:472
  9.8 0.0 collective-permute-done.got_ref
  9.9 0.8 %far.1 = (f32[32,8,512]{2,1,0:T(8,128)S(1)}, f32[32,1,64]{2,1,0:T(1,128)S(1)}) custom-call(f32[272,128]{1,0:T(8,128)S(1)} %get-tuple-element.20.own_ref, f32[272,128]{1,0:T(8,128)S(1)} %collective-permute-done.got_ref, f32[32,32]{1,0:T(8,128)S(1)} %get-tuple-element.21.d_ref, f32[3,8,512]{2,1,0:T(8,128)S(1)} %get-tuple-element.22.excess_ref, ...), custom_call_target="tpu_custom_call" | custom-call | tf_op jit(solution)/shard_map/far/pallas_call | solution.py:481
  10.7 12.6 %all_to_all.5.got_ref = f32[32,1,64]{2,1,0:T(1,128)S(1)} all-to-all(f32[32,1,64]{2,1,0:T(1,128)S(1)} %get-tuple-element.35), channel_id=1, replica_groups=mesh['blade'=8,'span'=4] {'blade','span'}, dimensions={0} | all-to-all | bytes 16384 | tf_op jit(solution)/shard_map/all_to_all | solution.py:490
  23.3 0.8 %finish.1 = (f32[32,8,512]{2,1,0:T(8,128)}, f32[64]{0:T(128)}) custom-call(f32[32,8,512]{2,1,0:T(8,128)S(1)} %get-tuple-element.34.adj_vmem, f32[32,1,64]{2,1,0:T(1,128)S(1)} %all_to_all.5.got_ref), custom_call_target="tpu_custom_call" | custom-call | tf_op jit(solution)/shard_map/finish/pallas_call | solution.py:491
Async XLA Ops:
  1.9 8.0 %collective-permute-start = (f32[272,128]{1,0:T(8,128)S(1)}, f32[272,128]{1,0:T(8,128)S(1)}, u32[]{:S(2)}, u32[]{:S(2)}) collective-permute-start(f32[272,128]{1,0:T(8,128)S(1)} %get-tuple-element.20.own_ref), channel_id=1, source_target_pairs={{1,2},{2,1},{5,6},{6,5},{9,10},{10,9},{13,14},{14,13},{17,18},{18,... | collective-permute-start | bytes 417800 | tf_op jit(solution)/shard_map/ppermute | solution.py:444
  2.6 6.1 %collective-permute-start.1 = (f32[268,128]{1,0:T(8,128)S(1)}, f32[268,128]{1,0:T(8,128)S(1)}, u32[]{:S(2)}, u32[]{:S(2)}) collective-permute-start(f32[268,128]{1,0:T(8,128)S(1)} %get-tuple-element.31.own_ref), channel_id=1, source_target_pairs={{0,1},{2,3},{1,0},{3,2},{4,5},{6,7},{5,4},{7,6},{8,9},{10,11},{9,8... | collective-permute-start | bytes 411656 | tf_op jit(solution)/shard_map/ppermute | solution.py:443

commit v10 on v9

--- a/solution.py
+++ b/solution.py
@@ -111,19 +111,20 @@
     size, cols = k_hbm.shape
     depth = size // rows
     chunks = cols // 128
-    pairs = [(frame_hbm, frame_ref), (res_hbm, res_ref)]
-    for c in range(chunks):
-        pairs.append((k_hbm.at[:, pl.ds(c * 128, 128)], k_ref.at[pl.ds(c * size, size)]))
+    pairs = [
+        (k_hbm.at[:, pl.ds(c * 128, 128)], k_ref.at[pl.ds(c * size, size)]) for c in range(chunks)
+    ]
+    pairs += [(frame_hbm, frame_ref), (res_hbm, res_ref)]
     pairs += [(excess_hbm, excess_ref), (d_hbm, d_ref), (map_hbm, map_ref)]
     copies = [pltpu.make_async_copy(a, b, sems.at[n]) for n, (a, b) in enumerate(pairs)]
-    for copy in copies:
-        copy.start()
+    for n, copy in enumerate(copies):
+        copy.start(priority=n % 2)
     sent = (near_ref, far_ref)
     picks = []
     for after, _ in sides():
         picks.append((jnp.where(after, rows - 1, 0), jnp.where(after, rows - 2, 1)))
-    copies[0].wait()
-    copies[1].wait()
+    copies[chunks].wait()
+    copies[chunks + 1].wait()
     for step in range(STEPS):
         frames_ref[step] = res_ref[frame_ref[step]]
     base = 2 * chunks * depth
@@ -136,7 +137,7 @@
         if ref.shape[0] > base + 3 * chunks:
             ref[base + 3 * chunks :, :] = jnp.zeros((ref.shape[0] - base - 3 * chunks, 128), F32)
     for c in range(chunks):
-        copies[2 + c].wait()
+        copies[c].wait()
         for ref, row_pair in zip(sent, picks):
             for n, row in enumerate(row_pair):
                 spot = (n * chunks + c) * depth
@@ -383,7 +384,7 @@
         copies.append(
             pltpu.make_async_copy(adj_vmem.at[piece], adj_hbm.at[piece], sems.at[n])
         )
-        copies[-1].start()
+        copies[-1].start(priority=n % 2)
     out_ref[...] = jnp.sum(got_ref[:, 0, :], axis=0)
     copies.append(pltpu.make_async_copy(out_ref, out_hbm, sems.at[PIECES]))
     copies[-1].start()

time: 24.3 us -> 24.4 us (level)
  no operation moved by 1% of the time
where the time goes in v10:
time: 24.4 us; the launch traced here: 24.3 us
  blocking collectives  12.7 us (52%)
  Pallas kernels  5.87 us (24%)
  starting transfers between devices  5.03 us (21%)
  between operations  0.69 us (3%)
    all_to_all x1, blocking collectives, per_device(): pieces = lax.all_to_all(partial, ('blade', 'span'), 0, 0, tiled=True)  12.7 us
    ppermute x1, starting transfers between devices, per_device(): near = lax.ppermute(own_near, 'span', within + [(b, a) for a, b in within])  4.36 us
    pallas_call x1, Pallas kernels, per_device(): pl.pallas_call(functools.partial(base_kernel, scale), out_shape=(field, p...  1.72 us
    pallas_call x1, Pallas kernels, per_device(): pl.pallas_call(functools.partial(load_kernel, rows), out_shape=(packed_fa...  1.32 us
    pallas_call x1, Pallas kernels, per_device(): pl.pallas_call(functools.partial(near_kernel, scale), out_shape=(field, s...  1.18 us
    pallas_call x1, Pallas kernels, per_device(): pl.pallas_call(finish_kernel, out_shape=(pltpu.HBM((depth, rows, cols), F...  0.83 us
    pallas_call x1, Pallas kernels, per_device(): pl.pallas_call(functools.partial(far_kernel, scale), out_shape=(field, su...  0.82 us
    ppermute x1, starting transfers between devices, per_device(): far = lax.ppermute(own_far, 'span', across + [(b, a) for a, b in across])  0.67 us
  transfers between devices with their start and end apart: 2, of which 0 were waited for; matrix products, arithmetic and copies ran while one was open for 0% of the time, Pallas kernels for 12%

profile of v10, /device:TPU:0, one launch (start us, length us, event | category | flops | bytes accessed | tf_op | source)
XLA Modules:
  0.0 24.3 jit_solution(8571226416871814466)
XLA Ops:
  0.6 1.3 %load.1 = (f32[272,128]{1,0:T(8,128)S(1)}, f32[268,128]{1,0:T(8,128)S(1)}, f32[1024,128]{1,0:T(8,128)S(1)}, f32[3,8,512]{2,1,0:T(8,128)S(1)}, f32[3,8,512]{2,1,0...) custom-call(s32[3]{0:T(128)} %frame_hbm.1, f32[256,512]{1,0:T(8,128)} %bitcast.6, f32[4,8,512]{2,1,0:T(8,128)} %bitcast.7, ...), custom_call_target="tpu_custom_call" | custom-call | tf_op jit(solution)/shard_map/load/pallas_call | solution.py:409
  2.0 0.7 %collective-permute-start = (f32[272,128]{1,0:T(8,128)S(1)}, f32[272,128]{1,0:T(8,128)S(1)}, u32[]{:S(2)}, u32[]{:S(2)}) collective-permute-start(f32[272,128]{1,0:T(8,128)S(1)} %get-tuple-element.20.own_ref), channel_id=1, source_target_pairs={{1,2},{2,1},{5,6},{6,5},{9,10},{10,9},{13,14},{14,13},{17,18},{18,... | collective-permute-start | bytes 417800 | tf_op jit(solution)/shard_map/ppermute | solution.py:445
  2.6 4.4 %collective-permute-start.1 = (f32[268,128]{1,0:T(8,128)S(1)}, f32[268,128]{1,0:T(8,128)S(1)}, u32[]{:S(2)}, u32[]{:S(2)}) collective-permute-start(f32[268,128]{1,0:T(8,128)S(1)} %get-tuple-element.31.own_ref), channel_id=1, source_target_pairs={{0,1},{2,3},{1,0},{3,2},{4,5},{6,7},{5,4},{7,6},{8,9},{10,11},{9,8... | collective-permute-start | bytes 411656 | tf_op jit(solution)/shard_map/ppermute | solution.py:444
  7.0 1.7 %base.1 = (f32[32,8,512]{2,1,0:T(8,128)S(1)}, f32[2,32,512]{2,1,0:T(8,128)S(1)}, f32[8,512]{1,0:T(8,128)S(1)}, bf16[64,192]{1,0:T(8,128)(2,1)S(1)}, bf16[2,256,192]{2,1,0:T(8,128)(2,1)S(1)}) custom-call(f32[1024,128]{1,0:T(8,128)S(1)} %get-tuple-element.23.k_ref, f32[3,8,512]{2,1,0:T(8,128)S(1)} %get-tuple-element.24.frames_ref, ...), custom_call_target="tpu_custom_call" | custom-call | tf_op jit(solution)/shard_map/base/pallas_call | solution.py:448
  8.7 0.0 collective-permute-done.1.got_ref
  8.7 1.2 %near.1 = (f32[32,8,512]{2,1,0:T(8,128)S(1)}, f32[32,1,64]{2,1,0:T(1,128)S(1)}) custom-call(f32[32,32]{1,0:T(8,128)S(1)} %get-tuple-element.21.d_ref, f32[3,8,512]{2,1,0:T(8,128)S(1)} %get-tuple-element.22.excess_ref, f32[2,32,512]{2,1,0:T(8,128)S(1)} %get-tuple-element.25.edge_ref, bf16[64,192]{1,0:T(8,128)(2,1)S(1)} %get-tuple-element.26.pair_ref, ...), custom_call_target="tpu_custom_call" | custom-call | tf_op jit(solution)/shard_map/near/pallas_call | solution.py:473
  9.9 0.0 collective-permute-done.got_ref
  9.9 0.8 %far.1 = (f32[32,8,512]{2,1,0:T(8,128)S(1)}, f32[32,1,64]{2,1,0:T(1,128)S(1)}) custom-call(f32[272,128]{1,0:T(8,128)S(1)} %get-tuple-element.20.own_ref, f32[272,128]{1,0:T(8,128)S(1)} %collective-permute-done.got_ref, f32[32,32]{1,0:T(8,128)S(1)} %get-tuple-element.21.d_ref, f32[3,8,512]{2,1,0:T(8,128)S(1)} %get-tuple-element.22.excess_ref, ...), custom_call_target="tpu_custom_call" | custom-call | tf_op jit(solution)/shard_map/far/pallas_call | solution.py:482
  10.8 12.7 %all_to_all.5.got_ref = f32[32,1,64]{2,1,0:T(1,128)S(1)} all-to-all(f32[32,1,64]{2,1,0:T(1,128)S(1)} %get-tuple-element.35), channel_id=1, replica_groups=mesh['blade'=8,'span'=4] {'blade','span'}, dimensions={0} | all-to-all | bytes 16384 | tf_op jit(solution)/shard_map/all_to_all | solution.py:491
  23.4 0.8 %finish.1 = (f32[32,8,512]{2,1,0:T(8,128)}, f32[64]{0:T(128)}) custom-call(f32[32,8,512]{2,1,0:T(8,128)S(1)} %get-tuple-element.34.adj_vmem, f32[32,1,64]{2,1,0:T(1,128)S(1)} %all_to_all.5.got_ref), custom_call_target="tpu_custom_call" | custom-call | tf_op jit(solution)/shard_map/finish/pallas_call | solution.py:492
Async XLA Ops:
  2.0 8.0 %collective-permute-start = (f32[272,128]{1,0:T(8,128)S(1)}, f32[272,128]{1,0:T(8,128)S(1)}, u32[]{:S(2)}, u32[]{:S(2)}) collective-permute-start(f32[272,128]{1,0:T(8,128)S(1)} %get-tuple-element.20.own_ref), channel_id=1, source_target_pairs={{1,2},{2,1},{5,6},{6,5},{9,10},{10,9},{13,14},{14,13},{17,18},{18,... | collective-permute-start | bytes 417800 | tf_op jit(solution)/shard_map/ppermute | solution.py:445
  2.6 6.1 %collective-permute-start.1 = (f32[268,128]{1,0:T(8,128)S(1)}, f32[268,128]{1,0:T(8,128)S(1)}, u32[]{:S(2)}, u32[]{:S(2)}) collective-permute-start(f32[268,128]{1,0:T(8,128)S(1)} %get-tuple-element.31.own_ref), channel_id=1, source_target_pairs={{0,1},{2,3},{1,0},{3,2},{4,5},{6,7},{5,4},{7,6},{8,9},{10,11},{9,8... | collective-permute-start | bytes 411656 | tf_op jit(solution)/shard_map/ppermute | solution.py:444

commit v11 on v9

--- a/solution.py
+++ b/solution.py
@@ -10,7 +10,6 @@
 
 STEPS = 3
 SEGS = 2048
-PIECES = 4
 F32 = jnp.float32
 BF16 = jnp.bfloat16
 VMEM = pl.BlockSpec(memory_space=pltpu.VMEM)
@@ -89,21 +88,22 @@
     return ref[pl.ds(chunk * depth * rows + row, depth, stride=rows), :]
 
 
+def far_rows(rows):
+    after = sides()[1][0]
+    return jnp.where(after, rows - 1, 0), jnp.where(after, rows - 2, 1)
+
+
 def load_kernel(
     rows,
     frame_hbm,
     k_hbm,
     res_hbm,
-    excess_hbm,
     d_hbm,
-    map_hbm,
     far_ref,
     near_ref,
     k_ref,
     frames_ref,
-    excess_ref,
     d_ref,
-    map_ref,
     frame_ref,
     res_ref,
     sems,
@@ -114,7 +114,7 @@
     pairs = [(frame_hbm, frame_ref), (res_hbm, res_ref)]
     for c in range(chunks):
         pairs.append((k_hbm.at[:, pl.ds(c * 128, 128)], k_ref.at[pl.ds(c * size, size)]))
-    pairs += [(excess_hbm, excess_ref), (d_hbm, d_ref), (map_hbm, map_ref)]
+    pairs.append((d_hbm, d_ref))
     copies = [pltpu.make_async_copy(a, b, sems.at[n]) for n, (a, b) in enumerate(pairs)]
     for copy in copies:
         copy.start()
@@ -149,9 +149,13 @@
     scale,
     k_ref,
     frames_ref,
+    d_ref,
+    excess_hbm,
+    map_hbm,
+    adj_ref,
+    two_ref,
     excess_ref,
-    d_ref,
-    adj_ref,
+    map_ref,
     edge_ref,
     contribution_ref,
     pair_ref,
@@ -162,8 +166,15 @@
     chord_ref,
     span_ref,
     factor_ref,
+    sems,
 ):
-    depth, rows, cols = adj_ref.shape
+    copies = [
+        pltpu.make_async_copy(excess_hbm, excess_ref, sems.at[0]),
+        pltpu.make_async_copy(map_hbm, map_ref, sems.at[1]),
+    ]
+    for copy in copies:
+        copy.start()
+    depth, rows, cols = chord_ref.shape
     size = depth * rows
     factor_ref[...] = jnp.broadcast_to(d_ref[:, 0:1], factor_ref.shape)
 
@@ -176,26 +187,22 @@
     pair_same = iota((two, two), 0) // depth == iota((two, two), 1) // depth
     row_of = iota((size, two), 0) % rows
     first_half = iota((size, two), 1) < depth
-    placed = []
-    for after, _ in sides():
-        edge = jnp.where(after, rows - 1, 0)
-        second = jnp.where(after, rows - 2, 1)
-        placed.append(row_of == jnp.where(first_half, edge, second))
-    mats, pairs, places = [], [], ([], [])
+    after = sides()[0][0]
+    edge = jnp.where(after, rows - 1, 0)
+    second = jnp.where(after, rows - 2, 1)
+    placed = row_of == jnp.where(first_half, edge, second)
+    mats, pairs, places = [], [], []
     for part in parts:
         column = dot(tall, part).astype(BF16)
         row = dot(part, tile)
         mats.append(jnp.where(same, dot(column, wide), 0.0).astype(BF16))
-        columns = dot(column, tile)
-        for found, target in zip(places, placed):
-            found.append(jnp.where(target, columns, 0.0).astype(BF16))
+        places.append(jnp.where(placed, dot(column, tile), 0.0).astype(BF16))
         pairs.append(
             jnp.where(pair_same, jnp.concatenate([row] * 2, axis=0), 0.0).astype(BF16)
         )
     mat_ref[...] = left_three(mats)
     pair_ref[...] = left_three(pairs)
-    for n in range(2):
-        place_ref[n] = left_three(places[n])
+    place_ref[...] = left_three(places)
 
     f = frames_ref[2]
     f_chord = shift_next(f, 1) - f
@@ -243,23 +250,29 @@
             found.append(source + frames_ref[0] if j == 0 else source)
         put(i, jnp.concatenate(found, axis=0))
     right = right_ref[...].reshape(3 * size, cols)
-    adj_ref[...] = dot(mat_ref[...], right).reshape(depth, rows, cols)
+    adj = dot(mat_ref[...], right)
+    for c in range(cols // 128):
+        adj_ref[c * size : (c + 1) * size, :] = adj[:, c * 128 : (c + 1) * 128]
 
     for n, (after, _) in enumerate(sides()):
         row = jnp.where(after, rows - 1, 0)
         for c in range(cols // 128):
             edge_ref[n, :, c * 128 : (c + 1) * 128] = row_of_each(first_ref, c, depth, rows, row)
+    for n, row in enumerate(far_rows(rows)):
+        for c in range(cols // 128):
+            two_ref[n, :, c * 128 : (c + 1) * 128] = row_of_each(adj_ref, c, depth, rows, row)
+    for copy in copies:
+        copy.wait()
     contribution_ref[...] = scale * (
         d_ref[0:1, 0:1] * f * excess_ref[2]
         + chunked(first_ref, 0, rows, size) * excess_ref[1]
-        + adj_ref[0] * excess_ref[0]
-    )
-
-
-def correction(n, got, own, d_ref, edge_ref, pair_ref, place_ref):
+        + chunked(adj_ref, 0, rows, size) * excess_ref[0]
+    )
+
+
+def correction(n, got, own, d_ref, edge_ref, pair_ref):
     _, depth, cols = edge_ref.shape
-    rows = place_ref.shape[1] // depth
-    after, inside = sides()[n]
+    _, inside = sides()[n]
     factor = d_ref[:, 0:1]
     half = 0.5 * packed_field(got, depth, cols, 0)
     half_next = 0.5 * packed_field(got, depth, cols, 1)
@@ -291,9 +304,7 @@
         + face * outer
         - half * edge_ref[n]
     )
-    found = dot(place_ref[n], right_three(jnp.concatenate([change, inner * e], axis=0)))
-    row = jnp.where(after, rows - 1, 0)
-    return found, jnp.where(iota((rows, cols), 0) == row, e[0:1, :], 0.0)
+    return right_three(jnp.concatenate([change, inner * e], axis=0)), e[0:1, :]
 
 
 def add_segments(total, contribution, picked_rows, map_ref):
@@ -316,22 +327,29 @@
     excess_ref,
     edge_ref,
     pair_ref,
+    map_vmem,
     place_ref,
-    map_vmem,
     base_ref,
     contribution_ref,
     own_ref,
     got_ref,
+    adj_hbm,
+    part_ref,
     adj_ref,
-    part_ref,
     map_ref,
-    map_sem,
+    sems,
 ):
-    map_copy = pltpu.make_async_copy(map_vmem, map_ref, map_sem)
+    map_copy = pltpu.make_async_copy(map_vmem, map_ref, sems.at[0])
     map_copy.start()
-    rows = base_ref.shape[1]
-    found, surface = correction(0, got_ref, own_ref, d_ref, edge_ref, pair_ref, place_ref)
-    adj_ref[...] = base_ref[...] + found.reshape(base_ref.shape)
+    depth, rows, cols = adj_ref.shape
+    size = depth * rows
+    sources, surface = correction(0, got_ref, own_ref, d_ref, edge_ref, pair_ref)
+    found = dot(place_ref[...], sources)
+    adj_ref[...] = (chunked(base_ref, 0, size, size) + found).reshape(depth, rows, cols)
+    adj_copy = pltpu.make_async_copy(adj_ref, adj_hbm, sems.at[1])
+    adj_copy.start()
+    row = jnp.where(sides()[0][0], rows - 1, 0)
+    surface = jnp.where(iota((rows, cols), 0) == row, surface, 0.0)
     contribution = contribution_ref[...] + scale * (
         surface * excess_ref[1] + found[0:rows, :] * excess_ref[0]
     )
@@ -339,6 +357,7 @@
     part_ref[...] = add_segments(
         jnp.zeros(part_ref.shape, F32), contribution, range(rows), map_ref
     )
+    adj_copy.wait()
 
 
 def far_kernel(
@@ -349,46 +368,48 @@
     excess_ref,
     edge_ref,
     pair_ref,
-    place_ref,
     map_vmem,
-    base_ref,
+    two_ref,
     part_in_ref,
-    adj_ref,
+    out_ref,
     part_ref,
     map_ref,
     map_sem,
 ):
     map_copy = pltpu.make_async_copy(map_vmem, map_ref, map_sem)
     map_copy.start()
-    rows = base_ref.shape[1]
-    found, surface = correction(1, got_ref, own_ref, d_ref, edge_ref, pair_ref, place_ref)
-    contribution = scale * (surface * excess_ref[1] + found[0:rows, :] * excess_ref[0])
-    after = sides()[1][0]
-    two = jnp.where(
-        after,
-        jnp.concatenate([contribution[rows - 1 :], contribution[rows - 2 : rows - 1]], axis=0),
-        contribution[0:2],
-    )
-    picked_rows = (jnp.where(after, rows - 1, 0), jnp.where(after, rows - 2, 1))
+    depth = two_ref.shape[1]
+    rows = excess_ref.shape[1]
+    sources, surface = correction(1, got_ref, own_ref, d_ref, edge_ref, pair_ref)
+    found = dot(pair_ref[...], sources)
+    edge, second = far_rows(rows)
+    contribution = scale * jnp.concatenate(
+        [
+            surface * excess_ref[1, pl.ds(edge, 1), :]
+            + found[0:1] * excess_ref[0, pl.ds(edge, 1), :],
+            found[depth : depth + 1] * excess_ref[0, pl.ds(second, 1), :],
+        ],
+        axis=0,
+    )
     map_copy.wait()
-    part_ref[...] = add_segments(part_in_ref[...], two, picked_rows, map_ref)
-    adj_ref[...] = base_ref[...] + found.reshape(base_ref.shape)
-
-
-def finish_kernel(adj_vmem, got_ref, adj_hbm, out_hbm, out_ref, sems):
-    step = adj_vmem.shape[0] // PIECES
+    part_ref[...] = add_segments(part_in_ref[...], contribution, (edge, second), map_ref)
+    out_ref[...] = two_ref[...] + found.reshape(two_ref.shape)
+
+
+def finish_kernel(_, two_ref, got_ref, adj_hbm, out_hbm, out_ref, sems):
     copies = []
-    for n in range(PIECES):
-        piece = pl.ds(n * step, step)
-        copies.append(
-            pltpu.make_async_copy(adj_vmem.at[piece], adj_hbm.at[piece], sems.at[n])
-        )
+    for n, row in enumerate(far_rows(adj_hbm.shape[1])):
+        copies.append(pltpu.make_async_copy(two_ref.at[n], adj_hbm.at[:, row, :], sems.at[n]))
         copies[-1].start()
     out_ref[...] = jnp.sum(got_ref[:, 0, :], axis=0)
-    copies.append(pltpu.make_async_copy(out_ref, out_hbm, sems.at[PIECES]))
+    copies.append(pltpu.make_async_copy(out_ref, out_hbm, sems.at[2]))
     copies[-1].start()
     for copy in copies:
         copy.wait()
+
+
+def in_hbm(x):
+    return pltpu.with_memory_space_constraint(x, pltpu.HBM)
 
 
 def per_device(
@@ -405,38 +426,29 @@
     chunks = cols // 128
     packed_far = pltpu.VMEM(((2 * depth + 4) * chunks, 128), F32)
     packed_near = pltpu.VMEM(((2 * depth + 3) * chunks, 128), F32)
-    own_far, own_near, k, picked, excess, inverse, ids = pl.pallas_call(
+    own_far, own_near, k, picked, inverse = pl.pallas_call(
         functools.partial(load_kernel, rows),
         out_shape=(
             packed_far,
             packed_near,
             pltpu.VMEM((chunks * size, 128), F32),
             pltpu.VMEM((STEPS, rows, cols), F32),
-            pltpu.VMEM((STEPS, rows, cols), F32),
             pltpu.VMEM((depth, depth), F32),
-            pltpu.VMEM((blocks, rows), jnp.int32),
         ),
-        in_specs=[HBM] * 6,
-        out_specs=(VMEM,) * 7,
+        in_specs=[HBM] * 4,
+        out_specs=(VMEM,) * 5,
         scratch_shapes=[
             pltpu.SMEM((STEPS,), jnp.int32),
             pltpu.VMEM((frames, rows, cols), F32),
-            pltpu.SemaphoreType.DMA((5 + chunks,)),
+            pltpu.SemaphoreType.DMA((3 + chunks,)),
         ],
         compiler_params=GRANT,
         name="load",
     )(
-        *(
-            pltpu.with_memory_space_constraint(x, pltpu.HBM)
-            for x in (
-                frame_index,
-                conductance.reshape(size, cols),
-                surface_residual[0],
-                surface_excess[0],
-                depth_inverse[0],
-                segment_map.T,
-            )
-        )
+        in_hbm(frame_index),
+        in_hbm(conductance.reshape(size, cols)),
+        in_hbm(surface_residual[0]),
+        in_hbm(depth_inverse[0]),
     )
     across = [(i, i + 1) for i in range(1, spans - 1, 2)]
     within = [(i, i + 1) for i in range(0, spans - 1, 2)]
@@ -444,17 +456,20 @@
     far = lax.ppermute(own_far, "span", across + [(b, a) for a, b in across])
     scale = 1.0 / math.sqrt(128.0 * STEPS)
     line = pltpu.VMEM((rows, cols), F32)
-    base, edge, contribution, pair, place = pl.pallas_call(
+    base, two, excess, ids, edge, contribution, pair, place = pl.pallas_call(
         functools.partial(base_kernel, scale),
         out_shape=(
-            field,
+            pltpu.VMEM((chunks * size, 128), F32),
+            pltpu.VMEM((2, depth, cols), F32),
+            pltpu.VMEM((STEPS, rows, cols), F32),
+            pltpu.VMEM((blocks, rows), jnp.int32),
             pltpu.VMEM((2, depth, cols), F32),
             line,
             pltpu.VMEM((2 * depth, 6 * depth), BF16),
-            pltpu.VMEM((2, size, 6 * depth), BF16),
+            pltpu.VMEM((size, 6 * depth), BF16),
         ),
-        in_specs=[VMEM] * 4,
-        out_specs=(VMEM,) * 5,
+        in_specs=[VMEM] * 3 + [HBM] * 2,
+        out_specs=(VMEM,) * 8,
         scratch_shapes=[
             pltpu.VMEM((size, 3 * size), BF16),
             pltpu.VMEM((3, size, cols), BF16),
@@ -462,41 +477,46 @@
             field,
             field,
             pltpu.VMEM((depth, 128), F32),
+            pltpu.SemaphoreType.DMA((2,)),
         ],
         compiler_params=GRANT,
         name="base",
-    )(k, picked, excess, inverse)
-    fixed = (inverse, excess, edge, pair, place, ids)
+    )(k, picked, inverse, in_hbm(surface_excess[0]), in_hbm(segment_map.T))
+    fixed = (inverse, excess, edge, pair, ids)
     sums = pltpu.VMEM((devices, 1, lanes), F32)
-    map_scratch = [pltpu.SMEM((blocks, rows), jnp.int32), pltpu.SemaphoreType.DMA]
-    base, partial = pl.pallas_call(
+    adjoint, partial = pl.pallas_call(
         functools.partial(near_kernel, scale),
-        out_shape=(field, sums),
+        out_shape=(pltpu.HBM((depth, rows, cols), F32), sums),
         in_specs=[VMEM] * 10,
-        out_specs=(VMEM,) * 2,
-        scratch_shapes=map_scratch,
+        out_specs=(HBM, VMEM),
+        scratch_shapes=[
+            field,
+            pltpu.SMEM((blocks, rows), jnp.int32),
+            pltpu.SemaphoreType.DMA((2,)),
+        ],
         compiler_params=GRANT,
         name="near",
-    )(*fixed, base, contribution, own_near, near)
-    adjoint, partial = pl.pallas_call(
+    )(*fixed, place, base, contribution, own_near, near)
+    two, partial = pl.pallas_call(
         functools.partial(far_kernel, scale),
-        out_shape=(field, sums),
-        in_specs=[VMEM] * 10,
+        out_shape=(pltpu.VMEM((2, depth, cols), F32), sums),
+        in_specs=[VMEM] * 9,
         out_specs=(VMEM,) * 2,
-        scratch_shapes=map_scratch,
+        scratch_shapes=[pltpu.SMEM((blocks, rows), jnp.int32), pltpu.SemaphoreType.DMA],
         compiler_params=GRANT,
         name="far",
-    )(own_far, far, *fixed, base, partial)
+    )(own_far, far, *fixed, two, partial)
     pieces = lax.all_to_all(partial, ("blade", "span"), 0, 0, tiled=True)
     adjoint, owned = pl.pallas_call(
         finish_kernel,
         out_shape=(pltpu.HBM((depth, rows, cols), F32), pltpu.HBM((lanes,), F32)),
-        in_specs=[VMEM] * 2,
+        in_specs=[HBM, VMEM, VMEM],
         out_specs=(HBM,) * 2,
-        scratch_shapes=[pltpu.VMEM((lanes,), F32), pltpu.SemaphoreType.DMA((PIECES + 1,))],
+        scratch_shapes=[pltpu.VMEM((lanes,), F32), pltpu.SemaphoreType.DMA((3,))],
+        input_output_aliases={0: 0},
         compiler_params=GRANT,
         name="finish",
-    )(adjoint, pltpu.with_memory_space_constraint(pieces, pltpu.VMEM))
+    )(in_hbm(adjoint), two, pltpu.with_memory_space_constraint(pieces, pltpu.VMEM))
     return (adjoint[None], owned)
 
 

time: 24.3 us -> 24.1 us (level)
  blocking collectives: 12.6 us -> 12.2 us
    all_to_all x1, blocking collectives: 12.6 us -> 12.2 us  [per_device(): pieces = lax.all_to_all(partial, ('blade', 'span'), 0, 0, tiled=True)]
    pallas_call x3, Pallas kernels: 3.73 us -> 4.07 us  [the longest x1 1.79 us: per_device(): pl.pallas_call(functools.partial(base_kernel, scale), out_shape=(pltpu.VM...]
  transfers between devices with their start and end apart: 2 -> 2, of which waited for: 0 -> 0; matrix products, arithmetic and copies ran while one was open for 0% -> 0% of each run, Pallas kernels for 12% -> 14%
where the time goes in v11:
time: 24.1 us; the launch traced here: 23.9 us
  blocking collectives  12.2 us (51%)
  Pallas kernels  5.98 us (25%)
  starting transfers between devices  5.03 us (21%)
  between operations  0.69 us (3%)
    all_to_all x1, blocking collectives, per_device(): pieces = lax.all_to_all(partial, ('blade', 'span'), 0, 0, tiled=True)  12.2 us
    ppermute x1, starting transfers between devices, per_device(): near = lax.ppermute(own_near, 'span', within + [(b, a) for a, b in within])  4.36 us
    pallas_call x1, Pallas kernels, per_device(): pl.pallas_call(functools.partial(base_kernel, scale), out_shape=(pltpu.VM...  1.79 us
    pallas_call x1, Pallas kernels, per_device(): pl.pallas_call(functools.partial(near_kernel, scale), out_shape=(pltpu.HB...  1.52 us
    pallas_call x1, Pallas kernels, per_device(): pl.pallas_call(functools.partial(load_kernel, rows), out_shape=(packed_fa...  1.22 us
    pallas_call x1, Pallas kernels, per_device(): pl.pallas_call(functools.partial(far_kernel, scale), out_shape=(pltpu.VME...  0.77 us
    pallas_call x1, Pallas kernels, per_device(): pl.pallas_call(finish_kernel, out_shape=(pltpu.HBM((depth, rows, cols), F...  0.68 us
    ppermute x1, starting transfers between devices, per_device(): far = lax.ppermute(own_far, 'span', across + [(b, a) for a, b in across])  0.67 us
  transfers between devices with their start and end apart: 2, of which 0 were waited for; matrix products, arithmetic and copies ran while one was open for 0% of the time, Pallas kernels for 14%

profile of v11, /device:TPU:0, one launch (start us, length us, event | category | flops | bytes accessed | tf_op | source)
XLA Modules:
  0.0 23.9 jit_solution(17001918667470599757)
XLA Ops:
  0.6 1.2 %load.1 = (f32[272,128]{1,0:T(8,128)S(1)}, f32[268,128]{1,0:T(8,128)S(1)}, f32[1024,128]{1,0:T(8,128)S(1)}, f32[3,8,512]{2,1,0:T(8,128)S(1)}, f32[32,32]{1,0:T(8,128)S(1)}) custom-call(s32[3]{0:T(128)} %frame_hbm.1, f32[256,512]{1,0:T(8,128)} %bitcast.6, f32[4,8,512]{2,1,0:T(8,128)} %bitcast.8, f32[32,32]{1,0:T(8,128)} %bitcast.10), custom_call_target="tpu_custom_call" | custom-call | tf_op jit(solution)/shard_map/load/pallas_call | solution.py:429
  1.9 0.7 %collective-permute-start.1 = (f32[272,128]{1,0:T(8,128)S(1)}, f32[272,128]{1,0:T(8,128)S(1)}, u32[]{:S(2)}, u32[]{:S(2)}) collective-permute-start(f32[272,128]{1,0:T(8,128)S(1)} %get-tuple-element.33.own_ref), channel_id=1, source_target_pairs={{1,2},{2,1},{5,6},{6,5},{9,10},{10,9},{13,14},{14,13},{17,18},{18,... | collective-permute-start | bytes 417800 | tf_op jit(solution)/shard_map/ppermute | solution.py:456
  2.5 4.4 %collective-permute-start = (f32[268,128]{1,0:T(8,128)S(1)}, f32[268,128]{1,0:T(8,128)S(1)}, u32[]{:S(2)}, u32[]{:S(2)}) collective-permute-start(f32[268,128]{1,0:T(8,128)S(1)} %get-tuple-element.31.own_ref), channel_id=1, source_target_pairs={{0,1},{2,3},{1,0},{3,2},{4,5},{6,7},{5,4},{7,6},{8,9},{10,11},{9,8... | collective-permute-start | bytes 411656 | tf_op jit(solution)/shard_map/ppermute | solution.py:455
  6.9 1.8 %base.1 = (f32[1024,128]{1,0:T(8,128)S(1)}, f32[2,32,512]{2,1,0:T(8,128)S(1)}, f32[3,8,512]{2,1,0:T(8,128)S(1)}, s32[4,8]{1,0:T(4,128)S(1)}, f32[2,32,512]{2,1,0...) custom-call(f32[1024,128]{1,0:T(8,128)S(1)} %get-tuple-element.22.k_ref, ...), custom_call_target="tpu_custom_call" | custom-call | tf_op jit(solution)/shard_map/base/pallas_call | solution.py:459
  8.7 0.0 collective-permute-done.got_ref
  8.7 1.5 %near.1 = (f32[32,8,512]{2,1,0:T(8,128)}, f32[32,1,64]{2,1,0:T(1,128)S(1)}) custom-call(f32[32,32]{1,0:T(8,128)S(1)} %get-tuple-element.21.d_ref, f32[3,8,512]{2,1,0:T(8,128)S(1)} %get-tuple-element.24.excess_ref, f32[2,32,512]{2,1,0:T(8,128)S(1)} %get-tuple-element.25.edge_ref, bf16[64,192]{1,0:T(8,128)(2,1)S(1)} %get-tuple-element.26.pair_ref, ...), custom_call_target="tpu_custom_call" | custom-call | tf_op jit(solution)/shard_map/near/pallas_call | solution.py:487
  10.2 0.0 collective-permute-done.1.got_ref
  10.2 0.8 %far.1 = (f32[2,32,512]{2,1,0:T(8,128)S(1)}, f32[32,1,64]{2,1,0:T(1,128)S(1)}) custom-call(f32[272,128]{1,0:T(8,128)S(1)} %get-tuple-element.33.own_ref, f32[272,128]{1,0:T(8,128)S(1)} %collective-permute-done.1.got_ref, f32[32,32]{1,0:T(8,128)S(1)} %get-tuple-element.21.d_ref, f32[3,8,512]{2,1,0:T(8,128)S(1)} %get-tuple-element.24.excess_ref, ...), custom_call_target="tpu_custom_call" | custom-call | tf_op jit(solution)/shard_map/far/pallas_call | solution.py:500
  11.0 12.2 %all_to_all.5.got_ref = f32[32,1,64]{2,1,0:T(1,128)S(1)} all-to-all(f32[32,1,64]{2,1,0:T(1,128)S(1)} %get-tuple-element.37), channel_id=1, replica_groups=mesh['blade'=8,'span'=4] {'blade','span'}, dimensions={0} | all-to-all | bytes 16384 | tf_op jit(solution)/shard_map/all_to_all | solution.py:509
  23.3 0.7 %finish.1 = (f32[32,8,512]{2,1,0:T(8,128)}, f32[64]{0:T(128)}) custom-call(f32[32,8,512]{2,1,0:T(8,128)} %get-tuple-element.32._, f32[2,32,512]{2,1,0:T(8,128)S(1)} %get-tuple-element.36.two_ref, f32[32,1,64]{2,1,0:T(1,128)S(1)} %all_to_all.5.got_ref), custom_call_target="tpu_custom_call", output_to_operand_aliasing={{0}: (0, {})} | custom-call | tf_op jit(solution)/shard_map/finish/pallas_call | solution.py:510
Async XLA Ops:
  1.9 8.4 %collective-permute-start.1 = (f32[272,128]{1,0:T(8,128)S(1)}, f32[272,128]{1,0:T(8,128)S(1)}, u32[]{:S(2)}, u32[]{:S(2)}) collective-permute-start(f32[272,128]{1,0:T(8,128)S(1)} %get-tuple-element.33.own_ref), channel_id=1, source_target_pairs={{1,2},{2,1},{5,6},{6,5},{9,10},{10,9},{13,14},{14,13},{17,18},{18,... | collective-permute-start | bytes 417800 | tf_op jit(solution)/shard_map/ppermute | solution.py:456
  2.5 6.2 %collective-permute-start = (f32[268,128]{1,0:T(8,128)S(1)}, f32[268,128]{1,0:T(8,128)S(1)}, u32[]{:S(2)}, u32[]{:S(2)}) collective-permute-start(f32[268,128]{1,0:T(8,128)S(1)} %get-tuple-element.31.own_ref), channel_id=1, source_target_pairs={{0,1},{2,3},{1,0},{3,2},{4,5},{6,7},{5,4},{7,6},{8,9},{10,11},{9,8... | collective-permute-start | bytes 411656 | tf_op jit(solution)/shard_map/ppermute | solution.py:455

commit v12 on v11

--- a/solution.py
+++ b/solution.py
@@ -333,21 +333,18 @@
     contribution_ref,
     own_ref,
     got_ref,
-    adj_hbm,
+    adj_ref,
     part_ref,
-    adj_ref,
     map_ref,
-    sems,
+    map_sem,
 ):
-    map_copy = pltpu.make_async_copy(map_vmem, map_ref, sems.at[0])
+    map_copy = pltpu.make_async_copy(map_vmem, map_ref, map_sem)
     map_copy.start()
     depth, rows, cols = adj_ref.shape
     size = depth * rows
     sources, surface = correction(0, got_ref, own_ref, d_ref, edge_ref, pair_ref)
     found = dot(place_ref[...], sources)
     adj_ref[...] = (chunked(base_ref, 0, size, size) + found).reshape(depth, rows, cols)
-    adj_copy = pltpu.make_async_copy(adj_ref, adj_hbm, sems.at[1])
-    adj_copy.start()
     row = jnp.where(sides()[0][0], rows - 1, 0)
     surface = jnp.where(iota((rows, cols), 0) == row, surface, 0.0)
     contribution = contribution_ref[...] + scale * (
@@ -357,7 +354,6 @@
     part_ref[...] = add_segments(
         jnp.zeros(part_ref.shape, F32), contribution, range(rows), map_ref
     )
-    adj_copy.wait()
 
 
 def far_kernel(
@@ -396,14 +392,14 @@
     out_ref[...] = two_ref[...] + found.reshape(two_ref.shape)
 
 
-def finish_kernel(_, two_ref, got_ref, adj_hbm, out_hbm, out_ref, sems):
+def store_kernel(adj_ref, two_ref, adj_hbm, sems):
+    copy = pltpu.make_async_copy(adj_ref, adj_hbm, sems.at[2])
+    copy.start()
+    copy.wait()
     copies = []
     for n, row in enumerate(far_rows(adj_hbm.shape[1])):
         copies.append(pltpu.make_async_copy(two_ref.at[n], adj_hbm.at[:, row, :], sems.at[n]))
         copies[-1].start()
-    out_ref[...] = jnp.sum(got_ref[:, 0, :], axis=0)
-    copies.append(pltpu.make_async_copy(out_ref, out_hbm, sems.at[2]))
-    copies[-1].start()
     for copy in copies:
         copy.wait()
 
@@ -484,16 +480,13 @@
     )(k, picked, inverse, in_hbm(surface_excess[0]), in_hbm(segment_map.T))
     fixed = (inverse, excess, edge, pair, ids)
     sums = pltpu.VMEM((devices, 1, lanes), F32)
+    map_scratch = [pltpu.SMEM((blocks, rows), jnp.int32), pltpu.SemaphoreType.DMA]
     adjoint, partial = pl.pallas_call(
         functools.partial(near_kernel, scale),
-        out_shape=(pltpu.HBM((depth, rows, cols), F32), sums),
+        out_shape=(field, sums),
         in_specs=[VMEM] * 10,
-        out_specs=(HBM, VMEM),
-        scratch_shapes=[
-            field,
-            pltpu.SMEM((blocks, rows), jnp.int32),
-            pltpu.SemaphoreType.DMA((2,)),
-        ],
+        out_specs=(VMEM,) * 2,
+        scratch_shapes=map_scratch,
         compiler_params=GRANT,
         name="near",
     )(*fixed, place, base, contribution, own_near, near)
@@ -502,22 +495,24 @@
         out_shape=(pltpu.VMEM((2, depth, cols), F32), sums),
         in_specs=[VMEM] * 9,
         out_specs=(VMEM,) * 2,
-        scratch_shapes=[pltpu.SMEM((blocks, rows), jnp.int32), pltpu.SemaphoreType.DMA],
+        scratch_shapes=map_scratch,
         compiler_params=GRANT,
         name="far",
     )(own_far, far, *fixed, two, partial)
     pieces = lax.all_to_all(partial, ("blade", "span"), 0, 0, tiled=True)
-    adjoint, owned = pl.pallas_call(
-        finish_kernel,
-        out_shape=(pltpu.HBM((depth, rows, cols), F32), pltpu.HBM((lanes,), F32)),
-        in_specs=[HBM, VMEM, VMEM],
-        out_specs=(HBM,) * 2,
-        scratch_shapes=[pltpu.VMEM((lanes,), F32), pltpu.SemaphoreType.DMA((3,))],
-        input_output_aliases={0: 0},
+    adjoint = pl.pallas_call(
+        store_kernel,
+        out_shape=pltpu.HBM((depth, rows, cols), F32),
+        in_specs=[VMEM] * 2,
+        out_specs=HBM,
+        scratch_shapes=[pltpu.SemaphoreType.DMA((3,))],
+        cost_estimate=pl.CostEstimate(
+            flops=0, bytes_accessed=4 * size * cols * 2, transcendentals=0
+        ),
         compiler_params=GRANT,
-        name="finish",
-    )(in_hbm(adjoint), two, pltpu.with_memory_space_constraint(pieces, pltpu.VMEM))
-    return (adjoint[None], owned)
+        name="store",
+    )(adjoint, two)
+    return (adjoint[None], jnp.sum(pieces, axis=(0, 1)))
 
 
 def solution(mesh):

time: 24.1 us -> 24.8 us (1.029)
  blocking collectives: 12.2 us -> 0 us
  waiting for transfers between devices: 0.01 us -> 5.68 us
  starting transfers between devices: 5.03 us -> 10.7 us
  Pallas kernels: 5.98 us -> 7.03 us
  other arithmetic: 0 us -> 0.56 us
    all_to_all x1 -> x0, blocking collectives: 12.2 us -> none  [per_device(): pieces = lax.all_to_all(partial, ('blade', 'span'), 0, 0, tiled=True)]
    all_to_all x0 -> x1, waiting for transfers between devices: none -> 5.67 us  [per_device(): pieces = lax.all_to_all(partial, ('blade', 'span'), 0, 0, tiled=True)]
    all_to_all x0 -> x1, starting transfers between devices: none -> 5.63 us  [per_device(): pieces = lax.all_to_all(partial, ('blade', 'span'), 0, 0, tiled=True)]
    pallas_call x1, Pallas kernels: 0.77 us -> 1.36 us  [per_device(): pl.pallas_call(functools.partial(far_kernel, scale), out_shape=(pltpu.VME...]
    reduce_sum x0 -> x1, other arithmetic: none -> 0.56 us  [per_device(): return (adjoint[None], jnp.sum(pieces, axis=(0, 1)))]
    pallas_call x2, Pallas kernels: 2.2 us -> 2.65 us  [the longest x1 1.47 us: per_device(): pl.pallas_call(store_kernel, out_shape=pltpu.HBM((depth, rows, cols), F32...]
  transfers between devices with their start and end apart: 2 -> 3, of which waited for: 0 -> 1; matrix products, arithmetic and copies ran while one was open for 0% -> 0% of each run, Pallas kernels for 14% -> 18%
where the time goes in v12:
time: 24.8 us; the launch traced here: 24.6 us
  starting transfers between devices  10.7 us (43%)
  Pallas kernels  7.03 us (28%)
  waiting for transfers between devices  5.68 us (23%)
  between operations  0.7 us (3%)
  other arithmetic  0.56 us (2%)
    all_to_all x1, waiting for transfers between devices, per_device(): pieces = lax.all_to_all(partial, ('blade', 'span'), 0, 0, tiled=True)  5.67 us
    all_to_all x1, starting transfers between devices, per_device(): pieces = lax.all_to_all(partial, ('blade', 'span'), 0, 0, tiled=True)  5.63 us
    ppermute x1, starting transfers between devices, per_device(): near = lax.ppermute(own_near, 'span', within + [(b, a) for a, b in within])  4.36 us
    pallas_call x1, Pallas kernels, per_device(): pl.pallas_call(functools.partial(base_kernel, scale), out_shape=(pltpu.VM...  1.79 us
    pallas_call x1, Pallas kernels, per_device(): pl.pallas_call(store_kernel, out_shape=pltpu.HBM((depth, rows, cols), F32...  1.47 us
    pallas_call x1, Pallas kernels, per_device(): pl.pallas_call(functools.partial(far_kernel, scale), out_shape=(pltpu.VME...  1.36 us
    pallas_call x1, Pallas kernels, per_device(): pl.pallas_call(functools.partial(load_kernel, rows), out_shape=(packed_fa...  1.22 us
    pallas_call x1, Pallas kernels, per_device(): pl.pallas_call(functools.partial(near_kernel, scale), out_shape=(field, s...  1.18 us
  transfers between devices with their start and end apart: 3, of which 1 were waited for; matrix products, arithmetic and copies ran while one was open for 0% of the time, Pallas kernels for 18%

profile of v12, /device:TPU:0, one launch (start us, length us, event | category | flops | bytes accessed | tf_op | source)
XLA Modules:
  0.0 24.6 jit_solution(15250861308254536302)
XLA Ops:
  0.6 1.2 %load.1 = (f32[272,128]{1,0:T(8,128)S(1)}, f32[268,128]{1,0:T(8,128)S(1)}, f32[1024,128]{1,0:T(8,128)S(1)}, f32[3,8,512]{2,1,0:T(8,128)S(1)}, f32[32,32]{1,0:T(8,128)S(1)}) custom-call(s32[3]{0:T(128)} %frame_hbm.1, f32[256,512]{1,0:T(8,128)} %bitcast.6, f32[4,8,512]{2,1,0:T(8,128)} %bitcast.8, f32[32,32]{1,0:T(8,128)} %bitcast.10), custom_call_target="tpu_custom_call" | custom-call | tf_op jit(solution)/shard_map/load/pallas_call | solution.py:425
  1.9 0.7 %collective-permute-start.1 = (f32[272,128]{1,0:T(8,128)S(1)}, f32[272,128]{1,0:T(8,128)S(1)}, u32[]{:S(2)}, u32[]{:S(2)}) collective-permute-start(f32[272,128]{1,0:T(8,128)S(1)} %get-tuple-element.31.own_ref), channel_id=1, source_target_pairs={{1,2},{2,1},{5,6},{6,5},{9,10},{10,9},{13,14},{14,13},{17,18},{18,... | collective-permute-start | bytes 417800 | tf_op jit(solution)/shard_map/ppermute | solution.py:452
  2.5 4.4 %collective-permute-start = (f32[268,128]{1,0:T(8,128)S(1)}, f32[268,128]{1,0:T(8,128)S(1)}, u32[]{:S(2)}, u32[]{:S(2)}) collective-permute-start(f32[268,128]{1,0:T(8,128)S(1)} %get-tuple-element.29.own_ref), channel_id=1, source_target_pairs={{0,1},{2,3},{1,0},{3,2},{4,5},{6,7},{5,4},{7,6},{8,9},{10,11},{9,8... | collective-permute-start | bytes 411656 | tf_op jit(solution)/shard_map/ppermute | solution.py:451
  6.9 1.8 %base.1 = (f32[1024,128]{1,0:T(8,128)S(1)}, f32[2,32,512]{2,1,0:T(8,128)S(1)}, f32[3,8,512]{2,1,0:T(8,128)S(1)}, s32[4,8]{1,0:T(4,128)S(1)}, f32[2,32,512]{2,1,0...) custom-call(f32[1024,128]{1,0:T(8,128)S(1)} %get-tuple-element.20.k_ref, ...), custom_call_target="tpu_custom_call" | custom-call | tf_op jit(solution)/shard_map/base/pallas_call | solution.py:455
  8.7 0.0 collective-permute-done.got_ref
  8.7 1.2 %near.1 = (f32[32,8,512]{2,1,0:T(8,128)S(1)}, f32[32,1,64]{2,1,0:T(1,128)S(1)}) custom-call(f32[32,32]{1,0:T(8,128)S(1)} %get-tuple-element.19.d_ref, f32[3,8,512]{2,1,0:T(8,128)S(1)} %get-tuple-element.22.excess_ref, f32[2,32,512]{2,1,0:T(8,128)S(1)} %get-tuple-element.23.edge_ref, bf16[64,192]{1,0:T(8,128)(2,1)S(1)} %get-tuple-element.24.pair_ref, ...), custom_call_target="tpu_custom_call" | custom-call | tf_op jit(solution)/shard_map/near/pallas_call | solution.py:484
  9.9 0.0 collective-permute-done.1.got_ref
  9.9 1.4 %far.1 = (f32[2,32,512]{2,1,0:T(8,128)S(1)}, f32[32,1,64]{2,1,0:T(1,128)}) custom-call(f32[272,128]{1,0:T(8,128)S(1)} %get-tuple-element.31.own_ref, f32[272,128]{1,0:T(8,128)S(1)} %collective-permute-done.1.got_ref, f32[32,32]{1,0:T(8,128)S(1)} %get-tuple-element.19.d_ref, f32[3,8,512]{2,1,0:T(8,128)S(1)} %get-tuple-element.22.excess_ref, ...), custom_call_target="tpu_custom_call" | custom-call | tf_op jit(solution)/shard_map/far/pallas_call | solution.py:493
  11.3 5.6 %all-to-all-start = ((f32[32,1,64]{2,1,0:T(1,128)}), f32[32,1,64]{2,1,0:T(1,128)S(1)}, u32[]{:S(2)}, u32[]{:S(2)}) async-start(f32[32,1,64]{2,1,0:T(1,128)} %get-tuple-element.35), calls=%async_computation | async-start | bytes 32768 | tf_op jit(solution)/shard_map/all_to_all | solution.py:502
  16.9 1.5 %store.1 = f32[32,8,512]{2,1,0:T(8,128)} custom-call(f32[32,8,512]{2,1,0:T(8,128)S(1)} %get-tuple-element.30.adj_ref, f32[2,32,512]{2,1,0:T(8,128)S(1)} %get-tuple-element.34.two_ref), custom_call_target="tpu_custom_call" | custom-call | bytes 1048576 | tf_op jit(solution)/shard_map/store/pallas_call | solution.py:503
  18.4 5.7 %all-to-all-done = f32[32,1,64]{2,1,0:T(1,128)S(1)} async-done(((f32[32,1,64]{2,1,0:T(1,128)}), f32[32,1,64]{2,1,0:T(1,128)S(1)}, u32[]{:S(2)}, u32[]{:S(2)}) %all-to-all-start) | async-done | bytes 8224 | tf_op jit(solution)/shard_map/all_to_all | solution.py:502
  24.1 0.6 %reduce_sum.9 = f32[64]{0:T(128)} reduce(f32[32,1,64]{2,1,0:T(1,128)S(1)} %all-to-all-done, f32[]{:T(128)} %constant.0.clone.1), dimensions={0,1}, to_apply=%region_0.0 | reduce | flops 1984 | bytes 8452 | tf_op jit(solution)/shard_map/reduce_sum | solution.py:515
Async XLA Ops:
  1.9 8.0 %collective-permute-start.1 = (f32[272,128]{1,0:T(8,128)S(1)}, f32[272,128]{1,0:T(8,128)S(1)}, u32[]{:S(2)}, u32[]{:S(2)}) collective-permute-start(f32[272,128]{1,0:T(8,128)S(1)} %get-tuple-element.31.own_ref), channel_id=1, source_target_pairs={{1,2},{2,1},{5,6},{6,5},{9,10},{10,9},{13,14},{14,13},{17,18},{18,... | collective-permute-start | bytes 417800 | tf_op jit(solution)/shard_map/ppermute | solution.py:452
  2.5 6.2 %collective-permute-start = (f32[268,128]{1,0:T(8,128)S(1)}, f32[268,128]{1,0:T(8,128)S(1)}, u32[]{:S(2)}, u32[]{:S(2)}) collective-permute-start(f32[268,128]{1,0:T(8,128)S(1)} %get-tuple-element.29.own_ref), channel_id=1, source_target_pairs={{0,1},{2,3},{1,0},{3,2},{4,5},{6,7},{5,4},{7,6},{8,9},{10,11},{9,8... | collective-permute-start | bytes 411656 | tf_op jit(solution)/shard_map/ppermute | solution.py:451
  11.3 12.8 %all-to-all-start = ((f32[32,1,64]{2,1,0:T(1,128)}), f32[32,1,64]{2,1,0:T(1,128)S(1)}, u32[]{:S(2)}, u32[]{:S(2)}) async-start(f32[32,1,64]{2,1,0:T(1,128)} %get-tuple-element.35), calls=%async_computation | async-start | bytes 32768 | tf_op jit(solution)/shard_map/all_to_all | solution.py:502

commit v13 on v11

--- a/solution.py
+++ b/solution.py
@@ -31,27 +31,59 @@
     return jnp.concatenate([high, low, high], axis=1)
 
 
-def right_three(x):
-    high, low = split(x)
-    return jnp.concatenate([high, high, low], axis=0)
+def right_three(chunks):
+    columns = []
+    for x in chunks:
+        high, low = split(x)
+        columns.append(jnp.concatenate([high, high, low], axis=0))
+    return jnp.concatenate(columns, axis=1)
 
 
 def iota(shape, dim):
     return lax.broadcasted_iota(jnp.int32, shape, dim)
 
 
-def shift_next(x, axis):
-    size = x.shape[axis]
-    return jnp.where(iota(x.shape, axis) == size - 1, 0.0, pltpu.roll(x, size - 1, axis))
-
-
-def shift_prev(x, axis, first):
-    return jnp.where(iota(x.shape, axis) == 0, first, pltpu.roll(x, 1, axis))
-
-
-def divergence(v, weight, half, axis):
-    flux = weight * (shift_next(v, axis) - v)
-    return flux - shift_prev(flux, axis, half * v)
+def pieces_of(x):
+    return [x[:, c : c + 128] for c in range(0, x.shape[1], 128)]
+
+
+def chord_next(chunks):
+    last = iota(chunks[0].shape, 1) == 127
+    moved = [pltpu.roll(x, 127, 1) for x in chunks] + [0.0]
+    return [jnp.where(last, moved[c + 1], moved[c]) for c in range(len(chunks))]
+
+
+def chord_prev(chunks, first):
+    start = iota(chunks[0].shape, 1) == 0
+    moved = [first] + [pltpu.roll(x, 1, 1) for x in chunks]
+    return [jnp.where(start, moved[c], moved[c + 1]) for c in range(len(chunks))]
+
+
+def row_next(x):
+    rows = x.shape[0]
+    return jnp.where(iota(x.shape, 0) == rows - 1, 0.0, pltpu.roll(x, rows - 1, 0))
+
+
+def row_prev(x, first):
+    return jnp.where(iota(x.shape, 0) == 0, first, pltpu.roll(x, 1, 0))
+
+
+def both(fn, *lists):
+    return [fn(*items) for items in zip(*lists)]
+
+
+def chord_faces(half):
+    return both(lambda h, n: h + n, half, chord_next(half))
+
+
+def chord_flow(v, faces, half):
+    flux = both(lambda w, n, x: w * (n - x), faces, chord_next(v), v)
+    return both(lambda f, p: f - p, flux, chord_prev(flux, half[0] * v[0]))
+
+
+def span_flow(v, face, half):
+    flux = face * (row_next(v) - v)
+    return flux - row_prev(flux, half * v)
 
 
 def sides():
@@ -68,20 +100,17 @@
 
 def chunked(ref, start, count, step):
     chunks = ref.shape[0] // step
-    return jnp.concatenate(
-        [ref[c * step + start : c * step + start + count, :] for c in range(chunks)], axis=1
-    )
-
-
-def packed_field(ref, depth, cols, n):
-    chunks = cols // 128
-    return chunked(ref.at[n * chunks * depth : (n + 1) * chunks * depth], 0, depth, depth)
-
-
-def packed_line(ref, depth, cols, n):
-    chunks = cols // 128
+    return [ref[c * step + start : c * step + start + count, :] for c in range(chunks)]
+
+
+def packed_field(ref, depth, chunks, n):
+    base = n * chunks * depth
+    return [ref[base + c * depth : base + (c + 1) * depth, :] for c in range(chunks)]
+
+
+def packed_line(ref, depth, chunks, n):
     base = (2 * depth + n) * chunks
-    return chunked(ref.at[base : base + chunks], 0, 1, 1)
+    return [ref[base + c : base + c + 1, :] for c in range(chunks)]
 
 
 def row_of_each(ref, chunk, depth, rows, row):
@@ -158,6 +187,7 @@
     map_ref,
     edge_ref,
     contribution_ref,
+    surface_ref,
     pair_ref,
     place_ref,
     mat_ref,
@@ -174,7 +204,9 @@
     ]
     for copy in copies:
         copy.start()
-    depth, rows, cols = chord_ref.shape
+    depth = d_ref.shape[0]
+    _, rows, cols = frames_ref.shape
+    chunks = cols // 128
     size = depth * rows
     factor_ref[...] = jnp.broadcast_to(d_ref[:, 0:1], factor_ref.shape)
 
@@ -204,54 +236,68 @@
     pair_ref[...] = left_three(pairs)
     place_ref[...] = left_three(places)
 
-    f = frames_ref[2]
-    f_chord = shift_next(f, 1) - f
-    f_span = shift_next(f, 0) - f
-
-    def put(i, both):
-        high, low = split(both)
+    f = pieces_of(frames_ref[2])
+    f_chord = both(lambda n, x: n - x, chord_next(f), f)
+    f_span = both(lambda x: row_next(x) - x, f)
+
+    def put(i, first, second):
         span = pl.ds(i * rows, 2 * rows)
-        right_ref[0, span, :] = high
-        right_ref[1, span, :] = high
-        right_ref[2, span, :] = low
+        for c in range(chunks):
+            lanes = slice(c * 128, (c + 1) * 128)
+            high, low = split(jnp.concatenate([first[c], second[c]], axis=0))
+            right_ref[0, span, lanes] = high
+            right_ref[1, span, lanes] = high
+            right_ref[2, span, lanes] = low
+
+    def write(ref, j, items):
+        for c in range(chunks):
+            ref[c * size + j * rows : c * size + (j + 1) * rows, :] = items[c]
+
+    def read(ref, j):
+        return chunked(ref, j * rows, rows, size)
 
     for i in range(0, depth, 2):
         found = []
         for j in (i, i + 1):
-            half = 0.5 * chunked(k_ref, j * rows, rows, size)
-            w_chord = half + shift_next(half, 1)
-            w_span = half + shift_next(half, 0)
-            chord_ref[j] = w_chord
-            span_ref[j] = w_span
-            edge = half * f
-            flux_chord = w_chord * f_chord
-            flux_span = w_span * f_span
-            moved = f + flux_chord - shift_prev(flux_chord, 1, edge)
-            moved = moved + flux_span - shift_prev(flux_span, 0, edge)
-            factor = jnp.concatenate(
-                [jnp.broadcast_to(factor_ref[j : j + 1, :], (rows, 128))] * (cols // 128), axis=1
-            )
-            source = factor * moved
-            found.append(source + frames_ref[1] if j == 0 else source)
-        put(i, jnp.concatenate(found, axis=0))
+            half = both(lambda x: 0.5 * x, read(k_ref, j))
+            w_chord = chord_faces(half)
+            w_span = both(lambda h: h + row_next(h), half)
+            write(chord_ref, j, w_chord)
+            write(span_ref, j, w_span)
+            edge = both(lambda h, x: h * x, half, f)
+            flux = both(lambda w, x: w * x, w_chord, f_chord)
+            before = chord_prev(flux, edge[0])
+            factor = jnp.broadcast_to(factor_ref[j : j + 1, :], (rows, 128))
+            source = []
+            for c in range(chunks):
+                flux_span = w_span[c] * f_span[c]
+                moved = f[c] + flux[c] - before[c] + flux_span - row_prev(flux_span, edge[c])
+                source.append(factor * moved)
+            if j == 0:
+                source = both(lambda x, g: x + g, source, pieces_of(frames_ref[1]))
+            found.append(source)
+        put(i, *found)
     right = right_ref[...].reshape(3 * size, cols)
     first = dot(mat_ref[...], right)
-    for c in range(cols // 128):
+    for c in range(chunks):
         first_ref[c * size : (c + 1) * size, :] = first[:, c * 128 : (c + 1) * 128]
 
     for i in range(0, depth, 2):
         found = []
         for j in (i, i + 1):
-            v = chunked(first_ref, j * rows, rows, size)
-            half = 0.5 * chunked(k_ref, j * rows, rows, size)
-            source = (
-                v + divergence(v, chord_ref[j], half, 1) + divergence(v, span_ref[j], half, 0)
+            v = read(first_ref, j)
+            half = both(lambda x: 0.5 * x, read(k_ref, j))
+            chord = chord_flow(v, read(chord_ref, j), half)
+            source = both(
+                lambda x, a, w, h: x + a + span_flow(x, w, h), v, chord, read(span_ref, j), half
             )
-            found.append(source + frames_ref[0] if j == 0 else source)
-        put(i, jnp.concatenate(found, axis=0))
+            if j == 0:
+                source = both(lambda x, g: x + g, source, pieces_of(frames_ref[0]))
+            found.append(source)
+        put(i, *found)
     right = right_ref[...].reshape(3 * size, cols)
     adj = dot(mat_ref[...], right)
-    for c in range(cols // 128):
+    for c in range(chunks):
         adj_ref[c * size : (c + 1) * size, :] = adj[:, c * 128 : (c + 1) * 128]
 
     for n, (after, _) in enumerate(sides()):
@@ -263,48 +309,70 @@
             two_ref[n, :, c * 128 : (c + 1) * 128] = row_of_each(adj_ref, c, depth, rows, row)
     for copy in copies:
         copy.wait()
-    contribution_ref[...] = scale * (
-        d_ref[0:1, 0:1] * f * excess_ref[2]
-        + chunked(first_ref, 0, rows, size) * excess_ref[1]
-        + chunked(adj_ref, 0, rows, size) * excess_ref[0]
-    )
+    row = jnp.where(iota((depth, depth), 0) == iota((depth, depth), 1), d_ref[0:1, :], 0.0)
+    surface_ref[...] = jnp.broadcast_to(jnp.sum(row, axis=1, keepdims=True), surface_ref.shape)
+    parts = (d_ref[0:1, 0:1] * f[c] for c in range(chunks))
+    for c, (own, mid, end) in enumerate(zip(parts, read(first_ref, 0), read(adj_ref, 0))):
+        lanes = slice(c * 128, (c + 1) * 128)
+        contribution_ref[:, lanes] = scale * (
+            own * excess_ref[2, :, lanes]
+            + mid * excess_ref[1, :, lanes]
+            + end * excess_ref[0, :, lanes]
+        )
 
 
 def correction(n, got, own, d_ref, edge_ref, pair_ref):
     _, depth, cols = edge_ref.shape
+    chunks = cols // 128
     _, inside = sides()[n]
-    factor = d_ref[:, 0:1]
-    half = 0.5 * packed_field(got, depth, cols, 0)
-    half_next = 0.5 * packed_field(got, depth, cols, 1)
-    half_own = 0.5 * packed_field(own, depth, cols, 0)
-    inner = half_own + 0.5 * packed_field(own, depth, cols, 1)
-    f = packed_line(got, depth, cols, 0)
-    frame = packed_line(got, depth, cols, 1)
-    f_next = packed_line(got, depth, cols, 2)
-    f_own = packed_line(own, depth, cols, 0)
-    face = half + half_own
-    flux = (half + shift_next(half, 1)) * (shift_next(f, 1) - f)
-    moved = (
-        f
-        + flux
-        - shift_prev(flux, 1, half * f)
-        + (half + half_next) * (f_next - f)
-        + face * (f_own - f)
-    )
-    outer = factor * moved + jnp.where(iota((depth, 1), 0) == 0, frame, 0.0)
-    sources = [factor * (face * f - half * f_own), jnp.where(inside, outer, 0.0)]
-    found = dot(pair_ref[...], right_three(jnp.concatenate(sources, axis=0)))
-    e = found[0:depth]
-    outer = found[depth:]
-    w_chord = half_own + shift_next(half_own, 1)
-    change = (
-        e
-        + divergence(e, w_chord, half_own, 1)
-        - (half + half_own + inner) * e
-        + face * outer
-        - half * edge_ref[n]
-    )
-    return right_three(jnp.concatenate([change, inner * e], axis=0)), e[0:1, :]
+    factor = jnp.broadcast_to(d_ref[:, 0:1], (depth, 128))
+    at_surface = iota((depth, 128), 0) == 0
+
+    def halved(ref, which):
+        return both(lambda x: 0.5 * x, packed_field(ref, depth, chunks, which))
+
+    half = halved(got, 0)
+    half_next = halved(got, 1)
+    half_own = halved(own, 0)
+    inner = both(lambda a, b: a + b, half_own, halved(own, 1))
+    f = packed_line(got, depth, chunks, 0)
+    frame = packed_line(got, depth, chunks, 1)
+    f_next = packed_line(got, depth, chunks, 2)
+    f_own = packed_line(own, depth, chunks, 0)
+    face = both(lambda a, b: a + b, half, half_own)
+    step = both(lambda a, b: a - b, chord_next(f), f)
+    flux = both(lambda w, x: w * x, chord_faces(half), step)
+    before = chord_prev(flux, half[0] * f[0])
+    sources = []
+    for c in range(chunks):
+        moved = (
+            f[c]
+            + flux[c]
+            - before[c]
+            + (half[c] + half_next[c]) * (f_next[c] - f[c])
+            + face[c] * (f_own[c] - f[c])
+        )
+        outer = factor * moved + jnp.where(at_surface, frame[c], 0.0)
+        within = factor * (face[c] * f[c] - half[c] * f_own[c])
+        sources.append(jnp.concatenate([within, jnp.where(inside, outer, 0.0)], axis=0))
+    found = pieces_of(dot(pair_ref[...], right_three(sources)))
+    e = both(lambda x: x[0:depth], found)
+    chord = chord_flow(e, chord_faces(half_own), half_own)
+    change = []
+    for c in range(chunks):
+        change.append(
+            e[c]
+            + chord[c]
+            - (half[c] + half_own[c] + inner[c]) * e[c]
+            + face[c] * found[c][depth:]
+            - half[c] * edge_ref[n, :, c * 128 : (c + 1) * 128]
+        )
+    second = both(lambda a, b: a * b, inner, e)
+    return change, second, both(lambda x: x[0:1, :], e)
+
+
+def stacked(change, second):
+    return right_three(both(lambda a, b: jnp.concatenate([a, b], axis=0), change, second))
 
 
 def add_segments(total, contribution, picked_rows, map_ref):
@@ -313,8 +381,7 @@
     lane = iota(shape, 1)
     segment = jnp.where(lane < lanes, iota(shape, 0) * lanes + lane, -1)
     found = jnp.zeros(shape, F32)
-    for block in range(contribution.shape[1] // 128):
-        part = contribution[:, block * 128 : (block + 1) * 128]
+    for block, part in enumerate(contribution):
         sums = jnp.sum(part, axis=1, keepdims=True)
         for n, row in enumerate(picked_rows):
             found += jnp.where(segment == map_ref[block, row], sums[n : n + 1, :], 0.0)
@@ -343,16 +410,24 @@
     map_copy.start()
     depth, rows, cols = adj_ref.shape
     size = depth * rows
-    sources, surface = correction(0, got_ref, own_ref, d_ref, edge_ref, pair_ref)
-    found = dot(place_ref[...], sources)
-    adj_ref[...] = (chunked(base_ref, 0, size, size) + found).reshape(depth, rows, cols)
+    change, second, surface = correction(0, got_ref, own_ref, d_ref, edge_ref, pair_ref)
+    found = pieces_of(dot(place_ref[...], stacked(change, second)))
+    for c, old in enumerate(chunked(base_ref, 0, size, size)):
+        adj_ref[:, :, c * 128 : (c + 1) * 128] = (old + found[c]).reshape(depth, rows, 128)
     adj_copy = pltpu.make_async_copy(adj_ref, adj_hbm, sems.at[1])
     adj_copy.start()
-    row = jnp.where(sides()[0][0], rows - 1, 0)
-    surface = jnp.where(iota((rows, cols), 0) == row, surface, 0.0)
-    contribution = contribution_ref[...] + scale * (
-        surface * excess_ref[1] + found[0:rows, :] * excess_ref[0]
-    )
+    at_edge = iota((rows, 128), 0) == jnp.where(sides()[0][0], rows - 1, 0)
+    contribution = []
+    for c in range(cols // 128):
+        lanes = slice(c * 128, (c + 1) * 128)
+        contribution.append(
+            contribution_ref[:, lanes]
+            + scale
+            * (
+                jnp.where(at_edge, surface[c], 0.0) * excess_ref[1, :, lanes]
+                + found[c][0:rows] * excess_ref[0, :, lanes]
+            )
+        )
     map_copy.wait()
     part_ref[...] = add_segments(
         jnp.zeros(part_ref.shape, F32), contribution, range(rows), map_ref
@@ -369,6 +444,7 @@
     edge_ref,
     pair_ref,
     map_vmem,
+    surface_ref,
     two_ref,
     part_in_ref,
     out_ref,
@@ -378,21 +454,25 @@
 ):
     map_copy = pltpu.make_async_copy(map_vmem, map_ref, map_sem)
     map_copy.start()
-    depth = two_ref.shape[1]
+    depth, cols = two_ref.shape[1:]
     rows = excess_ref.shape[1]
-    sources, surface = correction(1, got_ref, own_ref, d_ref, edge_ref, pair_ref)
-    found = dot(pair_ref[...], sources)
-    edge, second = far_rows(rows)
-    contribution = scale * jnp.concatenate(
-        [
-            surface * excess_ref[1, pl.ds(edge, 1), :]
-            + found[0:1] * excess_ref[0, pl.ds(edge, 1), :],
-            found[depth : depth + 1] * excess_ref[0, pl.ds(second, 1), :],
-        ],
-        axis=0,
+    change, second, surface = correction(1, got_ref, own_ref, d_ref, edge_ref, pair_ref)
+    found = dot(pair_ref[...], stacked(change, second))
+    edge_row, second_row = far_rows(rows)
+    weight = surface_ref[...]
+    middle = pieces_of(excess_ref[1, pl.ds(edge_row, 1), :])
+    last = pieces_of(excess_ref[0, pl.ds(edge_row, 1), :])
+    last_second = pieces_of(excess_ref[0, pl.ds(second_row, 1), :])
+    contribution = []
+    for c in range(cols // 128):
+        at_edge = jnp.sum(weight * change[c], axis=0, keepdims=True)
+        at_second = jnp.sum(weight * second[c], axis=0, keepdims=True)
+        lines = [surface[c] * middle[c] + at_edge * last[c], at_second * last_second[c]]
+        contribution.append(scale * jnp.concatenate(lines, axis=0))
+    map_copy.wait()
+    part_ref[...] = add_segments(
+        part_in_ref[...], contribution, (edge_row, second_row), map_ref
     )
-    map_copy.wait()
-    part_ref[...] = add_segments(part_in_ref[...], contribution, (edge, second), map_ref)
     out_ref[...] = two_ref[...] + found.reshape(two_ref.shape)
 
 
@@ -456,7 +536,7 @@
     far = lax.ppermute(own_far, "span", across + [(b, a) for a, b in across])
     scale = 1.0 / math.sqrt(128.0 * STEPS)
     line = pltpu.VMEM((rows, cols), F32)
-    base, two, excess, ids, edge, contribution, pair, place = pl.pallas_call(
+    base, two, excess, ids, edge, contribution, surface, pair, place = pl.pallas_call(
         functools.partial(base_kernel, scale),
         out_shape=(
             pltpu.VMEM((chunks * size, 128), F32),
@@ -465,17 +545,18 @@
             pltpu.VMEM((blocks, rows), jnp.int32),
             pltpu.VMEM((2, depth, cols), F32),
             line,
+            pltpu.VMEM((depth, 128), F32),
             pltpu.VMEM((2 * depth, 6 * depth), BF16),
             pltpu.VMEM((size, 6 * depth), BF16),
         ),
         in_specs=[VMEM] * 3 + [HBM] * 2,
-        out_specs=(VMEM,) * 8,
+        out_specs=(VMEM,) * 9,
         scratch_shapes=[
             pltpu.VMEM((size, 3 * size), BF16),
             pltpu.VMEM((3, size, cols), BF16),
             pltpu.VMEM((chunks * size, 128), F32),
-            field,
-            field,
+            pltpu.VMEM((chunks * size, 128), F32),
+            pltpu.VMEM((chunks * size, 128), F32),
             pltpu.VMEM((depth, 128), F32),
             pltpu.SemaphoreType.DMA((2,)),
         ],
@@ -500,12 +581,12 @@
     two, partial = pl.pallas_call(
         functools.partial(far_kernel, scale),
         out_shape=(pltpu.VMEM((2, depth, cols), F32), sums),
-        in_specs=[VMEM] * 9,
+        in_specs=[VMEM] * 10,
         out_specs=(VMEM,) * 2,
         scratch_shapes=[pltpu.SMEM((blocks, rows), jnp.int32), pltpu.SemaphoreType.DMA],
         compiler_params=GRANT,
         name="far",
-    )(own_far, far, *fixed, two, partial)
+    )(own_far, far, *fixed, surface, two, partial)
     pieces = lax.all_to_all(partial, ("blade", "span"), 0, 0, tiled=True)
     adjoint, owned = pl.pallas_call(
         finish_kernel,

time: 24.1 us -> 24.5 us (1.017)
  Pallas kernels: 5.98 us -> 6.53 us
    pallas_call x1, Pallas kernels: 0.77 us -> 1.08 us  [per_device(): pl.pallas_call(functools.partial(far_kernel, scale), out_shape=(pltpu.VME...]
    pallas_call x1, Pallas kernels: 1.79 us -> 2.05 us  [per_device(): pl.pallas_call(functools.partial(base_kernel, scale), out_shape=(pltpu.VM...]
  transfers between devices with their start and end apart: 2 -> 2, of which waited for: 0 -> 0; matrix products, arithmetic and copies ran while one was open for 0% -> 0% of each run, Pallas kernels for 14% -> 15%
where the time goes in v13:
time: 24.5 us; the launch traced here: 24.3 us
  blocking collectives  12 us (49%)
  Pallas kernels  6.53 us (27%)
  starting transfers between devices  5.03 us (21%)
  between operations  0.69 us (3%)
    all_to_all x1, blocking collectives, per_device(): pieces = lax.all_to_all(partial, ('blade', 'span'), 0, 0, tiled=True)  12 us
    ppermute x1, starting transfers between devices, per_device(): near = lax.ppermute(own_near, 'span', within + [(b, a) for a, b in within])  4.36 us
    pallas_call x1, Pallas kernels, per_device(): pl.pallas_call(functools.partial(base_kernel, scale), out_shape=(pltpu.VM...  2.05 us
    pallas_call x1, Pallas kernels, per_device(): pl.pallas_call(functools.partial(near_kernel, scale), out_shape=(pltpu.HB...  1.5 us
    pallas_call x1, Pallas kernels, per_device(): pl.pallas_call(functools.partial(load_kernel, rows), out_shape=(packed_fa...  1.22 us
    pallas_call x1, Pallas kernels, per_device(): pl.pallas_call(functools.partial(far_kernel, scale), out_shape=(pltpu.VME...  1.08 us
    pallas_call x1, Pallas kernels, per_device(): pl.pallas_call(finish_kernel, out_shape=(pltpu.HBM((depth, rows, cols), F...  0.68 us
    ppermute x1, starting transfers between devices, per_device(): far = lax.ppermute(own_far, 'span', across + [(b, a) for a, b in across])  0.67 us
  transfers between devices with their start and end apart: 2, of which 0 were waited for; matrix products, arithmetic and copies ran while one was open for 0% of the time, Pallas kernels for 15%

profile of v13, /device:TPU:0, one launch (start us, length us, event | category | flops | bytes accessed | tf_op | source)
XLA Modules:
  0.0 24.3 jit_solution(134228134900829376)
XLA Ops:
  0.6 1.2 %load.1 = (f32[272,128]{1,0:T(8,128)S(1)}, f32[268,128]{1,0:T(8,128)S(1)}, f32[1024,128]{1,0:T(8,128)S(1)}, f32[3,8,512]{2,1,0:T(8,128)S(1)}, f32[32,32]{1,0:T(8,128)S(1)}) custom-call(s32[3]{0:T(128)} %frame_hbm.1, f32[256,512]{1,0:T(8,128)} %bitcast.6, f32[4,8,512]{2,1,0:T(8,128)} %bitcast.8, f32[32,32]{1,0:T(8,128)} %bitcast.10), custom_call_target="tpu_custom_call" | custom-call | tf_op jit(solution)/shard_map/load/pallas_call | solution.py:509
  1.9 0.7 %collective-permute-start.1 = (f32[272,128]{1,0:T(8,128)S(1)}, f32[272,128]{1,0:T(8,128)S(1)}, u32[]{:S(2)}, u32[]{:S(2)}) collective-permute-start(f32[272,128]{1,0:T(8,128)S(1)} %get-tuple-element.34.own_ref), channel_id=1, source_target_pairs={{1,2},{2,1},{5,6},{6,5},{9,10},{10,9},{13,14},{14,13},{17,18},{18,... | collective-permute-start | bytes 417800 | tf_op jit(solution)/shard_map/ppermute | solution.py:536
  2.5 4.4 %collective-permute-start = (f32[268,128]{1,0:T(8,128)S(1)}, f32[268,128]{1,0:T(8,128)S(1)}, u32[]{:S(2)}, u32[]{:S(2)}) collective-permute-start(f32[268,128]{1,0:T(8,128)S(1)} %get-tuple-element.32.own_ref), channel_id=1, source_target_pairs={{0,1},{2,3},{1,0},{3,2},{4,5},{6,7},{5,4},{7,6},{8,9},{10,11},{9,8... | collective-permute-start | bytes 411656 | tf_op jit(solution)/shard_map/ppermute | solution.py:535
  6.9 2.0 %base.1 = (f32[1024,128]{1,0:T(8,128)S(1)}, f32[2,32,512]{2,1,0:T(8,128)S(1)}, f32[3,8,512]{2,1,0:T(8,128)S(1)}, s32[4,8]{1,0:T(4,128)S(1)}, f32[2,32,512]{2,1,0...) custom-call(f32[1024,128]{1,0:T(8,128)S(1)} %get-tuple-element.23.k_, ...), custom_call_target="tpu_custom_call" | custom-call | tf_op jit(solution)/shard_map/base/pallas_call | solution.py:539
  8.9 0.0 collective-permute-done.got_ref
  9.0 1.5 %near.1 = (f32[32,8,512]{2,1,0:T(8,128)}, f32[32,1,64]{2,1,0:T(1,128)S(1)}) custom-call(f32[32,32]{1,0:T(8,128)S(1)} %get-tuple-element.22.d_ref, f32[3,8,512]{2,1,0:T(8,128)S(1)} %get-tuple-element.25.excess_ref, f32[2,32,512]{2,1,0:T(8,128)S(1)} %get-tuple-element.26.edge_ref, bf16[64,192]{1,0:T(8,128)(2,1)S(1)} %get-tuple-element.27.pair_ref, ...), custom_call_target="tpu_custom_call" | custom-call | tf_op jit(solution)/shard_map/near/pallas_call | solution.py:568
  10.5 0.0 collective-permute-done.1.got_ref
  10.5 1.1 %far.1 = (f32[2,32,512]{2,1,0:T(8,128)S(1)}, f32[32,1,64]{2,1,0:T(1,128)S(1)}) custom-call(f32[272,128]{1,0:T(8,128)S(1)} %get-tuple-element.34.own_ref, f32[272,128]{1,0:T(8,128)S(1)} %collective-permute-done.1.got_ref, f32[32,32]{1,0:T(8,128)S(1)} %get-tuple-element.22.d_ref, f32[3,8,512]{2,1,0:T(8,128)S(1)} %get-tuple-element.25.excess_ref, ...), custom_call_target="tpu_custom_call" | custom-call | tf_op jit(solution)/shard_map/far/pallas_call | solution.py:581
  11.6 12.0 %all_to_all.5.got_ref = f32[32,1,64]{2,1,0:T(1,128)S(1)} all-to-all(f32[32,1,64]{2,1,0:T(1,128)S(1)} %get-tuple-element.39), channel_id=1, replica_groups=mesh['blade'=8,'span'=4] {'blade','span'}, dimensions={0} | all-to-all | bytes 16384 | tf_op jit(solution)/shard_map/all_to_all | solution.py:590
  23.6 0.7 %finish.1 = (f32[32,8,512]{2,1,0:T(8,128)}, f32[64]{0:T(128)}) custom-call(f32[32,8,512]{2,1,0:T(8,128)} %get-tuple-element.33._, f32[2,32,512]{2,1,0:T(8,128)S(1)} %get-tuple-element.38.two_ref, f32[32,1,64]{2,1,0:T(1,128)S(1)} %all_to_all.5.got_ref), custom_call_target="tpu_custom_call", output_to_operand_aliasing={{0}: (0, {})} | custom-call | tf_op jit(solution)/shard_map/finish/pallas_call | solution.py:591
Async XLA Ops:
  1.9 8.6 %collective-permute-start.1 = (f32[272,128]{1,0:T(8,128)S(1)}, f32[272,128]{1,0:T(8,128)S(1)}, u32[]{:S(2)}, u32[]{:S(2)}) collective-permute-start(f32[272,128]{1,0:T(8,128)S(1)} %get-tuple-element.34.own_ref), channel_id=1, source_target_pairs={{1,2},{2,1},{5,6},{6,5},{9,10},{10,9},{13,14},{14,13},{17,18},{18,... | collective-permute-start | bytes 417800 | tf_op jit(solution)/shard_map/ppermute | solution.py:536
  2.5 6.4 %collective-permute-start = (f32[268,128]{1,0:T(8,128)S(1)}, f32[268,128]{1,0:T(8,128)S(1)}, u32[]{:S(2)}, u32[]{:S(2)}) collective-permute-start(f32[268,128]{1,0:T(8,128)S(1)} %get-tuple-element.32.own_ref), channel_id=1, source_target_pairs={{0,1},{2,3},{1,0},{3,2},{4,5},{6,7},{5,4},{7,6},{8,9},{10,11},{9,8... | collective-permute-start | bytes 411656 | tf_op jit(solution)/shard_map/ppermute | solution.py:535

commit v14 on v11

--- a/solution.py
+++ b/solution.py
@@ -122,6 +122,12 @@
     picks = []
     for after, _ in sides():
         picks.append((jnp.where(after, rows - 1, 0), jnp.where(after, rows - 2, 1)))
+    for c in range(chunks):
+        copies[2 + c].wait()
+        for ref, row_pair in zip(sent, picks):
+            for n, row in enumerate(row_pair):
+                spot = (n * chunks + c) * depth
+                ref[spot : spot + depth, :] = row_of_each(k_ref, c, depth, rows, row)
     copies[0].wait()
     copies[1].wait()
     for step in range(STEPS):
@@ -135,12 +141,6 @@
                 ref[spot : spot + 1, :] = line[:, c * 128 : (c + 1) * 128]
         if ref.shape[0] > base + 3 * chunks:
             ref[base + 3 * chunks :, :] = jnp.zeros((ref.shape[0] - base - 3 * chunks, 128), F32)
-    for c in range(chunks):
-        copies[2 + c].wait()
-        for ref, row_pair in zip(sent, picks):
-            for n, row in enumerate(row_pair):
-                spot = (n * chunks + c) * depth
-                ref[spot : spot + depth, :] = row_of_each(k_ref, c, depth, rows, row)
     for copy in copies[2 + chunks :]:
         copy.wait()
 
@@ -150,8 +150,11 @@
     k_ref,
     frames_ref,
     d_ref,
+    own_near_ref,
+    own_far_ref,
     excess_hbm,
     map_hbm,
+    own_ref,
     adj_ref,
     two_ref,
     excess_ref,
@@ -204,6 +207,15 @@
     pair_ref[...] = left_three(pairs)
     place_ref[...] = left_three(places)
 
+    for n, ref in enumerate((own_near_ref, own_far_ref)):
+        half = 0.5 * packed_field(ref, depth, cols, 0)
+        inner = half + 0.5 * packed_field(ref, depth, cols, 1)
+        w_next = half + shift_next(half, 1)
+        w_prev = half + shift_prev(half, 1, 0.0)
+        for which, x in enumerate((half, inner, w_next, w_prev)):
+            own_ref[n, which] = x
+        own_ref[n, 4] = 1.0 - (w_next + w_prev) - (half + inner)
+
     f = frames_ref[2]
     f_chord = shift_next(f, 1) - f
     f_span = shift_next(f, 0) - f
@@ -270,24 +282,21 @@
     )
 
 
-def correction(n, got, own, d_ref, edge_ref, pair_ref):
+def correction(n, got, sent, d_ref, own_ref, edge_ref, pair_ref):
     _, depth, cols = edge_ref.shape
     _, inside = sides()[n]
     factor = d_ref[:, 0:1]
     half = 0.5 * packed_field(got, depth, cols, 0)
     half_next = 0.5 * packed_field(got, depth, cols, 1)
-    half_own = 0.5 * packed_field(own, depth, cols, 0)
-    inner = half_own + 0.5 * packed_field(own, depth, cols, 1)
     f = packed_line(got, depth, cols, 0)
     frame = packed_line(got, depth, cols, 1)
     f_next = packed_line(got, depth, cols, 2)
-    f_own = packed_line(own, depth, cols, 0)
-    face = half + half_own
-    flux = (half + shift_next(half, 1)) * (shift_next(f, 1) - f)
+    f_own = packed_line(sent, depth, cols, 0)
+    face = half + own_ref[n, 0]
     moved = (
         f
-        + flux
-        - shift_prev(flux, 1, half * f)
+        + (half + shift_next(half, 1)) * (shift_next(f, 1) - f)
+        + (half + shift_prev(half, 1, 0.0)) * (shift_prev(f, 1, 0.0) - f)
         + (half + half_next) * (f_next - f)
         + face * (f_own - f)
     )
@@ -296,15 +305,14 @@
     found = dot(pair_ref[...], right_three(jnp.concatenate(sources, axis=0)))
     e = found[0:depth]
     outer = found[depth:]
-    w_chord = half_own + shift_next(half_own, 1)
     change = (
-        e
-        + divergence(e, w_chord, half_own, 1)
-        - (half + half_own + inner) * e
+        own_ref[n, 4] * e
+        + own_ref[n, 2] * shift_next(e, 1)
+        + own_ref[n, 3] * shift_prev(e, 1, 0.0)
         + face * outer
-        - half * edge_ref[n]
-    )
-    return right_three(jnp.concatenate([change, inner * e], axis=0)), e[0:1, :]
+        - half * (e + edge_ref[n])
+    )
+    return right_three(jnp.concatenate([change, own_ref[n, 1] * e], axis=0)), e[0:1, :]
 
 
 def add_segments(total, contribution, picked_rows, map_ref):
@@ -324,6 +332,7 @@
 def near_kernel(
     scale,
     d_ref,
+    own_ref,
     excess_ref,
     edge_ref,
     pair_ref,
@@ -331,7 +340,7 @@
     place_ref,
     base_ref,
     contribution_ref,
-    own_ref,
+    sent_ref,
     got_ref,
     adj_hbm,
     part_ref,
@@ -343,7 +352,7 @@
     map_copy.start()
     depth, rows, cols = adj_ref.shape
     size = depth * rows
-    sources, surface = correction(0, got_ref, own_ref, d_ref, edge_ref, pair_ref)
+    sources, surface = correction(0, got_ref, sent_ref, d_ref, own_ref, edge_ref, pair_ref)
     found = dot(place_ref[...], sources)
     adj_ref[...] = (chunked(base_ref, 0, size, size) + found).reshape(depth, rows, cols)
     adj_copy = pltpu.make_async_copy(adj_ref, adj_hbm, sems.at[1])
@@ -362,9 +371,10 @@
 
 def far_kernel(
     scale,
-    own_ref,
+    sent_ref,
     got_ref,
     d_ref,
+    own_ref,
     excess_ref,
     edge_ref,
     pair_ref,
@@ -380,7 +390,7 @@
     map_copy.start()
     depth = two_ref.shape[1]
     rows = excess_ref.shape[1]
-    sources, surface = correction(1, got_ref, own_ref, d_ref, edge_ref, pair_ref)
+    sources, surface = correction(1, got_ref, sent_ref, d_ref, own_ref, edge_ref, pair_ref)
     found = dot(pair_ref[...], sources)
     edge, second = far_rows(rows)
     contribution = scale * jnp.concatenate(
@@ -456,9 +466,10 @@
     far = lax.ppermute(own_far, "span", across + [(b, a) for a, b in across])
     scale = 1.0 / math.sqrt(128.0 * STEPS)
     line = pltpu.VMEM((rows, cols), F32)
-    base, two, excess, ids, edge, contribution, pair, place = pl.pallas_call(
+    own, base, two, excess, ids, edge, contribution, pair, place = pl.pallas_call(
         functools.partial(base_kernel, scale),
         out_shape=(
+            pltpu.VMEM((2, 5, depth, cols), F32),
             pltpu.VMEM((chunks * size, 128), F32),
             pltpu.VMEM((2, depth, cols), F32),
             pltpu.VMEM((STEPS, rows, cols), F32),
@@ -468,8 +479,8 @@
             pltpu.VMEM((2 * depth, 6 * depth), BF16),
             pltpu.VMEM((size, 6 * depth), BF16),
         ),
-        in_specs=[VMEM] * 3 + [HBM] * 2,
-        out_specs=(VMEM,) * 8,
+        in_specs=[VMEM] * 5 + [HBM] * 2,
+        out_specs=(VMEM,) * 9,
         scratch_shapes=[
             pltpu.VMEM((size, 3 * size), BF16),
             pltpu.VMEM((3, size, cols), BF16),
@@ -481,13 +492,13 @@
         ],
         compiler_params=GRANT,
         name="base",
-    )(k, picked, inverse, in_hbm(surface_excess[0]), in_hbm(segment_map.T))
-    fixed = (inverse, excess, edge, pair, ids)
+    )(k, picked, inverse, own_near, own_far, in_hbm(surface_excess[0]), in_hbm(segment_map.T))
+    fixed = (inverse, own, excess, edge, pair, ids)
     sums = pltpu.VMEM((devices, 1, lanes), F32)
     adjoint, partial = pl.pallas_call(
         functools.partial(near_kernel, scale),
         out_shape=(pltpu.HBM((depth, rows, cols), F32), sums),
-        in_specs=[VMEM] * 10,
+        in_specs=[VMEM] * 11,
         out_specs=(HBM, VMEM),
         scratch_shapes=[
             field,
@@ -500,7 +511,7 @@
     two, partial = pl.pallas_call(
         functools.partial(far_kernel, scale),
         out_shape=(pltpu.VMEM((2, depth, cols), F32), sums),
-        in_specs=[VMEM] * 9,
+        in_specs=[VMEM] * 10,
         out_specs=(VMEM,) * 2,
         scratch_shapes=[pltpu.SMEM((blocks, rows), jnp.int32), pltpu.SemaphoreType.DMA],
         compiler_params=GRANT,

time: 24.1 us -> 24.2 us (level)
  Pallas kernels: 5.98 us -> 6.39 us
  blocking collectives: 12.2 us -> 11.9 us
    pallas_call x1, Pallas kernels: 1.79 us -> 2.34 us  [per_device(): pl.pallas_call(functools.partial(base_kernel, scale), out_shape=(pltpu.VM...]
    all_to_all x1, blocking collectives: 12.2 us -> 11.9 us  [per_device(): pieces = lax.all_to_all(partial, ('blade', 'span'), 0, 0, tiled=True)]
  transfers between devices with their start and end apart: 2 -> 2, of which waited for: 0 -> 0; matrix products, arithmetic and copies ran while one was open for 0% -> 0% of each run, Pallas kernels for 14% -> 16%
where the time goes in v14:
time: 24.2 us; the launch traced here: 24 us
  blocking collectives  11.9 us (49%)
  Pallas kernels  6.39 us (26%)
  starting transfers between devices  5.03 us (21%)
  between operations  0.69 us (3%)
    all_to_all x1, blocking collectives, per_device(): pieces = lax.all_to_all(partial, ('blade', 'span'), 0, 0, tiled=True)  11.9 us
    ppermute x1, starting transfers between devices, per_device(): near = lax.ppermute(own_near, 'span', within + [(b, a) for a, b in within])  4.36 us
    pallas_call x1, Pallas kernels, per_device(): pl.pallas_call(functools.partial(base_kernel, scale), out_shape=(pltpu.VM...  2.34 us
    pallas_call x1, Pallas kernels, per_device(): pl.pallas_call(functools.partial(near_kernel, scale), out_shape=(pltpu.HB...  1.42 us
    pallas_call x1, Pallas kernels, per_device(): pl.pallas_call(functools.partial(load_kernel, rows), out_shape=(packed_fa...  1.25 us
    pallas_call x1, Pallas kernels, per_device(): pl.pallas_call(functools.partial(far_kernel, scale), out_shape=(pltpu.VME...  0.7 us
    pallas_call x1, Pallas kernels, per_device(): pl.pallas_call(finish_kernel, out_shape=(pltpu.HBM((depth, rows, cols), F...  0.68 us
    ppermute x1, starting transfers between devices, per_device(): far = lax.ppermute(own_far, 'span', across + [(b, a) for a, b in across])  0.67 us
  transfers between devices with their start and end apart: 2, of which 0 were waited for; matrix products, arithmetic and copies ran while one was open for 0% of the time, Pallas kernels for 16%

profile of v14, /device:TPU:0, one launch (start us, length us, event | category | flops | bytes accessed | tf_op | source)
XLA Modules:
  0.0 24.0 jit_solution(1821207694534361287)
XLA Ops:
  0.6 1.3 %load.1 = (f32[272,128]{1,0:T(8,128)S(1)}, f32[268,128]{1,0:T(8,128)S(1)}, f32[1024,128]{1,0:T(8,128)S(1)}, f32[3,8,512]{2,1,0:T(8,128)S(1)}, f32[32,32]{1,0:T(8,128)S(1)}) custom-call(s32[3]{0:T(128)} %frame_hbm.1, f32[256,512]{1,0:T(8,128)} %bitcast.6, f32[4,8,512]{2,1,0:T(8,128)} %bitcast.8, f32[32,32]{1,0:T(8,128)} %bitcast.10), custom_call_target="tpu_custom_call" | custom-call | tf_op jit(solution)/shard_map/load/pallas_call | solution.py:439
  1.9 0.7 %collective-permute-start.1 = (f32[272,128]{1,0:T(8,128)S(1)}, f32[272,128]{1,0:T(8,128)S(1)}, u32[]{:S(2)}, u32[]{:S(2)}) collective-permute-start(f32[272,128]{1,0:T(8,128)S(1)} %get-tuple-element.26.own_far_ref.sent_ref), channel_id=1, source_target_pairs={{1,2},{2,1},{5,6},{6,5},{9,10},{10,9},{13,14},{14,13},{17,18},{18,... | collective-permute-start | bytes 417800 | tf_op jit(solution)/shard_map/ppermute | solution.py:466
  2.6 4.4 %collective-permute-start = (f32[268,128]{1,0:T(8,128)S(1)}, f32[268,128]{1,0:T(8,128)S(1)}, u32[]{:S(2)}, u32[]{:S(2)}) collective-permute-start(f32[268,128]{1,0:T(8,128)S(1)} %get-tuple-element.25.own_near_ref.sent_ref), channel_id=1, source_target_pairs={{0,1},{2,3},{1,0},{3,2},{4,5},{6,7},{5,4},{7,6},{8,9},{10,11},{9,8... | collective-permute-start | bytes 411656 | tf_op jit(solution)/shard_map/ppermute | solution.py:465
  6.9 2.3 %base.1 = (f32[2,5,32,512]{3,2,1,0:T(8,128)S(1)}, f32[1024,128]{1,0:T(8,128)S(1)}, f32[2,32,512]{2,1,0:T(8,128)S(1)}, f32[3,8,512]{2,1,0:T(8,128)S(1)}, s32[4,8]...) custom-call(f32[1024,128]{1,0:T(8,128)S(1)} %get-tuple-element.23.k_, ...), custom_call_target="tpu_custom_call" | custom-call | tf_op jit(solution)/shard_map/base/pallas_call | solution.py:469
  9.3 0.0 collective-permute-done.got_ref
  9.3 1.4 %near.1 = (f32[32,8,512]{2,1,0:T(8,128)}, f32[32,1,64]{2,1,0:T(1,128)S(1)}) custom-call(f32[32,32]{1,0:T(8,128)S(1)} %get-tuple-element.22.d_ref, f32[2,5,32,512]{3,2,1,0:T(8,128)S(1)} %get-tuple-element.27.own_ref, f32[3,8,512]{2,1,0:T(8,128)S(1)} %get-tuple-element.28.excess_ref, f32[2,32,512]{2,1,0:T(8,128)S(1)} %get-tuple-element.29.edge_ref, ...), custom_call_target="tpu_custom_call" | custom-call | tf_op jit(solution)/shard_map/near/pallas_call | solution.py:498
  10.7 0.0 collective-permute-done.1.got_ref
  10.7 0.7 %far.1 = (f32[2,32,512]{2,1,0:T(8,128)S(1)}, f32[32,1,64]{2,1,0:T(1,128)S(1)}) custom-call(f32[272,128]{1,0:T(8,128)S(1)} %get-tuple-element.26.own_far_ref.sent_ref, f32[272,128]{1,0:T(8,128)S(1)} %collective-permute-done.1.got_ref, f32[32,32]{1,0:T(8,128)S(1)} %get-tuple-element.22.d_ref, f32[2,5,32,512]{3,2,1,0:T(8,128)S(1)} %get-tuple-element.27.own_ref, ...), custom_call_target="tpu_custom_call" | custom-call | tf_op jit(solution)/shard_map/far/pallas_call | solution.py:511
  11.4 11.9 %all_to_all.5.got_ref = f32[32,1,64]{2,1,0:T(1,128)S(1)} all-to-all(f32[32,1,64]{2,1,0:T(1,128)S(1)} %get-tuple-element.39), channel_id=1, replica_groups=mesh['blade'=8,'span'=4] {'blade','span'}, dimensions={0} | all-to-all | bytes 16384 | tf_op jit(solution)/shard_map/all_to_all | solution.py:520
  23.3 0.7 %finish.1 = (f32[32,8,512]{2,1,0:T(8,128)}, f32[64]{0:T(128)}) custom-call(f32[32,8,512]{2,1,0:T(8,128)} %get-tuple-element.35._, f32[2,32,512]{2,1,0:T(8,128)S(1)} %get-tuple-element.38.two_ref, f32[32,1,64]{2,1,0:T(1,128)S(1)} %all_to_all.5.got_ref), custom_call_target="tpu_custom_call", output_to_operand_aliasing={{0}: (0, {})} | custom-call | tf_op jit(solution)/shard_map/finish/pallas_call | solution.py:521
Async XLA Ops:
  1.9 8.8 %collective-permute-start.1 = (f32[272,128]{1,0:T(8,128)S(1)}, f32[272,128]{1,0:T(8,128)S(1)}, u32[]{:S(2)}, u32[]{:S(2)}) collective-permute-start(f32[272,128]{1,0:T(8,128)S(1)} %get-tuple-element.26.own_far_ref.sent_ref), channel_id=1, source_target_pairs={{1,2},{2,1},{5,6},{6,5},{9,10},{10,9},{13,14},{14,13},{17,18},{18,... | collective-permute-start | bytes 417800 | tf_op jit(solution)/shard_map/ppermute | solution.py:466
  2.6 6.7 %collective-permute-start = (f32[268,128]{1,0:T(8,128)S(1)}, f32[268,128]{1,0:T(8,128)S(1)}, u32[]{:S(2)}, u32[]{:S(2)}) collective-permute-start(f32[268,128]{1,0:T(8,128)S(1)} %get-tuple-element.25.own_near_ref.sent_ref), channel_id=1, source_target_pairs={{0,1},{2,3},{1,0},{3,2},{4,5},{6,7},{5,4},{7,6},{8,9},{10,11},{9,8... | collective-permute-start | bytes 411656 | tf_op jit(solution)/shard_map/ppermute | solution.py:465

commit v15 on v11

--- a/solution.py
+++ b/solution.py
@@ -210,15 +210,24 @@
 
     def put(i, both):
         high, low = split(both)
-        span = pl.ds(i * rows, 2 * rows)
+        span = pl.ds(pl.multiple_of(i * rows, 2 * rows), 2 * rows)
         right_ref[0, span, :] = high
         right_ref[1, span, :] = high
         right_ref[2, span, :] = low
 
-    for i in range(0, depth, 2):
+    def at(ref, j):
+        return jnp.concatenate(
+            [
+                ref[pl.ds(pl.multiple_of(c * size + j * rows, rows), rows), :]
+                for c in range(cols // 128)
+            ],
+            axis=1,
+        )
+
+    def first_sweep(n, _):
         found = []
-        for j in (i, i + 1):
-            half = 0.5 * chunked(k_ref, j * rows, rows, size)
+        for j in (2 * n, 2 * n + 1):
+            half = 0.5 * at(k_ref, j)
             w_chord = half + shift_next(half, 1)
             w_span = half + shift_next(half, 0)
             chord_ref[j] = w_chord
@@ -229,26 +238,32 @@
             moved = f + flux_chord - shift_prev(flux_chord, 1, edge)
             moved = moved + flux_span - shift_prev(flux_span, 0, edge)
             factor = jnp.concatenate(
-                [jnp.broadcast_to(factor_ref[j : j + 1, :], (rows, 128))] * (cols // 128), axis=1
+                [jnp.broadcast_to(factor_ref[pl.ds(j, 1), :], (rows, 128))] * (cols // 128),
+                axis=1,
             )
-            source = factor * moved
-            found.append(source + frames_ref[1] if j == 0 else source)
-        put(i, jnp.concatenate(found, axis=0))
+            found.append(factor * moved + jnp.where(j == 0, frames_ref[1], 0.0))
+        put(2 * n, jnp.concatenate(found, axis=0))
+        return 0
+
+    lax.fori_loop(0, depth // 2, first_sweep, 0, unroll=2)
     right = right_ref[...].reshape(3 * size, cols)
     first = dot(mat_ref[...], right)
     for c in range(cols // 128):
         first_ref[c * size : (c + 1) * size, :] = first[:, c * 128 : (c + 1) * 128]
 
-    for i in range(0, depth, 2):
+    def second_sweep(n, _):
         found = []
-        for j in (i, i + 1):
-            v = chunked(first_ref, j * rows, rows, size)
-            half = 0.5 * chunked(k_ref, j * rows, rows, size)
+        for j in (2 * n, 2 * n + 1):
+            v = at(first_ref, j)
+            half = 0.5 * at(k_ref, j)
             source = (
                 v + divergence(v, chord_ref[j], half, 1) + divergence(v, span_ref[j], half, 0)
             )
-            found.append(source + frames_ref[0] if j == 0 else source)
-        put(i, jnp.concatenate(found, axis=0))
+            found.append(source + jnp.where(j == 0, frames_ref[0], 0.0))
+        put(2 * n, jnp.concatenate(found, axis=0))
+        return 0
+
+    lax.fori_loop(0, depth // 2, second_sweep, 0, unroll=2)
     right = right_ref[...].reshape(3 * size, cols)
     adj = dot(mat_ref[...], right)
     for c in range(cols // 128):
@@ -276,18 +291,19 @@
     factor = d_ref[:, 0:1]
     half = 0.5 * packed_field(got, depth, cols, 0)
     half_next = 0.5 * packed_field(got, depth, cols, 1)
-    half_own = 0.5 * packed_field(own, depth, cols, 0)
-    inner = half_own + 0.5 * packed_field(own, depth, cols, 1)
     f = packed_line(got, depth, cols, 0)
     frame = packed_line(got, depth, cols, 1)
     f_next = packed_line(got, depth, cols, 2)
     f_own = packed_line(own, depth, cols, 0)
+    half_own = 0.5 * packed_field(own, depth, cols, 0)
+    inner = half_own + 0.5 * packed_field(own, depth, cols, 1)
+    w_next = half_own + shift_next(half_own, 1)
+    w_prev = half_own + shift_prev(half_own, 1, 0.0)
     face = half + half_own
-    flux = (half + shift_next(half, 1)) * (shift_next(f, 1) - f)
     moved = (
         f
-        + flux
-        - shift_prev(flux, 1, half * f)
+        + (half + shift_next(half, 1)) * (shift_next(f, 1) - f)
+        + (half + shift_prev(half, 1, 0.0)) * (shift_prev(f, 1, 0.0) - f)
         + (half + half_next) * (f_next - f)
         + face * (f_own - f)
     )
@@ -296,13 +312,12 @@
     found = dot(pair_ref[...], right_three(jnp.concatenate(sources, axis=0)))
     e = found[0:depth]
     outer = found[depth:]
-    w_chord = half_own + shift_next(half_own, 1)
     change = (
-        e
-        + divergence(e, w_chord, half_own, 1)
-        - (half + half_own + inner) * e
+        (1.0 - (w_next + w_prev) - (half_own + inner)) * e
+        + w_next * shift_next(e, 1)
+        + w_prev * shift_prev(e, 1, 0.0)
         + face * outer
-        - half * edge_ref[n]
+        - half * (e + edge_ref[n])
     )
     return right_three(jnp.concatenate([change, inner * e], axis=0)), e[0:1, :]
 

time: 24.1 us -> 26.1 us (1.083)
  Pallas kernels: 5.98 us -> 8.28 us
  blocking collectives: 12.2 us -> 11.9 us
    pallas_call x1, Pallas kernels: 1.79 us -> 4.25 us  [per_device(): pl.pallas_call(functools.partial(base_kernel, scale), out_shape=(pltpu.VM...]
    all_to_all x1, blocking collectives: 12.2 us -> 11.9 us  [per_device(): pieces = lax.all_to_all(partial, ('blade', 'span'), 0, 0, tiled=True)]
  transfers between devices with their start and end apart: 2 -> 2, of which waited for: 0 -> 0; matrix products, arithmetic and copies ran while one was open for 0% -> 0% of each run, Pallas kernels for 14% -> 22%
where the time goes in v15:
time: 26.1 us; the launch traced here: 25.9 us
  blocking collectives  11.9 us (46%)
  Pallas kernels  8.28 us (32%)
  starting transfers between devices  5.03 us (19%)
  between operations  0.69 us (3%)
    all_to_all x1, blocking collectives, per_device(): pieces = lax.all_to_all(partial, ('blade', 'span'), 0, 0, tiled=True)  11.9 us
    ppermute x1, starting transfers between devices, per_device(): near = lax.ppermute(own_near, 'span', within + [(b, a) for a, b in within])  4.36 us
    pallas_call x1, Pallas kernels, per_device(): pl.pallas_call(functools.partial(base_kernel, scale), out_shape=(pltpu.VM...  4.25 us
    pallas_call x1, Pallas kernels, per_device(): pl.pallas_call(functools.partial(near_kernel, scale), out_shape=(pltpu.HB...  1.42 us
    pallas_call x1, Pallas kernels, per_device(): pl.pallas_call(functools.partial(load_kernel, rows), out_shape=(packed_fa...  1.22 us
    pallas_call x1, Pallas kernels, per_device(): pl.pallas_call(functools.partial(far_kernel, scale), out_shape=(pltpu.VME...  0.7 us
    pallas_call x1, Pallas kernels, per_device(): pl.pallas_call(finish_kernel, out_shape=(pltpu.HBM((depth, rows, cols), F...  0.68 us
    ppermute x1, starting transfers between devices, per_device(): far = lax.ppermute(own_far, 'span', across + [(b, a) for a, b in across])  0.67 us
  transfers between devices with their start and end apart: 2, of which 0 were waited for; matrix products, arithmetic and copies ran while one was open for 0% of the time, Pallas kernels for 22%

profile of v15, /device:TPU:0, one launch (start us, length us, event | category | flops | bytes accessed | tf_op | source)
XLA Modules:
  0.0 25.9 jit_solution(5382683251547253482)
XLA Ops:
  0.6 1.2 %load.1 = (f32[272,128]{1,0:T(8,128)S(1)}, f32[268,128]{1,0:T(8,128)S(1)}, f32[1024,128]{1,0:T(8,128)S(1)}, f32[3,8,512]{2,1,0:T(8,128)S(1)}, f32[32,32]{1,0:T(8,128)S(1)}) custom-call(s32[3]{0:T(128)} %frame_hbm.1, f32[256,512]{1,0:T(8,128)} %bitcast.6, f32[4,8,512]{2,1,0:T(8,128)} %bitcast.8, f32[32,32]{1,0:T(8,128)} %bitcast.10), custom_call_target="tpu_custom_call" | custom-call | tf_op jit(solution)/shard_map/load/pallas_call | solution.py:444
  1.9 0.7 %collective-permute-start.1 = (f32[272,128]{1,0:T(8,128)S(1)}, f32[272,128]{1,0:T(8,128)S(1)}, u32[]{:S(2)}, u32[]{:S(2)}) collective-permute-start(f32[272,128]{1,0:T(8,128)S(1)} %get-tuple-element.33.own_ref), channel_id=1, source_target_pairs={{1,2},{2,1},{5,6},{6,5},{9,10},{10,9},{13,14},{14,13},{17,18},{18,... | collective-permute-start | bytes 417800 | tf_op jit(solution)/shard_map/ppermute | solution.py:471
  2.5 4.4 %collective-permute-start = (f32[268,128]{1,0:T(8,128)S(1)}, f32[268,128]{1,0:T(8,128)S(1)}, u32[]{:S(2)}, u32[]{:S(2)}) collective-permute-start(f32[268,128]{1,0:T(8,128)S(1)} %get-tuple-element.31.own_ref), channel_id=1, source_target_pairs={{0,1},{2,3},{1,0},{3,2},{4,5},{6,7},{5,4},{7,6},{8,9},{10,11},{9,8... | collective-permute-start | bytes 411656 | tf_op jit(solution)/shard_map/ppermute | solution.py:470
  6.9 4.3 %base.1 = (f32[1024,128]{1,0:T(8,128)S(1)}, f32[2,32,512]{2,1,0:T(8,128)S(1)}, f32[3,8,512]{2,1,0:T(8,128)S(1)}, s32[4,8]{1,0:T(4,128)S(1)}, f32[2,32,512]{2,1,0...) custom-call(f32[1024,128]{1,0:T(8,128)S(1)} %get-tuple-element.22.k_ref, ...), custom_call_target="tpu_custom_call" | custom-call | tf_op jit(solution)/shard_map/base/pallas_call | solution.py:474
  11.2 0.0 collective-permute-done.got_ref
  11.2 1.4 %near.1 = (f32[32,8,512]{2,1,0:T(8,128)}, f32[32,1,64]{2,1,0:T(1,128)S(1)}) custom-call(f32[32,32]{1,0:T(8,128)S(1)} %get-tuple-element.21.d_ref, f32[3,8,512]{2,1,0:T(8,128)S(1)} %get-tuple-element.24.excess_ref, f32[2,32,512]{2,1,0:T(8,128)S(1)} %get-tuple-element.25.edge_ref, bf16[64,192]{1,0:T(8,128)(2,1)S(1)} %get-tuple-element.26.pair_ref, ...), custom_call_target="tpu_custom_call" | custom-call | tf_op jit(solution)/shard_map/near/pallas_call | solution.py:502
  12.6 0.0 collective-permute-done.1.got_ref
  12.6 0.7 %far.1 = (f32[2,32,512]{2,1,0:T(8,128)S(1)}, f32[32,1,64]{2,1,0:T(1,128)S(1)}) custom-call(f32[272,128]{1,0:T(8,128)S(1)} %get-tuple-element.33.own_ref, f32[272,128]{1,0:T(8,128)S(1)} %collective-permute-done.1.got_ref, f32[32,32]{1,0:T(8,128)S(1)} %get-tuple-element.21.d_ref, f32[3,8,512]{2,1,0:T(8,128)S(1)} %get-tuple-element.24.excess_ref, ...), custom_call_target="tpu_custom_call" | custom-call | tf_op jit(solution)/shard_map/far/pallas_call | solution.py:515
  13.3 11.9 %all_to_all.5.got_ref = f32[32,1,64]{2,1,0:T(1,128)S(1)} all-to-all(f32[32,1,64]{2,1,0:T(1,128)S(1)} %get-tuple-element.37), channel_id=1, replica_groups=mesh['blade'=8,'span'=4] {'blade','span'}, dimensions={0} | all-to-all | bytes 16384 | tf_op jit(solution)/shard_map/all_to_all | solution.py:524
  25.2 0.7 %finish.1 = (f32[32,8,512]{2,1,0:T(8,128)}, f32[64]{0:T(128)}) custom-call(f32[32,8,512]{2,1,0:T(8,128)} %get-tuple-element.32._, f32[2,32,512]{2,1,0:T(8,128)S(1)} %get-tuple-element.36.two_ref, f32[32,1,64]{2,1,0:T(1,128)S(1)} %all_to_all.5.got_ref), custom_call_target="tpu_custom_call", output_to_operand_aliasing={{0}: (0, {})} | custom-call | tf_op jit(solution)/shard_map/finish/pallas_call | solution.py:525
Async XLA Ops:
  1.9 10.7 %collective-permute-start.1 = (f32[272,128]{1,0:T(8,128)S(1)}, f32[272,128]{1,0:T(8,128)S(1)}, u32[]{:S(2)}, u32[]{:S(2)}) collective-permute-start(f32[272,128]{1,0:T(8,128)S(1)} %get-tuple-element.33.own_ref), channel_id=1, source_target_pairs={{1,2},{2,1},{5,6},{6,5},{9,10},{10,9},{13,14},{14,13},{17,18},{18,... | collective-permute-start | bytes 417800 | tf_op jit(solution)/shard_map/ppermute | solution.py:471
  2.5 8.6 %collective-permute-start = (f32[268,128]{1,0:T(8,128)S(1)}, f32[268,128]{1,0:T(8,128)S(1)}, u32[]{:S(2)}, u32[]{:S(2)}) collective-permute-start(f32[268,128]{1,0:T(8,128)S(1)} %get-tuple-element.31.own_ref), channel_id=1, source_target_pairs={{0,1},{2,3},{1,0},{3,2},{4,5},{6,7},{5,4},{7,6},{8,9},{10,11},{9,8... | collective-permute-start | bytes 411656 | tf_op jit(solution)/shard_map/ppermute | solution.py:470

commit v16 on v15

--- a/solution.py
+++ b/solution.py
@@ -10,6 +10,7 @@
 
 STEPS = 3
 SEGS = 2048
+GROUP = 2
 F32 = jnp.float32
 BF16 = jnp.bfloat16
 VMEM = pl.BlockSpec(memory_space=pltpu.VMEM)
@@ -210,60 +211,52 @@
 
     def put(i, both):
         high, low = split(both)
-        span = pl.ds(pl.multiple_of(i * rows, 2 * rows), 2 * rows)
+        span = pl.ds(i * rows, 2 * rows)
         right_ref[0, span, :] = high
         right_ref[1, span, :] = high
         right_ref[2, span, :] = low
 
-    def at(ref, j):
-        return jnp.concatenate(
-            [
-                ref[pl.ds(pl.multiple_of(c * size + j * rows, rows), rows), :]
-                for c in range(cols // 128)
-            ],
-            axis=1,
-        )
-
-    def first_sweep(n, _):
+    def lines_of(ref, i):
+        return [chunked(ref, j * rows, rows, size) for j in range(i, i + GROUP)]
+
+    for i in range(0, depth, GROUP):
+        halves = [0.5 * x for x in lines_of(k_ref, i)]
+        factors = [jnp.broadcast_to(factor_ref[j : j + 1, :], (rows, 128)) for j in range(i, i + GROUP)]
+        chords = [half + shift_next(half, 1) for half in halves]
+        spans = [half + shift_next(half, 0) for half in halves]
         found = []
-        for j in (2 * n, 2 * n + 1):
-            half = 0.5 * at(k_ref, j)
-            w_chord = half + shift_next(half, 1)
-            w_span = half + shift_next(half, 0)
-            chord_ref[j] = w_chord
-            span_ref[j] = w_span
+        for half, factor, w_chord, w_span in zip(halves, factors, chords, spans):
             edge = half * f
             flux_chord = w_chord * f_chord
             flux_span = w_span * f_span
             moved = f + flux_chord - shift_prev(flux_chord, 1, edge)
             moved = moved + flux_span - shift_prev(flux_span, 0, edge)
-            factor = jnp.concatenate(
-                [jnp.broadcast_to(factor_ref[pl.ds(j, 1), :], (rows, 128))] * (cols // 128),
-                axis=1,
-            )
-            found.append(factor * moved + jnp.where(j == 0, frames_ref[1], 0.0))
-        put(2 * n, jnp.concatenate(found, axis=0))
-        return 0
-
-    lax.fori_loop(0, depth // 2, first_sweep, 0, unroll=2)
+            found.append(jnp.concatenate([factor] * (cols // 128), axis=1) * moved)
+        if i == 0:
+            found[0] = found[0] + frames_ref[1]
+        for n in range(GROUP):
+            chord_ref[i + n] = chords[n]
+            span_ref[i + n] = spans[n]
+        for n in range(0, GROUP, 2):
+            put(i + n, jnp.concatenate(found[n : n + 2], axis=0))
     right = right_ref[...].reshape(3 * size, cols)
     first = dot(mat_ref[...], right)
     for c in range(cols // 128):
         first_ref[c * size : (c + 1) * size, :] = first[:, c * 128 : (c + 1) * 128]
 
-    def second_sweep(n, _):
-        found = []
-        for j in (2 * n, 2 * n + 1):
-            v = at(first_ref, j)
-            half = 0.5 * at(k_ref, j)
-            source = (
-                v + divergence(v, chord_ref[j], half, 1) + divergence(v, span_ref[j], half, 0)
-            )
-            found.append(source + jnp.where(j == 0, frames_ref[0], 0.0))
-        put(2 * n, jnp.concatenate(found, axis=0))
-        return 0
-
-    lax.fori_loop(0, depth // 2, second_sweep, 0, unroll=2)
+    for i in range(0, depth, GROUP):
+        halves = [0.5 * x for x in lines_of(k_ref, i)]
+        values = lines_of(first_ref, i)
+        chords = [chord_ref[i + n] for n in range(GROUP)]
+        spans = [span_ref[i + n] for n in range(GROUP)]
+        found = [
+            v + divergence(v, w_chord, half, 1) + divergence(v, w_span, half, 0)
+            for v, w_chord, w_span, half in zip(values, chords, spans, halves)
+        ]
+        if i == 0:
+            found[0] = found[0] + frames_ref[0]
+        for n in range(0, GROUP, 2):
+            put(i + n, jnp.concatenate(found[n : n + 2], axis=0))
     right = right_ref[...].reshape(3 * size, cols)
     adj = dot(mat_ref[...], right)
     for c in range(cols // 128):

time: 26.1 us -> 24.1 us (0.923)
  Pallas kernels: 8.28 us -> 5.83 us
  blocking collectives: 11.9 us -> 12.3 us
    pallas_call x1, Pallas kernels: 4.25 us -> 1.81 us  [per_device(): pl.pallas_call(functools.partial(base_kernel, scale), out_shape=(pltpu.VM...]
    all_to_all x1, blocking collectives: 11.9 us -> 12.3 us  [per_device(): pieces = lax.all_to_all(partial, ('blade', 'span'), 0, 0, tiled=True)]
  transfers between devices with their start and end apart: 2 -> 2, of which waited for: 0 -> 0; matrix products, arithmetic and copies ran while one was open for 0% -> 0% of each run, Pallas kernels for 22% -> 14%
where the time goes in v16:
time: 24.1 us; the launch traced here: 23.9 us
  blocking collectives  12.3 us (51%)
  Pallas kernels  5.83 us (24%)
  starting transfers between devices  5.03 us (21%)
  between operations  0.69 us (3%)
    all_to_all x1, blocking collectives, per_device(): pieces = lax.all_to_all(partial, ('blade', 'span'), 0, 0, tiled=True)  12.3 us
    ppermute x1, starting transfers between devices, per_device(): near = lax.ppermute(own_near, 'span', within + [(b, a) for a, b in within])  4.36 us
    pallas_call x1, Pallas kernels, per_device(): pl.pallas_call(functools.partial(base_kernel, scale), out_shape=(pltpu.VM...  1.81 us
    pallas_call x1, Pallas kernels, per_device(): pl.pallas_call(functools.partial(near_kernel, scale), out_shape=(pltpu.HB...  1.42 us
    pallas_call x1, Pallas kernels, per_device(): pl.pallas_call(functools.partial(load_kernel, rows), out_shape=(packed_fa...  1.22 us
    pallas_call x1, Pallas kernels, per_device(): pl.pallas_call(functools.partial(far_kernel, scale), out_shape=(pltpu.VME...  0.7 us
    pallas_call x1, Pallas kernels, per_device(): pl.pallas_call(finish_kernel, out_shape=(pltpu.HBM((depth, rows, cols), F...  0.68 us
    ppermute x1, starting transfers between devices, per_device(): far = lax.ppermute(own_far, 'span', across + [(b, a) for a, b in across])  0.67 us
  transfers between devices with their start and end apart: 2, of which 0 were waited for; matrix products, arithmetic and copies ran while one was open for 0% of the time, Pallas kernels for 14%

profile of v16, /device:TPU:0, one launch (start us, length us, event | category | flops | bytes accessed | tf_op | source)
XLA Modules:
  0.0 23.9 jit_solution(8489581670532927641)
XLA Ops:
  0.6 1.2 %load.1 = (f32[272,128]{1,0:T(8,128)S(1)}, f32[268,128]{1,0:T(8,128)S(1)}, f32[1024,128]{1,0:T(8,128)S(1)}, f32[3,8,512]{2,1,0:T(8,128)S(1)}, f32[32,32]{1,0:T(8,128)S(1)}) custom-call(s32[3]{0:T(128)} %frame_hbm.1, f32[256,512]{1,0:T(8,128)} %bitcast.6, f32[4,8,512]{2,1,0:T(8,128)} %bitcast.8, f32[32,32]{1,0:T(8,128)} %bitcast.10), custom_call_target="tpu_custom_call" | custom-call | tf_op jit(solution)/shard_map/load/pallas_call | solution.py:437
  1.9 0.7 %collective-permute-start.1 = (f32[272,128]{1,0:T(8,128)S(1)}, f32[272,128]{1,0:T(8,128)S(1)}, u32[]{:S(2)}, u32[]{:S(2)}) collective-permute-start(f32[272,128]{1,0:T(8,128)S(1)} %get-tuple-element.33.own_ref), channel_id=1, source_target_pairs={{1,2},{2,1},{5,6},{6,5},{9,10},{10,9},{13,14},{14,13},{17,18},{18,... | collective-permute-start | bytes 417800 | tf_op jit(solution)/shard_map/ppermute | solution.py:464
  2.5 4.4 %collective-permute-start = (f32[268,128]{1,0:T(8,128)S(1)}, f32[268,128]{1,0:T(8,128)S(1)}, u32[]{:S(2)}, u32[]{:S(2)}) collective-permute-start(f32[268,128]{1,0:T(8,128)S(1)} %get-tuple-element.31.own_ref), channel_id=1, source_target_pairs={{0,1},{2,3},{1,0},{3,2},{4,5},{6,7},{5,4},{7,6},{8,9},{10,11},{9,8... | collective-permute-start | bytes 411656 | tf_op jit(solution)/shard_map/ppermute | solution.py:463
  6.9 1.8 %base.1 = (f32[1024,128]{1,0:T(8,128)S(1)}, f32[2,32,512]{2,1,0:T(8,128)S(1)}, f32[3,8,512]{2,1,0:T(8,128)S(1)}, s32[4,8]{1,0:T(4,128)S(1)}, f32[2,32,512]{2,1,0...) custom-call(f32[1024,128]{1,0:T(8,128)S(1)} %get-tuple-element.22.k_ref, ...), custom_call_target="tpu_custom_call" | custom-call | tf_op jit(solution)/shard_map/base/pallas_call | solution.py:467
  8.7 0.0 collective-permute-done.got_ref
  8.7 1.4 %near.1 = (f32[32,8,512]{2,1,0:T(8,128)}, f32[32,1,64]{2,1,0:T(1,128)S(1)}) custom-call(f32[32,32]{1,0:T(8,128)S(1)} %get-tuple-element.21.d_ref, f32[3,8,512]{2,1,0:T(8,128)S(1)} %get-tuple-element.24.excess_ref, f32[2,32,512]{2,1,0:T(8,128)S(1)} %get-tuple-element.25.edge_ref, bf16[64,192]{1,0:T(8,128)(2,1)S(1)} %get-tuple-element.26.pair_ref, ...), custom_call_target="tpu_custom_call" | custom-call | tf_op jit(solution)/shard_map/near/pallas_call | solution.py:495
  10.2 0.0 collective-permute-done.1.got_ref
  10.2 0.7 %far.1 = (f32[2,32,512]{2,1,0:T(8,128)S(1)}, f32[32,1,64]{2,1,0:T(1,128)S(1)}) custom-call(f32[272,128]{1,0:T(8,128)S(1)} %get-tuple-element.33.own_ref, f32[272,128]{1,0:T(8,128)S(1)} %collective-permute-done.1.got_ref, f32[32,32]{1,0:T(8,128)S(1)} %get-tuple-element.21.d_ref, f32[3,8,512]{2,1,0:T(8,128)S(1)} %get-tuple-element.24.excess_ref, ...), custom_call_target="tpu_custom_call" | custom-call | tf_op jit(solution)/shard_map/far/pallas_call | solution.py:508
  10.9 12.3 %all_to_all.5.got_ref = f32[32,1,64]{2,1,0:T(1,128)S(1)} all-to-all(f32[32,1,64]{2,1,0:T(1,128)S(1)} %get-tuple-element.37), channel_id=1, replica_groups=mesh['blade'=8,'span'=4] {'blade','span'}, dimensions={0} | all-to-all | bytes 16384 | tf_op jit(solution)/shard_map/all_to_all | solution.py:517
  23.2 0.7 %finish.1 = (f32[32,8,512]{2,1,0:T(8,128)}, f32[64]{0:T(128)}) custom-call(f32[32,8,512]{2,1,0:T(8,128)} %get-tuple-element.32._, f32[2,32,512]{2,1,0:T(8,128)S(1)} %get-tuple-element.36.two_ref, f32[32,1,64]{2,1,0:T(1,128)S(1)} %all_to_all.5.got_ref), custom_call_target="tpu_custom_call", output_to_operand_aliasing={{0}: (0, {})} | custom-call | tf_op jit(solution)/shard_map/finish/pallas_call | solution.py:518
Async XLA Ops:
  1.9 8.3 %collective-permute-start.1 = (f32[272,128]{1,0:T(8,128)S(1)}, f32[272,128]{1,0:T(8,128)S(1)}, u32[]{:S(2)}, u32[]{:S(2)}) collective-permute-start(f32[272,128]{1,0:T(8,128)S(1)} %get-tuple-element.33.own_ref), channel_id=1, source_target_pairs={{1,2},{2,1},{5,6},{6,5},{9,10},{10,9},{13,14},{14,13},{17,18},{18,... | collective-permute-start | bytes 417800 | tf_op jit(solution)/shard_map/ppermute | solution.py:464
  2.5 6.2 %collective-permute-start = (f32[268,128]{1,0:T(8,128)S(1)}, f32[268,128]{1,0:T(8,128)S(1)}, u32[]{:S(2)}, u32[]{:S(2)}) collective-permute-start(f32[268,128]{1,0:T(8,128)S(1)} %get-tuple-element.31.own_ref), channel_id=1, source_target_pairs={{0,1},{2,3},{1,0},{3,2},{4,5},{6,7},{5,4},{7,6},{8,9},{10,11},{9,8... | collective-permute-start | bytes 411656 | tf_op jit(solution)/shard_map/ppermute | solution.py:463

commit v17 on v16

--- a/solution.py
+++ b/solution.py
@@ -11,6 +11,7 @@
 STEPS = 3
 SEGS = 2048
 GROUP = 2
+PARTS = 4
 F32 = jnp.float32
 BF16 = jnp.bfloat16
 VMEM = pl.BlockSpec(memory_space=pltpu.VMEM)
@@ -95,7 +96,6 @@
 
 
 def load_kernel(
-    rows,
     frame_hbm,
     k_hbm,
     res_hbm,
@@ -109,12 +109,13 @@
     res_ref,
     sems,
 ):
-    size, cols = k_hbm.shape
-    depth = size // rows
+    depth, rows, cols = k_ref.shape
     chunks = cols // 128
+    step = depth // PARTS
     pairs = [(frame_hbm, frame_ref), (res_hbm, res_ref)]
-    for c in range(chunks):
-        pairs.append((k_hbm.at[:, pl.ds(c * 128, 128)], k_ref.at[pl.ds(c * size, size)]))
+    for n in range(PARTS):
+        part = pl.ds(n * step, step)
+        pairs.append((k_hbm.at[part], k_ref.at[part]))
     pairs.append((d_hbm, d_ref))
     copies = [pltpu.make_async_copy(a, b, sems.at[n]) for n, (a, b) in enumerate(pairs)]
     for copy in copies:
@@ -125,24 +126,31 @@
         picks.append((jnp.where(after, rows - 1, 0), jnp.where(after, rows - 2, 1)))
     copies[0].wait()
     copies[1].wait()
-    for step in range(STEPS):
-        frames_ref[step] = res_ref[frame_ref[step]]
+    for n in range(STEPS):
+        frames_ref[n] = res_ref[frame_ref[n]]
     base = 2 * chunks * depth
     for ref, (edge, second) in zip(sent, picks):
-        for n, (step, row) in enumerate(((2, edge), (1, edge), (2, second))):
-            line = frames_ref[step, pl.ds(row, 1), :]
+        for n, (frame, row) in enumerate(((2, edge), (1, edge), (2, second))):
+            line = frames_ref[frame, pl.ds(row, 1), :]
             for c in range(chunks):
                 spot = base + n * chunks + c
                 ref[spot : spot + 1, :] = line[:, c * 128 : (c + 1) * 128]
         if ref.shape[0] > base + 3 * chunks:
             ref[base + 3 * chunks :, :] = jnp.zeros((ref.shape[0] - base - 3 * chunks, 128), F32)
-    for c in range(chunks):
-        copies[2 + c].wait()
-        for ref, row_pair in zip(sent, picks):
-            for n, row in enumerate(row_pair):
-                spot = (n * chunks + c) * depth
-                ref[spot : spot + depth, :] = row_of_each(k_ref, c, depth, rows, row)
-    for copy in copies[2 + chunks :]:
+    near_after = sides()[0][0]
+    for part in range(PARTS):
+        copies[2 + part].wait()
+        here = slice(part * step, (part + 1) * step)
+        for n, (first, last) in enumerate(((0, rows - 1), (1, rows - 2))):
+            first, last = k_ref[here, first, :], k_ref[here, last, :]
+            for ref, x in (
+                (near_ref, jnp.where(near_after, last, first)),
+                (far_ref, jnp.where(near_after, first, last)),
+            ):
+                for c in range(chunks):
+                    spot = (n * chunks + c) * depth + part * step
+                    ref[spot : spot + step, :] = x[:, c * 128 : (c + 1) * 128]
+    for copy in copies[2 + PARTS :]:
         copy.wait()
 
 
@@ -220,7 +228,7 @@
         return [chunked(ref, j * rows, rows, size) for j in range(i, i + GROUP)]
 
     for i in range(0, depth, GROUP):
-        halves = [0.5 * x for x in lines_of(k_ref, i)]
+        halves = [0.5 * k_ref[i + n] for n in range(GROUP)]
         factors = [jnp.broadcast_to(factor_ref[j : j + 1, :], (rows, 128)) for j in range(i, i + GROUP)]
         chords = [half + shift_next(half, 1) for half in halves]
         spans = [half + shift_next(half, 0) for half in halves]
@@ -245,7 +253,7 @@
         first_ref[c * size : (c + 1) * size, :] = first[:, c * 128 : (c + 1) * 128]
 
     for i in range(0, depth, GROUP):
-        halves = [0.5 * x for x in lines_of(k_ref, i)]
+        halves = [0.5 * k_ref[i + n] for n in range(GROUP)]
         values = lines_of(first_ref, i)
         chords = [chord_ref[i + n] for n in range(GROUP)]
         spans = [span_ref[i + n] for n in range(GROUP)]
@@ -435,11 +443,11 @@
     packed_far = pltpu.VMEM(((2 * depth + 4) * chunks, 128), F32)
     packed_near = pltpu.VMEM(((2 * depth + 3) * chunks, 128), F32)
     own_far, own_near, k, picked, inverse = pl.pallas_call(
-        functools.partial(load_kernel, rows),
+        load_kernel,
         out_shape=(
             packed_far,
             packed_near,
-            pltpu.VMEM((chunks * size, 128), F32),
+            field,
             pltpu.VMEM((STEPS, rows, cols), F32),
             pltpu.VMEM((depth, depth), F32),
         ),
@@ -448,13 +456,13 @@
         scratch_shapes=[
             pltpu.SMEM((STEPS,), jnp.int32),
             pltpu.VMEM((frames, rows, cols), F32),
-            pltpu.SemaphoreType.DMA((3 + chunks,)),
+            pltpu.SemaphoreType.DMA((3 + PARTS,)),
         ],
         compiler_params=GRANT,
         name="load",
     )(
         in_hbm(frame_index),
-        in_hbm(conductance.reshape(size, cols)),
+        in_hbm(conductance[0]),
         in_hbm(surface_residual[0]),
         in_hbm(depth_inverse[0]),
     )

time: 24.1 us -> 24.1 us (level)
  transfers between devices with their start and end apart: 2 -> 2, of which waited for: 0 -> 0; matrix products, arithmetic and copies ran while one was open for 0% -> 0% of each run, Pallas kernels for 14% -> 13%
where the time goes in v17:
time: 24.1 us; the launch traced here: 23.9 us
  blocking collectives  12.3 us (51%)
  Pallas kernels  5.82 us (24%)
  starting transfers between devices  5.03 us (21%)
  between operations  0.69 us (3%)
    all_to_all x1, blocking collectives, per_device(): pieces = lax.all_to_all(partial, ('blade', 'span'), 0, 0, tiled=True)  12.3 us
    ppermute x1, starting transfers between devices, per_device(): near = lax.ppermute(own_near, 'span', within + [(b, a) for a, b in within])  4.36 us
    pallas_call x1, Pallas kernels, per_device(): pl.pallas_call(functools.partial(base_kernel, scale), out_shape=(pltpu.VM...  1.8 us
    pallas_call x1, Pallas kernels, per_device(): pl.pallas_call(functools.partial(near_kernel, scale), out_shape=(pltpu.HB...  1.42 us
    pallas_call x1, Pallas kernels, per_device(): pl.pallas_call(load_kernel, out_shape=(packed_far, packed_near, field, pl...  1.22 us
    pallas_call x1, Pallas kernels, per_device(): pl.pallas_call(functools.partial(far_kernel, scale), out_shape=(pltpu.VME...  0.7 us
    pallas_call x1, Pallas kernels, per_device(): pl.pallas_call(finish_kernel, out_shape=(pltpu.HBM((depth, rows, cols), F...  0.68 us
    ppermute x1, starting transfers between devices, per_device(): far = lax.ppermute(own_far, 'span', across + [(b, a) for a, b in across])  0.67 us
  transfers between devices with their start and end apart: 2, of which 0 were waited for; matrix products, arithmetic and copies ran while one was open for 0% of the time, Pallas kernels for 13%

profile of v17, /device:TPU:0, one launch (start us, length us, event | category | flops | bytes accessed | tf_op | source)
XLA Modules:
  0.0 23.9 jit_solution(608542814000432903)
XLA Ops:
  0.6 1.2 %load.1 = (f32[272,128]{1,0:T(8,128)S(1)}, f32[268,128]{1,0:T(8,128)S(1)}, f32[32,8,512]{2,1,0:T(8,128)S(1)}, f32[3,8,512]{2,1,0:T(8,128)S(1)}, f32[32,32]{1,0:T(8,128)S(1)}) custom-call(s32[3]{0:T(128)} %frame_hbm.1, f32[32,8,512]{2,1,0:T(8,128)} %bitcast.6, f32[4,8,512]{2,1,0:T(8,128)} %bitcast.8, f32[32,32]{1,0:T(8,128)} %bitcast.10), custom_call_target="tpu_custom_call" | custom-call | tf_op jit(solution)/shard_map/load/pallas_call | solution.py:445
  1.9 0.7 %collective-permute-start.1 = (f32[272,128]{1,0:T(8,128)S(1)}, f32[272,128]{1,0:T(8,128)S(1)}, u32[]{:S(2)}, u32[]{:S(2)}) collective-permute-start(f32[272,128]{1,0:T(8,128)S(1)} %get-tuple-element.33.own_ref), channel_id=1, source_target_pairs={{1,2},{2,1},{5,6},{6,5},{9,10},{10,9},{13,14},{14,13},{17,18},{18,... | collective-permute-start | bytes 417800 | tf_op jit(solution)/shard_map/ppermute | solution.py:472
  2.5 4.4 %collective-permute-start = (f32[268,128]{1,0:T(8,128)S(1)}, f32[268,128]{1,0:T(8,128)S(1)}, u32[]{:S(2)}, u32[]{:S(2)}) collective-permute-start(f32[268,128]{1,0:T(8,128)S(1)} %get-tuple-element.31.own_ref), channel_id=1, source_target_pairs={{0,1},{2,3},{1,0},{3,2},{4,5},{6,7},{5,4},{7,6},{8,9},{10,11},{9,8... | collective-permute-start | bytes 411656 | tf_op jit(solution)/shard_map/ppermute | solution.py:471
  6.9 1.8 %base.1 = (f32[1024,128]{1,0:T(8,128)S(1)}, f32[2,32,512]{2,1,0:T(8,128)S(1)}, f32[3,8,512]{2,1,0:T(8,128)S(1)}, s32[4,8]{1,0:T(4,128)S(1)}, f32[2,32,512]{2,1,0...) custom-call(f32[32,8,512]{2,1,0:T(8,128)S(1)} %get-tuple-element.22.k_ref, ...), custom_call_target="tpu_custom_call" | custom-call | tf_op jit(solution)/shard_map/base/pallas_call | solution.py:475
  8.7 0.0 collective-permute-done.got_ref
  8.7 1.4 %near.1 = (f32[32,8,512]{2,1,0:T(8,128)}, f32[32,1,64]{2,1,0:T(1,128)S(1)}) custom-call(f32[32,32]{1,0:T(8,128)S(1)} %get-tuple-element.21.d_ref, f32[3,8,512]{2,1,0:T(8,128)S(1)} %get-tuple-element.24.excess_ref, f32[2,32,512]{2,1,0:T(8,128)S(1)} %get-tuple-element.25.edge_ref, bf16[64,192]{1,0:T(8,128)(2,1)S(1)} %get-tuple-element.26.pair_ref, ...), custom_call_target="tpu_custom_call" | custom-call | tf_op jit(solution)/shard_map/near/pallas_call | solution.py:503
  10.1 0.0 collective-permute-done.1.got_ref
  10.1 0.7 %far.1 = (f32[2,32,512]{2,1,0:T(8,128)S(1)}, f32[32,1,64]{2,1,0:T(1,128)S(1)}) custom-call(f32[272,128]{1,0:T(8,128)S(1)} %get-tuple-element.33.own_ref, f32[272,128]{1,0:T(8,128)S(1)} %collective-permute-done.1.got_ref, f32[32,32]{1,0:T(8,128)S(1)} %get-tuple-element.21.d_ref, f32[3,8,512]{2,1,0:T(8,128)S(1)} %get-tuple-element.24.excess_ref, ...), custom_call_target="tpu_custom_call" | custom-call | tf_op jit(solution)/shard_map/far/pallas_call | solution.py:516
  10.9 12.3 %all_to_all.5.got_ref = f32[32,1,64]{2,1,0:T(1,128)S(1)} all-to-all(f32[32,1,64]{2,1,0:T(1,128)S(1)} %get-tuple-element.37), channel_id=1, replica_groups=mesh['blade'=8,'span'=4] {'blade','span'}, dimensions={0} | all-to-all | bytes 16384 | tf_op jit(solution)/shard_map/all_to_all | solution.py:525
  23.2 0.7 %finish.1 = (f32[32,8,512]{2,1,0:T(8,128)}, f32[64]{0:T(128)}) custom-call(f32[32,8,512]{2,1,0:T(8,128)} %get-tuple-element.32._, f32[2,32,512]{2,1,0:T(8,128)S(1)} %get-tuple-element.36.two_ref, f32[32,1,64]{2,1,0:T(1,128)S(1)} %all_to_all.5.got_ref), custom_call_target="tpu_custom_call", output_to_operand_aliasing={{0}: (0, {})} | custom-call | tf_op jit(solution)/shard_map/finish/pallas_call | solution.py:526
Async XLA Ops:
  1.9 8.3 %collective-permute-start.1 = (f32[272,128]{1,0:T(8,128)S(1)}, f32[272,128]{1,0:T(8,128)S(1)}, u32[]{:S(2)}, u32[]{:S(2)}) collective-permute-start(f32[272,128]{1,0:T(8,128)S(1)} %get-tuple-element.33.own_ref), channel_id=1, source_target_pairs={{1,2},{2,1},{5,6},{6,5},{9,10},{10,9},{13,14},{14,13},{17,18},{18,... | collective-permute-start | bytes 417800 | tf_op jit(solution)/shard_map/ppermute | solution.py:472
  2.5 6.2 %collective-permute-start = (f32[268,128]{1,0:T(8,128)S(1)}, f32[268,128]{1,0:T(8,128)S(1)}, u32[]{:S(2)}, u32[]{:S(2)}) collective-permute-start(f32[268,128]{1,0:T(8,128)S(1)} %get-tuple-element.31.own_ref), channel_id=1, source_target_pairs={{0,1},{2,3},{1,0},{3,2},{4,5},{6,7},{5,4},{7,6},{8,9},{10,11},{9,8... | collective-permute-start | bytes 411656 | tf_op jit(solution)/shard_map/ppermute | solution.py:471

commit v18 on v17

--- a/solution.py
+++ b/solution.py
@@ -127,7 +127,11 @@
     copies[0].wait()
     copies[1].wait()
     for n in range(STEPS):
-        frames_ref[n] = res_ref[frame_ref[n]]
+        wanted = jnp.broadcast_to(frame_ref[0:1, n : n + 1], (rows, cols))
+        total = jnp.zeros((rows, cols), F32)
+        for frame in range(res_ref.shape[0]):
+            total = jnp.where(wanted == frame, res_ref[frame], total)
+        frames_ref[n] = total
     base = 2 * chunks * depth
     for ref, (edge, second) in zip(sent, picks):
         for n, (frame, row) in enumerate(((2, edge), (1, edge), (2, second))):
@@ -454,14 +458,14 @@
         in_specs=[HBM] * 4,
         out_specs=(VMEM,) * 5,
         scratch_shapes=[
-            pltpu.SMEM((STEPS,), jnp.int32),
+            pltpu.VMEM((1, STEPS), jnp.int32),
             pltpu.VMEM((frames, rows, cols), F32),
             pltpu.SemaphoreType.DMA((3 + PARTS,)),
         ],
         compiler_params=GRANT,
         name="load",
     )(
-        in_hbm(frame_index),
+        in_hbm(frame_index.reshape(1, STEPS)),
         in_hbm(conductance[0]),
         in_hbm(surface_residual[0]),
         in_hbm(depth_inverse[0]),

time: 24.1 us -> 24.1 us (level)
  transfers between devices with their start and end apart: 2 -> 2, of which waited for: 0 -> 0; matrix products, arithmetic and copies ran while one was open for 0% -> 0% of each run, Pallas kernels for 13% -> 14%
where the time goes in v18:
time: 24.1 us; the launch traced here: 23.9 us
  blocking collectives  12.3 us (51%)
  Pallas kernels  5.84 us (24%)
  starting transfers between devices  5.03 us (21%)
  between operations  0.69 us (3%)
    all_to_all x1, blocking collectives, per_device(): pieces = lax.all_to_all(partial, ('blade', 'span'), 0, 0, tiled=True)  12.3 us
    ppermute x1, starting transfers between devices, per_device(): near = lax.ppermute(own_near, 'span', within + [(b, a) for a, b in within])  4.36 us
    pallas_call x1, Pallas kernels, per_device(): pl.pallas_call(functools.partial(base_kernel, scale), out_shape=(pltpu.VM...  1.81 us
    pallas_call x1, Pallas kernels, per_device(): pl.pallas_call(functools.partial(near_kernel, scale), out_shape=(pltpu.HB...  1.42 us
    pallas_call x1, Pallas kernels, per_device(): pl.pallas_call(load_kernel, out_shape=(packed_far, packed_near, field, pl...  1.23 us
    pallas_call x1, Pallas kernels, per_device(): pl.pallas_call(functools.partial(far_kernel, scale), out_shape=(pltpu.VME...  0.7 us
    pallas_call x1, Pallas kernels, per_device(): pl.pallas_call(finish_kernel, out_shape=(pltpu.HBM((depth, rows, cols), F...  0.68 us
    ppermute x1, starting transfers between devices, per_device(): far = lax.ppermute(own_far, 'span', across + [(b, a) for a, b in across])  0.67 us
  transfers between devices with their start and end apart: 2, of which 0 were waited for; matrix products, arithmetic and copies ran while one was open for 0% of the time, Pallas kernels for 14%

profile of v18, /device:TPU:0, one launch (start us, length us, event | category | flops | bytes accessed | tf_op | source)
XLA Modules:
  0.0 23.9 jit_solution(7245016039051885839)
XLA Ops:
  0.6 1.2 %load.1 = (f32[272,128]{1,0:T(8,128)S(1)}, f32[268,128]{1,0:T(8,128)S(1)}, f32[32,8,512]{2,1,0:T(8,128)S(1)}, f32[3,8,512]{2,1,0:T(8,128)S(1)}, f32[32,32]{1,0:T(8,128)S(1)}) custom-call(s32[1,3]{1,0:T(1,128)} %bitcast.13, f32[32,8,512]{2,1,0:T(8,128)} %bitcast.7, f32[4,8,512]{2,1,0:T(8,128)} %bitcast.9, f32[32,32]{1,0:T(8,128)} %bitcast.11), custom_call_target="tpu_custom_call" | custom-call | tf_op jit(solution)/shard_map/load/pallas_call | solution.py:449
  1.9 0.7 %collective-permute-start.1 = (f32[272,128]{1,0:T(8,128)S(1)}, f32[272,128]{1,0:T(8,128)S(1)}, u32[]{:S(2)}, u32[]{:S(2)}) collective-permute-start(f32[272,128]{1,0:T(8,128)S(1)} %get-tuple-element.33.own_ref), channel_id=1, source_target_pairs={{1,2},{2,1},{5,6},{6,5},{9,10},{10,9},{13,14},{14,13},{17,18},{18,... | collective-permute-start | bytes 417800 | tf_op jit(solution)/shard_map/ppermute | solution.py:476
  2.5 4.4 %collective-permute-start = (f32[268,128]{1,0:T(8,128)S(1)}, f32[268,128]{1,0:T(8,128)S(1)}, u32[]{:S(2)}, u32[]{:S(2)}) collective-permute-start(f32[268,128]{1,0:T(8,128)S(1)} %get-tuple-element.31.own_ref), channel_id=1, source_target_pairs={{0,1},{2,3},{1,0},{3,2},{4,5},{6,7},{5,4},{7,6},{8,9},{10,11},{9,8... | collective-permute-start | bytes 411656 | tf_op jit(solution)/shard_map/ppermute | solution.py:475
  6.9 1.8 %base.1 = (f32[1024,128]{1,0:T(8,128)S(1)}, f32[2,32,512]{2,1,0:T(8,128)S(1)}, f32[3,8,512]{2,1,0:T(8,128)S(1)}, s32[4,8]{1,0:T(4,128)S(1)}, f32[2,32,512]{2,1,0...) custom-call(f32[32,8,512]{2,1,0:T(8,128)S(1)} %get-tuple-element.22.k_ref, ...), custom_call_target="tpu_custom_call" | custom-call | tf_op jit(solution)/shard_map/base/pallas_call | solution.py:479
  8.7 0.0 collective-permute-done.got_ref
  8.7 1.4 %near.1 = (f32[32,8,512]{2,1,0:T(8,128)}, f32[32,1,64]{2,1,0:T(1,128)S(1)}) custom-call(f32[32,32]{1,0:T(8,128)S(1)} %get-tuple-element.21.d_ref, f32[3,8,512]{2,1,0:T(8,128)S(1)} %get-tuple-element.24.excess_ref, f32[2,32,512]{2,1,0:T(8,128)S(1)} %get-tuple-element.25.edge_ref, bf16[64,192]{1,0:T(8,128)(2,1)S(1)} %get-tuple-element.26.pair_ref, ...), custom_call_target="tpu_custom_call" | custom-call | tf_op jit(solution)/shard_map/near/pallas_call | solution.py:507
  10.2 0.0 collective-permute-done.1.got_ref
  10.2 0.7 %far.1 = (f32[2,32,512]{2,1,0:T(8,128)S(1)}, f32[32,1,64]{2,1,0:T(1,128)S(1)}) custom-call(f32[272,128]{1,0:T(8,128)S(1)} %get-tuple-element.33.own_ref, f32[272,128]{1,0:T(8,128)S(1)} %collective-permute-done.1.got_ref, f32[32,32]{1,0:T(8,128)S(1)} %get-tuple-element.21.d_ref, f32[3,8,512]{2,1,0:T(8,128)S(1)} %get-tuple-element.24.excess_ref, ...), custom_call_target="tpu_custom_call" | custom-call | tf_op jit(solution)/shard_map/far/pallas_call | solution.py:520
  10.9 12.3 %all_to_all.5.got_ref = f32[32,1,64]{2,1,0:T(1,128)S(1)} all-to-all(f32[32,1,64]{2,1,0:T(1,128)S(1)} %get-tuple-element.37), channel_id=1, replica_groups=mesh['blade'=8,'span'=4] {'blade','span'}, dimensions={0} | all-to-all | bytes 16384 | tf_op jit(solution)/shard_map/all_to_all | solution.py:529
  23.2 0.7 %finish.1 = (f32[32,8,512]{2,1,0:T(8,128)}, f32[64]{0:T(128)}) custom-call(f32[32,8,512]{2,1,0:T(8,128)} %get-tuple-element.32._, f32[2,32,512]{2,1,0:T(8,128)S(1)} %get-tuple-element.36.two_ref, f32[32,1,64]{2,1,0:T(1,128)S(1)} %all_to_all.5.got_ref), custom_call_target="tpu_custom_call", output_to_operand_aliasing={{0}: (0, {})} | custom-call | tf_op jit(solution)/shard_map/finish/pallas_call | solution.py:530
Async XLA Ops:
  1.9 8.3 %collective-permute-start.1 = (f32[272,128]{1,0:T(8,128)S(1)}, f32[272,128]{1,0:T(8,128)S(1)}, u32[]{:S(2)}, u32[]{:S(2)}) collective-permute-start(f32[272,128]{1,0:T(8,128)S(1)} %get-tuple-element.33.own_ref), channel_id=1, source_target_pairs={{1,2},{2,1},{5,6},{6,5},{9,10},{10,9},{13,14},{14,13},{17,18},{18,... | collective-permute-start | bytes 417800 | tf_op jit(solution)/shard_map/ppermute | solution.py:476
  2.5 6.2 %collective-permute-start = (f32[268,128]{1,0:T(8,128)S(1)}, f32[268,128]{1,0:T(8,128)S(1)}, u32[]{:S(2)}, u32[]{:S(2)}) collective-permute-start(f32[268,128]{1,0:T(8,128)S(1)} %get-tuple-element.31.own_ref), channel_id=1, source_target_pairs={{0,1},{2,3},{1,0},{3,2},{4,5},{6,7},{5,4},{7,6},{8,9},{10,11},{9,8... | collective-permute-start | bytes 411656 | tf_op jit(solution)/shard_map/ppermute | solution.py:475

commit v19 on v17

--- a/solution.py
+++ b/solution.py
@@ -11,7 +11,6 @@
 STEPS = 3
 SEGS = 2048
 GROUP = 2
-PARTS = 4
 F32 = jnp.float32
 BF16 = jnp.bfloat16
 VMEM = pl.BlockSpec(memory_space=pltpu.VMEM)
@@ -102,34 +101,32 @@
     d_hbm,
     far_ref,
     near_ref,
-    k_ref,
     frames_ref,
     d_ref,
     frame_ref,
     res_ref,
+    edge_ref,
     sems,
 ):
-    depth, rows, cols = k_ref.shape
+    depth, rows, cols = k_hbm.shape
     chunks = cols // 128
-    step = depth // PARTS
-    pairs = [(frame_hbm, frame_ref), (res_hbm, res_ref)]
-    for n in range(PARTS):
-        part = pl.ds(n * step, step)
-        pairs.append((k_hbm.at[part], k_ref.at[part]))
-    pairs.append((d_hbm, d_ref))
+    sent = (near_ref, far_ref)
+    afters = [after for after, _ in sides()]
+    pairs = []
+    for n, after in enumerate(afters):
+        first = jnp.where(after, rows - 2, 0)
+        pairs.append((k_hbm.at[:, pl.ds(first, 2), :], edge_ref.at[n, :, 0:2, :]))
+    pairs += [(frame_hbm, frame_ref), (res_hbm, res_ref), (d_hbm, d_ref)]
     copies = [pltpu.make_async_copy(a, b, sems.at[n]) for n, (a, b) in enumerate(pairs)]
     for copy in copies:
         copy.start()
-    sent = (near_ref, far_ref)
-    picks = []
-    for after, _ in sides():
-        picks.append((jnp.where(after, rows - 1, 0), jnp.where(after, rows - 2, 1)))
-    copies[0].wait()
-    copies[1].wait()
+    copies[2].wait()
+    copies[3].wait()
     for n in range(STEPS):
         frames_ref[n] = res_ref[frame_ref[n]]
     base = 2 * chunks * depth
-    for ref, (edge, second) in zip(sent, picks):
+    for ref, after in zip(sent, afters):
+        edge, second = jnp.where(after, rows - 1, 0), jnp.where(after, rows - 2, 1)
         for n, (frame, row) in enumerate(((2, edge), (1, edge), (2, second))):
             line = frames_ref[frame, pl.ds(row, 1), :]
             for c in range(chunks):
@@ -137,21 +134,14 @@
                 ref[spot : spot + 1, :] = line[:, c * 128 : (c + 1) * 128]
         if ref.shape[0] > base + 3 * chunks:
             ref[base + 3 * chunks :, :] = jnp.zeros((ref.shape[0] - base - 3 * chunks, 128), F32)
-    near_after = sides()[0][0]
-    for part in range(PARTS):
-        copies[2 + part].wait()
-        here = slice(part * step, (part + 1) * step)
-        for n, (first, last) in enumerate(((0, rows - 1), (1, rows - 2))):
-            first, last = k_ref[here, first, :], k_ref[here, last, :]
-            for ref, x in (
-                (near_ref, jnp.where(near_after, last, first)),
-                (far_ref, jnp.where(near_after, first, last)),
-            ):
-                for c in range(chunks):
-                    spot = (n * chunks + c) * depth + part * step
-                    ref[spot : spot + step, :] = x[:, c * 128 : (c + 1) * 128]
-    for copy in copies[2 + PARTS :]:
-        copy.wait()
+    for n, after in enumerate(afters):
+        copies[n].wait()
+        low, high = edge_ref[n, :, 0, :], edge_ref[n, :, 1, :]
+        for which, x in enumerate((jnp.where(after, high, low), jnp.where(after, low, high))):
+            for c in range(chunks):
+                spot = (which * chunks + c) * depth
+                sent[n][spot : spot + depth, :] = x[:, c * 128 : (c + 1) * 128]
+    copies[4].wait()
 
 
 def base_kernel(
@@ -442,21 +432,21 @@
     chunks = cols // 128
     packed_far = pltpu.VMEM(((2 * depth + 4) * chunks, 128), F32)
     packed_near = pltpu.VMEM(((2 * depth + 3) * chunks, 128), F32)
-    own_far, own_near, k, picked, inverse = pl.pallas_call(
+    own_far, own_near, picked, inverse = pl.pallas_call(
         load_kernel,
         out_shape=(
             packed_far,
             packed_near,
-            field,
             pltpu.VMEM((STEPS, rows, cols), F32),
             pltpu.VMEM((depth, depth), F32),
         ),
         in_specs=[HBM] * 4,
-        out_specs=(VMEM,) * 5,
+        out_specs=(VMEM,) * 4,
         scratch_shapes=[
             pltpu.SMEM((STEPS,), jnp.int32),
             pltpu.VMEM((frames, rows, cols), F32),
-            pltpu.SemaphoreType.DMA((3 + PARTS,)),
+            pltpu.VMEM((2, depth, 8, cols), F32),
+            pltpu.SemaphoreType.DMA((5,)),
         ],
         compiler_params=GRANT,
         name="load",
@@ -497,7 +487,7 @@
         ],
         compiler_params=GRANT,
         name="base",
-    )(k, picked, inverse, in_hbm(surface_excess[0]), in_hbm(segment_map.T))
+    )(conductance[0], picked, inverse, in_hbm(surface_excess[0]), in_hbm(segment_map.T))
     fixed = (inverse, excess, edge, pair, ids)
     sums = pltpu.VMEM((devices, 1, lanes), F32)
     adjoint, partial = pl.pallas_call(

time: 24.1 us -> 24 us (level)
  transfers between devices with their start and end apart: 2 -> 2, of which waited for: 0 -> 0; matrix products, arithmetic and copies ran while one was open for 0% -> 0% of each run, Pallas kernels for 13% -> 14%
where the time goes in v19:
time: 24 us; the launch traced here: 23.8 us
  blocking collectives  12.3 us (51%)
  Pallas kernels  5.79 us (24%)
  starting transfers between devices  5.03 us (21%)
  between operations  0.7 us (3%)
    all_to_all x1, blocking collectives, per_device(): pieces = lax.all_to_all(partial, ('blade', 'span'), 0, 0, tiled=True)  12.3 us
    ppermute x1, starting transfers between devices, per_device(): near = lax.ppermute(own_near, 'span', within + [(b, a) for a, b in within])  4.36 us
    pallas_call x1, Pallas kernels, per_device(): pl.pallas_call(functools.partial(base_kernel, scale), out_shape=(pltpu.VM...  1.8 us
    pallas_call x1, Pallas kernels, per_device(): pl.pallas_call(functools.partial(near_kernel, scale), out_shape=(pltpu.HB...  1.42 us
    pallas_call x1, Pallas kernels, per_device(): pl.pallas_call(load_kernel, out_shape=(packed_far, packed_near, pltpu.VME...  1.18 us
    pallas_call x1, Pallas kernels, per_device(): pl.pallas_call(functools.partial(far_kernel, scale), out_shape=(pltpu.VME...  0.7 us
    pallas_call x1, Pallas kernels, per_device(): pl.pallas_call(finish_kernel, out_shape=(pltpu.HBM((depth, rows, cols), F...  0.68 us
    ppermute x1, starting transfers between devices, per_device(): far = lax.ppermute(own_far, 'span', across + [(b, a) for a, b in across])  0.67 us
  transfers between devices with their start and end apart: 2, of which 0 were waited for; matrix products, arithmetic and copies ran while one was open for 0% of the time, Pallas kernels for 14%

profile of v19, /device:TPU:0, one launch (start us, length us, event | category | flops | bytes accessed | tf_op | source)
XLA Modules:
  0.0 23.8 jit_solution(11443670242638955860)
XLA Ops:
  0.6 0.0 copy-start
  0.6 1.2 %load.1 = (f32[272,128]{1,0:T(8,128)S(1)}, f32[268,128]{1,0:T(8,128)S(1)}, f32[3,8,512]{2,1,0:T(8,128)S(1)}, f32[32,32]{1,0:T(8,128)S(1)}) custom-call(s32[3]{0:T(128)} %frame_hbm.1, f32[32,8,512]{2,1,0:T(8,128)} %bitcast.6, f32[4,8,512]{2,1,0:T(8,128)} %bitcast.9, f32[32,32]{1,0:T(8,128)} %bitcast.11), custom_call_target="tpu_custom_call" | custom-call | tf_op jit(solution)/shard_map/load/pallas_call | solution.py:435
  1.8 0.7 %collective-permute-start.1 = (f32[272,128]{1,0:T(8,128)S(1)}, f32[272,128]{1,0:T(8,128)S(1)}, u32[]{:S(2)}, u32[]{:S(2)}) collective-permute-start(f32[272,128]{1,0:T(8,128)S(1)} %get-tuple-element.31.own_ref), channel_id=1, source_target_pairs={{1,2},{2,1},{5,6},{6,5},{9,10},{10,9},{13,14},{14,13},{17,18},{18,... | collective-permute-start | bytes 417800 | tf_op jit(solution)/shard_map/ppermute | solution.py:462
  2.5 4.4 %collective-permute-start = (f32[268,128]{1,0:T(8,128)S(1)}, f32[268,128]{1,0:T(8,128)S(1)}, u32[]{:S(2)}, u32[]{:S(2)}) collective-permute-start(f32[268,128]{1,0:T(8,128)S(1)} %get-tuple-element.29.own_ref), channel_id=1, source_target_pairs={{0,1},{2,3},{1,0},{3,2},{4,5},{6,7},{5,4},{7,6},{8,9},{10,11},{9,8... | collective-permute-start | bytes 411656 | tf_op jit(solution)/shard_map/ppermute | solution.py:461
  6.9 0.0 copy-done
  6.9 1.8 %base.1 = (f32[1024,128]{1,0:T(8,128)S(1)}, f32[2,32,512]{2,1,0:T(8,128)S(1)}, f32[3,8,512]{2,1,0:T(8,128)S(1)}, s32[4,8]{1,0:T(4,128)S(1)}, f32[2,32,512]{2,1,0...) custom-call(f32[32,8,512]{2,1,0:T(8,128)S(1)} %bitcast.7, ...), custom_call_target="tpu_custom_call" | custom-call | tf_op jit(solution)/shard_map/base/pallas_call | solution.py:465
  8.7 0.0 collective-permute-done.got_ref
  8.7 1.4 %near.1 = (f32[32,8,512]{2,1,0:T(8,128)}, f32[32,1,64]{2,1,0:T(1,128)S(1)}) custom-call(f32[32,32]{1,0:T(8,128)S(1)} %get-tuple-element.20.d_ref, f32[3,8,512]{2,1,0:T(8,128)S(1)} %get-tuple-element.22.excess_ref, f32[2,32,512]{2,1,0:T(8,128)S(1)} %get-tuple-element.23.edge_ref, bf16[64,192]{1,0:T(8,128)(2,1)S(1)} %get-tuple-element.24.pair_ref, ...), custom_call_target="tpu_custom_call" | custom-call | tf_op jit(solution)/shard_map/near/pallas_call | solution.py:493
  10.1 0.0 collective-permute-done.1.got_ref
  10.1 0.7 %far.1 = (f32[2,32,512]{2,1,0:T(8,128)S(1)}, f32[32,1,64]{2,1,0:T(1,128)S(1)}) custom-call(f32[272,128]{1,0:T(8,128)S(1)} %get-tuple-element.31.own_ref, f32[272,128]{1,0:T(8,128)S(1)} %collective-permute-done.1.got_ref, f32[32,32]{1,0:T(8,128)S(1)} %get-tuple-element.20.d_ref, f32[3,8,512]{2,1,0:T(8,128)S(1)} %get-tuple-element.22.excess_ref, ...), custom_call_target="tpu_custom_call" | custom-call | tf_op jit(solution)/shard_map/far/pallas_call | solution.py:506
  10.8 12.3 %all_to_all.5.got_ref = f32[32,1,64]{2,1,0:T(1,128)S(1)} all-to-all(f32[32,1,64]{2,1,0:T(1,128)S(1)} %get-tuple-element.35), channel_id=1, replica_groups=mesh['blade'=8,'span'=4] {'blade','span'}, dimensions={0} | all-to-all | bytes 16384 | tf_op jit(solution)/shard_map/all_to_all | solution.py:515
  23.2 0.7 %finish.1 = (f32[32,8,512]{2,1,0:T(8,128)}, f32[64]{0:T(128)}) custom-call(f32[32,8,512]{2,1,0:T(8,128)} %get-tuple-element.30._, f32[2,32,512]{2,1,0:T(8,128)S(1)} %get-tuple-element.34.two_ref, f32[32,1,64]{2,1,0:T(1,128)S(1)} %all_to_all.5.got_ref), custom_call_target="tpu_custom_call", output_to_operand_aliasing={{0}: (0, {})} | custom-call | tf_op jit(solution)/shard_map/finish/pallas_call | solution.py:516
Async XLA Ops:
  0.6 6.2 %copy-start = (f32[1,32,8,512]{3,2,1,0:T(8,128)S(1)}, f32[1,32,8,512]{3,2,1,0:T(8,128)}, u32[]{:S(2)}) copy-start(f32[1,32,8,512]{3,2,1,0:T(8,128)} %param.6) | copy-start | bytes 1572868
  1.8 8.3 %collective-permute-start.1 = (f32[272,128]{1,0:T(8,128)S(1)}, f32[272,128]{1,0:T(8,128)S(1)}, u32[]{:S(2)}, u32[]{:S(2)}) collective-permute-start(f32[272,128]{1,0:T(8,128)S(1)} %get-tuple-element.31.own_ref), channel_id=1, source_target_pairs={{1,2},{2,1},{5,6},{6,5},{9,10},{10,9},{13,14},{14,13},{17,18},{18,... | collective-permute-start | bytes 417800 | tf_op jit(solution)/shard_map/ppermute | solution.py:462
  2.5 6.2 %collective-permute-start = (f32[268,128]{1,0:T(8,128)S(1)}, f32[268,128]{1,0:T(8,128)S(1)}, u32[]{:S(2)}, u32[]{:S(2)}) collective-permute-start(f32[268,128]{1,0:T(8,128)S(1)} %get-tuple-element.29.own_ref), channel_id=1, source_target_pairs={{0,1},{2,3},{1,0},{3,2},{4,5},{6,7},{5,4},{7,6},{8,9},{10,11},{9,8... | collective-permute-start | bytes 411656 | tf_op jit(solution)/shard_map/ppermute | solution.py:461

commit v20 on v19

--- a/solution.py
+++ b/solution.py
@@ -94,13 +94,32 @@
     return jnp.where(after, rows - 1, 0), jnp.where(after, rows - 2, 1)
 
 
+def put_lines(ref, frames_ref, depth, rows, after):
+    chunks = frames_ref.shape[2] // 128
+    base = 2 * chunks * depth
+    edge, second = jnp.where(after, rows - 1, 0), jnp.where(after, rows - 2, 1)
+    for n, (frame, row) in enumerate(((2, edge), (1, edge), (2, second))):
+        line = frames_ref[frame, pl.ds(row, 1), :]
+        for c in range(chunks):
+            spot = base + n * chunks + c
+            ref[spot : spot + 1, :] = line[:, c * 128 : (c + 1) * 128]
+    if ref.shape[0] > base + 3 * chunks:
+        ref[base + 3 * chunks :, :] = jnp.zeros((ref.shape[0] - base - 3 * chunks, 128), F32)
+
+
+def put_rows(ref, depth, items):
+    for which, x in enumerate(items):
+        for c in range(x.shape[1] // 128):
+            spot = (which * (x.shape[1] // 128) + c) * depth
+            ref[spot : spot + depth, :] = x[:, c * 128 : (c + 1) * 128]
+
+
 def load_kernel(
     frame_hbm,
     k_hbm,
     res_hbm,
     d_hbm,
     far_ref,
-    near_ref,
     frames_ref,
     d_ref,
     frame_ref,
@@ -109,39 +128,36 @@
     sems,
 ):
     depth, rows, cols = k_hbm.shape
-    chunks = cols // 128
-    sent = (near_ref, far_ref)
-    afters = [after for after, _ in sides()]
-    pairs = []
-    for n, after in enumerate(afters):
-        first = jnp.where(after, rows - 2, 0)
-        pairs.append((k_hbm.at[:, pl.ds(first, 2), :], edge_ref.at[n, :, 0:2, :]))
-    pairs += [(frame_hbm, frame_ref), (res_hbm, res_ref), (d_hbm, d_ref)]
+    after = sides()[1][0]
+    first = jnp.where(after, rows - 2, 0)
+    pairs = (
+        (frame_hbm, frame_ref),
+        (res_hbm, res_ref),
+        (k_hbm.at[:, pl.ds(first, 2), :], edge_ref.at[:, 0:2, :]),
+        (d_hbm, d_ref),
+    )
     copies = [pltpu.make_async_copy(a, b, sems.at[n]) for n, (a, b) in enumerate(pairs)]
     for copy in copies:
         copy.start()
-    copies[2].wait()
-    copies[3].wait()
+    copies[0].wait()
+    copies[1].wait()
     for n in range(STEPS):
         frames_ref[n] = res_ref[frame_ref[n]]
-    base = 2 * chunks * depth
-    for ref, after in zip(sent, afters):
-        edge, second = jnp.where(after, rows - 1, 0), jnp.where(after, rows - 2, 1)
-        for n, (frame, row) in enumerate(((2, edge), (1, edge), (2, second))):
-            line = frames_ref[frame, pl.ds(row, 1), :]
-            for c in range(chunks):
-                spot = base + n * chunks + c
-                ref[spot : spot + 1, :] = line[:, c * 128 : (c + 1) * 128]
-        if ref.shape[0] > base + 3 * chunks:
-            ref[base + 3 * chunks :, :] = jnp.zeros((ref.shape[0] - base - 3 * chunks, 128), F32)
-    for n, after in enumerate(afters):
-        copies[n].wait()
-        low, high = edge_ref[n, :, 0, :], edge_ref[n, :, 1, :]
-        for which, x in enumerate((jnp.where(after, high, low), jnp.where(after, low, high))):
-            for c in range(chunks):
-                spot = (which * chunks + c) * depth
-                sent[n][spot : spot + depth, :] = x[:, c * 128 : (c + 1) * 128]
-    copies[4].wait()
+    put_lines(far_ref, frames_ref, depth, rows, after)
+    copies[2].wait()
+    low, high = edge_ref[:, 0, :], edge_ref[:, 1, :]
+    put_rows(far_ref, depth, (jnp.where(after, high, low), jnp.where(after, low, high)))
+    copies[3].wait()
+
+
+def pack_kernel(k_ref, frames_ref, near_ref):
+    depth, rows, _ = k_ref.shape
+    after = sides()[0][0]
+    put_lines(near_ref, frames_ref, depth, rows, after)
+    items = []
+    for first, last in ((0, rows - 1), (1, rows - 2)):
+        items.append(jnp.where(after, k_ref[:, last, :], k_ref[:, first, :]))
+    put_rows(near_ref, depth, items)
 
 
 def base_kernel(
@@ -432,21 +448,20 @@
     chunks = cols // 128
     packed_far = pltpu.VMEM(((2 * depth + 4) * chunks, 128), F32)
     packed_near = pltpu.VMEM(((2 * depth + 3) * chunks, 128), F32)
-    own_far, own_near, picked, inverse = pl.pallas_call(
+    own_far, picked, inverse = pl.pallas_call(
         load_kernel,
         out_shape=(
             packed_far,
-            packed_near,
             pltpu.VMEM((STEPS, rows, cols), F32),
             pltpu.VMEM((depth, depth), F32),
         ),
         in_specs=[HBM] * 4,
-        out_specs=(VMEM,) * 4,
+        out_specs=(VMEM,) * 3,
         scratch_shapes=[
             pltpu.SMEM((STEPS,), jnp.int32),
             pltpu.VMEM((frames, rows, cols), F32),
-            pltpu.VMEM((2, depth, 8, cols), F32),
-            pltpu.SemaphoreType.DMA((5,)),
+            pltpu.VMEM((depth, 8, cols), F32),
+            pltpu.SemaphoreType.DMA((4,)),
         ],
         compiler_params=GRANT,
         name="load",
@@ -456,6 +471,15 @@
         in_hbm(surface_residual[0]),
         in_hbm(depth_inverse[0]),
     )
+    k = conductance[0]
+    own_near = pl.pallas_call(
+        pack_kernel,
+        out_shape=packed_near,
+        in_specs=[VMEM] * 2,
+        out_specs=VMEM,
+        compiler_params=GRANT,
+        name="pack",
+    )(k, picked)
     across = [(i, i + 1) for i in range(1, spans - 1, 2)]
     within = [(i, i + 1) for i in range(0, spans - 1, 2)]
     near = lax.ppermute(own_near, "span", within + [(b, a) for a, b in within])
@@ -487,7 +511,7 @@
         ],
         compiler_params=GRANT,
         name="base",
-    )(conductance[0], picked, inverse, in_hbm(surface_excess[0]), in_hbm(segment_map.T))
+    )(k, picked, inverse, in_hbm(surface_excess[0]), in_hbm(segment_map.T))
     fixed = (inverse, excess, edge, pair, ids)
     sums = pltpu.VMEM((devices, 1, lanes), F32)
     adjoint, partial = pl.pallas_call(

time: 24 us -> 23.9 us (level)
    pallas_call x1 -> x2, Pallas kernels: 1.18 us -> 1.13 us  [the longest x1 1.07 us: per_device(): pl.pallas_call(load_kernel, out_shape=(packed_far, pltpu.VMEM((STEPS, row...]
where the time goes in v20:
time: 23.9 us; the launch traced here: 23.7 us
  blocking collectives  12.3 us (51%)
  Pallas kernels  5.74 us (24%)
  starting transfers between devices  5.03 us (21%)
  between operations  0.71 us (3%)
    all_to_all x1, blocking collectives, per_device(): pieces = lax.all_to_all(partial, ('blade', 'span'), 0, 0, tiled=True)  12.3 us
    ppermute x1, starting transfers between devices, per_device(): near = lax.ppermute(own_near, 'span', within + [(b, a) for a, b in within])  4.36 us
    pallas_call x1, Pallas kernels, per_device(): pl.pallas_call(functools.partial(base_kernel, scale), out_shape=(pltpu.VM...  1.81 us
    pallas_call x1, Pallas kernels, per_device(): pl.pallas_call(functools.partial(near_kernel, scale), out_shape=(pltpu.HB...  1.42 us
    pallas_call x1, Pallas kernels, per_device(): pl.pallas_call(load_kernel, out_shape=(packed_far, pltpu.VMEM((STEPS, row...  1.07 us
    pallas_call x1, Pallas kernels, per_device(): pl.pallas_call(functools.partial(far_kernel, scale), out_shape=(pltpu.VME...  0.7 us
    pallas_call x1, Pallas kernels, per_device(): pl.pallas_call(finish_kernel, out_shape=(pltpu.HBM((depth, rows, cols), F...  0.68 us
    ppermute x1, starting transfers between devices, per_device(): far = lax.ppermute(own_far, 'span', across + [(b, a) for a, b in across])  0.67 us
  transfers between devices with their start and end apart: 2, of which 0 were waited for; matrix products, arithmetic and copies ran while one was open for 0% of the time, Pallas kernels for 14%

profile of v20, /device:TPU:0, one launch (start us, length us, event | category | flops | bytes accessed | tf_op | source)
XLA Modules:
  0.0 23.7 jit_solution(18171832004079065298)
XLA Ops:
  0.6 0.0 copy-start
  0.6 1.1 %load.1 = (f32[272,128]{1,0:T(8,128)S(1)}, f32[3,8,512]{2,1,0:T(8,128)S(1)}, f32[32,32]{1,0:T(8,128)S(1)}) custom-call(s32[3]{0:T(128)} %frame_hbm.1, f32[32,8,512]{2,1,0:T(8,128)} %bitcast.6, f32[4,8,512]{2,1,0:T(8,128)} %bitcast.10, f32[32,32]{1,0:T(8,128)} %bitcast.12), custom_call_target="tpu_custom_call" | custom-call | tf_op jit(solution)/shard_map/load/pallas_call | solution.py:451
  1.7 0.7 %collective-permute-start.1 = (f32[272,128]{1,0:T(8,128)S(1)}, f32[272,128]{1,0:T(8,128)S(1)}, u32[]{:S(2)}, u32[]{:S(2)}) collective-permute-start(f32[272,128]{1,0:T(8,128)S(1)} %get-tuple-element.29.own_ref), channel_id=1, source_target_pairs={{1,2},{2,1},{5,6},{6,5},{9,10},{10,9},{13,14},{14,13},{17,18},{18,... | collective-permute-start | bytes 417800 | tf_op jit(solution)/shard_map/ppermute | solution.py:486
  2.4 0.0 copy-done
  2.4 0.1 pack.1.own_ref
  2.5 4.4 %collective-permute-start = (f32[268,128]{1,0:T(8,128)S(1)}, f32[268,128]{1,0:T(8,128)S(1)}, u32[]{:S(2)}, u32[]{:S(2)}) collective-permute-start(f32[268,128]{1,0:T(8,128)S(1)} %pack.1.own_ref), channel_id=1, source_target_pairs={{0,1},{2,3},{1,0},{3,2},{4,5},{6,7},{5,4},{7,6},{8,9},{10,11},{9,8... | collective-permute-start | bytes 411656 | tf_op jit(solution)/shard_map/ppermute | solution.py:485
  6.8 1.8 %base.1 = (f32[1024,128]{1,0:T(8,128)S(1)}, f32[2,32,512]{2,1,0:T(8,128)S(1)}, f32[3,8,512]{2,1,0:T(8,128)S(1)}, s32[4,8]{1,0:T(4,128)S(1)}, f32[2,32,512]{2,1,0...) custom-call(f32[32,8,512]{2,1,0:T(8,128)S(1)} %bitcast.8, ...), custom_call_target="tpu_custom_call" | custom-call | tf_op jit(solution)/shard_map/base/pallas_call | solution.py:489
  8.6 0.0 collective-permute-done.got_ref
  8.7 1.4 %near.1 = (f32[32,8,512]{2,1,0:T(8,128)}, f32[32,1,64]{2,1,0:T(1,128)S(1)}) custom-call(f32[32,32]{1,0:T(8,128)S(1)} %get-tuple-element.19.d_ref, f32[3,8,512]{2,1,0:T(8,128)S(1)} %get-tuple-element.21.excess_ref, f32[2,32,512]{2,1,0:T(8,128)S(1)} %get-tuple-element.22.edge_ref, bf16[64,192]{1,0:T(8,128)(2,1)S(1)} %get-tuple-element.23.pair_ref, ...), custom_call_target="tpu_custom_call" | custom-call | tf_op jit(solution)/shard_map/near/pallas_call | solution.py:517
  10.1 0.0 collective-permute-done.1.got_ref
  10.1 0.7 %far.1 = (f32[2,32,512]{2,1,0:T(8,128)S(1)}, f32[32,1,64]{2,1,0:T(1,128)S(1)}) custom-call(f32[272,128]{1,0:T(8,128)S(1)} %get-tuple-element.29.own_ref, f32[272,128]{1,0:T(8,128)S(1)} %collective-permute-done.1.got_ref, f32[32,32]{1,0:T(8,128)S(1)} %get-tuple-element.19.d_ref, f32[3,8,512]{2,1,0:T(8,128)S(1)} %get-tuple-element.21.excess_ref, ...), custom_call_target="tpu_custom_call" | custom-call | tf_op jit(solution)/shard_map/far/pallas_call | solution.py:530
  10.8 12.3 %all_to_all.5.got_ref = f32[32,1,64]{2,1,0:T(1,128)S(1)} all-to-all(f32[32,1,64]{2,1,0:T(1,128)S(1)} %get-tuple-element.33), channel_id=1, replica_groups=mesh['blade'=8,'span'=4] {'blade','span'}, dimensions={0} | all-to-all | bytes 16384 | tf_op jit(solution)/shard_map/all_to_all | solution.py:539
  23.1 0.7 %finish.1 = (f32[32,8,512]{2,1,0:T(8,128)}, f32[64]{0:T(128)}) custom-call(f32[32,8,512]{2,1,0:T(8,128)} %get-tuple-element.28._, f32[2,32,512]{2,1,0:T(8,128)S(1)} %get-tuple-element.32.two_ref, f32[32,1,64]{2,1,0:T(1,128)S(1)} %all_to_all.5.got_ref), custom_call_target="tpu_custom_call", output_to_operand_aliasing={{0}: (0, {})} | custom-call | tf_op jit(solution)/shard_map/finish/pallas_call | solution.py:540
Async XLA Ops:
  0.6 1.8 %copy-start = (f32[1,32,8,512]{3,2,1,0:T(8,128)S(1)}, f32[1,32,8,512]{3,2,1,0:T(8,128)}, u32[]{:S(2)}) copy-start(f32[1,32,8,512]{3,2,1,0:T(8,128)} %param.6) | copy-start | bytes 1572868
  1.7 8.4 %collective-permute-start.1 = (f32[272,128]{1,0:T(8,128)S(1)}, f32[272,128]{1,0:T(8,128)S(1)}, u32[]{:S(2)}, u32[]{:S(2)}) collective-permute-start(f32[272,128]{1,0:T(8,128)S(1)} %get-tuple-element.29.own_ref), channel_id=1, source_target_pairs={{1,2},{2,1},{5,6},{6,5},{9,10},{10,9},{13,14},{14,13},{17,18},{18,... | collective-permute-start | bytes 417800 | tf_op jit(solution)/shard_map/ppermute | solution.py:486
  2.5 6.2 %collective-permute-start = (f32[268,128]{1,0:T(8,128)S(1)}, f32[268,128]{1,0:T(8,128)S(1)}, u32[]{:S(2)}, u32[]{:S(2)}) collective-permute-start(f32[268,128]{1,0:T(8,128)S(1)} %pack.1.own_ref), channel_id=1, source_target_pairs={{0,1},{2,3},{1,0},{3,2},{4,5},{6,7},{5,4},{7,6},{8,9},{10,11},{9,8... | collective-permute-start | bytes 411656 | tf_op jit(solution)/shard_map/ppermute | solution.py:485

commit v21 on v20

--- a/solution.py
+++ b/solution.py
@@ -94,12 +94,10 @@
     return jnp.where(after, rows - 1, 0), jnp.where(after, rows - 2, 1)
 
 
-def put_lines(ref, frames_ref, depth, rows, after):
-    chunks = frames_ref.shape[2] // 128
+def put_lines(ref, depth, lines):
+    chunks = lines[0].shape[1] // 128
     base = 2 * chunks * depth
-    edge, second = jnp.where(after, rows - 1, 0), jnp.where(after, rows - 2, 1)
-    for n, (frame, row) in enumerate(((2, edge), (1, edge), (2, second))):
-        line = frames_ref[frame, pl.ds(row, 1), :]
+    for n, line in enumerate(lines):
         for c in range(chunks):
             spot = base + n * chunks + c
             ref[spot : spot + 1, :] = line[:, c * 128 : (c + 1) * 128]
@@ -120,7 +118,7 @@
     res_hbm,
     d_hbm,
     far_ref,
-    frames_ref,
+    index_ref,
     d_ref,
     frame_ref,
     res_ref,
@@ -132,7 +130,7 @@
     first = jnp.where(after, rows - 2, 0)
     pairs = (
         (frame_hbm, frame_ref),
-        (res_hbm, res_ref),
+        (res_hbm.at[:, pl.ds(first, 2), :], res_ref.at[:, 0:2, :]),
         (k_hbm.at[:, pl.ds(first, 2), :], edge_ref.at[:, 0:2, :]),
         (d_hbm, d_ref),
     )
@@ -142,18 +140,32 @@
     copies[0].wait()
     copies[1].wait()
     for n in range(STEPS):
-        frames_ref[n] = res_ref[frame_ref[n]]
-    put_lines(far_ref, frames_ref, depth, rows, after)
+        index_ref[n : n + 1, :] = jnp.full((1, 128), frame_ref[n], jnp.int32)
+    lines = []
+    for step, near in ((2, True), (1, True), (2, False)):
+        low, high = res_ref[frame_ref[step], 0:1, :], res_ref[frame_ref[step], 1:2, :]
+        lines.append(jnp.where(after, high, low) if near else jnp.where(after, low, high))
+    put_lines(far_ref, depth, lines)
     copies[2].wait()
     low, high = edge_ref[:, 0, :], edge_ref[:, 1, :]
     put_rows(far_ref, depth, (jnp.where(after, high, low), jnp.where(after, low, high)))
     copies[3].wait()
 
 
-def pack_kernel(k_ref, frames_ref, near_ref):
-    depth, rows, _ = k_ref.shape
+def pack_kernel(k_ref, res_ref, index_ref, near_ref, frames_ref):
+    depth, rows, cols = k_ref.shape
     after = sides()[0][0]
-    put_lines(near_ref, frames_ref, depth, rows, after)
+    for n in range(STEPS):
+        wanted = jnp.concatenate(
+            [jnp.broadcast_to(index_ref[n : n + 1, :], (rows, 128))] * (cols // 128), axis=1
+        )
+        picked = res_ref[0]
+        for frame in range(1, res_ref.shape[0]):
+            picked = jnp.where(wanted == frame, res_ref[frame], picked)
+        frames_ref[n] = picked
+    edge, second = jnp.where(after, rows - 1, 0), jnp.where(after, rows - 2, 1)
+    lines = [frames_ref[n, pl.ds(row, 1), :] for n, row in ((2, edge), (1, edge), (2, second))]
+    put_lines(near_ref, depth, lines)
     items = []
     for first, last in ((0, rows - 1), (1, rows - 2)):
         items.append(jnp.where(after, k_ref[:, last, :], k_ref[:, first, :]))
@@ -448,11 +460,11 @@
     chunks = cols // 128
     packed_far = pltpu.VMEM(((2 * depth + 4) * chunks, 128), F32)
     packed_near = pltpu.VMEM(((2 * depth + 3) * chunks, 128), F32)
-    own_far, picked, inverse = pl.pallas_call(
+    own_far, index, inverse = pl.pallas_call(
         load_kernel,
         out_shape=(
             packed_far,
-            pltpu.VMEM((STEPS, rows, cols), F32),
+            pltpu.VMEM((STEPS, 128), jnp.int32),
             pltpu.VMEM((depth, depth), F32),
         ),
         in_specs=[HBM] * 4,
@@ -472,14 +484,14 @@
         in_hbm(depth_inverse[0]),
     )
     k = conductance[0]
-    own_near = pl.pallas_call(
+    own_near, picked = pl.pallas_call(
         pack_kernel,
-        out_shape=packed_near,
-        in_specs=[VMEM] * 2,
-        out_specs=VMEM,
+        out_shape=(packed_near, pltpu.VMEM((STEPS, rows, cols), F32)),
+        in_specs=[VMEM] * 3,
+        out_specs=(VMEM,) * 2,
         compiler_params=GRANT,
         name="pack",
-    )(k, picked)
+    )(k, surface_residual[0], index)
     across = [(i, i + 1) for i in range(1, spans - 1, 2)]
     within = [(i, i + 1) for i in range(0, spans - 1, 2)]
     near = lax.ppermute(own_near, "span", within + [(b, a) for a, b in within])

time: 23.9 us -> 23.9 us (level)
  no operation moved by 1% of the time
where the time goes in v21:
time: 23.9 us; the launch traced here: 23.7 us
  blocking collectives  12.2 us (51%)
  Pallas kernels  5.75 us (24%)
  starting transfers between devices  5.03 us (21%)
  between operations  0.73 us (3%)
    all_to_all x1, blocking collectives, per_device(): pieces = lax.all_to_all(partial, ('blade', 'span'), 0, 0, tiled=True)  12.2 us
    ppermute x1, starting transfers between devices, per_device(): near = lax.ppermute(own_near, 'span', within + [(b, a) for a, b in within])  4.36 us
    pallas_call x1, Pallas kernels, per_device(): pl.pallas_call(functools.partial(base_kernel, scale), out_shape=(pltpu.VM...  1.81 us
    pallas_call x1, Pallas kernels, per_device(): pl.pallas_call(functools.partial(near_kernel, scale), out_shape=(pltpu.HB...  1.42 us
    pallas_call x1, Pallas kernels, per_device(): pl.pallas_call(load_kernel, out_shape=(packed_far, pltpu.VMEM((STEPS, 128...  1.07 us
    pallas_call x1, Pallas kernels, per_device(): pl.pallas_call(functools.partial(far_kernel, scale), out_shape=(pltpu.VME...  0.7 us
    pallas_call x1, Pallas kernels, per_device(): pl.pallas_call(finish_kernel, out_shape=(pltpu.HBM((depth, rows, cols), F...  0.68 us
    ppermute x1, starting transfers between devices, per_device(): far = lax.ppermute(own_far, 'span', across + [(b, a) for a, b in across])  0.67 us
  transfers between devices with their start and end apart: 2, of which 0 were waited for; matrix products, arithmetic and copies ran while one was open for 0% of the time, Pallas kernels for 14%

profile of v21, /device:TPU:0, one launch (start us, length us, event | category | flops | bytes accessed | tf_op | source)
XLA Modules:
  0.0 23.7 jit_solution(10079836310535002424)
XLA Ops:
  0.6 0.0 copy-start
  0.6 0.0 copy-start.1
  0.7 1.1 %load.1 = (f32[272,128]{1,0:T(8,128)S(1)}, s32[3,128]{1,0:T(4,128)S(1)}, f32[32,32]{1,0:T(8,128)S(1)}) custom-call(s32[3]{0:T(128)} %frame_hbm.1, f32[32,8,512]{2,1,0:T(8,128)} %bitcast.6, f32[4,8,512]{2,1,0:T(8,128)} %bitcast.9, f32[32,32]{1,0:T(8,128)} %bitcast.13), custom_call_target="tpu_custom_call" | custom-call | tf_op jit(solution)/shard_map/load/pallas_call | solution.py:463
  1.7 0.7 %collective-permute-start.1 = (f32[272,128]{1,0:T(8,128)S(1)}, f32[272,128]{1,0:T(8,128)S(1)}, u32[]{:S(2)}, u32[]{:S(2)}) collective-permute-start(f32[272,128]{1,0:T(8,128)S(1)} %get-tuple-element.33.own_ref), channel_id=1, source_target_pairs={{1,2},{2,1},{5,6},{6,5},{9,10},{10,9},{13,14},{14,13},{17,18},{18,... | collective-permute-start | bytes 417800 | tf_op jit(solution)/shard_map/ppermute | solution.py:498
  2.4 0.0 copy-done
  2.4 0.0 copy-done.1
  2.4 0.1 pack.1
  2.5 4.4 %collective-permute-start = (f32[268,128]{1,0:T(8,128)S(1)}, f32[268,128]{1,0:T(8,128)S(1)}, u32[]{:S(2)}, u32[]{:S(2)}) collective-permute-start(f32[268,128]{1,0:T(8,128)S(1)} %get-tuple-element.31.own_ref), channel_id=1, source_target_pairs={{0,1},{2,3},{1,0},{3,2},{4,5},{6,7},{5,4},{7,6},{8,9},{10,11},{9,8... | collective-permute-start | bytes 411656 | tf_op jit(solution)/shard_map/ppermute | solution.py:497
  6.9 1.8 %base.1 = (f32[1024,128]{1,0:T(8,128)S(1)}, f32[2,32,512]{2,1,0:T(8,128)S(1)}, f32[3,8,512]{2,1,0:T(8,128)S(1)}, s32[4,8]{1,0:T(4,128)S(1)}, f32[2,32,512]{2,1,0...) custom-call(f32[32,8,512]{2,1,0:T(8,128)S(1)} %bitcast.8, ...), custom_call_target="tpu_custom_call" | custom-call | tf_op jit(solution)/shard_map/base/pallas_call | solution.py:501
  8.7 0.0 collective-permute-done.got_ref
  8.7 1.4 %near.1 = (f32[32,8,512]{2,1,0:T(8,128)}, f32[32,1,64]{2,1,0:T(1,128)S(1)}) custom-call(f32[32,32]{1,0:T(8,128)S(1)} %get-tuple-element.21.d_ref, f32[3,8,512]{2,1,0:T(8,128)S(1)} %get-tuple-element.24.excess_ref, f32[2,32,512]{2,1,0:T(8,128)S(1)} %get-tuple-element.25.edge_ref, bf16[64,192]{1,0:T(8,128)(2,1)S(1)} %get-tuple-element.26.pair_ref, ...), custom_call_target="tpu_custom_call" | custom-call | tf_op jit(solution)/shard_map/near/pallas_call | solution.py:529
  10.1 0.0 collective-permute-done.1.got_ref
  10.1 0.7 %far.1 = (f32[2,32,512]{2,1,0:T(8,128)S(1)}, f32[32,1,64]{2,1,0:T(1,128)S(1)}) custom-call(f32[272,128]{1,0:T(8,128)S(1)} %get-tuple-element.33.own_ref, f32[272,128]{1,0:T(8,128)S(1)} %collective-permute-done.1.got_ref, f32[32,32]{1,0:T(8,128)S(1)} %get-tuple-element.21.d_ref, f32[3,8,512]{2,1,0:T(8,128)S(1)} %get-tuple-element.24.excess_ref, ...), custom_call_target="tpu_custom_call" | custom-call | tf_op jit(solution)/shard_map/far/pallas_call | solution.py:542
  10.8 12.2 %all_to_all.5.got_ref = f32[32,1,64]{2,1,0:T(1,128)S(1)} all-to-all(f32[32,1,64]{2,1,0:T(1,128)S(1)} %get-tuple-element.37), channel_id=1, replica_groups=mesh['blade'=8,'span'=4] {'blade','span'}, dimensions={0} | all-to-all | bytes 16384 | tf_op jit(solution)/shard_map/all_to_all | solution.py:551
  23.1 0.7 %finish.1 = (f32[32,8,512]{2,1,0:T(8,128)}, f32[64]{0:T(128)}) custom-call(f32[32,8,512]{2,1,0:T(8,128)} %get-tuple-element.32._, f32[2,32,512]{2,1,0:T(8,128)S(1)} %get-tuple-element.36.two_ref, f32[32,1,64]{2,1,0:T(1,128)S(1)} %all_to_all.5.got_ref), custom_call_target="tpu_custom_call", output_to_operand_aliasing={{0}: (0, {})} | custom-call | tf_op jit(solution)/shard_map/finish/pallas_call | solution.py:552
Async XLA Ops:
  0.6 1.8 %copy-start = (f32[1,32,8,512]{3,2,1,0:T(8,128)S(1)}, f32[1,32,8,512]{3,2,1,0:T(8,128)}, u32[]{:S(2)}) copy-start(f32[1,32,8,512]{3,2,1,0:T(8,128)} %param.6) | copy-start | bytes 1572868
  0.6 1.8 %copy-start.1 = (f32[1,4,8,512]{3,2,1,0:T(8,128)S(1)}, f32[1,4,8,512]{3,2,1,0:T(8,128)}, u32[]{:S(2)}) copy-start(f32[1,4,8,512]{3,2,1,0:T(8,128)} %param.8) | copy-start | bytes 196612
  1.7 8.4 %collective-permute-start.1 = (f32[272,128]{1,0:T(8,128)S(1)}, f32[272,128]{1,0:T(8,128)S(1)}, u32[]{:S(2)}, u32[]{:S(2)}) collective-permute-start(f32[272,128]{1,0:T(8,128)S(1)} %get-tuple-element.33.own_ref), channel_id=1, source_target_pairs={{1,2},{2,1},{5,6},{6,5},{9,10},{10,9},{13,14},{14,13},{17,18},{18,... | collective-permute-start | bytes 417800 | tf_op jit(solution)/shard_map/ppermute | solution.py:498
  2.5 6.2 %collective-permute-start = (f32[268,128]{1,0:T(8,128)S(1)}, f32[268,128]{1,0:T(8,128)S(1)}, u32[]{:S(2)}, u32[]{:S(2)}) collective-permute-start(f32[268,128]{1,0:T(8,128)S(1)} %get-tuple-element.31.own_ref), channel_id=1, source_target_pairs={{0,1},{2,3},{1,0},{3,2},{4,5},{6,7},{5,4},{7,6},{8,9},{10,11},{9,8... | collective-permute-start | bytes 411656 | tf_op jit(solution)/shard_map/ppermute | solution.py:497

commit v22 on v20

--- a/solution.py
+++ b/solution.py
@@ -292,7 +292,15 @@
     )
 
 
-def correction(n, got, own, d_ref, edge_ref, pair_ref):
+def own_weights(own, depth, cols):
+    half = 0.5 * packed_field(own, depth, cols, 0)
+    inner = half + 0.5 * packed_field(own, depth, cols, 1)
+    w_next = half + shift_next(half, 1)
+    w_prev = half + shift_prev(half, 1, 0.0)
+    return half, inner, w_next, w_prev, 1.0 - (w_next + w_prev) - (half + inner)
+
+
+def correction(n, got, own, weights, d_ref, edge_ref, pair_ref):
     _, depth, cols = edge_ref.shape
     _, inside = sides()[n]
     factor = d_ref[:, 0:1]
@@ -302,10 +310,7 @@
     frame = packed_line(got, depth, cols, 1)
     f_next = packed_line(got, depth, cols, 2)
     f_own = packed_line(own, depth, cols, 0)
-    half_own = 0.5 * packed_field(own, depth, cols, 0)
-    inner = half_own + 0.5 * packed_field(own, depth, cols, 1)
-    w_next = half_own + shift_next(half_own, 1)
-    w_prev = half_own + shift_prev(half_own, 1, 0.0)
+    half_own, inner, w_next, w_prev, centre = weights
     face = half + half_own
     moved = (
         f
@@ -320,7 +325,7 @@
     e = found[0:depth]
     outer = found[depth:]
     change = (
-        (1.0 - (w_next + w_prev) - (half_own + inner)) * e
+        centre * e
         + w_next * shift_next(e, 1)
         + w_prev * shift_prev(e, 1, 0.0)
         + face * outer
@@ -353,10 +358,12 @@
     place_ref,
     base_ref,
     contribution_ref,
+    own_far_ref,
     own_ref,
     got_ref,
     adj_hbm,
     part_ref,
+    far_weights_ref,
     adj_ref,
     map_ref,
     sems,
@@ -365,7 +372,9 @@
     map_copy.start()
     depth, rows, cols = adj_ref.shape
     size = depth * rows
-    sources, surface = correction(0, got_ref, own_ref, d_ref, edge_ref, pair_ref)
+    sources, surface = correction(
+        0, got_ref, own_ref, own_weights(own_ref, depth, cols), d_ref, edge_ref, pair_ref
+    )
     found = dot(place_ref[...], sources)
     adj_ref[...] = (chunked(base_ref, 0, size, size) + found).reshape(depth, rows, cols)
     adj_copy = pltpu.make_async_copy(adj_ref, adj_hbm, sems.at[1])
@@ -375,6 +384,8 @@
     contribution = contribution_ref[...] + scale * (
         surface * excess_ref[1] + found[0:rows, :] * excess_ref[0]
     )
+    for n, x in enumerate(own_weights(own_far_ref, depth, cols)):
+        far_weights_ref[n] = x
     map_copy.wait()
     part_ref[...] = add_segments(
         jnp.zeros(part_ref.shape, F32), contribution, range(rows), map_ref
@@ -391,6 +402,7 @@
     edge_ref,
     pair_ref,
     map_vmem,
+    far_weights_ref,
     two_ref,
     part_in_ref,
     out_ref,
@@ -402,7 +414,9 @@
     map_copy.start()
     depth = two_ref.shape[1]
     rows = excess_ref.shape[1]
-    sources, surface = correction(1, got_ref, own_ref, d_ref, edge_ref, pair_ref)
+    sources, surface = correction(
+        1, got_ref, own_ref, [far_weights_ref[n] for n in range(5)], d_ref, edge_ref, pair_ref
+    )
     found = dot(pair_ref[...], sources)
     edge, second = far_rows(rows)
     contribution = scale * jnp.concatenate(
@@ -415,16 +429,23 @@
     )
     map_copy.wait()
     part_ref[...] = add_segments(part_in_ref[...], contribution, (edge, second), map_ref)
-    out_ref[...] = two_ref[...] + found.reshape(two_ref.shape)
+    after = sides()[1][0]
+    new_edge = two_ref[0] + found[0:depth]
+    new_second = two_ref[1] + found[depth:]
+    out_ref[:, 0, :] = jnp.where(after, new_second, new_edge)
+    out_ref[:, 1, :] = jnp.where(after, new_edge, new_second)
 
 
 def finish_kernel(_, two_ref, got_ref, adj_hbm, out_hbm, out_ref, sems):
-    copies = []
-    for n, row in enumerate(far_rows(adj_hbm.shape[1])):
-        copies.append(pltpu.make_async_copy(two_ref.at[n], adj_hbm.at[:, row, :], sems.at[n]))
-        copies[-1].start()
+    first = jnp.where(sides()[1][0], adj_hbm.shape[1] - 2, 0)
+    copies = [
+        pltpu.make_async_copy(
+            two_ref.at[:, 0:2, :], adj_hbm.at[:, pl.ds(first, 2), :], sems.at[0]
+        )
+    ]
+    copies[0].start()
     out_ref[...] = jnp.sum(got_ref[:, 0, :], axis=0)
-    copies.append(pltpu.make_async_copy(out_ref, out_hbm, sems.at[2]))
+    copies.append(pltpu.make_async_copy(out_ref, out_hbm, sems.at[1]))
     copies[-1].start()
     for copy in copies:
         copy.wait()
@@ -514,11 +535,15 @@
     )(k, picked, inverse, in_hbm(surface_excess[0]), in_hbm(segment_map.T))
     fixed = (inverse, excess, edge, pair, ids)
     sums = pltpu.VMEM((devices, 1, lanes), F32)
-    adjoint, partial = pl.pallas_call(
+    adjoint, partial, far_weights = pl.pallas_call(
         functools.partial(near_kernel, scale),
-        out_shape=(pltpu.HBM((depth, rows, cols), F32), sums),
-        in_specs=[VMEM] * 10,
-        out_specs=(HBM, VMEM),
+        out_shape=(
+            pltpu.HBM((depth, rows, cols), F32),
+            sums,
+            pltpu.VMEM((5, depth, cols), F32),
+        ),
+        in_specs=[VMEM] * 11,
+        out_specs=(HBM, VMEM, VMEM),
         scratch_shapes=[
             field,
             pltpu.SMEM((blocks, rows), jnp.int32),
@@ -526,23 +551,23 @@
         ],
         compiler_params=GRANT,
         name="near",
-    )(*fixed, place, base, contribution, own_near, near)
+    )(*fixed, place, base, contribution, own_far, own_near, near)
     two, partial = pl.pallas_call(
         functools.partial(far_kernel, scale),
-        out_shape=(pltpu.VMEM((2, depth, cols), F32), sums),
-        in_specs=[VMEM] * 9,
+        out_shape=(field, sums),
+        in_specs=[VMEM] * 10,
         out_specs=(VMEM,) * 2,
         scratch_shapes=[pltpu.SMEM((blocks, rows), jnp.int32), pltpu.SemaphoreType.DMA],
         compiler_params=GRANT,
         name="far",
-    )(own_far, far, *fixed, two, partial)
+    )(own_far, far, *fixed, far_weights, two, partial)
     pieces = lax.all_to_all(partial, ("blade", "span"), 0, 0, tiled=True)
     adjoint, owned = pl.pallas_call(
         finish_kernel,
         out_shape=(pltpu.HBM((depth, rows, cols), F32), pltpu.HBM((lanes,), F32)),
         in_specs=[HBM, VMEM, VMEM],
         out_specs=(HBM,) * 2,
-        scratch_shapes=[pltpu.VMEM((lanes,), F32), pltpu.SemaphoreType.DMA((3,))],
+        scratch_shapes=[pltpu.VMEM((lanes,), F32), pltpu.SemaphoreType.DMA((2,))],
         input_output_aliases={0: 0},
         compiler_params=GRANT,
         name="finish",

time: 23.9 us -> 23.9 us (level)
  no operation moved by 1% of the time
where the time goes in v22:
time: 23.9 us; the launch traced here: 23.7 us
  blocking collectives  12.3 us (51%)
  Pallas kernels  5.74 us (24%)
  starting transfers between devices  5.03 us (21%)
  between operations  0.71 us (3%)
    all_to_all x1, blocking collectives, per_device(): pieces = lax.all_to_all(partial, ('blade', 'span'), 0, 0, tiled=True)  12.3 us
    ppermute x1, starting transfers between devices, per_device(): near = lax.ppermute(own_near, 'span', within + [(b, a) for a, b in within])  4.36 us
    pallas_call x1, Pallas kernels, per_device(): pl.pallas_call(functools.partial(base_kernel, scale), out_shape=(pltpu.VM...  1.8 us
    pallas_call x1, Pallas kernels, per_device(): pl.pallas_call(functools.partial(near_kernel, scale), out_shape=(pltpu.HB...  1.42 us
    pallas_call x1, Pallas kernels, per_device(): pl.pallas_call(load_kernel, out_shape=(packed_far, pltpu.VMEM((STEPS, row...  1.07 us
    pallas_call x1, Pallas kernels, per_device(): pl.pallas_call(functools.partial(far_kernel, scale), out_shape=(field, su...  0.7 us
    pallas_call x1, Pallas kernels, per_device(): pl.pallas_call(finish_kernel, out_shape=(pltpu.HBM((depth, rows, cols), F...  0.69 us
    ppermute x1, starting transfers between devices, per_device(): far = lax.ppermute(own_far, 'span', across + [(b, a) for a, b in across])  0.67 us
  transfers between devices with their start and end apart: 2, of which 0 were waited for; matrix products, arithmetic and copies ran while one was open for 0% of the time, Pallas kernels for 14%

profile of v22, /device:TPU:0, one launch (start us, length us, event | category | flops | bytes accessed | tf_op | source)
XLA Modules:
  0.0 23.7 jit_solution(11950789844122956090)
XLA Ops:
  0.6 0.0 copy-start
  0.6 1.1 %load.1 = (f32[272,128]{1,0:T(8,128)S(1)}, f32[3,8,512]{2,1,0:T(8,128)S(1)}, f32[32,32]{1,0:T(8,128)S(1)}) custom-call(s32[3]{0:T(128)} %frame_hbm.1, f32[32,8,512]{2,1,0:T(8,128)} %bitcast.6, f32[4,8,512]{2,1,0:T(8,128)} %bitcast.10, f32[32,32]{1,0:T(8,128)} %bitcast.12), custom_call_target="tpu_custom_call" | custom-call | tf_op jit(solution)/shard_map/load/pallas_call | solution.py:472
  1.7 0.7 %collective-permute-start.1 = (f32[272,128]{1,0:T(8,128)S(1)}, f32[272,128]{1,0:T(8,128)S(1)}, u32[]{:S(2)}, u32[]{:S(2)}) collective-permute-start(f32[272,128]{1,0:T(8,128)S(1)} %get-tuple-element.29.own_far_ref.own_ref), channel_id=1, source_target_pairs={{1,2},{2,1},{5,6},{6,5},{9,10},{10,9},{13,14},{14,13},{17,18},{18,... | collective-permute-start | bytes 417800 | tf_op jit(solution)/shard_map/ppermute | solution.py:507
  2.4 0.0 copy-done
  2.4 0.1 pack.1.own_ref
  2.5 4.4 %collective-permute-start = (f32[268,128]{1,0:T(8,128)S(1)}, f32[268,128]{1,0:T(8,128)S(1)}, u32[]{:S(2)}, u32[]{:S(2)}) collective-permute-start(f32[268,128]{1,0:T(8,128)S(1)} %pack.1.own_ref), channel_id=1, source_target_pairs={{0,1},{2,3},{1,0},{3,2},{4,5},{6,7},{5,4},{7,6},{8,9},{10,11},{9,8... | collective-permute-start | bytes 411656 | tf_op jit(solution)/shard_map/ppermute | solution.py:506
  6.8 1.8 %base.1 = (f32[1024,128]{1,0:T(8,128)S(1)}, f32[2,32,512]{2,1,0:T(8,128)S(1)}, f32[3,8,512]{2,1,0:T(8,128)S(1)}, s32[4,8]{1,0:T(4,128)S(1)}, f32[2,32,512]{2,1,0...) custom-call(f32[32,8,512]{2,1,0:T(8,128)S(1)} %bitcast.8, ...), custom_call_target="tpu_custom_call" | custom-call | tf_op jit(solution)/shard_map/base/pallas_call | solution.py:510
  8.6 0.0 collective-permute-done.got_ref
  8.6 1.4 %near.1 = (f32[32,8,512]{2,1,0:T(8,128)}, f32[32,1,64]{2,1,0:T(1,128)S(1)}, f32[5,32,512]{2,1,0:T(8,128)S(1)}) custom-call(f32[32,32]{1,0:T(8,128)S(1)} %get-tuple-element.20.d_ref, f32[3,8,512]{2,1,0:T(8,128)S(1)} %get-tuple-element.22.excess_ref, f32[2,32,512]{2,1,0:T(8,128)S(1)} %get-tuple-element.23.edge_ref, ...), custom_call_target="tpu_custom_call" | custom-call | tf_op jit(solution)/shard_map/near/pallas_call | solution.py:538
  10.1 0.0 collective-permute-done.1.got_ref
  10.1 0.7 %far.1 = (f32[32,8,512]{2,1,0:T(8,128)S(1)}, f32[32,1,64]{2,1,0:T(1,128)S(1)}) custom-call(f32[272,128]{1,0:T(8,128)S(1)} %get-tuple-element.29.own_far_ref.own_ref, f32[272,128]{1,0:T(8,128)S(1)} %collective-permute-done.1.got_ref, f32[32,32]{1,0:T(8,128)S(1)} %get-tuple-element.20.d_ref, f32[3,8,512]{2,1,0:T(8,128)S(1)} %get-tuple-element.22.excess_ref, ...), custom_call_target="tpu_custom_call" | custom-call | tf_op jit(solution)/shard_map/far/pallas_call | solution.py:555
  10.8 12.3 %all_to_all.5.got_ref = f32[32,1,64]{2,1,0:T(1,128)S(1)} all-to-all(f32[32,1,64]{2,1,0:T(1,128)S(1)} %get-tuple-element.35), channel_id=1, replica_groups=mesh['blade'=8,'span'=4] {'blade','span'}, dimensions={0} | all-to-all | bytes 16384 | tf_op jit(solution)/shard_map/all_to_all | solution.py:564
  23.1 0.7 %finish.1 = (f32[32,8,512]{2,1,0:T(8,128)}, f32[64]{0:T(128)}) custom-call(f32[32,8,512]{2,1,0:T(8,128)} %get-tuple-element.30._, f32[32,8,512]{2,1,0:T(8,128)S(1)} %get-tuple-element.34.two_ref, f32[32,1,64]{2,1,0:T(1,128)S(1)} %all_to_all.5.got_ref), custom_call_target="tpu_custom_call", output_to_operand_aliasing={{0}: (0, {})} | custom-call | tf_op jit(solution)/shard_map/finish/pallas_call | solution.py:565
Async XLA Ops:
  0.6 1.8 %copy-start = (f32[1,32,8,512]{3,2,1,0:T(8,128)S(1)}, f32[1,32,8,512]{3,2,1,0:T(8,128)}, u32[]{:S(2)}) copy-start(f32[1,32,8,512]{3,2,1,0:T(8,128)} %param.6) | copy-start | bytes 1572868
  1.7 8.4 %collective-permute-start.1 = (f32[272,128]{1,0:T(8,128)S(1)}, f32[272,128]{1,0:T(8,128)S(1)}, u32[]{:S(2)}, u32[]{:S(2)}) collective-permute-start(f32[272,128]{1,0:T(8,128)S(1)} %get-tuple-element.29.own_far_ref.own_ref), channel_id=1, source_target_pairs={{1,2},{2,1},{5,6},{6,5},{9,10},{10,9},{13,14},{14,13},{17,18},{18,... | collective-permute-start | bytes 417800 | tf_op jit(solution)/shard_map/ppermute | solution.py:507
  2.5 6.2 %collective-permute-start = (f32[268,128]{1,0:T(8,128)S(1)}, f32[268,128]{1,0:T(8,128)S(1)}, u32[]{:S(2)}, u32[]{:S(2)}) collective-permute-start(f32[268,128]{1,0:T(8,128)S(1)} %pack.1.own_ref), channel_id=1, source_target_pairs={{0,1},{2,3},{1,0},{3,2},{4,5},{6,7},{5,4},{7,6},{8,9},{10,11},{9,8... | collective-permute-start | bytes 411656 | tf_op jit(solution)/shard_map/ppermute | solution.py:506

commit v23 on v20

--- a/solution.py
+++ b/solution.py
@@ -329,9 +329,8 @@
     return right_three(jnp.concatenate([change, inner * e], axis=0)), e[0:1, :]
 
 
-def add_segments(total, contribution, picked_rows, map_ref):
-    owners, _, lanes = total.shape
-    shape = (owners, 128)
+def add_segments(lanes, total, contribution, picked_rows, map_ref):
+    shape = (total.shape[0], 128)
     lane = iota(shape, 1)
     segment = jnp.where(lane < lanes, iota(shape, 0) * lanes + lane, -1)
     found = jnp.zeros(shape, F32)
@@ -340,10 +339,11 @@
         sums = jnp.sum(part, axis=1, keepdims=True)
         for n, row in enumerate(picked_rows):
             found += jnp.where(segment == map_ref[block, row], sums[n : n + 1, :], 0.0)
-    return total + found[:, None, :lanes]
+    return total + found[:, None, :]
 
 
 def near_kernel(
+    lanes,
     scale,
     d_ref,
     excess_ref,
@@ -377,12 +377,13 @@
     )
     map_copy.wait()
     part_ref[...] = add_segments(
-        jnp.zeros(part_ref.shape, F32), contribution, range(rows), map_ref
+        lanes, jnp.zeros(part_ref.shape, F32), contribution, range(rows), map_ref
     )
     adj_copy.wait()
 
 
 def far_kernel(
+    lanes,
     scale,
     own_ref,
     got_ref,
@@ -414,7 +415,7 @@
         axis=0,
     )
     map_copy.wait()
-    part_ref[...] = add_segments(part_in_ref[...], contribution, (edge, second), map_ref)
+    part_ref[...] = add_segments(lanes, part_in_ref[...], contribution, (edge, second), map_ref)
     out_ref[...] = two_ref[...] + found.reshape(two_ref.shape)
 
 
@@ -423,7 +424,7 @@
     for n, row in enumerate(far_rows(adj_hbm.shape[1])):
         copies.append(pltpu.make_async_copy(two_ref.at[n], adj_hbm.at[:, row, :], sems.at[n]))
         copies[-1].start()
-    out_ref[...] = jnp.sum(got_ref[:, 0, :], axis=0)
+    out_ref[...] = jnp.sum(got_ref[:, 0, : out_ref.shape[0]], axis=0)
     copies.append(pltpu.make_async_copy(out_ref, out_hbm, sems.at[2]))
     copies[-1].start()
     for copy in copies:
@@ -513,9 +514,9 @@
         name="base",
     )(k, picked, inverse, in_hbm(surface_excess[0]), in_hbm(segment_map.T))
     fixed = (inverse, excess, edge, pair, ids)
-    sums = pltpu.VMEM((devices, 1, lanes), F32)
+    sums = pltpu.VMEM((devices, 1, 128), F32)
     adjoint, partial = pl.pallas_call(
-        functools.partial(near_kernel, scale),
+        functools.partial(near_kernel, lanes, scale),
         out_shape=(pltpu.HBM((depth, rows, cols), F32), sums),
         in_specs=[VMEM] * 10,
         out_specs=(HBM, VMEM),
@@ -528,7 +529,7 @@
         name="near",
     )(*fixed, place, base, contribution, own_near, near)
     two, partial = pl.pallas_call(
-        functools.partial(far_kernel, scale),
+        functools.partial(far_kernel, lanes, scale),
         out_shape=(pltpu.VMEM((2, depth, cols), F32), sums),
         in_specs=[VMEM] * 9,
         out_specs=(VMEM,) * 2,

time: 23.9 us -> 23.9 us (level)
  no operation moved by 1% of the time
where the time goes in v23:
time: 23.9 us; the launch traced here: 23.7 us
  blocking collectives  12.3 us (51%)
  Pallas kernels  5.74 us (24%)
  starting transfers between devices  5.03 us (21%)
  between operations  0.71 us (3%)
    all_to_all x1, blocking collectives, per_device(): pieces = lax.all_to_all(partial, ('blade', 'span'), 0, 0, tiled=True)  12.3 us
    ppermute x1, starting transfers between devices, per_device(): near = lax.ppermute(own_near, 'span', within + [(b, a) for a, b in within])  4.36 us
    pallas_call x1, Pallas kernels, per_device(): pl.pallas_call(functools.partial(base_kernel, scale), out_shape=(pltpu.VM...  1.81 us
    pallas_call x1, Pallas kernels, per_device(): pl.pallas_call(functools.partial(near_kernel, lanes, scale), out_shape=(p...  1.42 us
    pallas_call x1, Pallas kernels, per_device(): pl.pallas_call(load_kernel, out_shape=(packed_far, pltpu.VMEM((STEPS, row...  1.07 us
    pallas_call x1, Pallas kernels, per_device(): pl.pallas_call(functools.partial(far_kernel, lanes, scale), out_shape=(pl...  0.7 us
    pallas_call x1, Pallas kernels, per_device(): pl.pallas_call(finish_kernel, out_shape=(pltpu.HBM((depth, rows, cols), F...  0.68 us
    ppermute x1, starting transfers between devices, per_device(): far = lax.ppermute(own_far, 'span', across + [(b, a) for a, b in across])  0.67 us
  transfers between devices with their start and end apart: 2, of which 0 were waited for; matrix products, arithmetic and copies ran while one was open for 0% of the time, Pallas kernels for 14%

profile of v23, /device:TPU:0, one launch (start us, length us, event | category | flops | bytes accessed | tf_op | source)
XLA Modules:
  0.0 23.7 jit_solution(12103502007460529296)
XLA Ops:
  0.6 0.0 copy-start
  0.6 1.1 %load.1 = (f32[272,128]{1,0:T(8,128)S(1)}, f32[3,8,512]{2,1,0:T(8,128)S(1)}, f32[32,32]{1,0:T(8,128)S(1)}) custom-call(s32[3]{0:T(128)} %frame_hbm.1, f32[32,8,512]{2,1,0:T(8,128)} %bitcast.6, f32[4,8,512]{2,1,0:T(8,128)} %bitcast.10, f32[32,32]{1,0:T(8,128)} %bitcast.12), custom_call_target="tpu_custom_call" | custom-call | tf_op jit(solution)/shard_map/load/pallas_call | solution.py:452
  1.7 0.7 %collective-permute-start.1 = (f32[272,128]{1,0:T(8,128)S(1)}, f32[272,128]{1,0:T(8,128)S(1)}, u32[]{:S(2)}, u32[]{:S(2)}) collective-permute-start(f32[272,128]{1,0:T(8,128)S(1)} %get-tuple-element.29.own_ref), channel_id=1, source_target_pairs={{1,2},{2,1},{5,6},{6,5},{9,10},{10,9},{13,14},{14,13},{17,18},{18,... | collective-permute-start | bytes 417800 | tf_op jit(solution)/shard_map/ppermute | solution.py:487
  2.4 0.0 copy-done
  2.4 0.1 pack.1.own_ref
  2.5 4.4 %collective-permute-start = (f32[268,128]{1,0:T(8,128)S(1)}, f32[268,128]{1,0:T(8,128)S(1)}, u32[]{:S(2)}, u32[]{:S(2)}) collective-permute-start(f32[268,128]{1,0:T(8,128)S(1)} %pack.1.own_ref), channel_id=1, source_target_pairs={{0,1},{2,3},{1,0},{3,2},{4,5},{6,7},{5,4},{7,6},{8,9},{10,11},{9,8... | collective-permute-start | bytes 411656 | tf_op jit(solution)/shard_map/ppermute | solution.py:486
  6.8 1.8 %base.1 = (f32[1024,128]{1,0:T(8,128)S(1)}, f32[2,32,512]{2,1,0:T(8,128)S(1)}, f32[3,8,512]{2,1,0:T(8,128)S(1)}, s32[4,8]{1,0:T(4,128)S(1)}, f32[2,32,512]{2,1,0...) custom-call(f32[32,8,512]{2,1,0:T(8,128)S(1)} %bitcast.8, ...), custom_call_target="tpu_custom_call" | custom-call | tf_op jit(solution)/shard_map/base/pallas_call | solution.py:490
  8.6 0.0 collective-permute-done.got_ref
  8.7 1.4 %near.1 = (f32[32,8,512]{2,1,0:T(8,128)}, f32[32,1,128]{2,1,0:T(1,128)S(1)}) custom-call(f32[32,32]{1,0:T(8,128)S(1)} %get-tuple-element.19.d_ref, f32[3,8,512]{2,1,0:T(8,128)S(1)} %get-tuple-element.21.excess_ref, f32[2,32,512]{2,1,0:T(8,128)S(1)} %get-tuple-element.22.edge_ref, bf16[64,192]{1,0:T(8,128)(2,1)S(1)} %get-tuple-element.23.pair_ref, ...), custom_call_target="tpu_custom_call" | custom-call | tf_op jit(solution)/shard_map/near/pallas_call | solution.py:518
  10.1 0.0 collective-permute-done.1.got_ref
  10.1 0.7 %far.1 = (f32[2,32,512]{2,1,0:T(8,128)S(1)}, f32[32,1,128]{2,1,0:T(1,128)S(1)}) custom-call(f32[272,128]{1,0:T(8,128)S(1)} %get-tuple-element.29.own_ref, f32[272,128]{1,0:T(8,128)S(1)} %collective-permute-done.1.got_ref, f32[32,32]{1,0:T(8,128)S(1)} %get-tuple-element.19.d_ref, f32[3,8,512]{2,1,0:T(8,128)S(1)} %get-tuple-element.21.excess_ref, ...), custom_call_target="tpu_custom_call" | custom-call | tf_op jit(solution)/shard_map/far/pallas_call | solution.py:531
  10.8 12.3 %all_to_all.5.got_ref = f32[32,1,128]{2,1,0:T(1,128)S(1)} all-to-all(f32[32,1,128]{2,1,0:T(1,128)S(1)} %get-tuple-element.33), channel_id=1, replica_groups=mesh['blade'=8,'span'=4] {'blade','span'}, dimensions={0} | all-to-all | bytes 32768 | tf_op jit(solution)/shard_map/all_to_all | solution.py:540
  23.1 0.7 %finish.1 = (f32[32,8,512]{2,1,0:T(8,128)}, f32[64]{0:T(128)}) custom-call(f32[32,8,512]{2,1,0:T(8,128)} %get-tuple-element.28._, f32[2,32,512]{2,1,0:T(8,128)S(1)} %get-tuple-element.32.two_ref, f32[32,1,128]{2,1,0:T(1,128)S(1)} %all_to_all.5.got_ref), custom_call_target="tpu_custom_call", output_to_operand_aliasing={{0}: (0, {})} | custom-call | tf_op jit(solution)/shard_map/finish/pallas_call | solution.py:541
Async XLA Ops:
  0.6 1.8 %copy-start = (f32[1,32,8,512]{3,2,1,0:T(8,128)S(1)}, f32[1,32,8,512]{3,2,1,0:T(8,128)}, u32[]{:S(2)}) copy-start(f32[1,32,8,512]{3,2,1,0:T(8,128)} %param.6) | copy-start | bytes 1572868
  1.7 8.4 %collective-permute-start.1 = (f32[272,128]{1,0:T(8,128)S(1)}, f32[272,128]{1,0:T(8,128)S(1)}, u32[]{:S(2)}, u32[]{:S(2)}) collective-permute-start(f32[272,128]{1,0:T(8,128)S(1)} %get-tuple-element.29.own_ref), channel_id=1, source_target_pairs={{1,2},{2,1},{5,6},{6,5},{9,10},{10,9},{13,14},{14,13},{17,18},{18,... | collective-permute-start | bytes 417800 | tf_op jit(solution)/shard_map/ppermute | solution.py:487
  2.5 6.2 %collective-permute-start = (f32[268,128]{1,0:T(8,128)S(1)}, f32[268,128]{1,0:T(8,128)S(1)}, u32[]{:S(2)}, u32[]{:S(2)}) collective-permute-start(f32[268,128]{1,0:T(8,128)S(1)} %pack.1.own_ref), channel_id=1, source_target_pairs={{0,1},{2,3},{1,0},{3,2},{4,5},{6,7},{5,4},{7,6},{8,9},{10,11},{9,8... | collective-permute-start | bytes 411656 | tf_op jit(solution)/shard_map/ppermute | solution.py:486

commit v24 on v21

--- a/solution.py
+++ b/solution.py
@@ -129,16 +129,16 @@
     after = sides()[1][0]
     first = jnp.where(after, rows - 2, 0)
     pairs = (
+        (k_hbm.at[:, pl.ds(first, 2), :], edge_ref.at[:, 0:2, :]),
         (frame_hbm, frame_ref),
         (res_hbm.at[:, pl.ds(first, 2), :], res_ref.at[:, 0:2, :]),
-        (k_hbm.at[:, pl.ds(first, 2), :], edge_ref.at[:, 0:2, :]),
         (d_hbm, d_ref),
     )
     copies = [pltpu.make_async_copy(a, b, sems.at[n]) for n, (a, b) in enumerate(pairs)]
     for copy in copies:
         copy.start()
-    copies[0].wait()
     copies[1].wait()
+    copies[2].wait()
     for n in range(STEPS):
         index_ref[n : n + 1, :] = jnp.full((1, 128), frame_ref[n], jnp.int32)
     lines = []
@@ -146,7 +146,7 @@
         low, high = res_ref[frame_ref[step], 0:1, :], res_ref[frame_ref[step], 1:2, :]
         lines.append(jnp.where(after, high, low) if near else jnp.where(after, low, high))
     put_lines(far_ref, depth, lines)
-    copies[2].wait()
+    copies[0].wait()
     low, high = edge_ref[:, 0, :], edge_ref[:, 1, :]
     put_rows(far_ref, depth, (jnp.where(after, high, low), jnp.where(after, low, high)))
     copies[3].wait()

time: 23.9 us -> 23.9 us (level)
  no operation moved by 1% of the time
where the time goes in v24:
time: 23.9 us; the launch traced here: 23.7 us
  blocking collectives  12.2 us (51%)
  Pallas kernels  5.74 us (24%)
  starting transfers between devices  5.03 us (21%)
  between operations  0.73 us (3%)
    all_to_all x1, blocking collectives, per_device(): pieces = lax.all_to_all(partial, ('blade', 'span'), 0, 0, tiled=True)  12.2 us
    ppermute x1, starting transfers between devices, per_device(): near = lax.ppermute(own_near, 'span', within + [(b, a) for a, b in within])  4.36 us
    pallas_call x1, Pallas kernels, per_device(): pl.pallas_call(functools.partial(base_kernel, scale), out_shape=(pltpu.VM...  1.81 us
    pallas_call x1, Pallas kernels, per_device(): pl.pallas_call(functools.partial(near_kernel, scale), out_shape=(pltpu.HB...  1.42 us
    pallas_call x1, Pallas kernels, per_device(): pl.pallas_call(load_kernel, out_shape=(packed_far, pltpu.VMEM((STEPS, 128...  1.05 us
    pallas_call x1, Pallas kernels, per_device(): pl.pallas_call(functools.partial(far_kernel, scale), out_shape=(pltpu.VME...  0.7 us
    pallas_call x1, Pallas kernels, per_device(): pl.pallas_call(finish_kernel, out_shape=(pltpu.HBM((depth, rows, cols), F...  0.68 us
    ppermute x1, starting transfers between devices, per_device(): far = lax.ppermute(own_far, 'span', across + [(b, a) for a, b in across])  0.67 us
  transfers between devices with their start and end apart: 2, of which 0 were waited for; matrix products, arithmetic and copies ran while one was open for 0% of the time, Pallas kernels for 14%

profile of v24, /device:TPU:0, one launch (start us, length us, event | category | flops | bytes accessed | tf_op | source)
XLA Modules:
  0.0 23.7 jit_solution(15655846530019789233)
XLA Ops:
  0.6 0.0 copy-start
  0.6 0.0 copy-start.1
  0.7 1.1 %load.1 = (f32[272,128]{1,0:T(8,128)S(1)}, s32[3,128]{1,0:T(4,128)S(1)}, f32[32,32]{1,0:T(8,128)S(1)}) custom-call(s32[3]{0:T(128)} %frame_hbm.1, f32[32,8,512]{2,1,0:T(8,128)} %bitcast.6, f32[4,8,512]{2,1,0:T(8,128)} %bitcast.9, f32[32,32]{1,0:T(8,128)} %bitcast.13), custom_call_target="tpu_custom_call" | custom-call | tf_op jit(solution)/shard_map/load/pallas_call | solution.py:463
  1.7 0.7 %collective-permute-start.1 = (f32[272,128]{1,0:T(8,128)S(1)}, f32[272,128]{1,0:T(8,128)S(1)}, u32[]{:S(2)}, u32[]{:S(2)}) collective-permute-start(f32[272,128]{1,0:T(8,128)S(1)} %get-tuple-element.33.own_ref), channel_id=1, source_target_pairs={{1,2},{2,1},{5,6},{6,5},{9,10},{10,9},{13,14},{14,13},{17,18},{18,... | collective-permute-start | bytes 417800 | tf_op jit(solution)/shard_map/ppermute | solution.py:498
  2.4 0.0 copy-done
  2.4 0.0 copy-done.1
  2.4 0.1 pack.1
  2.5 4.4 %collective-permute-start = (f32[268,128]{1,0:T(8,128)S(1)}, f32[268,128]{1,0:T(8,128)S(1)}, u32[]{:S(2)}, u32[]{:S(2)}) collective-permute-start(f32[268,128]{1,0:T(8,128)S(1)} %get-tuple-element.31.own_ref), channel_id=1, source_target_pairs={{0,1},{2,3},{1,0},{3,2},{4,5},{6,7},{5,4},{7,6},{8,9},{10,11},{9,8... | collective-permute-start | bytes 411656 | tf_op jit(solution)/shard_map/ppermute | solution.py:497
  6.8 1.8 %base.1 = (f32[1024,128]{1,0:T(8,128)S(1)}, f32[2,32,512]{2,1,0:T(8,128)S(1)}, f32[3,8,512]{2,1,0:T(8,128)S(1)}, s32[4,8]{1,0:T(4,128)S(1)}, f32[2,32,512]{2,1,0...) custom-call(f32[32,8,512]{2,1,0:T(8,128)S(1)} %bitcast.8, ...), custom_call_target="tpu_custom_call" | custom-call | tf_op jit(solution)/shard_map/base/pallas_call | solution.py:501
  8.7 0.0 collective-permute-done.got_ref
  8.7 1.4 %near.1 = (f32[32,8,512]{2,1,0:T(8,128)}, f32[32,1,64]{2,1,0:T(1,128)S(1)}) custom-call(f32[32,32]{1,0:T(8,128)S(1)} %get-tuple-element.21.d_ref, f32[3,8,512]{2,1,0:T(8,128)S(1)} %get-tuple-element.24.excess_ref, f32[2,32,512]{2,1,0:T(8,128)S(1)} %get-tuple-element.25.edge_ref, bf16[64,192]{1,0:T(8,128)(2,1)S(1)} %get-tuple-element.26.pair_ref, ...), custom_call_target="tpu_custom_call" | custom-call | tf_op jit(solution)/shard_map/near/pallas_call | solution.py:529
  10.1 0.0 collective-permute-done.1.got_ref
  10.1 0.7 %far.1 = (f32[2,32,512]{2,1,0:T(8,128)S(1)}, f32[32,1,64]{2,1,0:T(1,128)S(1)}) custom-call(f32[272,128]{1,0:T(8,128)S(1)} %get-tuple-element.33.own_ref, f32[272,128]{1,0:T(8,128)S(1)} %collective-permute-done.1.got_ref, f32[32,32]{1,0:T(8,128)S(1)} %get-tuple-element.21.d_ref, f32[3,8,512]{2,1,0:T(8,128)S(1)} %get-tuple-element.24.excess_ref, ...), custom_call_target="tpu_custom_call" | custom-call | tf_op jit(solution)/shard_map/far/pallas_call | solution.py:542
  10.8 12.2 %all_to_all.5.got_ref = f32[32,1,64]{2,1,0:T(1,128)S(1)} all-to-all(f32[32,1,64]{2,1,0:T(1,128)S(1)} %get-tuple-element.37), channel_id=1, replica_groups=mesh['blade'=8,'span'=4] {'blade','span'}, dimensions={0} | all-to-all | bytes 16384 | tf_op jit(solution)/shard_map/all_to_all | solution.py:551
  23.0 0.7 %finish.1 = (f32[32,8,512]{2,1,0:T(8,128)}, f32[64]{0:T(128)}) custom-call(f32[32,8,512]{2,1,0:T(8,128)} %get-tuple-element.32._, f32[2,32,512]{2,1,0:T(8,128)S(1)} %get-tuple-element.36.two_ref, f32[32,1,64]{2,1,0:T(1,128)S(1)} %all_to_all.5.got_ref), custom_call_target="tpu_custom_call", output_to_operand_aliasing={{0}: (0, {})} | custom-call | tf_op jit(solution)/shard_map/finish/pallas_call | solution.py:552
Async XLA Ops:
  0.6 1.8 %copy-start = (f32[1,32,8,512]{3,2,1,0:T(8,128)S(1)}, f32[1,32,8,512]{3,2,1,0:T(8,128)}, u32[]{:S(2)}) copy-start(f32[1,32,8,512]{3,2,1,0:T(8,128)} %param.6) | copy-start | bytes 1572868
  0.6 1.8 %copy-start.1 = (f32[1,4,8,512]{3,2,1,0:T(8,128)S(1)}, f32[1,4,8,512]{3,2,1,0:T(8,128)}, u32[]{:S(2)}) copy-start(f32[1,4,8,512]{3,2,1,0:T(8,128)} %param.8) | copy-start | bytes 196612
  1.7 8.4 %collective-permute-start.1 = (f32[272,128]{1,0:T(8,128)S(1)}, f32[272,128]{1,0:T(8,128)S(1)}, u32[]{:S(2)}, u32[]{:S(2)}) collective-permute-start(f32[272,128]{1,0:T(8,128)S(1)} %get-tuple-element.33.own_ref), channel_id=1, source_target_pairs={{1,2},{2,1},{5,6},{6,5},{9,10},{10,9},{13,14},{14,13},{17,18},{18,... | collective-permute-start | bytes 417800 | tf_op jit(solution)/shard_map/ppermute | solution.py:498
  2.5 6.2 %collective-permute-start = (f32[268,128]{1,0:T(8,128)S(1)}, f32[268,128]{1,0:T(8,128)S(1)}, u32[]{:S(2)}, u32[]{:S(2)}) collective-permute-start(f32[268,128]{1,0:T(8,128)S(1)} %get-tuple-element.31.own_ref), channel_id=1, source_target_pairs={{0,1},{2,3},{1,0},{3,2},{4,5},{6,7},{5,4},{7,6},{8,9},{10,11},{9,8... | collective-permute-start | bytes 411656 | tf_op jit(solution)/shard_map/ppermute | solution.py:497

commit v25 on v20

--- a/solution.py
+++ b/solution.py
@@ -10,7 +10,7 @@
 
 STEPS = 3
 SEGS = 2048
-GROUP = 2
+GROUP = 4
 F32 = jnp.float32
 BF16 = jnp.bfloat16
 VMEM = pl.BlockSpec(memory_space=pltpu.VMEM)

time: 23.9 us -> 23.9 us (level)
  no operation moved by 1% of the time
where the time goes in v25:
time: 23.9 us; the launch traced here: 23.7 us
  blocking collectives  12.3 us (51%)
  Pallas kernels  5.74 us (24%)
  starting transfers between devices  5.03 us (21%)
  between operations  0.71 us (3%)
    all_to_all x1, blocking collectives, per_device(): pieces = lax.all_to_all(partial, ('blade', 'span'), 0, 0, tiled=True)  12.3 us
    ppermute x1, starting transfers between devices, per_device(): near = lax.ppermute(own_near, 'span', within + [(b, a) for a, b in within])  4.36 us
    pallas_call x1, Pallas kernels, per_device(): pl.pallas_call(functools.partial(base_kernel, scale), out_shape=(pltpu.VM...  1.81 us
    pallas_call x1, Pallas kernels, per_device(): pl.pallas_call(functools.partial(near_kernel, scale), out_shape=(pltpu.HB...  1.42 us
    pallas_call x1, Pallas kernels, per_device(): pl.pallas_call(load_kernel, out_shape=(packed_far, pltpu.VMEM((STEPS, row...  1.07 us
    pallas_call x1, Pallas kernels, per_device(): pl.pallas_call(functools.partial(far_kernel, scale), out_shape=(pltpu.VME...  0.7 us
    pallas_call x1, Pallas kernels, per_device(): pl.pallas_call(finish_kernel, out_shape=(pltpu.HBM((depth, rows, cols), F...  0.68 us
    ppermute x1, starting transfers between devices, per_device(): far = lax.ppermute(own_far, 'span', across + [(b, a) for a, b in across])  0.67 us
  transfers between devices with their start and end apart: 2, of which 0 were waited for; matrix products, arithmetic and copies ran while one was open for 0% of the time, Pallas kernels for 14%

profile of v25, /device:TPU:0, one launch (start us, length us, event | category | flops | bytes accessed | tf_op | source)
XLA Modules:
  0.0 23.7 jit_solution(18171832004079065298)
XLA Ops:
  0.6 0.0 copy-start
  0.6 1.1 %load.1 = (f32[272,128]{1,0:T(8,128)S(1)}, f32[3,8,512]{2,1,0:T(8,128)S(1)}, f32[32,32]{1,0:T(8,128)S(1)}) custom-call(s32[3]{0:T(128)} %frame_hbm.1, f32[32,8,512]{2,1,0:T(8,128)} %bitcast.6, f32[4,8,512]{2,1,0:T(8,128)} %bitcast.10, f32[32,32]{1,0:T(8,128)} %bitcast.12), custom_call_target="tpu_custom_call" | custom-call | tf_op jit(solution)/shard_map/load/pallas_call | solution.py:451
  1.7 0.7 %collective-permute-start.1 = (f32[272,128]{1,0:T(8,128)S(1)}, f32[272,128]{1,0:T(8,128)S(1)}, u32[]{:S(2)}, u32[]{:S(2)}) collective-permute-start(f32[272,128]{1,0:T(8,128)S(1)} %get-tuple-element.29.own_ref), channel_id=1, source_target_pairs={{1,2},{2,1},{5,6},{6,5},{9,10},{10,9},{13,14},{14,13},{17,18},{18,... | collective-permute-start | bytes 417800 | tf_op jit(solution)/shard_map/ppermute | solution.py:486
  2.4 0.0 copy-done
  2.4 0.1 pack.1.own_ref
  2.5 4.4 %collective-permute-start = (f32[268,128]{1,0:T(8,128)S(1)}, f32[268,128]{1,0:T(8,128)S(1)}, u32[]{:S(2)}, u32[]{:S(2)}) collective-permute-start(f32[268,128]{1,0:T(8,128)S(1)} %pack.1.own_ref), channel_id=1, source_target_pairs={{0,1},{2,3},{1,0},{3,2},{4,5},{6,7},{5,4},{7,6},{8,9},{10,11},{9,8... | collective-permute-start | bytes 411656 | tf_op jit(solution)/shard_map/ppermute | solution.py:485
  6.8 1.8 %base.1 = (f32[1024,128]{1,0:T(8,128)S(1)}, f32[2,32,512]{2,1,0:T(8,128)S(1)}, f32[3,8,512]{2,1,0:T(8,128)S(1)}, s32[4,8]{1,0:T(4,128)S(1)}, f32[2,32,512]{2,1,0...) custom-call(f32[32,8,512]{2,1,0:T(8,128)S(1)} %bitcast.8, ...), custom_call_target="tpu_custom_call" | custom-call | tf_op jit(solution)/shard_map/base/pallas_call | solution.py:489
  8.6 0.0 collective-permute-done.got_ref
  8.7 1.4 %near.1 = (f32[32,8,512]{2,1,0:T(8,128)}, f32[32,1,64]{2,1,0:T(1,128)S(1)}) custom-call(f32[32,32]{1,0:T(8,128)S(1)} %get-tuple-element.19.d_ref, f32[3,8,512]{2,1,0:T(8,128)S(1)} %get-tuple-element.21.excess_ref, f32[2,32,512]{2,1,0:T(8,128)S(1)} %get-tuple-element.22.edge_ref, bf16[64,192]{1,0:T(8,128)(2,1)S(1)} %get-tuple-element.23.pair_ref, ...), custom_call_target="tpu_custom_call" | custom-call | tf_op jit(solution)/shard_map/near/pallas_call | solution.py:517
  10.1 0.0 collective-permute-done.1.got_ref
  10.1 0.7 %far.1 = (f32[2,32,512]{2,1,0:T(8,128)S(1)}, f32[32,1,64]{2,1,0:T(1,128)S(1)}) custom-call(f32[272,128]{1,0:T(8,128)S(1)} %get-tuple-element.29.own_ref, f32[272,128]{1,0:T(8,128)S(1)} %collective-permute-done.1.got_ref, f32[32,32]{1,0:T(8,128)S(1)} %get-tuple-element.19.d_ref, f32[3,8,512]{2,1,0:T(8,128)S(1)} %get-tuple-element.21.excess_ref, ...), custom_call_target="tpu_custom_call" | custom-call | tf_op jit(solution)/shard_map/far/pallas_call | solution.py:530
  10.8 12.3 %all_to_all.5.got_ref = f32[32,1,64]{2,1,0:T(1,128)S(1)} all-to-all(f32[32,1,64]{2,1,0:T(1,128)S(1)} %get-tuple-element.33), channel_id=1, replica_groups=mesh['blade'=8,'span'=4] {'blade','span'}, dimensions={0} | all-to-all | bytes 16384 | tf_op jit(solution)/shard_map/all_to_all | solution.py:539
  23.1 0.7 %finish.1 = (f32[32,8,512]{2,1,0:T(8,128)}, f32[64]{0:T(128)}) custom-call(f32[32,8,512]{2,1,0:T(8,128)} %get-tuple-element.28._, f32[2,32,512]{2,1,0:T(8,128)S(1)} %get-tuple-element.32.two_ref, f32[32,1,64]{2,1,0:T(1,128)S(1)} %all_to_all.5.got_ref), custom_call_target="tpu_custom_call", output_to_operand_aliasing={{0}: (0, {})} | custom-call | tf_op jit(solution)/shard_map/finish/pallas_call | solution.py:540
Async XLA Ops:
  0.6 1.8 %copy-start = (f32[1,32,8,512]{3,2,1,0:T(8,128)S(1)}, f32[1,32,8,512]{3,2,1,0:T(8,128)}, u32[]{:S(2)}) copy-start(f32[1,32,8,512]{3,2,1,0:T(8,128)} %param.6) | copy-start | bytes 1572868
  1.7 8.4 %collective-permute-start.1 = (f32[272,128]{1,0:T(8,128)S(1)}, f32[272,128]{1,0:T(8,128)S(1)}, u32[]{:S(2)}, u32[]{:S(2)}) collective-permute-start(f32[272,128]{1,0:T(8,128)S(1)} %get-tuple-element.29.own_ref), channel_id=1, source_target_pairs={{1,2},{2,1},{5,6},{6,5},{9,10},{10,9},{13,14},{14,13},{17,18},{18,... | collective-permute-start | bytes 417800 | tf_op jit(solution)/shard_map/ppermute | solution.py:486
  2.5 6.2 %collective-permute-start = (f32[268,128]{1,0:T(8,128)S(1)}, f32[268,128]{1,0:T(8,128)S(1)}, u32[]{:S(2)}, u32[]{:S(2)}) collective-permute-start(f32[268,128]{1,0:T(8,128)S(1)} %pack.1.own_ref), channel_id=1, source_target_pairs={{0,1},{2,3},{1,0},{3,2},{4,5},{6,7},{5,4},{7,6},{8,9},{10,11},{9,8... | collective-permute-start | bytes 411656 | tf_op jit(solution)/shard_map/ppermute | solution.py:485
